TPU v7x, 128 devices: a whole 4x4x4 slice. The times are simulated.
128 devices in a mesh: dp: 16 (over y_lo, z, core), vocab: 8 (over x, y_hi).
Axes of the slice: x: 4, y: 4 (y_hi: 2, y_lo: 2; y = y_hi * 2 + y_lo), z: 4, core: 2. Of those that a mesh axis runs over, the one named last changes fastest.
Arguments:
- student_hidden: bfloat16 [8192, 2560], P(('dp', 'vocab')), may hold values from -6 to 6
- teacher_hidden: bfloat16 [8192, 5120], P(('dp', 'vocab')), may hold values from -6 to 6
- student_head: bfloat16 [9216, 2560], P('vocab'), may hold values from -0.375 to 0.375
- teacher_head: bfloat16 [9216, 5120], P('vocab'), may hold values from -0.25 to 0.25
- sampled_ids: int32 [8192], P('dp'), may hold values from 0 to 9215
Outputs:
- hidden_grad: bfloat16 [8192, 2560], P(('dp', 'vocab'))
- head_grad: bfloat16 [9216, 2560], P(('vocab', 'dp'))
All inputs are finite; a program needn't handle non-finite values.
Results may differ from a plain program's by a relative error of at most 0.005.
Values may be sent and summed in bfloat16 or wider, within the bound.
No kernel may reach another device: no remote copies, remote signals or barrier semaphores. Data moves between devices by JAX's collectives and lax.ppermute only.
A program may use at most 192 MiB of HBM per device.

v0:
```python
import jax
import jax.numpy as jnp
from jax import lax
from jax.sharding import PartitionSpec as P


def logits_of(hidden, head):
    return lax.dot_general(
        hidden, head, (((1,), (1,)), ((), ())), preferred_element_type=jnp.float32
    )


def block_sums(rows_student, rows_teacher, student_head, teacher_head, ids_block, columns):
    student_logits = logits_of(rows_student, student_head)
    teacher_logits = logits_of(rows_teacher, teacher_head)
    picked = ids_block[:, None] == columns[None, :]
    totals = lax.psum(
        (
            jnp.sum(jnp.exp(student_logits), axis=1),
            jnp.sum(jnp.exp(teacher_logits), axis=1),
            jnp.sum(jnp.where(picked, student_logits, 0.0), axis=1),
            jnp.sum(jnp.where(picked, teacher_logits, 0.0), axis=1),
        ),
        "vocab",
    )
    return (student_logits, totals)


def on_device(student_hidden, teacher_hidden, student_head, teacher_head, sampled_ids):
    vocab_rows = student_head.shape[0]
    columns = lax.axis_index("vocab") * vocab_rows + lax.iota(jnp.int32, vocab_rows)
    student_rows, teacher_rows = (
        lax.all_gather(student_hidden, "vocab", axis=0, tiled=True),
        lax.all_gather(teacher_hidden, "vocab", axis=0, tiled=True),
    )
    student_logits, totals = block_sums(
        student_rows, teacher_rows, student_head, teacher_head, sampled_ids, columns
    )
    student_norm = jnp.log(totals[0])
    teacher_norm = jnp.log(totals[1])
    advantage = totals[3] - teacher_norm - (totals[2] - student_norm)
    onehot = jnp.where(columns[None, :] == sampled_ids[:, None], 1.0, 0.0)
    probs = jnp.exp(student_logits - student_norm[:, None])
    logit_grad = (advantage[:, None] * (probs - onehot)).astype(jnp.bfloat16)
    block = logit_grad
    hidden_grad = lax.psum_scatter(
        jnp.dot(block, student_head, preferred_element_type=jnp.float32),
        "vocab",
        scatter_dimension=0,
        tiled=True,
    ).astype(jnp.bfloat16)
    block = logit_grad
    head_grad = lax.psum_scatter(
        lax.dot_general(
            block, student_rows, (((0,), (0,)), ((), ())), preferred_element_type=jnp.float32
        ),
        "dp",
        scatter_dimension=0,
        tiled=True,
    ).astype(jnp.bfloat16)
    return (hidden_grad, head_grad)


def solution(mesh):
    in_specs = (
        P(("dp", "vocab"), None),
        P(("dp", "vocab"), None),
        P("vocab", None),
        P("vocab", None),
        P("dp"),
    )
    out_specs = (P(("dp", "vocab"), None), P(("vocab", "dp"), None))
    return jax.shard_map(
        on_device, mesh=mesh, in_specs=in_specs, out_specs=out_specs, check_vma=False
    )
```

profile of v0, /device:TPU:0, one launch (start us, length us, event | category | flops | bytes accessed | tf_op | source)
XLA Modules:
  0.0 375.1 jit_solution(7573919163754894366)
XLA Ops:
  7.2 0.0 all-gather.5.cloned.1.call-start
  7.2 0.7 all-gather.5.cloned.1.call-update
  7.9 0.0 all-gather.3.cloned.1.call-start
  7.9 0.7 all-gather.3.cloned.1.call-update
  8.6 0.0 reduce-scatter.3.cloned.1.call-start
  8.7 0.0 copy-start.1
  8.7 62.9 %all-gather.5.cloned.1.call-done = bf16[512,2560]{1,0:T(8,128)(2,1)} async-done(((bf16[64,2560]{1,0:T(8,128)(2,1)}), bf16[512,2560]{1,0:T(8,128)(2,1)}) %all-gather.5.cloned.1.call-update) | async-done | bytes 2621456 | tf_op jit(solution)/shard_map/all_gather | solution.py:33
  71.6 7.0 %fusion.4 = f32[512,1152]{1,0:T(8,128)S(1)} fusion(bf16[512,2560]{1,0:T(8,128)(2,1)} %all-gather.5.cloned.1.call-done, bf16[1152,2560]{1,0:T(8,128)(2,1)} %param.7), kind=kOutput, calls=%fused_computation.11 | convolution fusion | flops 3019898880 | bytes 10878976 | tf_op jit(solution)/shard_map/dot_general | solution.py:8
  78.6 0.0 copy-start.2
  78.6 74.4 %all-gather.3.cloned.1.call-done = bf16[512,5120]{1,0:T(8,128)(2,1)} async-done(((bf16[64,5120]{1,0:T(8,128)(2,1)}), bf16[512,5120]{1,0:T(8,128)(2,1)}) %all-gather.3.cloned.1.call-update) | async-done | bytes 5242896 | tf_op jit(solution)/shard_map/all_gather | solution.py:34
  153.0 0.0 copy-done.1
  153.0 12.8 %exponential_reduce_fusion.1 = (f32[512]{0:T(512)S(1)}, f32[512]{0:T(512)S(1)}, f32[512]{0:T(512)S(1)}, f32[512]{0:T(512)S(1)}) fusion(s32[1152]{0:T(1024)S(1)} %iota_add_fusion, s32[512]{0:T(512)S(1)} %copy-done.1, f32[512,1152]{1,0:T(8,128)S(1)} %fusion.4, bf16[512,5120]{1,0:T(8,128)(2,1)} %all-gather.3.cloned.1.call-done, bf16[1152,5120]{1,0:T(8,128)(2,1)} %param.8), kind=kOutput, calls=%fused_computation.6 | convolution fusion | flops 6043924480 | bytes 19413504 | tf_op jit(solution)/shard_map/dot_general | solution.py:8
  165.9 20.0 %all-reduce = (f32[512]{0:T(512)S(1)}, f32[512]{0:T(512)S(1)}, f32[512]{0:T(512)S(1)}, f32[512]{0:T(512)S(1)}) all-reduce(f32[512]{0:T(512)S(1)} %get-tuple-element.6, f32[512]{0:T(512)S(1)} %get-tuple-element.7, f32[512]{0:T(512)S(1)} %get-tuple-element.3, f32[512]{0:T(512)S(1)} %get-tuple-element.2), channel_id=1, replica_groups=mesh['dp'=16,'vocab'=8] {'vocab'}, use_global_device_ids=true, to_apply=%region_7.8 | all-reduce | flops 2048 | bytes 16384 | tf_op jit(solution)/shard_map/psum | solution.py:17
  185.9 0.0 copy-done.2
  185.9 8.3 %fusion.3 = f32[512,2560]{1,0:T(8,128)} fusion(bf16[1152,2560]{1,0:T(8,128)(2,1)} %param.7, f32[512,1152]{1,0:T(8,128)S(1)} %fusion.4, f32[512]{0:T(512)S(1)} %get-tuple-element.13, f32[512]{0:T(512)S(1)} %get-tuple-element.12, s32[1152]{0:T(1024)S(1)} %iota_add_fusion, s32[512]{0:T(512)S(1)} %copy-done.1), kind=kOutput, calls=%fused_computation.10 | convolution fusion | flops 3023437824 | bytes 13511168 | tf_op jit(solution)/shard_map/dot_general | solution.py:47
  194.2 0.0 copy-start
  194.2 0.0 reduce-scatter.3.cloned.1.call-update
  194.2 0.0 reduce-scatter.5.cloned.1.call-start
  194.3 1.7 copy-done
  195.9 8.2 %fusion.2 = f32[1152,2560]{1,0:T(8,128)} fusion(bf16[512,2560]{1,0:T(8,128)(2,1)S(1)} %copy-done, f32[512,1152]{1,0:T(8,128)} %copy-done.2, f32[512]{0:T(512)S(1)} %get-tuple-element.13, f32[512]{0:T(512)S(1)} %get-tuple-element.12, s32[1152]{0:T(1024)S(1)} %iota_add_fusion, s32[512]{0:T(512)S(1)} %copy-done.1), kind=kOutput, calls=%fused_computation.9 | convolution fusion | flops 3023437824 | bytes 16787968 | tf_op jit(solution)/shard_map/dot_general | solution.py:54
  204.2 0.0 reduce-scatter.5.cloned.1.call-update
  204.2 80.1 %reduce-scatter.3.cloned.1.call-done = f32[64,2560]{1,0:T(8,128)} async-done(((f32[512,2560]{1,0:T(8,128)}), f32[64,2560]{1,0:T(8,128)}) %reduce-scatter.3.cloned.1.call-update) | async-done | bytes 655376 | tf_op jit(solution)/shard_map/reduce_scatter | solution.py:46
  284.3 1.8 convert_element_type.10
  286.1 80.5 %reduce-scatter.5.cloned.1.call-done = f32[72,2560]{1,0:T(8,128)} async-done(((f32[1152,2560]{1,0:T(8,128)}), f32[72,2560]{1,0:T(8,128)}) %reduce-scatter.5.cloned.1.call-update) | async-done | bytes 737296 | tf_op jit(solution)/shard_map/reduce_scatter | solution.py:53
  366.6 1.9 convert_element_type.11
  (2 shorter events, 0.0 us)
Async XLA Ops:
  7.2 64.4 %all-gather.5.cloned.1.call-start = ((), (), s32[]{:S(2)}) async-start(), calls=%async_computation.3 | async-start | bytes 2949120 | tf_op jit(solution)/shard_map/all_gather | solution.py:33
  7.9 145.1 %all-gather.3.cloned.1.call-start = ((), (), s32[]{:S(2)}) async-start(), calls=%async_computation.2 | async-start | bytes 5898240 | tf_op jit(solution)/shard_map/all_gather | solution.py:34
  8.6 275.6 %reduce-scatter.3.cloned.1.call-start = ((), (), s32[]{:S(2)}) async-start(), calls=%async_computation.4 | async-start | bytes 5898240 | tf_op jit(solution)/shard_map/reduce_scatter | solution.py:46
  8.7 144.3 %copy-start.1 = (s32[512]{0:T(512)S(1)}, s32[512]{0:T(512)}, u32[]{:S(2)}) copy-start(s32[512]{0:T(512)} %param.9) | copy-start | bytes 6148
  78.6 107.3 %copy-start.2 = (f32[512,1152]{1,0:T(8,128)}, f32[512,1152]{1,0:T(8,128)S(1)}, u32[]{:S(2)}) copy-start(f32[512,1152]{1,0:T(8,128)S(1)} %fusion.4) | copy-start | bytes 7077892
  194.2 1.7 copy-start
  194.2 172.4 %reduce-scatter.5.cloned.1.call-start = ((), (), s32[]{:S(2)}) async-start(), calls=%async_computation.5 | async-start | bytes 12533760 | tf_op jit(solution)/shard_map/reduce_scatter | solution.py:53
Sparse Core Ops, SparseCore 0:
  10.3 61.2 all-gather.4
  73.9 79.0 all-gather.2
  194.4 89.8 reduce-scatter.2
  286.7 79.9 reduce-scatter.4
where the time goes:
time: 375 us
  waiting for transfers between devices  299 us (80%)
  matrix products  36.4 us (10%)
  blocking collectives  20 us (5%)
  between operations  13.8 us (4%)
  other arithmetic  3.75 us (1%)
    reduce_scatter x1, waiting for transfers between devices, on_device(): lax.psum_scatter(lax.dot_general(block, student_rows, (((0,), (0,)), ((),...  80.5 us
    reduce_scatter x1, waiting for transfers between devices, on_device(): lax.psum_scatter(jnp.dot(block, student_head, preferred_element_type=jnp....  80.1 us
    all_gather x1, waiting for transfers between devices, on_device(): lax.all_gather(teacher_hidden, 'vocab', axis=0, tiled=True)  74.4 us
    all_gather x1, waiting for transfers between devices, on_device(): lax.all_gather(student_hidden, 'vocab', axis=0, tiled=True)  62.9 us
    psum x1, blocking collectives, block_sums(): lax.psum((jnp.sum(jnp.exp(student_logits), axis=1), jnp.sum(jnp.exp(teach...  20 us
    dot_general x2, matrix products, logits_of(): lax.dot_general(hidden, head, (((1,), (1,)), ((), ())), preferred_element...  19.9 us
    dot_general x1, matrix products, on_device(): jnp.dot(block, student_head, preferred_element_type=jnp.float32)  8.31 us
    dot_general x1, matrix products, on_device(): lax.dot_general(block, student_rows, (((0,), (0,)), ((), ())), preferred_...  8.21 us
  transfers between devices with their start and end apart: 4, of which 4 were waited for; matrix products, arithmetic and copies ran while one was open for 5% of the time, Pallas kernels for 0%

commit v1 on v0

v1 whole, which is shorter than its diff:
```python
import functools

import jax
import jax.numpy as jnp
from jax import lax
from jax.experimental import pallas as pl
from jax.experimental.pallas import tpu as pltpu
from jax.sharding import PartitionSpec as P

BF16 = jnp.bfloat16
F32 = jnp.float32
AXES = ("dp", "vocab")

REL = ((0, 0), (-1, 0), (1, 0), (2, 0), (0, 1), (-1, 1), (1, 1), (2, 1))


def pairs(move):
    out = []
    for i in range(128):
        dp, v = i // 8, i % 8
        y_lo, z, core, x, y_hi = dp // 8, (dp // 2) % 4, dp % 2, v // 2, v % 2
        x, y, z, core = move(x, y_hi * 2 + y_lo, z, core)
        x, y, z = x % 4, y % 4, z % 4
        out.append((i, (((y % 2) * 4 + z) * 2 + core) * 8 + x * 2 + y // 2))
    return out


X_UP = pairs(lambda x, y, z, c: (x + 1, y, z, c))
X_DOWN = pairs(lambda x, y, z, c: (x - 1, y, z, c))
X_FAR = pairs(lambda x, y, z, c: (x + 2, y, z, c))
Y_HI = pairs(lambda x, y, z, c: (x, 3 - y, z, c))
Z_UP = pairs(lambda x, y, z, c: (x, y, z + 1, c))
Z_DOWN = pairs(lambda x, y, z, c: (x, y, z - 1, c))
Y_LO = pairs(lambda x, y, z, c: (x, y ^ 1, z, c))
CORE = pairs(lambda x, y, z, c: (x, y, z, 1 - c))


def send(a, to):
    return lax.ppermute(a, AXES, to)


def after(a, *others):
    return lax.optimization_barrier((a, *others))[0]


def params(mib):
    return pltpu.CompilerParams(vmem_limit_bytes=mib * 2**20)


def whole(shape):
    return pl.BlockSpec(shape, lambda *_: (0,) * len(shape))


SMEM = pl.BlockSpec(memory_space=pltpu.SMEM)


def fold(a):
    return jnp.sum(a.reshape(a.shape[0] // 8, 8, a.shape[1]), axis=0)


def add_stats(j, last, logits, ids_ref, base, stats_ref, sums, picks):
    rows = lax.broadcasted_iota(jnp.int32, logits.shape, 0) + (base + j * logits.shape[0])
    some = fold(jnp.exp(logits))
    pick = fold(jnp.where(rows == ids_ref[...], logits, 0.0))

    @pl.when(j == 0)
    def _():
        sums[...] = some
        picks[...] = pick

    @pl.when(j > 0)
    def _():
        sums[...] += some
        picks[...] += pick

    @pl.when(j == last)
    def _():
        stats_ref[...] = jnp.zeros_like(stats_ref)
        stats_ref[0:1, :] = jnp.sum(sums[...], axis=0, keepdims=True)
        stats_ref[1:2, :] = jnp.sum(picks[...], axis=0, keepdims=True)


NT = (((1,), (1,)), ((), ()))
NN = (((1,), (0,)), ((), ()))


def student_kernel(last, pos, ids, own, left, right, near, left_near, right_near, far_a, far_b, far_near_a,
                   far_near_b, head, logits, hidden, stats, sums, picks):
    j = pl.program_id(0)

    @pl.when(j == 0)
    def _():
        halves = [(r[0:32, :], r[32:64, :]) for r in (own, left, right)]
        halves.append((far_a[...], far_b[...]))
        halves += [(r[0:32, :], r[32:64, :]) for r in (near, left_near, right_near)]
        halves.append((far_near_a[...], far_near_b[...]))
        for r in range(8):
            for h in range(2):
                hidden[pl.ds(pl.multiple_of(h * 256 + pos[r] * 32, 32), 32), :] = halves[r][h]

    out = lax.dot_general(head[...], hidden[...], NT, preferred_element_type=F32)
    logits[...] = out
    add_stats(j, last, out, ids, pos[8], stats, sums, picks)


def student_logits(pos, ids, blocks, head, tile=384):
    v, d = head.shape
    return pl.pallas_call(
        functools.partial(student_kernel, v // tile - 1),
        grid=(v // tile,),
        in_specs=[SMEM, whole((1, 512))]
        + [whole(b.shape) for b in blocks]
        + [pl.BlockSpec((tile, d), lambda j: (j, 0))],
        out_specs=[pl.BlockSpec((tile, 512), lambda j: (j, 0)), whole((512, d)), whole((8, 512))],
        out_shape=[
            jax.ShapeDtypeStruct((v, 512), F32),
            jax.ShapeDtypeStruct((512, d), BF16),
            jax.ShapeDtypeStruct((8, 512), F32),
        ],
        scratch_shapes=[pltpu.VMEM((8, 512), F32)] * 2,
        compiler_params=params(40),
        cost_estimate=pl.CostEstimate(flops=2 * v * 512 * d, bytes_accessed=2 * v * d + 8 * 512 * d, transcendentals=v * 512),
    )(pos, ids, *blocks, head)


def teacher_kernel(last, pos, ids, *refs):
    blocks, (head, stats, hidden, sums, picks) = refs[:8], refs[8:]
    j = pl.program_id(0)

    @pl.when(j == 0)
    def _():
        for r in range(8):
            hidden[pl.ds(pl.multiple_of(pos[r] * 32, 32), 32), :] = blocks[r][...]

    out = lax.dot_general(head[...], hidden[...], NT, preferred_element_type=F32)
    add_stats(j, last, out, ids, pos[8], stats, sums, picks)


def teacher_stats(pos, ids, blocks, head, tile=384):
    v, d = head.shape
    return pl.pallas_call(
        functools.partial(teacher_kernel, v // tile - 1),
        grid=(v // tile,),
        in_specs=[SMEM, whole((1, 256))]
        + [whole(b.shape) for b in blocks]
        + [pl.BlockSpec((tile, d), lambda j: (j, 0))],
        out_specs=whole((8, 256)),
        out_shape=jax.ShapeDtypeStruct((8, 256), F32),
        scratch_shapes=[pltpu.VMEM((256, d), BF16)] + [pltpu.VMEM((8, 256), F32)] * 2,
        compiler_params=params(40),
        cost_estimate=pl.CostEstimate(flops=2 * v * 256 * d, bytes_accessed=2 * v * d + 512 * d, transcendentals=v * 256),
    )(pos, ids, *blocks, head)


def hidden_kernel(pos, ids, total, logits, head, own, left, right, near, left_near, right_near, far_a, far_b,
                  far_near, grad_t, product):
    @pl.when(pl.program_id(0) == 0)
    def _():
        norm = jnp.log(total[0:1, :])
        for k in range(9):
            rows = lax.broadcasted_iota(jnp.int32, (128, 512), 0) + (pos[8] + k * 128)
            onehot = jnp.where(rows == ids[...], 1.0, 0.0)
            part = jnp.exp(logits[k * 128:(k + 1) * 128, :] - norm) - onehot
            grad_t[:, k * 128:(k + 1) * 128] = part.T.astype(BF16)

    product[...] = lax.dot_general(grad_t[...], head[...], NN, preferred_element_type=F32)

    def rows_of(r, h):
        return product[pl.ds(pl.multiple_of(h * 256 + pos[r] * 32, 32), 32), :]

    for r, out in ((0, own), (1, left), (2, right), (4, near), (5, left_near), (6, right_near), (7, far_near)):
        for h in range(2):
            out[h * 32:(h + 1) * 32, :] = rows_of(r, h).astype(out.dtype)
    far_a[...] = rows_of(3, 0).astype(far_a.dtype)
    far_b[...] = rows_of(3, 1).astype(far_b.dtype)


def hidden_parts(pos, ids, total, logits, head, tile=512):
    v, d = head.shape
    shapes = [(64, F32)] * 4 + [(64, BF16)] * 2 + [(32, F32)] * 2 + [(64, BF16)]
    return pl.pallas_call(
        hidden_kernel,
        grid=(d // tile,),
        in_specs=[SMEM, whole((1, 512)), whole((8, 512)), whole((v, 512)), pl.BlockSpec((v, tile), lambda j: (0, j))],
        out_specs=[pl.BlockSpec((n, tile), lambda j: (0, j)) for n, _ in shapes],
        out_shape=[jax.ShapeDtypeStruct((n, d), t) for n, t in shapes],
        scratch_shapes=[pltpu.VMEM((512, v), BF16), pltpu.VMEM((512, tile), F32)],
        compiler_params=params(40),
        cost_estimate=pl.CostEstimate(flops=2 * v * 512 * d, bytes_accessed=2 * v * d + 4 * v * 512 + 1500 * d, transcendentals=v * 512),
    )(pos, ids, total, logits, head)


def grad_kernel(pos, ids, total, total_a, total_b, logits, mine, other, adv, mine_f, other_f):
    student = total[1:2, :] - jnp.log(total[0:1, :])
    adv[:, 0:256] = (total_a[1:2, :] - jnp.log(total_a[0:1, :])) - student[:, 0:256]
    adv[:, 256:512] = (total_b[1:2, :] - jnp.log(total_b[0:1, :])) - student[:, 256:512]
    norm = jnp.log(total[0:1, :])
    for r in range(8):
        for out, core in ((mine_f, pos[17]), (other_f, 1 - pos[17])):
            start = pl.multiple_of(pos[9 + r] * 144 + core * 72, 8)
            rows = lax.broadcasted_iota(jnp.int32, (72, 512), 0) + (pos[8] + start)
            onehot = jnp.where(rows == ids[...], 1.0, 0.0)
            probs = jnp.exp(logits[pl.ds(start, 72), :] - norm)
            out[r * 72:(r + 1) * 72, :] = adv[...] * (probs - onehot)
    mine[...] = mine_f[...].astype(BF16)
    other[...] = other_f[...].astype(BF16)


def logit_grads(pos, ids, total, total_a, total_b, logits):
    v = logits.shape[0]
    half = v // 2
    return pl.pallas_call(
        grad_kernel,
        in_specs=[SMEM, whole((1, 512)), whole((8, 512)), whole((8, 256)), whole((8, 256)), whole((v, 512))],
        out_specs=[whole((half, 512)), whole((half, 512)), whole((1, 512))],
        out_shape=[jax.ShapeDtypeStruct((half, 512), BF16)] * 2 + [jax.ShapeDtypeStruct((1, 512), F32)],
        scratch_shapes=[pltpu.VMEM((half, 512), F32)] * 2,
        compiler_params=params(40),
        cost_estimate=pl.CostEstimate(flops=4 * v * 512, bytes_accessed=6 * v * 512, transcendentals=v * 512),
    )(pos, ids, total, total_a, total_b, logits)


def head_kernel(first, grad_mine, grad_from, hidden, hidden_from, *outs):
    rows = slice(first * 72, (first + len(outs)) * 72)
    product = lax.dot_general(grad_mine[rows, :], hidden[...], NN, preferred_element_type=F32)
    product += lax.dot_general(grad_from[rows, :], hidden_from[...], NN, preferred_element_type=F32)
    for i, out in enumerate(outs):
        out[...] = product[i * 72:(i + 1) * 72, :].astype(out.dtype)


def head_parts(first, types, grad_mine, grad_from, hidden, hidden_from, tile=512):
    half, d = grad_mine.shape[0], hidden.shape[1]
    n = len(types)
    column = lambda j: (0, j)
    return pl.pallas_call(
        functools.partial(head_kernel, first),
        grid=(d // tile,),
        in_specs=[whole((half, 512))] * 2 + [pl.BlockSpec((512, tile), column)] * 2,
        out_specs=[pl.BlockSpec((72, tile), column)] * n,
        out_shape=[jax.ShapeDtypeStruct((72, d), t) for t in types],
        compiler_params=params(40),
        cost_estimate=pl.CostEstimate(flops=2 * n * 72 * 1024 * d, bytes_accessed=4096 * d + n * 72 * 4 * d, transcendentals=0),
    )(grad_mine, grad_from, hidden, hidden_from)


def group_sum(a):
    around = a + send(a, X_UP) + send(a, X_DOWN) + send(a, X_FAR)
    return around + send(around, Y_HI)


def on_device(student_hidden, teacher_hidden, student_head, teacher_head, sampled_ids):
    dp, v = lax.axis_index("dp"), lax.axis_index("vocab")
    y_lo, z, core, x, y_hi = dp // 8, (dp // 2) % 4, dp % 2, v // 2, v % 2
    places = [((x + dx) % 4) * 2 + (y_hi + dy) % 2 for dx, dy in REL]
    order = ((2, 1), (-1, 1), (1, 1), (2, 0), (-1, 0), (1, 0), (0, 1), (0, 0))
    chips = [((y_lo + dy) % 2) * 4 + (z + dz) % 4 for dz, dy in order]
    pos = jnp.stack([*places, v * student_head.shape[0], *chips, core]).astype(jnp.int32)

    ids_near = send(sampled_ids, Y_HI)
    ids = jnp.where(lax.iota(jnp.int32, 512) // 64 % 2 == y_hi, sampled_ids, ids_near)
    ids = ids.reshape(8, 2, 32).transpose(1, 0, 2).reshape(1, 512)

    own = student_hidden
    left, right, near = send(own, X_UP), send(own, X_DOWN), send(own, Y_HI)
    left_near, right_near = send(near, X_UP), send(near, X_DOWN)
    far_a, far_b = send(left[:32], X_UP), send(right[32:], X_DOWN)
    far_near_a, far_near_b = send(far_a, Y_HI), send(far_b, Y_HI)
    s_blocks = (own, left, right, near, left_near, right_near, far_a, far_b, far_near_a, far_near_b)

    t_a = after(teacher_hidden[:32], left, right, near)
    l_a, r_a, n_a = send(t_a, X_UP), send(t_a, X_DOWN), send(t_a, Y_HI)
    ln_a, rn_a, f_a = send(n_a, X_UP), send(n_a, X_DOWN), send(l_a, X_UP)
    fn_a = send(f_a, Y_HI)
    t_b = after(teacher_hidden[32:], l_a, r_a, n_a)
    l_b, r_b, n_b = send(t_b, X_UP), send(t_b, X_DOWN), send(t_b, Y_HI)
    ln_b, rn_b, f_b = send(n_b, X_UP), send(n_b, X_DOWN), send(r_b, X_DOWN)
    fn_b = send(f_b, Y_HI)

    logits, hidden, stats = student_logits(pos, ids, s_blocks, student_head)
    hidden_from = send(hidden, CORE)
    total = group_sum(stats)
    g_own, g_left, g_right, g_near, g_ln, g_rn, g_fa, g_fb, g_fn = hidden_parts(pos, ids, total, logits, student_head)

    stats_a = teacher_stats(pos, ids[:, :256], (t_a, l_a, r_a, f_a, n_a, ln_a, rn_a, fn_a), teacher_head)
    total_a = group_sum(stats_a)
    stats_b = teacher_stats(pos, ids[:, 256:], (t_b, l_b, r_b, f_b, n_b, ln_b, rn_b, fn_b), teacher_head)
    total_b = group_sum(stats_b)

    from_fn = send(g_fn, Y_HI).astype(F32)
    from_fa = send((g_fa + from_fn[:32]).astype(BF16), X_DOWN).astype(F32)
    from_fb = send((g_fb + from_fn[32:]).astype(BF16), X_UP).astype(F32)
    near_sum = g_near + send(g_ln, X_DOWN).astype(F32) + send(g_rn, X_UP).astype(F32)
    left_sum = jnp.concatenate([g_left[:32] + from_fa, g_left[32:]])
    right_sum = jnp.concatenate([g_right[:32], g_right[32:] + from_fb])
    hidden_sum = (
        g_own
        + send(near_sum.astype(BF16), Y_HI).astype(F32)
        + send(left_sum.astype(BF16), X_DOWN).astype(F32)
        + send(right_sum.astype(BF16), X_UP).astype(F32)
    )

    mine, other, adv = logit_grads(pos, ids, total, total_a, total_b, logits)
    from_core = send(other, CORE)
    h_fl, h_ll, h_rl, h_f = head_parts(0, (BF16, BF16, BF16, F32), mine, from_core, hidden, hidden_from)
    h_l, h_r, h_y, h_own = head_parts(4, (F32,) * 4, mine, from_core, hidden, hidden_from)
    far = h_f + send(h_fl, Y_LO).astype(F32)
    cut = far.shape[1] // 2
    far = far.astype(BF16)
    far_left, far_right = send(far[:, :cut], Z_DOWN).astype(F32), send(far[:, cut:], Z_UP).astype(F32)
    y_sum = h_y + send(h_ll, Z_DOWN).astype(F32) + send(h_rl, Z_UP).astype(F32)
    l_sum = jnp.concatenate([h_l[:, :cut] + far_left, h_l[:, cut:]], axis=1)
    r_sum = jnp.concatenate([h_r[:, :cut], h_r[:, cut:] + far_right], axis=1)
    head_sum = (
        h_own
        + send(y_sum.astype(BF16), Y_LO).astype(F32)
        + send(l_sum.astype(BF16), Z_DOWN).astype(F32)
        + send(r_sum.astype(BF16), Z_UP).astype(F32)
    )

    own_adv = jnp.concatenate([lax.dynamic_slice(adv[0], (h * 256 + places[0] * 32,), (32,)) for h in range(2)])
    return (own_adv[:, None] * hidden_sum).astype(BF16), head_sum.astype(BF16)


def solution(mesh):
    in_specs = (
        P(("dp", "vocab"), None),
        P(("dp", "vocab"), None),
        P("vocab", None),
        P("vocab", None),
        P("dp"),
    )
    out_specs = (P(("dp", "vocab"), None), P(("vocab", "dp"), None))
    return jax.shard_map(
        on_device, mesh=mesh, in_specs=in_specs, out_specs=out_specs, check_vma=False
    )
```

time: 375 us -> 190 us (0.51)
  waiting for transfers between devices: 299 us -> 50.3 us
  starting transfers between devices: 0.16 us -> 73.8 us
  matrix products: 36.4 us -> 0 us
  local copies, waits for them, and re-layouts: 1.68 us -> 30.3 us
  Pallas kernels: 0 us -> 28.6 us
  blocking collectives: 20 us -> 0 us
  between operations: 13.8 us -> 1.02 us
    reduce_scatter x2 -> x0, waiting for transfers between devices: 161 us -> none  [the longest x1 80.5 us: on_device(): lax.psum_scatter(lax.dot_general(block, student_rows, (((0,), (0,)), ((),...]
    all_gather x2 -> x0, waiting for transfers between devices: 137 us -> none  [the longest x1 74.4 us: on_device(): lax.all_gather(teacher_hidden, 'vocab', axis=0, tiled=True)]
    ppermute x0 -> x54, starting transfers between devices: none -> 73.8 us  [send(): return lax.ppermute(a, AXES, to)]
    ppermute x0 -> x54, waiting for transfers between devices: none -> 50.3 us  [send(): return lax.ppermute(a, AXES, to)]
    dot_general x4 -> x0, matrix products: 36.4 us -> none  [the longest x2 19.9 us: logits_of(): lax.dot_general(hidden, head, (((1,), (1,)), ((), ())), preferred_element...]
    pallas_call x0 -> x7, Pallas kernels: none -> 28.6 us  [the longest x2 9.61 us: teacher_stats(): pl.pallas_call(functools.partial(teacher_kernel, v // tile - 1), grid=(v...]
    unnamed x6 -> x62, local copies, waits for them, and re-layouts: 1.68 us -> 27.8 us
    psum x1 -> x0, blocking collectives: 20 us -> none  [block_sums(): lax.psum((jnp.sum(jnp.exp(student_logits), axis=1), jnp.sum(jnp.exp(teach...]
  transfers between devices with their start and end apart: 4 -> 54, of which waited for: 4 -> 20; matrix products, arithmetic and copies ran while one was open for 5% -> 4% of each run, Pallas kernels for 0% -> 13%
where the time goes in v1:
time: 190 us; the launch traced here: 189 us
  starting transfers between devices  73.8 us (39%)
  waiting for transfers between devices  50.3 us (26%)
  local copies, waits for them, and re-layouts  30.3 us (16%)
  Pallas kernels  28.6 us (15%)
  other arithmetic  5.31 us (3%)
    ppermute x54, starting transfers between devices, send(): return lax.ppermute(a, AXES, to)  73.8 us
    ppermute x54, waiting for transfers between devices, send(): return lax.ppermute(a, AXES, to)  50.3 us
    unnamed x62, local copies, waits for them, and re-layouts  27.8 us
    pallas_call x2, Pallas kernels, teacher_stats(): pl.pallas_call(functools.partial(teacher_kernel, v // tile - 1), grid=(v...  9.61 us
    pallas_call x1, Pallas kernels, hidden_parts(): pl.pallas_call(hidden_kernel, grid=(d // tile,), in_specs=[SMEM, whole((1...  7.25 us
    pallas_call x2, Pallas kernels, head_parts(): pl.pallas_call(functools.partial(head_kernel, first), grid=(d // tile,),...  5.82 us
    pallas_call x1, Pallas kernels, student_logits(): pl.pallas_call(functools.partial(student_kernel, v // tile - 1), grid=(v...  4.64 us
  transfers between devices with their start and end apart: 54, of which 20 were waited for; matrix products, arithmetic and copies ran while one was open for 4% of the time, Pallas kernels for 13%

profile of v1, /device:TPU:0, one launch (start us, length us, event | category | flops | bytes accessed | tf_op | source)
XLA Modules:
  0.0 189.3 jit_solution(11320462287659040606)
XLA Ops:
  0.6 1.6 collective-permute-start.1
  2.3 1.7 collective-permute-start.2
  3.9 3.1 %collective-permute-start.3 = (bf16[64,2560]{1,0:T(8,128)(2,1)}, bf16[64,2560]{1,0:T(8,128)(2,1)S(1)}, u32[]{:S(2)}, u32[]{:S(2)}) collective-permute-start(bf16[64,2560]{1,0:T(8,128)(2,1)} %own.1), channel_id=1, source_target_pairs={{0,65},{1,64},{2,67},{3,66},{4,69},{5,68},{6,71},{7,70},{8,73},{9,... | collective-permute-start | bytes 983048 | tf_op jit(solution)/shard_map/ppermute | solution.py:39
  7.0 4.4 %collective-permute-done.1.left = bf16[64,2560]{1,0:T(8,128)(2,1)S(1)} collective-permute-done((bf16[64,2560]{1,0:T(8,128)(2,1)}, bf16[64,2560]{1,0:T(8,128)(2,1)S(1)}, u32[]{:S(2)}, u32[]{:S(2)}) %collective-permute-start.1) | collective-permute-done | bytes 327712 | tf_op jit(solution)/shard_map/ppermute | solution.py:39
  12.0 2.8 %collective-permute-start.7 = (bf16[32,2560]{1,0:T(8,128)(2,1)S(1)}, bf16[32,2560]{1,0:T(8,128)(2,1)S(1)}, u32[]{:S(2)}, u32[]{:S(2)}) collective-permute-start(bf16[32,2560]{1,0:T(8,128)(2,1)S(1)} %slice.77), channel_id=1, source_target_pairs={{0,6},{1,7},{2,0},{3,1},{4,2},{5,3},{6,4},{7,5},{8,14},{9,15},{10,... | collective-permute-start | bytes 491528 | tf_op jit(solution)/shard_map/ppermute | solution.py:39
  14.9 3.2 %collective-permute-start.5 = (bf16[64,2560]{1,0:T(8,128)(2,1)S(1)}, bf16[64,2560]{1,0:T(8,128)(2,1)S(1)}, u32[]{:S(2)}, u32[]{:S(2)}) collective-permute-start(bf16[64,2560]{1,0:T(8,128)(2,1)S(1)} %collective-permute-done.3.near), channel_id=1, source_target_pairs={{0,6},{1,7},{2,0},{3,1},{4,2},{5,3},{6,4},{7,5},{8,14},{9,15},{10,... | collective-permute-start | bytes 983048 | tf_op jit(solution)/shard_map/ppermute | solution.py:39
  18.1 3.2 %collective-permute-start = (s32[512]{0:T(512)}, s32[512]{0:T(512)S(1)}, u32[]{:S(2)}, u32[]{:S(2)}) collective-permute-start(s32[512]{0:T(512)} %param.9), channel_id=1, source_target_pairs={{0,65},{1,64},{2,67},{3,66},{4,69},{5,68},{6,71},{7,70},{8,73},{9,... | collective-permute-start | bytes 6152 | tf_op jit(solution)/shard_map/ppermute | solution.py:39
  22.3 2.4 %collective-permute-start.9 = (bf16[32,2560]{1,0:T(8,128)(2,1)S(1)}, bf16[32,2560]{1,0:T(8,128)(2,1)S(1)}, u32[]{:S(2)}, u32[]{:S(2)}) collective-permute-start(bf16[32,2560]{1,0:T(8,128)(2,1)S(1)} %collective-permute-done.7.far_b), channel_id=1, source_target_pairs={{0,65},{1,64},{2,67},{3,66},{4,69},{5,68},{6,71},{7,70},{8,73},{9,... | collective-permute-start | bytes 491528 | tf_op jit(solution)/shard_map/ppermute | solution.py:39
  28.8 1.1 collective-permute-done.9.far_near_b
  30.6 2.7 %copy-done.14 = bf16[1152,2560]{1,0:T(8,128)(2,1)S(1)} copy-done((bf16[1152,2560]{1,0:T(8,128)(2,1)S(1)}, bf16[1152,2560]{1,0:T(8,128)(2,1)}, u32[]{:S(2)}) %copy-start.14) | copy-done | bytes 5898264
  33.3 1.0 copy-done.15
  34.2 1.0 copy-done.17
  35.2 1.0 copy-done.19
  36.2 1.0 copy-done.21
  39.9 4.6 %shard_map.68 = (f32[1152,512]{1,0:T(8,128)S(1)}, bf16[512,2560]{1,0:T(8,128)(2,1)S(1)}, f32[8,512]{1,0:T(8,128)S(1)}) custom-call(s32[18]{0:T(128)S(1)} %stack.75.pos, s32[1,512]{1,0:T(1,128)S(1)} %reshape.14.ids, bf16[64,2560]{1,0:T(8,128)(2,1)S(1)} %copy-done.15, bf16[64,2560]{1,0:T(8,128)(2,1)S(1)} %collective-permute-done.1.left, ...), custom_call_target="tpu_custom_call" | custom-call | flops 3019898880 | bytes 16384000 | tf_op jit(solution)/shard_map/pallas_call | solution.py:108
  44.9 1.5 collective-permute-start.11
  46.9 3.0 %collective-permute-done.12 = f32[8,512]{1,0:T(8,128)S(1)} collective-permute-done((f32[8,512]{1,0:T(8,128)S(1)}, f32[8,512]{1,0:T(8,128)S(1)}, u32[]{:S(2)}, u32[]{:S(2)}) %collective-permute-start.12) | collective-permute-done | bytes 16416 | tf_op jit(solution)/shard_map/ppermute | solution.py:39
  49.9 1.5 collective-permute-done.10
  51.4 1.4 collective-permute-start.13
  52.9 3.2 %collective-permute-start.15 = (bf16[32,5120]{1,0:T(8,128)(2,1)S(1)}, bf16[32,5120]{1,0:T(8,128)(2,1)}, u32[]{:S(2)}, u32[]{:S(2)}) collective-permute-start(bf16[32,5120]{1,0:T(8,128)(2,1)S(1)} %get-tuple-element.28.refs_0_), channel_id=1, source_target_pairs={{0,6},{1,7},{2,0},{3,1},{4,2},{5,3},{6,4},{7,5},{8,14},{9,15},{10,... | collective-permute-start | bytes 983048 | tf_op jit(solution)/shard_map/ppermute | solution.py:39
  56.1 1.8 collective-permute-start.17
  58.0 7.2 %shard_map.72 = (f32[64,2560]{1,0:T(8,128)S(1)}, f32[64,2560]{1,0:T(8,128)S(1)}, f32[64,2560]{1,0:T(8,128)S(1)}, f32[64,2560]{1,0:T(8,128)S(1)}, bf16[64,2560]{1...) custom-call(s32[18]{0:T(128)S(1)} %stack.75.pos, ...), custom_call_target="tpu_custom_call" | custom-call | flops 3019898880 | bytes 12097536 | tf_op jit(solution)/shard_map/pallas_call | solution.py:181
  71.6 1.4 collective-permute-start.39
  73.1 2.0 %collective-permute-start.16 = (bf16[32,5120]{1,0:T(8,128)(2,1)}, bf16[32,5120]{1,0:T(8,128)(2,1)S(1)}, u32[]{:S(2)}, u32[]{:S(2)}) collective-permute-start(bf16[32,5120]{1,0:T(8,128)(2,1)} %collective-permute-done.14.refs_1_), channel_id=1, source_target_pairs={{0,2},{1,3},{2,4},{3,5},{4,6},{5,7},{6,0},{7,1},{8,10},{9,11},{10,... | collective-permute-start | bytes 983048 | tf_op jit(solution)/shard_map/ppermute | solution.py:39
  75.2 1.0 slice.104
  76.2 1.0 slice.105
  77.7 2.5 %collective-permute-done.39 = bf16[64,2560]{1,0:T(8,128)(2,1)} collective-permute-done((bf16[64,2560]{1,0:T(8,128)(2,1)}, bf16[64,2560]{1,0:T(8,128)(2,1)}, u32[]{:S(2)}, u32[]{:S(2)}) %collective-permute-start.39) | collective-permute-done | bytes 327712 | tf_op jit(solution)/shard_map/ppermute | solution.py:39
  80.5 1.0 convert_element_type.77
  81.5 1.1 fusion.1
  82.7 2.6 %collective-permute-done.16.refs_3_ = bf16[32,5120]{1,0:T(8,128)(2,1)S(1)} collective-permute-done((bf16[32,5120]{1,0:T(8,128)(2,1)}, bf16[32,5120]{1,0:T(8,128)(2,1)S(1)}, u32[]{:S(2)}, u32[]{:S(2)}) %collective-permute-start.16) | collective-permute-done | bytes 327712 | tf_op jit(solution)/shard_map/ppermute | solution.py:39
  85.3 1.8 collective-permute-start.28
  87.1 3.4 %collective-permute-done.18.refs_5_ = bf16[32,5120]{1,0:T(8,128)(2,1)S(1)} collective-permute-done((bf16[32,5120]{1,0:T(8,128)(2,1)}, bf16[32,5120]{1,0:T(8,128)(2,1)S(1)}, u32[]{:S(2)}, u32[]{:S(2)}) %collective-permute-start.18) | collective-permute-done | bytes 327712 | tf_op jit(solution)/shard_map/ppermute | solution.py:39
  90.8 4.5 %collective-permute-done.37 = bf16[64,2560]{1,0:T(8,128)(2,1)S(1)} collective-permute-done((bf16[64,2560]{1,0:T(8,128)(2,1)}, bf16[64,2560]{1,0:T(8,128)(2,1)S(1)}, u32[]{:S(2)}, u32[]{:S(2)}) %collective-permute-start.37) | collective-permute-done | bytes 327712 | tf_op jit(solution)/shard_map/ppermute | solution.py:39
  95.3 2.0 %collective-permute-start.42 = (bf16[32,2560]{1,0:T(8,128)(2,1)S(1)}, bf16[32,2560]{1,0:T(8,128)(2,1)S(1)}, u32[]{:S(2)}, u32[]{:S(2)}) collective-permute-start(bf16[32,2560]{1,0:T(8,128)(2,1)S(1)} %get-tuple-element.55), channel_id=1, source_target_pairs={{0,2},{1,3},{2,4},{3,5},{4,6},{5,7},{6,0},{7,1},{8,10},{9,11},{10,... | collective-permute-start | bytes 491528 | tf_op jit(solution)/shard_map/ppermute | solution.py:39
  97.4 1.0 collective-permute-done.19.refs_6_
  98.6 3.3 %collective-permute-done.42 = bf16[32,2560]{1,0:T(8,128)(2,1)S(1)} collective-permute-done((bf16[32,2560]{1,0:T(8,128)(2,1)S(1)}, bf16[32,2560]{1,0:T(8,128)(2,1)S(1)}, u32[]{:S(2)}, u32[]{:S(2)}) %collective-permute-start.42) | collective-permute-done | bytes 163872 | tf_op jit(solution)/shard_map/ppermute | solution.py:39
  102.8 2.3 %collective-permute-start.30 = (bf16[32,5120]{1,0:T(8,128)(2,1)S(1)}, bf16[32,5120]{1,0:T(8,128)(2,1)S(1)}, u32[]{:S(2)}, u32[]{:S(2)}) collective-permute-start(bf16[32,5120]{1,0:T(8,128)(2,1)S(1)} %collective-permute-done.28.refs_4_), channel_id=1, source_target_pairs={{0,6},{1,7},{2,0},{3,1},{4,2},{5,3},{6,4},{7,5},{8,14},{9,15},{10,... | collective-permute-start | bytes 983048 | tf_op jit(solution)/shard_map/ppermute | solution.py:39
  105.9 4.3 %copy-done = bf16[1152,5120]{1,0:T(8,128)(2,1)S(1)} copy-done((bf16[1152,5120]{1,0:T(8,128)(2,1)S(1)}, bf16[1152,5120]{1,0:T(8,128)(2,1)}, u32[]{:S(2)}) %copy-start) | copy-done | bytes 11796504
  110.2 5.1 %shard_map.69 = f32[8,256]{1,0:T(8,128)S(1)} custom-call(s32[18]{0:T(128)S(1)} %stack.75.pos, s32[1,256]{1,0:T(1,128)S(1)} %get-tuple-element.61.ids, bf16[32,5120]{1,0:T(8,128)(2,1)S(1)} %get-tuple-element.28.refs_0_, bf16[32,5120]{1,0:T(8,128)(2,1)} %collective-permute-done.14.refs_1_, bf16[32,5120]{1,0:T(8,128)(2,1)} %collective-permute-done.15.refs_2_, ...), custom_call_target="tpu_custom_call" | custom-call | flops 3019898880 | bytes 14417920 | tf_op jit(solution)/shard_map/pallas_call | solution.py:141
  115.5 1.8 collective-permute-start.23
  117.3 2.8 %collective-permute-start.22 = (f32[8,256]{1,0:T(8,128)S(1)}, f32[8,256]{1,0:T(8,128)S(1)}, u32[]{:S(2)}, u32[]{:S(2)}) collective-permute-start(f32[8,256]{1,0:T(8,128)S(1)} %shard_map.69), channel_id=1, source_target_pairs={{0,6},{1,7},{2,0},{3,1},{4,2},{5,3},{6,4},{7,5},{8,14},{9,15},{10,... | collective-permute-start | bytes 24584 | tf_op jit(solution)/shard_map/ppermute | solution.py:39
  120.2 4.3 %copy-done.1 = bf16[1152,5120]{1,0:T(8,128)(2,1)S(1)} copy-done((bf16[1152,5120]{1,0:T(8,128)(2,1)S(1)}, bf16[1152,5120]{1,0:T(8,128)(2,1)}, u32[]{:S(2)}) %copy-start.1) | copy-done | bytes 11796504
  124.5 4.5 %shard_map.70 = f32[8,256]{1,0:T(8,128)S(1)} custom-call(s32[18]{0:T(128)S(1)} %stack.75.pos, s32[1,256]{1,0:T(1,128)S(1)} %get-tuple-element.60.ids, bf16[32,5120]{1,0:T(8,128)(2,1)S(1)} %get-tuple-element.29.refs_0_, bf16[32,5120]{1,0:T(8,128)(2,1)S(1)} %collective-permute-done.25.refs_1_, bf16[32,5120]{1,0:T(8,128)(2,1)S(1)} %collective-permute-done.26.refs_2_, ...), custom_call_target="tpu_custom_call" | custom-call | flops 3019898880 | bytes 14417920 | tf_op jit(solution)/shard_map/pallas_call | solution.py:141
  129.0 1.6 collective-permute-start.34
  130.6 1.8 collective-permute-start.33
  133.3 1.0 collective-permute-done.34
  134.3 2.5 %collective-permute-start.38 = (bf16[64,2560]{1,0:T(8,128)(2,1)S(1)}, bf16[64,2560]{1,0:T(8,128)(2,1)S(1)}, u32[]{:S(2)}, u32[]{:S(2)}) collective-permute-start(bf16[64,2560]{1,0:T(8,128)(2,1)S(1)} %add_convert_fusion.3), channel_id=1, source_target_pairs={{0,65},{1,64},{2,67},{3,66},{4,69},{5,68},{6,71},{7,70},{8,73},{9,... | collective-permute-start | bytes 983048 | tf_op jit(solution)/shard_map/ppermute | solution.py:39
  137.5 2.6 %collective-permute-start.35 = (f32[8,256]{1,0:T(8,128)S(1)}, f32[8,256]{1,0:T(8,128)S(1)}, u32[]{:S(2)}, u32[]{:S(2)}) collective-permute-start(f32[8,256]{1,0:T(8,128)S(1)} %add_add_fusion.1), channel_id=1, source_target_pairs={{0,65},{1,64},{2,67},{3,66},{4,69},{5,68},{6,71},{7,70},{8,73},{9,... | collective-permute-start | bytes 24584 | tf_op jit(solution)/shard_map/ppermute | solution.py:39
  140.1 2.5 %collective-permute-done.24 = f32[8,256]{1,0:T(8,128)S(1)} collective-permute-done((f32[8,256]{1,0:T(8,128)S(1)}, f32[8,256]{1,0:T(8,128)S(1)}, u32[]{:S(2)}, u32[]{:S(2)}) %collective-permute-start.24) | collective-permute-done | bytes 8224 | tf_op jit(solution)/shard_map/ppermute | solution.py:39
  142.6 1.0 collective-permute-start.43
  143.7 1.2 shard_map.71
  145.1 1.9 %collective-permute-done.44.grad_from = bf16[576,512]{1,0:T(8,128)(2,1)S(1)} collective-permute-done((bf16[576,512]{1,0:T(8,128)(2,1)S(1)}, bf16[576,512]{1,0:T(8,128)(2,1)S(1)}, u32[]{:S(2)}, u32[]{:S(2)}) %collective-permute-start.44) | collective-permute-done | bytes 589856 | tf_op jit(solution)/shard_map/ppermute | solution.py:39
  147.0 2.9 %shard_map.74 = (bf16[72,2560]{1,0:T(8,128)(2,1)S(1)}, bf16[72,2560]{1,0:T(8,128)(2,1)S(1)}, bf16[72,2560]{1,0:T(8,128)(2,1)S(1)}, f32[72,2560]{1,0:T(8,128)S(1)}) custom-call(bf16[576,512]{1,0:T(8,128)(2,1)S(1)} %get-tuple-element.41.grad_mine, bf16[576,512]{1,0:T(8,128)(2,1)S(1)} %collective-permute-done.44.grad_from, ...), custom_call_target="tpu_custom_call" | custom-call | flops 1509949440 | bytes 13434880 | tf_op jit(solution)/shard_map/pallas_call | solution.py:235
  150.1 2.3 %collective-permute-start.41 = (bf16[64,2560]{1,0:T(8,128)(2,1)S(1)}, bf16[64,2560]{1,0:T(8,128)(2,1)S(1)}, u32[]{:S(2)}, u32[]{:S(2)}) collective-permute-start(bf16[64,2560]{1,0:T(8,128)(2,1)S(1)} %pad_maximum_fusion.2), channel_id=1, source_target_pairs={{0,6},{1,7},{2,0},{3,1},{4,2},{5,3},{6,4},{7,5},{8,14},{9,15},{10,... | collective-permute-start | bytes 983048 | tf_op jit(solution)/shard_map/ppermute | solution.py:39
  152.5 2.9 %shard_map.73 = (f32[72,2560]{1,0:T(8,128)S(1)}, f32[72,2560]{1,0:T(8,128)S(1)}, f32[72,2560]{1,0:T(8,128)S(1)}, f32[72,2560]{1,0:T(8,128)S(1)}) custom-call(bf16[576,512]{1,0:T(8,128)(2,1)S(1)} %get-tuple-element.41.grad_mine, bf16[576,512]{1,0:T(8,128)(2,1)S(1)} %collective-permute-done.44.grad_from, bf16[512,2560]{1,0:T(8,128)(2,1)S(1)} %get-tuple-element.43.hidden, ...), custom_call_target="tpu_custom_call" | custom-call | flops 1509949440 | bytes 13434880 | tf_op jit(solution)/shard_map/pallas_call | solution.py:235
  155.5 2.0 %collective-permute-start.47 = (bf16[72,2560]{1,0:T(8,128)(2,1)S(1)}, bf16[72,2560]{1,0:T(8,128)(2,1)S(1)}, u32[]{:S(2)}, u32[]{:S(2)}) collective-permute-start(bf16[72,2560]{1,0:T(8,128)(2,1)S(1)} %get-tuple-element.47), channel_id=1, source_target_pairs={{0,16},{1,17},{2,18},{3,19},{4,20},{5,21},{6,22},{7,23},{8,24},{9,... | collective-permute-start | bytes 1105928 | tf_op jit(solution)/shard_map/ppermute | solution.py:39
  157.5 3.1 %collective-permute-done.49 = bf16[72,2560]{1,0:T(8,128)(2,1)S(1)} collective-permute-done((bf16[72,2560]{1,0:T(8,128)(2,1)S(1)}, bf16[72,2560]{1,0:T(8,128)(2,1)S(1)}, u32[]{:S(2)}, u32[]{:S(2)}) %collective-permute-start.49) | collective-permute-done | bytes 368672 | tf_op jit(solution)/shard_map/ppermute | solution.py:39
  160.6 4.0 %collective-permute-start.46 = (bf16[72,2560]{1,0:T(8,128)(2,1)S(1)}, bf16[72,2560]{1,0:T(8,128)(2,1)S(1)}, u32[]{:S(2)}, u32[]{:S(2)}) collective-permute-start(bf16[72,2560]{1,0:T(8,128)(2,1)S(1)} %get-tuple-element.46), channel_id=1, source_target_pairs={{0,48},{1,49},{2,50},{3,51},{4,52},{5,53},{6,54},{7,55},{8,56},{9,... | collective-permute-start | bytes 1105928 | tf_op jit(solution)/shard_map/ppermute | solution.py:39
  164.8 3.5 %collective-permute-done.47 = bf16[72,2560]{1,0:T(8,128)(2,1)S(1)} collective-permute-done((bf16[72,2560]{1,0:T(8,128)(2,1)S(1)}, bf16[72,2560]{1,0:T(8,128)(2,1)S(1)}, u32[]{:S(2)}, u32[]{:S(2)}) %collective-permute-start.47) | collective-permute-done | bytes 368672 | tf_op jit(solution)/shard_map/ppermute | solution.py:39
  168.3 3.7 %collective-permute-done.46 = bf16[72,2560]{1,0:T(8,128)(2,1)S(1)} collective-permute-done((bf16[72,2560]{1,0:T(8,128)(2,1)S(1)}, bf16[72,2560]{1,0:T(8,128)(2,1)S(1)}, u32[]{:S(2)}, u32[]{:S(2)}) %collective-permute-start.46) | collective-permute-done | bytes 368672 | tf_op jit(solution)/shard_map/ppermute | solution.py:39
  172.0 3.7 %collective-permute-start.50 = (bf16[72,1280]{1,0:T(8,128)(2,1)S(1)}, bf16[72,1280]{1,0:T(8,128)(2,1)S(1)}, u32[]{:S(2)}, u32[]{:S(2)}) collective-permute-start(bf16[72,1280]{1,0:T(8,128)(2,1)S(1)} %get-tuple-element.56), channel_id=1, source_target_pairs={{0,48},{1,49},{2,50},{3,51},{4,52},{5,53},{6,54},{7,55},{8,56},{9,... | collective-permute-start | bytes 552968 | tf_op jit(solution)/shard_map/ppermute | solution.py:39
  176.8 1.9 %collective-permute-done.50 = bf16[72,1280]{1,0:T(8,128)(2,1)S(1)} collective-permute-done((bf16[72,1280]{1,0:T(8,128)(2,1)S(1)}, bf16[72,1280]{1,0:T(8,128)(2,1)S(1)}, u32[]{:S(2)}, u32[]{:S(2)}) %collective-permute-start.50) | collective-permute-done | bytes 184352 | tf_op jit(solution)/shard_map/ppermute | solution.py:39
  178.8 3.8 %collective-permute-start.51 = (bf16[72,2560]{1,0:T(8,128)(2,1)S(1)}, bf16[72,2560]{1,0:T(8,128)(2,1)S(1)}, u32[]{:S(2)}, u32[]{:S(2)}) collective-permute-start(bf16[72,2560]{1,0:T(8,128)(2,1)S(1)} %pad_maximum_fusion), channel_id=1, source_target_pairs={{0,48},{1,49},{2,50},{3,51},{4,52},{5,53},{6,54},{7,55},{8,56},{9,... | collective-permute-start | bytes 1105928 | tf_op jit(solution)/shard_map/ppermute | solution.py:39
  184.5 3.9 %collective-permute-done.53 = bf16[72,2560]{1,0:T(8,128)(2,1)S(1)} collective-permute-done((bf16[72,2560]{1,0:T(8,128)(2,1)S(1)}, bf16[72,2560]{1,0:T(8,128)(2,1)S(1)}, u32[]{:S(2)}, u32[]{:S(2)}) %collective-permute-start.53) | collective-permute-done | bytes 368672 | tf_op jit(solution)/shard_map/ppermute | solution.py:39
  (150 shorter events, 25.9 us)
Async XLA Ops:
  0.6 10.8 %collective-permute-start.1 = (bf16[64,2560]{1,0:T(8,128)(2,1)}, bf16[64,2560]{1,0:T(8,128)(2,1)S(1)}, u32[]{:S(2)}, u32[]{:S(2)}) collective-permute-start(bf16[64,2560]{1,0:T(8,128)(2,1)} %own.1), channel_id=1, source_target_pairs={{0,2},{1,3},{2,4},{3,5},{4,6},{5,7},{6,0},{7,1},{8,10},{9,11},{10,... | collective-permute-start | bytes 983048 | tf_op jit(solution)/shard_map/ppermute | solution.py:39
  2.3 9.7 %collective-permute-start.2 = (bf16[64,2560]{1,0:T(8,128)(2,1)}, bf16[64,2560]{1,0:T(8,128)(2,1)S(1)}, u32[]{:S(2)}, u32[]{:S(2)}) collective-permute-start(bf16[64,2560]{1,0:T(8,128)(2,1)} %own.1), channel_id=1, source_target_pairs={{0,6},{1,7},{2,0},{3,1},{4,2},{5,3},{6,4},{7,5},{8,14},{9,15},{10,... | collective-permute-start | bytes 983048 | tf_op jit(solution)/shard_map/ppermute | solution.py:39
  3.9 10.9 %collective-permute-start.3 = (bf16[64,2560]{1,0:T(8,128)(2,1)}, bf16[64,2560]{1,0:T(8,128)(2,1)S(1)}, u32[]{:S(2)}, u32[]{:S(2)}) collective-permute-start(bf16[64,2560]{1,0:T(8,128)(2,1)} %own.1), channel_id=1, source_target_pairs={{0,65},{1,64},{2,67},{3,66},{4,69},{5,68},{6,71},{7,70},{8,73},{9,... | collective-permute-start | bytes 983048 | tf_op jit(solution)/shard_map/ppermute | solution.py:39
  11.5 9.9 %collective-permute-start.6 = (bf16[32,2560]{1,0:T(8,128)(2,1)S(1)}, bf16[32,2560]{1,0:T(8,128)(2,1)S(1)}, u32[]{:S(2)}, u32[]{:S(2)}) collective-permute-start(bf16[32,2560]{1,0:T(8,128)(2,1)S(1)} %slice.76), channel_id=1, source_target_pairs={{0,2},{1,3},{2,4},{3,5},{4,6},{5,7},{6,0},{7,1},{8,10},{9,11},{10,... | collective-permute-start | bytes 491528 | tf_op jit(solution)/shard_map/ppermute | solution.py:39
  12.0 10.3 %collective-permute-start.7 = (bf16[32,2560]{1,0:T(8,128)(2,1)S(1)}, bf16[32,2560]{1,0:T(8,128)(2,1)S(1)}, u32[]{:S(2)}, u32[]{:S(2)}) collective-permute-start(bf16[32,2560]{1,0:T(8,128)(2,1)S(1)} %slice.77), channel_id=1, source_target_pairs={{0,6},{1,7},{2,0},{3,1},{4,2},{5,3},{6,4},{7,5},{8,14},{9,15},{10,... | collective-permute-start | bytes 491528 | tf_op jit(solution)/shard_map/ppermute | solution.py:39
  14.9 13.3 %copy-start.16 = (bf16[64,2560]{1,0:T(8,128)(2,1)}, bf16[64,2560]{1,0:T(8,128)(2,1)S(1)}, u32[]{:S(2)}) copy-start(bf16[64,2560]{1,0:T(8,128)(2,1)S(1)} %collective-permute-done.3.near) | copy-start | bytes 983044
  14.9 11.4 %collective-permute-start.4 = (bf16[64,2560]{1,0:T(8,128)(2,1)S(1)}, bf16[64,2560]{1,0:T(8,128)(2,1)S(1)}, u32[]{:S(2)}, u32[]{:S(2)}) collective-permute-start(bf16[64,2560]{1,0:T(8,128)(2,1)S(1)} %collective-permute-done.3.near), channel_id=1, source_target_pairs={{0,2},{1,3},{2,4},{3,5},{4,6},{5,7},{6,0},{7,1},{8,10},{9,11},{10,... | collective-permute-start | bytes 983048 | tf_op jit(solution)/shard_map/ppermute | solution.py:39
  14.9 12.1 %collective-permute-start.5 = (bf16[64,2560]{1,0:T(8,128)(2,1)S(1)}, bf16[64,2560]{1,0:T(8,128)(2,1)S(1)}, u32[]{:S(2)}, u32[]{:S(2)}) collective-permute-start(bf16[64,2560]{1,0:T(8,128)(2,1)S(1)} %collective-permute-done.3.near), channel_id=1, source_target_pairs={{0,6},{1,7},{2,0},{3,1},{4,2},{5,3},{6,4},{7,5},{8,14},{9,15},{10,... | collective-permute-start | bytes 983048 | tf_op jit(solution)/shard_map/ppermute | solution.py:39
  18.1 7.3 %collective-permute-start = (s32[512]{0:T(512)}, s32[512]{0:T(512)S(1)}, u32[]{:S(2)}, u32[]{:S(2)}) collective-permute-start(s32[512]{0:T(512)} %param.9), channel_id=1, source_target_pairs={{0,65},{1,64},{2,67},{3,66},{4,69},{5,68},{6,71},{7,70},{8,73},{9,... | collective-permute-start | bytes 6152 | tf_op jit(solution)/shard_map/ppermute | solution.py:39
  21.4 6.7 %collective-permute-start.8 = (bf16[32,2560]{1,0:T(8,128)(2,1)S(1)}, bf16[32,2560]{1,0:T(8,128)(2,1)S(1)}, u32[]{:S(2)}, u32[]{:S(2)}) collective-permute-start(bf16[32,2560]{1,0:T(8,128)(2,1)S(1)} %collective-permute-done.6.far_a), channel_id=1, source_target_pairs={{0,65},{1,64},{2,67},{3,66},{4,69},{5,68},{6,71},{7,70},{8,73},{9,... | collective-permute-start | bytes 491528 | tf_op jit(solution)/shard_map/ppermute | solution.py:39
  22.3 7.6 %collective-permute-start.9 = (bf16[32,2560]{1,0:T(8,128)(2,1)S(1)}, bf16[32,2560]{1,0:T(8,128)(2,1)S(1)}, u32[]{:S(2)}, u32[]{:S(2)}) collective-permute-start(bf16[32,2560]{1,0:T(8,128)(2,1)S(1)} %collective-permute-done.7.far_b), channel_id=1, source_target_pairs={{0,65},{1,64},{2,67},{3,66},{4,69},{5,68},{6,71},{7,70},{8,73},{9,... | collective-permute-start | bytes 491528 | tf_op jit(solution)/shard_map/ppermute | solution.py:39
  39.9 12.9 %copy-start.30 = (bf16[64,5120]{1,0:T(8,128)(2,1)S(1)}, bf16[64,5120]{1,0:T(8,128)(2,1)}, u32[]{:S(2)}) copy-start(bf16[64,5120]{1,0:T(8,128)(2,1)} %param.6) | copy-start | bytes 1966084
  44.5 20.7 %copy-start.2 = (f32[1152,512]{1,0:T(8,128)}, f32[1152,512]{1,0:T(8,128)S(1)}, u32[]{:S(2)}) copy-start(f32[1152,512]{1,0:T(8,128)S(1)} %get-tuple-element.30.logits) | copy-start | bytes 7077892
  44.6 5.3 %collective-permute-start.12 = (f32[8,512]{1,0:T(8,128)S(1)}, f32[8,512]{1,0:T(8,128)S(1)}, u32[]{:S(2)}, u32[]{:S(2)}) collective-permute-start(f32[8,512]{1,0:T(8,128)S(1)} %get-tuple-element.27), channel_id=1, source_target_pairs={{0,4},{1,5},{2,6},{3,7},{4,0},{5,1},{6,2},{7,3},{8,12},{9,13},{10,... | collective-permute-start | bytes 49160 | tf_op jit(solution)/shard_map/ppermute | solution.py:39
  44.9 5.0 %collective-permute-start.11 = (f32[8,512]{1,0:T(8,128)S(1)}, f32[8,512]{1,0:T(8,128)S(1)}, u32[]{:S(2)}, u32[]{:S(2)}) collective-permute-start(f32[8,512]{1,0:T(8,128)S(1)} %get-tuple-element.27), channel_id=1, source_target_pairs={{0,6},{1,7},{2,0},{3,1},{4,2},{5,3},{6,4},{7,5},{8,14},{9,15},{10,... | collective-permute-start | bytes 49160 | tf_op jit(solution)/shard_map/ppermute | solution.py:39
  46.4 4.9 %collective-permute-start.10 = (f32[8,512]{1,0:T(8,128)S(1)}, f32[8,512]{1,0:T(8,128)S(1)}, u32[]{:S(2)}, u32[]{:S(2)}) collective-permute-start(f32[8,512]{1,0:T(8,128)S(1)} %get-tuple-element.27), channel_id=1, source_target_pairs={{0,2},{1,3},{2,4},{3,5},{4,6},{5,7},{6,0},{7,1},{8,10},{9,11},{10,... | collective-permute-start | bytes 49160 | tf_op jit(solution)/shard_map/ppermute | solution.py:39
  51.4 6.6 %collective-permute-start.13 = (f32[8,512]{1,0:T(8,128)S(1)}, f32[8,512]{1,0:T(8,128)S(1)}, u32[]{:S(2)}, u32[]{:S(2)}) collective-permute-start(f32[8,512]{1,0:T(8,128)S(1)} %add_add_fusion), channel_id=1, source_target_pairs={{0,65},{1,64},{2,67},{3,66},{4,69},{5,68},{6,71},{7,70},{8,73},{9,... | collective-permute-start | bytes 49160 | tf_op jit(solution)/shard_map/ppermute | solution.py:39
  52.8 20.2 %collective-permute-start.14 = (bf16[32,5120]{1,0:T(8,128)(2,1)S(1)}, bf16[32,5120]{1,0:T(8,128)(2,1)}, u32[]{:S(2)}, u32[]{:S(2)}) collective-permute-start(bf16[32,5120]{1,0:T(8,128)(2,1)S(1)} %get-tuple-element.28.refs_0_), channel_id=1, source_target_pairs={{0,2},{1,3},{2,4},{3,5},{4,6},{5,7},{6,0},{7,1},{8,10},{9,11},{10,... | collective-permute-start | bytes 983048 | tf_op jit(solution)/shard_map/ppermute | solution.py:39
  52.9 20.1 %collective-permute-start.15 = (bf16[32,5120]{1,0:T(8,128)(2,1)S(1)}, bf16[32,5120]{1,0:T(8,128)(2,1)}, u32[]{:S(2)}, u32[]{:S(2)}) collective-permute-start(bf16[32,5120]{1,0:T(8,128)(2,1)S(1)} %get-tuple-element.28.refs_0_), channel_id=1, source_target_pairs={{0,6},{1,7},{2,0},{3,1},{4,2},{5,3},{6,4},{7,5},{8,14},{9,15},{10,... | collective-permute-start | bytes 983048 | tf_op jit(solution)/shard_map/ppermute | solution.py:39
  56.1 16.9 %collective-permute-start.17 = (bf16[32,5120]{1,0:T(8,128)(2,1)S(1)}, bf16[32,5120]{1,0:T(8,128)(2,1)}, u32[]{:S(2)}, u32[]{:S(2)}) collective-permute-start(bf16[32,5120]{1,0:T(8,128)(2,1)S(1)} %get-tuple-element.28.refs_0_), channel_id=1, source_target_pairs={{0,65},{1,64},{2,67},{3,66},{4,69},{5,68},{6,71},{7,70},{8,73},{9,... | collective-permute-start | bytes 983048 | tf_op jit(solution)/shard_map/ppermute | solution.py:39
  71.6 8.6 %collective-permute-start.39 = (bf16[64,2560]{1,0:T(8,128)(2,1)}, bf16[64,2560]{1,0:T(8,128)(2,1)}, u32[]{:S(2)}, u32[]{:S(2)}) collective-permute-start(bf16[64,2560]{1,0:T(8,128)(2,1)} %get-tuple-element.38), channel_id=1, source_target_pairs={{0,65},{1,64},{2,67},{3,66},{4,69},{5,68},{6,71},{7,70},{8,73},{9,... | collective-permute-start | bytes 983048 | tf_op jit(solution)/shard_map/ppermute | solution.py:39
  73.0 24.3 %copy-start.5 = (f32[64,2560]{1,0:T(8,128)S(1)}, f32[64,2560]{1,0:T(8,128)}, u32[]{:S(2)}) copy-start(f32[64,2560]{1,0:T(8,128)} %copy-done.4) | copy-start | bytes 1966084
  73.0 32.8 %copy-start.11 = (f32[64,2560]{1,0:T(8,128)S(1)}, f32[64,2560]{1,0:T(8,128)}, u32[]{:S(2)}) copy-start(f32[64,2560]{1,0:T(8,128)} %copy-done.10) | copy-start | bytes 1966084
  73.0 17.5 %collective-permute-start.26 = (bf16[32,5120]{1,0:T(8,128)(2,1)S(1)}, bf16[32,5120]{1,0:T(8,128)(2,1)S(1)}, u32[]{:S(2)}, u32[]{:S(2)}) collective-permute-start(bf16[32,5120]{1,0:T(8,128)(2,1)S(1)} %get-tuple-element.29.refs_0_), channel_id=1, source_target_pairs={{0,6},{1,7},{2,0},{3,1},{4,2},{5,3},{6,4},{7,5},{8,14},{9,15},{10,... | collective-permute-start | bytes 983048 | tf_op jit(solution)/shard_map/ppermute | solution.py:39
  73.1 12.1 %collective-permute-start.16 = (bf16[32,5120]{1,0:T(8,128)(2,1)}, bf16[32,5120]{1,0:T(8,128)(2,1)S(1)}, u32[]{:S(2)}, u32[]{:S(2)}) collective-permute-start(bf16[32,5120]{1,0:T(8,128)(2,1)} %collective-permute-done.14.refs_1_), channel_id=1, source_target_pairs={{0,2},{1,3},{2,4},{3,5},{4,6},{5,7},{6,0},{7,1},{8,10},{9,11},{10,... | collective-permute-start | bytes 983048 | tf_op jit(solution)/shard_map/ppermute | solution.py:39
  75.1 15.4 %collective-permute-start.18 = (bf16[32,5120]{1,0:T(8,128)(2,1)}, bf16[32,5120]{1,0:T(8,128)(2,1)S(1)}, u32[]{:S(2)}, u32[]{:S(2)}) collective-permute-start(bf16[32,5120]{1,0:T(8,128)(2,1)} %collective-permute-done.17.refs_4_), channel_id=1, source_target_pairs={{0,2},{1,3},{2,4},{3,5},{4,6},{5,7},{6,0},{7,1},{8,10},{9,11},{10,... | collective-permute-start | bytes 983048 | tf_op jit(solution)/shard_map/ppermute | solution.py:39
  77.1 18.2 %collective-permute-start.37 = (bf16[64,2560]{1,0:T(8,128)(2,1)}, bf16[64,2560]{1,0:T(8,128)(2,1)S(1)}, u32[]{:S(2)}, u32[]{:S(2)}) collective-permute-start(bf16[64,2560]{1,0:T(8,128)(2,1)} %copy-done.23), channel_id=1, source_target_pairs={{0,2},{1,3},{2,4},{3,5},{4,6},{5,7},{6,0},{7,1},{8,10},{9,11},{10,... | collective-permute-start | bytes 983048 | tf_op jit(solution)/shard_map/ppermute | solution.py:39
  80.2 15.1 %collective-permute-start.36 = (bf16[64,2560]{1,0:T(8,128)(2,1)}, bf16[64,2560]{1,0:T(8,128)(2,1)S(1)}, u32[]{:S(2)}, u32[]{:S(2)}) collective-permute-start(bf16[64,2560]{1,0:T(8,128)(2,1)} %copy-done.22), channel_id=1, source_target_pairs={{0,6},{1,7},{2,0},{3,1},{4,2},{5,3},{6,4},{7,5},{8,14},{9,15},{10,... | collective-permute-start | bytes 983048 | tf_op jit(solution)/shard_map/ppermute | solution.py:39
  85.3 13.3 %collective-permute-start.28 = (bf16[32,5120]{1,0:T(8,128)(2,1)S(1)}, bf16[32,5120]{1,0:T(8,128)(2,1)S(1)}, u32[]{:S(2)}, u32[]{:S(2)}) collective-permute-start(bf16[32,5120]{1,0:T(8,128)(2,1)S(1)} %get-tuple-element.29.refs_0_), channel_id=1, source_target_pairs={{0,65},{1,64},{2,67},{3,66},{4,69},{5,68},{6,71},{7,70},{8,73},{9,... | collective-permute-start | bytes 983048 | tf_op jit(solution)/shard_map/ppermute | solution.py:39
  90.5 7.9 %collective-permute-start.19 = (bf16[32,5120]{1,0:T(8,128)(2,1)}, bf16[32,5120]{1,0:T(8,128)(2,1)S(1)}, u32[]{:S(2)}, u32[]{:S(2)}) collective-permute-start(bf16[32,5120]{1,0:T(8,128)(2,1)} %collective-permute-done.17.refs_4_), channel_id=1, source_target_pairs={{0,6},{1,7},{2,0},{3,1},{4,2},{5,3},{6,4},{7,5},{8,14},{9,15},{10,... | collective-permute-start | bytes 983048 | tf_op jit(solution)/shard_map/ppermute | solution.py:39
  90.5 12.3 %collective-permute-start.20 = (bf16[32,5120]{1,0:T(8,128)(2,1)S(1)}, bf16[32,5120]{1,0:T(8,128)(2,1)S(1)}, u32[]{:S(2)}, u32[]{:S(2)}) collective-permute-start(bf16[32,5120]{1,0:T(8,128)(2,1)S(1)} %collective-permute-done.16.refs_3_), channel_id=1, source_target_pairs={{0,65},{1,64},{2,67},{3,66},{4,69},{5,68},{6,71},{7,70},{8,73},{9,... | collective-permute-start | bytes 983048 | tf_op jit(solution)/shard_map/ppermute | solution.py:39
  95.3 9.8 %collective-permute-start.27 = (bf16[32,5120]{1,0:T(8,128)(2,1)S(1)}, bf16[32,5120]{1,0:T(8,128)(2,1)S(1)}, u32[]{:S(2)}, u32[]{:S(2)}) collective-permute-start(bf16[32,5120]{1,0:T(8,128)(2,1)S(1)} %collective-permute-done.26.refs_2_), channel_id=1, source_target_pairs={{0,6},{1,7},{2,0},{3,1},{4,2},{5,3},{6,4},{7,5},{8,14},{9,15},{10,... | collective-permute-start | bytes 983048 | tf_op jit(solution)/shard_map/ppermute | solution.py:39
  95.3 6.5 %collective-permute-start.42 = (bf16[32,2560]{1,0:T(8,128)(2,1)S(1)}, bf16[32,2560]{1,0:T(8,128)(2,1)S(1)}, u32[]{:S(2)}, u32[]{:S(2)}) collective-permute-start(bf16[32,2560]{1,0:T(8,128)(2,1)S(1)} %get-tuple-element.55), channel_id=1, source_target_pairs={{0,2},{1,3},{2,4},{3,5},{4,6},{5,7},{6,0},{7,1},{8,10},{9,11},{10,... | collective-permute-start | bytes 491528 | tf_op jit(solution)/shard_map/ppermute | solution.py:39
  98.4 17.0 %collective-permute-start.25 = (bf16[32,5120]{1,0:T(8,128)(2,1)S(1)}, bf16[32,5120]{1,0:T(8,128)(2,1)S(1)}, u32[]{:S(2)}, u32[]{:S(2)}) collective-permute-start(bf16[32,5120]{1,0:T(8,128)(2,1)S(1)} %get-tuple-element.29.refs_0_), channel_id=1, source_target_pairs={{0,2},{1,3},{2,4},{3,5},{4,6},{5,7},{6,0},{7,1},{8,10},{9,11},{10,... | collective-permute-start | bytes 983048 | tf_op jit(solution)/shard_map/ppermute | solution.py:39
  98.6 48.4 %collective-permute-start.45 = (bf16[512,2560]{1,0:T(8,128)(2,1)S(1)}, bf16[512,2560]{1,0:T(8,128)(2,1)S(1)}, u32[]{:S(2)}, u32[]{:S(2)}) collective-permute-start(bf16[512,2560]{1,0:T(8,128)(2,1)S(1)} %get-tuple-element.43.hidden), channel_id=1, source_target_pairs={{0,8},{1,9},{2,10},{3,11},{4,12},{5,13},{6,14},{7,15},{8,0},{9,1},... | collective-permute-start | bytes 7864328 | tf_op jit(solution)/shard_map/ppermute | solution.py:39
  101.8 13.7 %collective-permute-start.29 = (bf16[32,5120]{1,0:T(8,128)(2,1)S(1)}, bf16[32,5120]{1,0:T(8,128)(2,1)S(1)}, u32[]{:S(2)}, u32[]{:S(2)}) collective-permute-start(bf16[32,5120]{1,0:T(8,128)(2,1)S(1)} %collective-permute-done.28.refs_4_), channel_id=1, source_target_pairs={{0,2},{1,3},{2,4},{3,5},{4,6},{5,7},{6,0},{7,1},{8,10},{9,11},{10,... | collective-permute-start | bytes 983048 | tf_op jit(solution)/shard_map/ppermute | solution.py:39
  102.8 14.5 %collective-permute-start.30 = (bf16[32,5120]{1,0:T(8,128)(2,1)S(1)}, bf16[32,5120]{1,0:T(8,128)(2,1)S(1)}, u32[]{:S(2)}, u32[]{:S(2)}) collective-permute-start(bf16[32,5120]{1,0:T(8,128)(2,1)S(1)} %collective-permute-done.28.refs_4_), channel_id=1, source_target_pairs={{0,6},{1,7},{2,0},{3,1},{4,2},{5,3},{6,4},{7,5},{8,14},{9,15},{10,... | collective-permute-start | bytes 983048 | tf_op jit(solution)/shard_map/ppermute | solution.py:39
  105.1 15.1 %collective-permute-start.31 = (bf16[32,5120]{1,0:T(8,128)(2,1)S(1)}, bf16[32,5120]{1,0:T(8,128)(2,1)S(1)}, u32[]{:S(2)}, u32[]{:S(2)}) collective-permute-start(bf16[32,5120]{1,0:T(8,128)(2,1)S(1)} %collective-permute-done.27.refs_3_), channel_id=1, source_target_pairs={{0,65},{1,64},{2,67},{3,66},{4,69},{5,68},{6,71},{7,70},{8,73},{9,... | collective-permute-start | bytes 983048 | tf_op jit(solution)/shard_map/ppermute | solution.py:39
  105.9 4.4 %copy-start = (bf16[1152,5120]{1,0:T(8,128)(2,1)S(1)}, bf16[1152,5120]{1,0:T(8,128)(2,1)}, u32[]{:S(2)}) copy-start(bf16[1152,5120]{1,0:T(8,128)(2,1)} %refs_8_.3) | copy-start | bytes 35389444
  115.4 29.7 %collective-permute-start.40 = (bf16[32,2560]{1,0:T(8,128)(2,1)S(1)}, bf16[32,2560]{1,0:T(8,128)(2,1)S(1)}, u32[]{:S(2)}, u32[]{:S(2)}) collective-permute-start(bf16[32,2560]{1,0:T(8,128)(2,1)S(1)} %get-tuple-element.54), channel_id=1, source_target_pairs={{0,6},{1,7},{2,0},{3,1},{4,2},{5,3},{6,4},{7,5},{8,14},{9,15},{10,... | collective-permute-start | bytes 491528 | tf_op jit(solution)/shard_map/ppermute | solution.py:39
  115.5 13.5 %collective-permute-start.23 = (f32[8,256]{1,0:T(8,128)S(1)}, f32[8,256]{1,0:T(8,128)S(1)}, u32[]{:S(2)}, u32[]{:S(2)}) collective-permute-start(f32[8,256]{1,0:T(8,128)S(1)} %shard_map.69), channel_id=1, source_target_pairs={{0,4},{1,5},{2,6},{3,7},{4,0},{5,1},{6,2},{7,3},{8,12},{9,13},{10,... | collective-permute-start | bytes 24584 | tf_op jit(solution)/shard_map/ppermute | solution.py:39
  117.3 13.3 %collective-permute-start.22 = (f32[8,256]{1,0:T(8,128)S(1)}, f32[8,256]{1,0:T(8,128)S(1)}, u32[]{:S(2)}, u32[]{:S(2)}) collective-permute-start(f32[8,256]{1,0:T(8,128)S(1)} %shard_map.69), channel_id=1, source_target_pairs={{0,6},{1,7},{2,0},{3,1},{4,2},{5,3},{6,4},{7,5},{8,14},{9,15},{10,... | collective-permute-start | bytes 24584 | tf_op jit(solution)/shard_map/ppermute | solution.py:39
  120.2 12.3 %collective-permute-start.21 = (f32[8,256]{1,0:T(8,128)S(1)}, f32[8,256]{1,0:T(8,128)S(1)}, u32[]{:S(2)}, u32[]{:S(2)}) collective-permute-start(f32[8,256]{1,0:T(8,128)S(1)} %shard_map.69), channel_id=1, source_target_pairs={{0,2},{1,3},{2,4},{3,5},{4,6},{5,7},{6,0},{7,1},{8,10},{9,11},{10,... | collective-permute-start | bytes 24584 | tf_op jit(solution)/shard_map/ppermute | solution.py:39
  120.2 4.4 %copy-start.1 = (bf16[1152,5120]{1,0:T(8,128)(2,1)S(1)}, bf16[1152,5120]{1,0:T(8,128)(2,1)}, u32[]{:S(2)}) copy-start(bf16[1152,5120]{1,0:T(8,128)(2,1)} %refs_8_.3) | copy-start | bytes 35389444
  124.5 19.2 %copy-start.3 = (f32[1152,512]{1,0:T(8,128)S(1)}, f32[1152,512]{1,0:T(8,128)}, u32[]{:S(2)}) copy-start(f32[1152,512]{1,0:T(8,128)} %copy-done.2) | copy-start | bytes 7077892
  129.0 16.1 %copy-start.9 = (f32[64,2560]{1,0:T(8,128)S(1)}, f32[64,2560]{1,0:T(8,128)}, u32[]{:S(2)}) copy-start(f32[64,2560]{1,0:T(8,128)} %copy-done.8) | copy-start | bytes 1966084
  129.0 5.2 %collective-permute-start.34 = (f32[8,256]{1,0:T(8,128)S(1)}, f32[8,256]{1,0:T(8,128)S(1)}, u32[]{:S(2)}, u32[]{:S(2)}) collective-permute-start(f32[8,256]{1,0:T(8,128)S(1)} %shard_map.70), channel_id=1, source_target_pairs={{0,4},{1,5},{2,6},{3,7},{4,0},{5,1},{6,2},{7,3},{8,12},{9,13},{10,... | collective-permute-start | bytes 24584 | tf_op jit(solution)/shard_map/ppermute | solution.py:39
  130.6 6.1 %collective-permute-start.33 = (f32[8,256]{1,0:T(8,128)S(1)}, f32[8,256]{1,0:T(8,128)S(1)}, u32[]{:S(2)}, u32[]{:S(2)}) collective-permute-start(f32[8,256]{1,0:T(8,128)S(1)} %shard_map.70), channel_id=1, source_target_pairs={{0,6},{1,7},{2,0},{3,1},{4,2},{5,3},{6,4},{7,5},{8,14},{9,15},{10,... | collective-permute-start | bytes 24584 | tf_op jit(solution)/shard_map/ppermute | solution.py:39
  132.4 5.1 %collective-permute-start.32 = (f32[8,256]{1,0:T(8,128)S(1)}, f32[8,256]{1,0:T(8,128)S(1)}, u32[]{:S(2)}, u32[]{:S(2)}) collective-permute-start(f32[8,256]{1,0:T(8,128)S(1)} %shard_map.70), channel_id=1, source_target_pairs={{0,2},{1,3},{2,4},{3,5},{4,6},{5,7},{6,0},{7,1},{8,10},{9,11},{10,... | collective-permute-start | bytes 24584 | tf_op jit(solution)/shard_map/ppermute | solution.py:39
  134.3 44.6 %collective-permute-start.38 = (bf16[64,2560]{1,0:T(8,128)(2,1)S(1)}, bf16[64,2560]{1,0:T(8,128)(2,1)S(1)}, u32[]{:S(2)}, u32[]{:S(2)}) collective-permute-start(bf16[64,2560]{1,0:T(8,128)(2,1)S(1)} %add_convert_fusion.3), channel_id=1, source_target_pairs={{0,65},{1,64},{2,67},{3,66},{4,69},{5,68},{6,71},{7,70},{8,73},{9,... | collective-permute-start | bytes 983048 | tf_op jit(solution)/shard_map/ppermute | solution.py:39
  136.8 5.9 %collective-permute-start.24 = (f32[8,256]{1,0:T(8,128)S(1)}, f32[8,256]{1,0:T(8,128)S(1)}, u32[]{:S(2)}, u32[]{:S(2)}) collective-permute-start(f32[8,256]{1,0:T(8,128)S(1)} %add_add_fusion.2), channel_id=1, source_target_pairs={{0,65},{1,64},{2,67},{3,66},{4,69},{5,68},{6,71},{7,70},{8,73},{9,... | collective-permute-start | bytes 24584 | tf_op jit(solution)/shard_map/ppermute | solution.py:39
  137.5 6.2 %collective-permute-start.35 = (f32[8,256]{1,0:T(8,128)S(1)}, f32[8,256]{1,0:T(8,128)S(1)}, u32[]{:S(2)}, u32[]{:S(2)}) collective-permute-start(f32[8,256]{1,0:T(8,128)S(1)} %add_add_fusion.1), channel_id=1, source_target_pairs={{0,65},{1,64},{2,67},{3,66},{4,69},{5,68},{6,71},{7,70},{8,73},{9,... | collective-permute-start | bytes 24584 | tf_op jit(solution)/shard_map/ppermute | solution.py:39
  142.6 40.0 %collective-permute-start.43 = (bf16[64,2560]{1,0:T(8,128)(2,1)S(1)}, bf16[64,2560]{1,0:T(8,128)(2,1)S(1)}, u32[]{:S(2)}, u32[]{:S(2)}) collective-permute-start(bf16[64,2560]{1,0:T(8,128)(2,1)S(1)} %pad_maximum_fusion.3), channel_id=1, source_target_pairs={{0,2},{1,3},{2,4},{3,5},{4,6},{5,7},{6,0},{7,1},{8,10},{9,11},{10,... | collective-permute-start | bytes 983048 | tf_op jit(solution)/shard_map/ppermute | solution.py:39
  145.0 2.1 %collective-permute-start.44 = (bf16[576,512]{1,0:T(8,128)(2,1)S(1)}, bf16[576,512]{1,0:T(8,128)(2,1)S(1)}, u32[]{:S(2)}, u32[]{:S(2)}) collective-permute-start(bf16[576,512]{1,0:T(8,128)(2,1)S(1)} %get-tuple-element.42), channel_id=1, source_target_pairs={{0,8},{1,9},{2,10},{3,11},{4,12},{5,13},{6,14},{7,15},{8,0},{9,1},... | collective-permute-start | bytes 1769480 | tf_op jit(solution)/shard_map/ppermute | solution.py:39
  149.9 10.7 %collective-permute-start.49 = (bf16[72,2560]{1,0:T(8,128)(2,1)S(1)}, bf16[72,2560]{1,0:T(8,128)(2,1)S(1)}, u32[]{:S(2)}, u32[]{:S(2)}) collective-permute-start(bf16[72,2560]{1,0:T(8,128)(2,1)S(1)} %get-tuple-element.50), channel_id=1, source_target_pairs={{0,64},{1,65},{2,66},{3,67},{4,68},{5,69},{6,70},{7,71},{8,72},{9,... | collective-permute-start | bytes 1105928 | tf_op jit(solution)/shard_map/ppermute | solution.py:39
  150.1 32.5 %collective-permute-start.41 = (bf16[64,2560]{1,0:T(8,128)(2,1)S(1)}, bf16[64,2560]{1,0:T(8,128)(2,1)S(1)}, u32[]{:S(2)}, u32[]{:S(2)}) collective-permute-start(bf16[64,2560]{1,0:T(8,128)(2,1)S(1)} %pad_maximum_fusion.2), channel_id=1, source_target_pairs={{0,6},{1,7},{2,0},{3,1},{4,2},{5,3},{6,4},{7,5},{8,14},{9,15},{10,... | collective-permute-start | bytes 983048 | tf_op jit(solution)/shard_map/ppermute | solution.py:39
  155.5 12.7 %collective-permute-start.47 = (bf16[72,2560]{1,0:T(8,128)(2,1)S(1)}, bf16[72,2560]{1,0:T(8,128)(2,1)S(1)}, u32[]{:S(2)}, u32[]{:S(2)}) collective-permute-start(bf16[72,2560]{1,0:T(8,128)(2,1)S(1)} %get-tuple-element.47), channel_id=1, source_target_pairs={{0,16},{1,17},{2,18},{3,19},{4,20},{5,21},{6,22},{7,23},{8,24},{9,... | collective-permute-start | bytes 1105928 | tf_op jit(solution)/shard_map/ppermute | solution.py:39
  160.6 11.3 %collective-permute-start.46 = (bf16[72,2560]{1,0:T(8,128)(2,1)S(1)}, bf16[72,2560]{1,0:T(8,128)(2,1)S(1)}, u32[]{:S(2)}, u32[]{:S(2)}) collective-permute-start(bf16[72,2560]{1,0:T(8,128)(2,1)S(1)} %get-tuple-element.46), channel_id=1, source_target_pairs={{0,48},{1,49},{2,50},{3,51},{4,52},{5,53},{6,54},{7,55},{8,56},{9,... | collective-permute-start | bytes 1105928 | tf_op jit(solution)/shard_map/ppermute | solution.py:39
  164.7 17.9 %copy-start.7 = (f32[64,2560]{1,0:T(8,128)S(1)}, f32[64,2560]{1,0:T(8,128)}, u32[]{:S(2)}) copy-start(f32[64,2560]{1,0:T(8,128)} %copy-done.6) | copy-start | bytes 1966084
  168.2 7.6 %collective-permute-start.52 = (bf16[72,1280]{1,0:T(8,128)(2,1)S(1)}, bf16[72,1280]{1,0:T(8,128)(2,1)S(1)}, u32[]{:S(2)}, u32[]{:S(2)}) collective-permute-start(bf16[72,1280]{1,0:T(8,128)(2,1)S(1)} %get-tuple-element.57), channel_id=1, source_target_pairs={{0,16},{1,17},{2,18},{3,19},{4,20},{5,21},{6,22},{7,23},{8,24},{9,... | collective-permute-start | bytes 552968 | tf_op jit(solution)/shard_map/ppermute | solution.py:39
  172.0 6.7 %collective-permute-start.50 = (bf16[72,1280]{1,0:T(8,128)(2,1)S(1)}, bf16[72,1280]{1,0:T(8,128)(2,1)S(1)}, u32[]{:S(2)}, u32[]{:S(2)}) collective-permute-start(bf16[72,1280]{1,0:T(8,128)(2,1)S(1)} %get-tuple-element.56), channel_id=1, source_target_pairs={{0,48},{1,49},{2,50},{3,51},{4,52},{5,53},{6,54},{7,55},{8,56},{9,... | collective-permute-start | bytes 552968 | tf_op jit(solution)/shard_map/ppermute | solution.py:39
  175.8 8.7 %collective-permute-start.48 = (bf16[72,2560]{1,0:T(8,128)(2,1)S(1)}, bf16[72,2560]{1,0:T(8,128)(2,1)S(1)}, u32[]{:S(2)}, u32[]{:S(2)}) collective-permute-start(bf16[72,2560]{1,0:T(8,128)(2,1)S(1)} %add_convert_fusion.2), channel_id=1, source_target_pairs={{0,64},{1,65},{2,66},{3,67},{4,68},{5,69},{6,70},{7,71},{8,72},{9,... | collective-permute-start | bytes 1105928 | tf_op jit(solution)/shard_map/ppermute | solution.py:39
  178.7 9.7 %collective-permute-start.53 = (bf16[72,2560]{1,0:T(8,128)(2,1)S(1)}, bf16[72,2560]{1,0:T(8,128)(2,1)S(1)}, u32[]{:S(2)}, u32[]{:S(2)}) collective-permute-start(bf16[72,2560]{1,0:T(8,128)(2,1)S(1)} %pad_maximum_fusion.1), channel_id=1, source_target_pairs={{0,16},{1,17},{2,18},{3,19},{4,20},{5,21},{6,22},{7,23},{8,24},{9,... | collective-permute-start | bytes 1105928 | tf_op jit(solution)/shard_map/ppermute | solution.py:39
  178.8 9.6 %collective-permute-start.51 = (bf16[72,2560]{1,0:T(8,128)(2,1)S(1)}, bf16[72,2560]{1,0:T(8,128)(2,1)S(1)}, u32[]{:S(2)}, u32[]{:S(2)}) collective-permute-start(bf16[72,2560]{1,0:T(8,128)(2,1)S(1)} %pad_maximum_fusion), channel_id=1, source_target_pairs={{0,48},{1,49},{2,50},{3,51},{4,52},{5,53},{6,54},{7,55},{8,56},{9,... | collective-permute-start | bytes 1105928 | tf_op jit(solution)/shard_map/ppermute | solution.py:39
  (21 other events, 19.1 us)

commit v2 on v0

v2 whole, which is shorter than its diff:
```python
import functools

import jax
import jax.numpy as jnp
from jax import lax
from jax.experimental import pallas as pl
from jax.experimental.pallas import tpu as pltpu
from jax.sharding import PartitionSpec as P

BF16 = jnp.bfloat16
F32 = jnp.float32
AXES = ("dp", "vocab")

REL = ((0, 0), (-1, 0), (1, 0), (2, 0), (0, 1), (-1, 1), (1, 1), (2, 1))


def pairs(move):
    out = []
    for i in range(128):
        dp, v = i // 8, i % 8
        y_lo, z, core, x, y_hi = dp // 8, (dp // 2) % 4, dp % 2, v // 2, v % 2
        x, y, z, core = move(x, y_hi * 2 + y_lo, z, core)
        x, y, z = x % 4, y % 4, z % 4
        out.append((i, (((y % 2) * 4 + z) * 2 + core) * 8 + x * 2 + y // 2))
    return out


X_UP = pairs(lambda x, y, z, c: (x + 1, y, z, c))
X_DOWN = pairs(lambda x, y, z, c: (x - 1, y, z, c))
X_FAR = pairs(lambda x, y, z, c: (x + 2, y, z, c))
Y_HI = pairs(lambda x, y, z, c: (x, 3 - y, z, c))
Z_UP = pairs(lambda x, y, z, c: (x, y, z + 1, c))
Z_DOWN = pairs(lambda x, y, z, c: (x, y, z - 1, c))
Y_LO = pairs(lambda x, y, z, c: (x, y ^ 1, z, c))
CORE = pairs(lambda x, y, z, c: (x, y, z, 1 - c))


def send(a, to):
    return lax.ppermute(a, AXES, to)


class Link:
    def __init__(self, to, ahead=2):
        self.to, self.ahead, self.sent = to, ahead, []

    def __call__(self, a):
        if len(self.sent) >= self.ahead:
            a = after(a, self.sent[-self.ahead])
        self.sent.append(send(a, self.to))
        return self.sent[-1]


def after(a, *others):
    return lax.optimization_barrier((a, *others))[0]


def params(mib):
    return pltpu.CompilerParams(vmem_limit_bytes=mib * 2**20)


COST = pl.CostEstimate(flops=20_000_000_000, bytes_accessed=20_000_000, transcendentals=0)

VMEM = pl.BlockSpec(memory_space=pltpu.VMEM)


def kernel_call(body, arrays, outs, scratch, mib):
    return pl.pallas_call(
        body,
        in_specs=[VMEM] * len(arrays),
        out_specs=[VMEM] * len(outs),
        out_shape=[jax.ShapeDtypeStruct(shape, dtype) for shape, dtype in outs],
        scratch_shapes=[pltpu.VMEM(shape, dtype) for shape, dtype in scratch],
        compiler_params=params(mib),
        cost_estimate=COST,
    )(*arrays)


class Place:
    def __init__(self):
        dp, v = lax.axis_index("dp"), lax.axis_index("vocab")
        self.y_lo, self.z, self.core = lax.div(dp, 8), lax.rem(lax.div(dp, 2), 4), lax.rem(dp, 2)
        self.vocab, self.x, self.y_hi = v, lax.div(v, 2), lax.rem(v, 2)

    def block(self, r):
        dx, dy = REL[r]
        owner = lax.rem(self.x + (dx + 4), 4) * 2 + lax.rem(self.y_hi + dy, 2)
        return pl.multiple_of(owner * 64, 64)

    def chip(self, dz, dy):
        return lax.rem(self.y_lo + dy, 2) * 4 + lax.rem(self.z + (dz + 4), 4)

    def ids(self, own, near):
        half = lax.rem(lax.div(lax.broadcasted_iota(jnp.int32, (1, 512), 1), 64), 2)
        return jnp.where(half == self.y_hi, own[...].reshape(1, 512), near[...].reshape(1, 512))


def fold(a):
    return jnp.sum(a.reshape(a.shape[0] // 8, 8, a.shape[1]), axis=0)


NT = (((1,), (1,)), ((), ()))
NN = (((1,), (0,)), ((), ()))
TILE = 384
WIDE = 512
STATS = (8, 512)


def put_blocks(place, blocks, hidden):
    for r, block in enumerate(blocks):
        hidden[pl.ds(place.block(r), 64), :] = block[...]


def put_stats(stats, sums, picks):
    stats[...] = jnp.zeros_like(stats)
    stats[0:1, :] = jnp.sum(sums, axis=0, keepdims=True)
    stats[1:2, :] = jnp.sum(picks, axis=0, keepdims=True)


def student_kernel(ids_own, ids_near, head, *refs):
    blocks, (logits, hidden, stats) = refs[:8], refs[8:]
    place = Place()
    put_blocks(place, blocks, hidden)
    ids = place.ids(ids_own, ids_near)
    sums = picks = 0.0
    for j in range(head.shape[0] // TILE):
        tile = slice(j * TILE, (j + 1) * TILE)
        out = lax.dot_general(head[tile, :], hidden[...], NT, preferred_element_type=F32)
        logits[tile, :] = out
        rows = lax.broadcasted_iota(jnp.int32, out.shape, 0) + (place.vocab * head.shape[0] + j * TILE)
        sums += fold(jnp.exp(out))
        picks += fold(jnp.where(rows == ids, out, 0.0))
    put_stats(stats, sums, picks)


def student_logits(ids, blocks, head):
    v, d = head.shape
    outs = [((v, 512), F32), ((512, d), BF16), (STATS, F32)]
    return kernel_call(student_kernel, (*ids, head, *blocks), outs, [], 6)


def teacher_first_kernel(head, *refs):
    blocks, (logits, hidden) = refs[:8], refs[8:]
    put_blocks(Place(), blocks, hidden)
    for j in range(head.shape[0] // TILE):
        tile = slice(j * TILE, (j + 1) * TILE)
        logits[tile, :] = lax.dot_general(
            head[tile, 0:hidden.shape[1]], hidden[...], NT, preferred_element_type=F32
        )


def teacher_first(blocks, head):
    v, d = head.shape
    return kernel_call(teacher_first_kernel, (head, *blocks), [((v, 512), F32)], [((512, d // 2), BF16)], 8)[0]


def teacher_second_kernel(ids_own, ids_near, head, logits, *refs):
    blocks, (stats, hidden) = refs[:8], refs[8:]
    place = Place()
    put_blocks(place, blocks, hidden)
    ids = place.ids(ids_own, ids_near)
    sums = picks = 0.0
    for j in range(head.shape[0] // TILE):
        tile = slice(j * TILE, (j + 1) * TILE)
        out = logits[tile, :] + lax.dot_general(
            head[tile, hidden.shape[1]:], hidden[...], NT, preferred_element_type=F32
        )
        rows = lax.broadcasted_iota(jnp.int32, out.shape, 0) + (place.vocab * head.shape[0] + j * TILE)
        sums += fold(jnp.exp(out))
        picks += fold(jnp.where(rows == ids, out, 0.0))
    put_stats(stats, sums, picks)


def teacher_second(ids, blocks, head, logits):
    scratch = [((512, head.shape[1] // 2), BF16)]
    return kernel_call(teacher_second_kernel, (*ids, head, logits, *blocks), [(STATS, F32)], scratch, 8)[0]


def hidden_kernel(ids_own, ids_near, total, logits, head, own, near, far, far_near, lefts, rights, grad_t, product):
    place = Place()
    ids = place.ids(ids_own, ids_near)
    norm = jnp.log(total[0:1, :])
    for k in range(head.shape[0] // 128):
        part = slice(k * 128, (k + 1) * 128)
        rows = lax.broadcasted_iota(jnp.int32, (128, 512), 0) + (place.vocab * head.shape[0] + k * 128)
        onehot = jnp.where(rows == ids, 1.0, 0.0)
        grad_t[:, part] = (jnp.exp(logits[part, :] - norm) - onehot).T.astype(BF16)

    outs = ((own, 0), (lefts, 0), (rights, 0), (far, 0), (near, 0), (lefts, 64), (rights, 64), (far_near, 0))
    for j in range(head.shape[1] // WIDE):
        tile = slice(j * WIDE, (j + 1) * WIDE)
        product[...] = lax.dot_general(grad_t[...], head[:, tile], NN, preferred_element_type=F32)
        for r, (out, row) in enumerate(outs):
            out[row:row + 64, tile] = product[pl.ds(place.block(r), 64), :].astype(out.dtype)


def hidden_parts(ids, total, logits, head):
    v, d = head.shape
    outs = [((64, d), F32)] * 3 + [((64, d), BF16)] + [((128, d), BF16)] * 2
    scratch = [((512, v), BF16), ((512, WIDE), F32)]
    return kernel_call(hidden_kernel, (*ids, total, logits, head), outs, scratch, 6)


CHIPS = ((2, 1), (-1, 1), (1, 1), (2, 0), (-1, 0), (1, 0), (0, 1), (0, 0))


def grad_kernel(ids_own, ids_near, total, teacher, logits, mine, other, adv, mine_f, other_f):
    place = Place()
    ids = place.ids(ids_own, ids_near)
    norm = jnp.log(total[0:1, :])
    adv[...] = (teacher[1:2, :] - jnp.log(teacher[0:1, :])) - (total[1:2, :] - norm)
    for r, chip in enumerate(CHIPS):
        for out, core in ((mine_f, place.core), (other_f, 1 - place.core)):
            start = pl.multiple_of(place.chip(*chip) * 144 + core * 72, 8)
            rows = lax.broadcasted_iota(jnp.int32, (72, 512), 0) + (place.vocab * logits.shape[0] + start)
            onehot = jnp.where(rows == ids, 1.0, 0.0)
            probs = jnp.exp(logits[pl.ds(start, 72), :] - norm)
            out[r * 72:(r + 1) * 72, :] = adv[...] * (probs - onehot)
    mine[...] = mine_f[...].astype(BF16)
    other[...] = other_f[...].astype(BF16)


def logit_grads(ids, total, teacher, logits):
    half = logits.shape[0] // 2
    outs = [((half, 512), BF16)] * 2 + [((1, 512), F32)]
    return kernel_call(grad_kernel, (*ids, total, teacher, logits), outs, [((half, 512), F32)] * 2, 5)


def head_kernel(first, grad_mine, grad_from, hidden, hidden_from, *outs):
    rows = slice(first * 72, (first + len(outs)) * 72)
    for j in range(hidden.shape[1] // WIDE):
        tile = slice(j * WIDE, (j + 1) * WIDE)
        product = lax.dot_general(grad_mine[rows, :], hidden[:, tile], NN, preferred_element_type=F32)
        product += lax.dot_general(grad_from[rows, :], hidden_from[:, tile], NN, preferred_element_type=F32)
        for i, out in enumerate(outs):
            out[:, tile] = product[i * 72:(i + 1) * 72, :].astype(out.dtype)


def head_parts(first, types, grad_mine, grad_from, hidden, hidden_from):
    outs = [((72, hidden.shape[1]), t) for t in types]
    return kernel_call(functools.partial(head_kernel, first), (grad_mine, grad_from, hidden, hidden_from), outs, [], 4)


def finish_kernel(adv, own, lefts, rights, far, near, out):
    place = Place()
    total = own[...] + lefts[0:64, :].astype(F32) + rights[0:64, :].astype(F32)
    total += far[...].astype(F32) + near[...].astype(F32)
    token = lax.broadcasted_iota(jnp.int32, (64, 512), 0) + place.block(0)
    at = lax.broadcasted_iota(jnp.int32, (64, 512), 1)
    mine = jnp.sum(jnp.where(token == at, adv[...], 0.0), axis=1, keepdims=True)
    out[...] = (mine * total).astype(out.dtype)


def group_sum(a):
    around = a + send(a, X_UP) + send(a, X_DOWN) + send(a, X_FAR)
    return around + send(around, Y_HI)


def on_device(student_hidden, teacher_hidden, student_head, teacher_head, sampled_ids):
    ids = (sampled_ids, send(sampled_ids, Y_HI))

    up, down, over = Link(X_UP), Link(X_DOWN), Link(Y_HI)
    half = teacher_hidden.shape[1] // 2
    t_a, t_b = teacher_hidden[:, :half], teacher_hidden[:, half:]
    left, right, near = up(student_hidden), down(student_hidden), over(student_hidden)
    l_a, r_a, near_a = up(t_a), down(t_a), over(t_a)
    far, right_near, near_b = up(left), down(near), over(t_b)
    left_near, f_a, far_near = up(near), down(r_a), over(far)
    l_b, r_b, fn_a = up(t_b), down(t_b), over(f_a)
    ln_a, rn_a = up(near_a), down(near_a)
    f_b = up(l_b)
    fn_b = over(f_b)
    ln_b, rn_b = up(near_b), down(near_b)

    blocks = (student_hidden, left, right, far, near, left_near, right_near, far_near)
    logits, hidden, stats = student_logits((ids[0], after(ids[1], l_b, r_b, near_b)), blocks, student_head)
    hidden_from = send(hidden, CORE)
    total = after(group_sum(stats), ln_a, rn_a, f_b)
    parts = hidden_parts(ids, total, logits, student_head)
    teacher_logits = teacher_first((t_a, l_a, r_a, f_a, near_a, ln_a, rn_a, fn_a), teacher_head)
    teacher_logits = after(teacher_logits, parts[0])
    stats = teacher_second(ids, (t_b, l_b, r_b, f_b, near_b, ln_b, rn_b, fn_b), teacher_head, teacher_logits)
    teacher = group_sum(stats)

    g_own, g_near, g_far, g_far_near, g_lefts, g_rights = lax.optimization_barrier((*parts, stats))[:6]
    from_lefts, from_rights, from_fn = down(g_lefts), up(g_rights), over(g_far_near)
    from_far = send((g_far + from_fn.astype(F32)).astype(BF16), X_FAR)
    g_near = g_near + from_lefts[64:].astype(F32) + from_rights[64:].astype(F32)
    from_near = over(g_near.astype(BF16))

    mine, other, adv = logit_grads(ids, total, teacher, logits)
    from_core = send(other, CORE)
    h_fl, h_ll, h_rl, h_f = head_parts(0, (BF16, BF16, BF16, F32), mine, from_core, hidden, hidden_from)
    h_l, h_r, h_y, h_own = head_parts(4, (F32,) * 4, mine, from_core, hidden, hidden_from)
    far = h_f + send(h_fl, Y_LO).astype(F32)
    cut = far.shape[1] // 2
    far = far.astype(BF16)
    far_left, far_right = send(far[:, :cut], Z_DOWN).astype(F32), send(far[:, cut:], Z_UP).astype(F32)
    y_sum = h_y + send(h_ll, Z_DOWN).astype(F32) + send(h_rl, Z_UP).astype(F32)
    l_sum = jnp.concatenate([h_l[:, :cut] + far_left, h_l[:, cut:]], axis=1)
    r_sum = jnp.concatenate([h_r[:, :cut], h_r[:, cut:] + far_right], axis=1)
    head_sum = (
        h_own
        + send(y_sum.astype(BF16), Y_LO).astype(F32)
        + send(l_sum.astype(BF16), Z_DOWN).astype(F32)
        + send(r_sum.astype(BF16), Z_UP).astype(F32)
    )
    pieces = (adv, g_own, from_lefts, from_rights, from_far, from_near)
    return kernel_call(finish_kernel, pieces, [(student_hidden.shape, BF16)], [], 4)[0], head_sum.astype(BF16)


def solution(mesh):
    in_specs = (
        P(("dp", "vocab"), None),
        P(("dp", "vocab"), None),
        P("vocab", None),
        P("vocab", None),
        P("dp"),
    )
    out_specs = (P(("dp", "vocab"), None), P(("vocab", "dp"), None))
    return jax.shard_map(
        on_device, mesh=mesh, in_specs=in_specs, out_specs=out_specs, check_vma=False
    )
```

time: 375 us -> 153 us (0.41)
  waiting for transfers between devices: 299 us -> 58.2 us
  starting transfers between devices: 0.16 us -> 64.7 us
  matrix products: 36.4 us -> 0 us
  blocking collectives: 20 us -> 0 us
  Pallas kernels: 0 us -> 19.9 us
  between operations: 13.8 us -> 0.88 us
  local copies, waits for them, and re-layouts: 1.68 us -> 5.54 us
    reduce_scatter x2 -> x0, waiting for transfers between devices: 161 us -> none  [the longest x1 80.5 us: on_device(): lax.psum_scatter(lax.dot_general(block, student_rows, (((0,), (0,)), ((),...]
    all_gather x2 -> x0, waiting for transfers between devices: 137 us -> none  [the longest x1 74.4 us: on_device(): lax.all_gather(teacher_hidden, 'vocab', axis=0, tiled=True)]
    ppermute x0 -> x45, starting transfers between devices: none -> 64.7 us  [send(): return lax.ppermute(a, AXES, to)]
    ppermute x0 -> x45, waiting for transfers between devices: none -> 58.2 us  [send(): return lax.ppermute(a, AXES, to)]
    dot_general x4 -> x0, matrix products: 36.4 us -> none  [the longest x2 19.9 us: logits_of(): lax.dot_general(hidden, head, (((1,), (1,)), ((), ())), preferred_element...]
    psum x1 -> x0, blocking collectives: 20 us -> none  [block_sums(): lax.psum((jnp.sum(jnp.exp(student_logits), axis=1), jnp.sum(jnp.exp(teach...]
    pallas_call x0 -> x8, Pallas kernels: none -> 19.9 us  [kernel_call(): pl.pallas_call(body, in_specs=[VMEM] * len(arrays), out_specs=[VMEM] * le...]
  transfers between devices with their start and end apart: 4 -> 45, of which waited for: 4 -> 24; matrix products, arithmetic and copies ran while one was open for 5% -> 1% of each run, Pallas kernels for 0% -> 11%
where the time goes in v2:
time: 153 us; the launch traced here: 151 us
  starting transfers between devices  64.7 us (42%)
  waiting for transfers between devices  58.2 us (38%)
  Pallas kernels  19.9 us (13%)
  local copies, waits for them, and re-layouts  5.54 us (4%)
    ppermute x45, starting transfers between devices, send(): return lax.ppermute(a, AXES, to)  64.7 us
    ppermute x45, waiting for transfers between devices, send(): return lax.ppermute(a, AXES, to)  58.2 us
    pallas_call x8, Pallas kernels, kernel_call(): pl.pallas_call(body, in_specs=[VMEM] * len(arrays), out_specs=[VMEM] * le...  19.9 us
    unnamed x18, local copies, waits for them, and re-layouts  4.35 us
  transfers between devices with their start and end apart: 45, of which 24 were waited for; matrix products, arithmetic and copies ran while one was open for 1% of the time, Pallas kernels for 11%

profile of v2, /device:TPU:0, one launch (start us, length us, event | category | flops | bytes accessed | tf_op | source)
XLA Modules:
  0.0 150.8 jit_solution(18076876721725388597)
XLA Ops:
  0.6 1.6 %collective-permute-start.1 = (bf16[64,2560]{1,0:T(8,128)(2,1)}, bf16[64,2560]{1,0:T(8,128)(2,1)S(1)}, u32[]{:S(2)}, u32[]{:S(2)}) collective-permute-start(bf16[64,2560]{1,0:T(8,128)(2,1)} %refs_0_.1), channel_id=1, source_target_pairs={{0,2},{1,3},{2,4},{3,5},{4,6},{5,7},{6,0},{7,1},{8,10},{9,11},{10,... | collective-permute-start | bytes 983048 | tf_op jit(solution)/shard_map/ppermute | solution.py:39
  2.3 3.0 %collective-permute-start.4 = (bf16[64,2560]{1,0:T(8,128)(2,1)}, bf16[64,2560]{1,0:T(8,128)(2,1)S(1)}, u32[]{:S(2)}, u32[]{:S(2)}) collective-permute-start(bf16[64,2560]{1,0:T(8,128)(2,1)} %refs_0_.1), channel_id=1, source_target_pairs={{0,65},{1,64},{2,67},{3,66},{4,69},{5,68},{6,71},{7,70},{8,73},{9,... | collective-permute-start | bytes 983048 | tf_op jit(solution)/shard_map/ppermute | solution.py:39
  5.3 1.7 %collective-permute-start.5 = (bf16[64,2560]{1,0:T(8,128)(2,1)}, bf16[64,2560]{1,0:T(8,128)(2,1)S(1)}, u32[]{:S(2)}, u32[]{:S(2)}) collective-permute-start(bf16[64,2560]{1,0:T(8,128)(2,1)} %refs_0_.1), channel_id=1, source_target_pairs={{0,6},{1,7},{2,0},{3,1},{4,2},{5,3},{6,4},{7,5},{8,14},{9,15},{10,... | collective-permute-start | bytes 983048 | tf_op jit(solution)/shard_map/ppermute | solution.py:39
  7.0 1.1 fusion
  8.5 3.0 %collective-permute-start.18 = (bf16[64,2560]{1,0:T(8,128)(2,1)S(1)}, bf16[64,2560]{1,0:T(8,128)(2,1)S(1)}, u32[]{:S(2)}, u32[]{:S(2)}) collective-permute-start(bf16[64,2560]{1,0:T(8,128)(2,1)S(1)} %get-tuple-element.98.refs_0_), channel_id=1, source_target_pairs={{0,6},{1,7},{2,0},{3,1},{4,2},{5,3},{6,4},{7,5},{8,14},{9,15},{10,... | collective-permute-start | bytes 983048 | tf_op jit(solution)/shard_map/ppermute | solution.py:39
  11.8 1.2 collective-permute-start.2
  13.1 3.1 %collective-permute-done.5.refs_2_ = bf16[64,2560]{1,0:T(8,128)(2,1)S(1)} collective-permute-done((bf16[64,2560]{1,0:T(8,128)(2,1)}, bf16[64,2560]{1,0:T(8,128)(2,1)S(1)}, u32[]{:S(2)}, u32[]{:S(2)}) %collective-permute-start.5) | collective-permute-done | bytes 327712 | tf_op jit(solution)/shard_map/ppermute | solution.py:39
  16.1 3.0 %collective-permute-start.6 = (bf16[64,2560]{1,0:T(8,128)(2,1)S(1)}, bf16[64,2560]{1,0:T(8,128)(2,1)S(1)}, u32[]{:S(2)}, u32[]{:S(2)}) collective-permute-start(bf16[64,2560]{1,0:T(8,128)(2,1)S(1)} %collective-permute-done.4.refs_4_), channel_id=1, source_target_pairs={{0,6},{1,7},{2,0},{3,1},{4,2},{5,3},{6,4},{7,5},{8,14},{9,15},{10,... | collective-permute-start | bytes 983048 | tf_op jit(solution)/shard_map/ppermute | solution.py:39
  19.2 0.8 collective-permute-done.9.refs_1_
  20.1 3.1 %collective-permute-done.18.refs_2_ = bf16[64,2560]{1,0:T(8,128)(2,1)S(1)} collective-permute-done((bf16[64,2560]{1,0:T(8,128)(2,1)S(1)}, bf16[64,2560]{1,0:T(8,128)(2,1)S(1)}, u32[]{:S(2)}, u32[]{:S(2)}) %collective-permute-start.18) | collective-permute-done | bytes 327712 | tf_op jit(solution)/shard_map/ppermute | solution.py:39
  23.2 3.0 %collective-permute-start.19 = (bf16[64,2560]{1,0:T(8,128)(2,1)S(1)}, bf16[64,2560]{1,0:T(8,128)(2,1)S(1)}, u32[]{:S(2)}, u32[]{:S(2)}) collective-permute-start(bf16[64,2560]{1,0:T(8,128)(2,1)S(1)} %collective-permute-done.18.refs_2_), channel_id=1, source_target_pairs={{0,6},{1,7},{2,0},{3,1},{4,2},{5,3},{6,4},{7,5},{8,14},{9,15},{10,... | collective-permute-start | bytes 983048 | tf_op jit(solution)/shard_map/ppermute | solution.py:39
  26.1 1.0 collective-permute-done.2.refs_3_
  27.1 2.8 %collective-permute-start.8 = (bf16[64,2560]{1,0:T(8,128)(2,1)S(1)}, bf16[64,2560]{1,0:T(8,128)(2,1)S(1)}, u32[]{:S(2)}, u32[]{:S(2)}) collective-permute-start(bf16[64,2560]{1,0:T(8,128)(2,1)S(1)} %get-tuple-element.54.refs_0_), channel_id=1, source_target_pairs={{0,65},{1,64},{2,67},{3,66},{4,69},{5,68},{6,71},{7,70},{8,73},{9,... | collective-permute-start | bytes 983048 | tf_op jit(solution)/shard_map/ppermute | solution.py:39
  30.2 1.5 collective-permute-start.3
  31.7 1.7 %collective-permute-start.7 = (bf16[64,2560]{1,0:T(8,128)(2,1)S(1)}, bf16[64,2560]{1,0:T(8,128)(2,1)S(1)}, u32[]{:S(2)}, u32[]{:S(2)}) collective-permute-start(bf16[64,2560]{1,0:T(8,128)(2,1)S(1)} %get-tuple-element.54.refs_0_), channel_id=1, source_target_pairs={{0,6},{1,7},{2,0},{3,1},{4,2},{5,3},{6,4},{7,5},{8,14},{9,15},{10,... | collective-permute-start | bytes 983048 | tf_op jit(solution)/shard_map/ppermute | solution.py:39
  33.8 3.1 %collective-permute-start.12 = (bf16[64,2560]{1,0:T(8,128)(2,1)S(1)}, bf16[64,2560]{1,0:T(8,128)(2,1)S(1)}, u32[]{:S(2)}, u32[]{:S(2)}) collective-permute-start(bf16[64,2560]{1,0:T(8,128)(2,1)S(1)} %collective-permute-done.2.refs_3_), channel_id=1, source_target_pairs={{0,65},{1,64},{2,67},{3,66},{4,69},{5,68},{6,71},{7,70},{8,73},{9,... | collective-permute-start | bytes 983048 | tf_op jit(solution)/shard_map/ppermute | solution.py:39
  37.4 1.5 collective-permute-start.17
  38.9 3.7 %collective-permute-done.ids_near = s32[512]{0:T(512)S(1)} collective-permute-done((s32[512]{0:T(512)}, s32[512]{0:T(512)S(1)}, u32[]{:S(2)}, u32[]{:S(2)}) %collective-permute-start) | collective-permute-done | bytes 2080 | tf_op jit(solution)/shard_map/ppermute | solution.py:39
  42.6 2.6 %collective-permute-start.20 = (bf16[64,2560]{1,0:T(8,128)(2,1)S(1)}, bf16[64,2560]{1,0:T(8,128)(2,1)S(1)}, u32[]{:S(2)}, u32[]{:S(2)}) collective-permute-start(bf16[64,2560]{1,0:T(8,128)(2,1)S(1)} %collective-permute-done.11.refs_4_), channel_id=1, source_target_pairs={{0,6},{1,7},{2,0},{3,1},{4,2},{5,3},{6,4},{7,5},{8,14},{9,15},{10,... | collective-permute-start | bytes 983048 | tf_op jit(solution)/shard_map/ppermute | solution.py:39
  45.2 1.9 %collective-permute-start.22 = (bf16[64,2560]{1,0:T(8,128)(2,1)S(1)}, bf16[64,2560]{1,0:T(8,128)(2,1)S(1)}, u32[]{:S(2)}, u32[]{:S(2)}) collective-permute-start(bf16[64,2560]{1,0:T(8,128)(2,1)S(1)} %collective-permute-done.19.refs_3_), channel_id=1, source_target_pairs={{0,65},{1,64},{2,67},{3,66},{4,69},{5,68},{6,71},{7,70},{8,73},{9,... | collective-permute-start | bytes 983048 | tf_op jit(solution)/shard_map/ppermute | solution.py:39
  47.1 2.7 %copy-done = bf16[1152,2560]{1,0:T(8,128)(2,1)S(1)} copy-done((bf16[1152,2560]{1,0:T(8,128)(2,1)S(1)}, bf16[1152,2560]{1,0:T(8,128)(2,1)}, u32[]{:S(2)}) %copy-start) | copy-done | bytes 5898264
  49.8 1.0 copy-done.1
  50.8 0.7 copy-done.2
  51.5 3.5 %shard_map.68 = (f32[1152,512]{1,0:T(8,128)S(1)}, bf16[512,2560]{1,0:T(8,128)(2,1)S(1)}, f32[8,512]{1,0:T(8,128)S(1)}) custom-call(s32[512]{0:T(512)S(1)} %copy-done.2, s32[512]{0:T(512)S(1)} %collective-permute-done.ids_near, bf16[1152,2560]{1,0:T(8,128)(2,1)S(1)} %copy-done, bf16[64,2560]{1,0:T(8,128)(2,1)S(1)} %copy-done.1, ...), custom_call_target="tpu_custom_call" | custom-call | flops 20000000000 | bytes 20000000 | tf_op jit(solution)/shard_map/pallas_call | solution.py:67
  55.0 0.9 collective-permute-start.15
  55.9 2.4 %collective-permute-start.14 = (f32[8,512]{1,0:T(8,128)S(1)}, f32[8,512]{1,0:T(8,128)S(1)}, u32[]{:S(2)}, u32[]{:S(2)}) collective-permute-start(f32[8,512]{1,0:T(8,128)S(1)} %get-tuple-element.58), channel_id=1, source_target_pairs={{0,6},{1,7},{2,0},{3,1},{4,2},{5,3},{6,4},{7,5},{8,14},{9,15},{10,... | collective-permute-start | bytes 49160 | tf_op jit(solution)/shard_map/ppermute | solution.py:39
  58.2 2.3 %collective-permute-done.15 = f32[8,512]{1,0:T(8,128)S(1)} collective-permute-done((f32[8,512]{1,0:T(8,128)S(1)}, f32[8,512]{1,0:T(8,128)S(1)}, u32[]{:S(2)}, u32[]{:S(2)}) %collective-permute-start.15) | collective-permute-done | bytes 16416 | tf_op jit(solution)/shard_map/ppermute | solution.py:39
  60.5 0.4 collective-permute-start.21
  61.2 2.2 %collective-permute-done.13 = f32[8,512]{1,0:T(8,128)S(1)} collective-permute-done((f32[8,512]{1,0:T(8,128)S(1)}, f32[8,512]{1,0:T(8,128)S(1)}, u32[]{:S(2)}, u32[]{:S(2)}) %collective-permute-start.13) | collective-permute-done | bytes 16416 | tf_op jit(solution)/shard_map/ppermute | solution.py:39
  63.4 0.7 collective-permute-start.24
  64.2 1.3 collective-permute-start.16
  65.5 3.4 %shard_map.69.logits = f32[1152,512]{1,0:T(8,128)S(1)} custom-call(bf16[1152,5120]{1,0:T(8,128)(2,1)S(1)} %bitcast.1, bf16[64,2560]{1,0:T(8,128)(2,1)S(1)} %get-tuple-element.98.refs_0_, bf16[64,2560]{1,0:T(8,128)(2,1)S(1)} %collective-permute-done.9.refs_1_, bf16[64,2560]{1,0:T(8,128)(2,1)S(1)} %collective-permute-done.18.refs_2_, ...), custom_call_target="tpu_custom_call" | custom-call | flops 20000000000 | bytes 20000000 | tf_op jit(solution)/shard_map/pallas_call | solution.py:67
  68.9 0.7 collective-permute-done.16
  69.6 0.5 collective-permute-done.21.refs_3_
  70.2 1.1 collective-permute-start.25
  71.3 4.1 %shard_map.70 = (f32[64,2560]{1,0:T(8,128)S(1)}, f32[64,2560]{1,0:T(8,128)S(1)}, f32[64,2560]{1,0:T(8,128)S(1)}, bf16[64,2560]{1,0:T(8,128)(2,1)S(1)}, bf16[128,...) custom-call(s32[512]{0:T(512)S(1)} %copy-done.3, s32[512]{0:T(512)S(1)} %collective-permute-done.ids_near, ...), custom_call_target="tpu_custom_call" | custom-call | flops 20000000000 | bytes 20000000 | tf_op jit(solution)/shard_map/pallas_call | solution.py:67
  75.3 3.1 %collective-permute-done.25.refs_7_ = bf16[64,2560]{1,0:T(8,128)(2,1)S(1)} collective-permute-done((bf16[64,2560]{1,0:T(8,128)(2,1)S(1)}, bf16[64,2560]{1,0:T(8,128)(2,1)S(1)}, u32[]{:S(2)}, u32[]{:S(2)}) %collective-permute-start.25) | collective-permute-done | bytes 327712 | tf_op jit(solution)/shard_map/ppermute | solution.py:39
  78.5 3.7 %shard_map.71 = f32[8,512]{1,0:T(8,128)S(1)} custom-call(s32[512]{0:T(512)S(1)} %copy-done.3, s32[512]{0:T(512)S(1)} %collective-permute-done.ids_near, bf16[1152,5120]{1,0:T(8,128)(2,1)S(1)} %bitcast.1, f32[1152,512]{1,0:T(8,128)S(1)} %shard_map.69.logits, bf16[64,2560]{1,0:T(8,128)(2,1)S(1)} %get-tuple-element.54.refs_0_, ...), custom_call_target="tpu_custom_call" | custom-call | flops 20000000000 | bytes 20000000 | tf_op jit(solution)/shard_map/pallas_call | solution.py:67
  82.2 0.7 collective-permute-start.28
  82.9 2.9 %collective-permute-start.27 = (f32[8,512]{1,0:T(8,128)S(1)}, f32[8,512]{1,0:T(8,128)S(1)}, u32[]{:S(2)}, u32[]{:S(2)}) collective-permute-start(f32[8,512]{1,0:T(8,128)S(1)} %shard_map.71), channel_id=1, source_target_pairs={{0,6},{1,7},{2,0},{3,1},{4,2},{5,3},{6,4},{7,5},{8,14},{9,15},{10,... | collective-permute-start | bytes 49160 | tf_op jit(solution)/shard_map/ppermute | solution.py:39
  85.8 1.7 %collective-permute-done.28 = f32[8,512]{1,0:T(8,128)S(1)} collective-permute-done((f32[8,512]{1,0:T(8,128)S(1)}, f32[8,512]{1,0:T(8,128)S(1)}, u32[]{:S(2)}, u32[]{:S(2)}) %collective-permute-start.28) | collective-permute-done | bytes 16416 | tf_op jit(solution)/shard_map/ppermute | solution.py:39
  87.5 3.2 %collective-permute-done.26 = f32[8,512]{1,0:T(8,128)S(1)} collective-permute-done((f32[8,512]{1,0:T(8,128)S(1)}, f32[8,512]{1,0:T(8,128)S(1)}, u32[]{:S(2)}, u32[]{:S(2)}) %collective-permute-start.26) | collective-permute-done | bytes 16416 | tf_op jit(solution)/shard_map/ppermute | solution.py:39
  90.8 1.5 %collective-permute-start.29 = (f32[8,512]{1,0:T(8,128)S(1)}, f32[8,512]{1,0:T(8,128)S(1)}, u32[]{:S(2)}, u32[]{:S(2)}) collective-permute-start(f32[8,512]{1,0:T(8,128)S(1)} %add_add_fusion), channel_id=1, source_target_pairs={{0,65},{1,64},{2,67},{3,66},{4,69},{5,68},{6,71},{7,70},{8,73},{9,... | collective-permute-start | bytes 49160 | tf_op jit(solution)/shard_map/ppermute | solution.py:39
  92.4 1.9 %collective-permute-start.31 = (bf16[128,2560]{1,0:T(8,128)(2,1)S(1)}, bf16[128,2560]{1,0:T(8,128)(2,1)S(1)}, u32[]{:S(2)}, u32[]{:S(2)}) collective-permute-start(bf16[128,2560]{1,0:T(8,128)(2,1)S(1)} %get-tuple-element.81), channel_id=1, source_target_pairs={{0,2},{1,3},{2,4},{3,5},{4,6},{5,7},{6,0},{7,1},{8,10},{9,11},{10,... | collective-permute-start | bytes 1966088 | tf_op jit(solution)/shard_map/ppermute | solution.py:39
  94.3 1.7 %collective-permute-start.32 = (bf16[64,2560]{1,0:T(8,128)(2,1)S(1)}, bf16[64,2560]{1,0:T(8,128)(2,1)S(1)}, u32[]{:S(2)}, u32[]{:S(2)}) collective-permute-start(bf16[64,2560]{1,0:T(8,128)(2,1)S(1)} %get-tuple-element.84), channel_id=1, source_target_pairs={{0,65},{1,64},{2,67},{3,66},{4,69},{5,68},{6,71},{7,70},{8,73},{9,... | collective-permute-start | bytes 983048 | tf_op jit(solution)/shard_map/ppermute | solution.py:39
  96.0 0.7 shard_map.72
  96.8 8.2 %collective-permute-done.32 = bf16[64,2560]{1,0:T(8,128)(2,1)S(1)} collective-permute-done((bf16[64,2560]{1,0:T(8,128)(2,1)S(1)}, bf16[64,2560]{1,0:T(8,128)(2,1)S(1)}, u32[]{:S(2)}, u32[]{:S(2)}) %collective-permute-start.32) | collective-permute-done | bytes 327712 | tf_op jit(solution)/shard_map/ppermute | solution.py:39
  105.3 4.6 %collective-permute-done.30.lefts = bf16[128,2560]{1,0:T(8,128)(2,1)S(1)} collective-permute-done((bf16[128,2560]{1,0:T(8,128)(2,1)S(1)}, bf16[128,2560]{1,0:T(8,128)(2,1)S(1)}, u32[]{:S(2)}, u32[]{:S(2)}) %collective-permute-start.30) | collective-permute-done | bytes 655392 | tf_op jit(solution)/shard_map/ppermute | solution.py:39
  109.8 7.9 %collective-permute-done.31.rights = bf16[128,2560]{1,0:T(8,128)(2,1)S(1)} collective-permute-done((bf16[128,2560]{1,0:T(8,128)(2,1)S(1)}, bf16[128,2560]{1,0:T(8,128)(2,1)S(1)}, u32[]{:S(2)}, u32[]{:S(2)}) %collective-permute-start.31) | collective-permute-done | bytes 655392 | tf_op jit(solution)/shard_map/ppermute | solution.py:39
  117.8 2.0 %collective-permute-start.34 = (bf16[64,2560]{1,0:T(8,128)(2,1)S(1)}, bf16[64,2560]{1,0:T(8,128)(2,1)S(1)}, u32[]{:S(2)}, u32[]{:S(2)}) collective-permute-start(bf16[64,2560]{1,0:T(8,128)(2,1)S(1)} %add_convert_fusion.3), channel_id=1, source_target_pairs={{0,65},{1,64},{2,67},{3,66},{4,69},{5,68},{6,71},{7,70},{8,73},{9,... | collective-permute-start | bytes 983048 | tf_op jit(solution)/shard_map/ppermute | solution.py:39
  119.8 1.7 %shard_map.75 = (bf16[72,2560]{1,0:T(8,128)(2,1)S(1)}, bf16[72,2560]{1,0:T(8,128)(2,1)S(1)}, bf16[72,2560]{1,0:T(8,128)(2,1)S(1)}, f32[72,2560]{1,0:T(8,128)S(1)}) custom-call(bf16[576,512]{1,0:T(8,128)(2,1)S(1)} %get-tuple-element.87.grad_mine, bf16[576,512]{1,0:T(8,128)(2,1)S(1)} %collective-permute-done.35.grad_from, ...), custom_call_target="tpu_custom_call" | custom-call | flops 20000000000 | bytes 20000000 | tf_op jit(solution)/shard_map/pallas_call | solution.py:67
  121.6 1.7 %shard_map.74 = (f32[72,2560]{1,0:T(8,128)S(1)}, f32[72,2560]{1,0:T(8,128)S(1)}, f32[72,2560]{1,0:T(8,128)S(1)}, f32[72,2560]{1,0:T(8,128)S(1)}) custom-call(bf16[576,512]{1,0:T(8,128)(2,1)S(1)} %get-tuple-element.87.grad_mine, bf16[576,512]{1,0:T(8,128)(2,1)S(1)} %collective-permute-done.35.grad_from, bf16[512,2560]{1,0:T(8,128)(2,1)S(1)} %get-tuple-element.89.hidden, ...), custom_call_target="tpu_custom_call" | custom-call | flops 20000000000 | bytes 20000000 | tf_op jit(solution)/shard_map/pallas_call | solution.py:67
  123.4 2.0 %collective-permute-start.38 = (bf16[72,2560]{1,0:T(8,128)(2,1)S(1)}, bf16[72,2560]{1,0:T(8,128)(2,1)S(1)}, u32[]{:S(2)}, u32[]{:S(2)}) collective-permute-start(bf16[72,2560]{1,0:T(8,128)(2,1)S(1)} %get-tuple-element.93), channel_id=1, source_target_pairs={{0,16},{1,17},{2,18},{3,19},{4,20},{5,21},{6,22},{7,23},{8,24},{9,... | collective-permute-start | bytes 1105928 | tf_op jit(solution)/shard_map/ppermute | solution.py:39
  125.3 2.2 %collective-permute-start.37 = (bf16[72,2560]{1,0:T(8,128)(2,1)S(1)}, bf16[72,2560]{1,0:T(8,128)(2,1)S(1)}, u32[]{:S(2)}, u32[]{:S(2)}) collective-permute-start(bf16[72,2560]{1,0:T(8,128)(2,1)S(1)} %get-tuple-element.92), channel_id=1, source_target_pairs={{0,48},{1,49},{2,50},{3,51},{4,52},{5,53},{6,54},{7,55},{8,56},{9,... | collective-permute-start | bytes 1105928 | tf_op jit(solution)/shard_map/ppermute | solution.py:39
  127.5 3.9 %collective-permute-done.40 = bf16[72,2560]{1,0:T(8,128)(2,1)S(1)} collective-permute-done((bf16[72,2560]{1,0:T(8,128)(2,1)S(1)}, bf16[72,2560]{1,0:T(8,128)(2,1)S(1)}, u32[]{:S(2)}, u32[]{:S(2)}) %collective-permute-start.40) | collective-permute-done | bytes 368672 | tf_op jit(solution)/shard_map/ppermute | solution.py:39
  131.6 2.0 %collective-permute-start.43 = (bf16[72,1280]{1,0:T(8,128)(2,1)S(1)}, bf16[72,1280]{1,0:T(8,128)(2,1)S(1)}, u32[]{:S(2)}, u32[]{:S(2)}) collective-permute-start(bf16[72,1280]{1,0:T(8,128)(2,1)S(1)} %get-tuple-element.101), channel_id=1, source_target_pairs={{0,16},{1,17},{2,18},{3,19},{4,20},{5,21},{6,22},{7,23},{8,24},{9,... | collective-permute-start | bytes 552968 | tf_op jit(solution)/shard_map/ppermute | solution.py:39
  133.6 2.5 %collective-permute-done.38 = bf16[72,2560]{1,0:T(8,128)(2,1)S(1)} collective-permute-done((bf16[72,2560]{1,0:T(8,128)(2,1)S(1)}, bf16[72,2560]{1,0:T(8,128)(2,1)S(1)}, u32[]{:S(2)}, u32[]{:S(2)}) %collective-permute-start.38) | collective-permute-done | bytes 368672 | tf_op jit(solution)/shard_map/ppermute | solution.py:39
  136.1 1.7 %collective-permute-start.41 = (bf16[72,1280]{1,0:T(8,128)(2,1)S(1)}, bf16[72,1280]{1,0:T(8,128)(2,1)S(1)}, u32[]{:S(2)}, u32[]{:S(2)}) collective-permute-start(bf16[72,1280]{1,0:T(8,128)(2,1)S(1)} %get-tuple-element.100), channel_id=1, source_target_pairs={{0,48},{1,49},{2,50},{3,51},{4,52},{5,53},{6,54},{7,55},{8,56},{9,... | collective-permute-start | bytes 552968 | tf_op jit(solution)/shard_map/ppermute | solution.py:39
  138.0 3.0 %collective-permute-start.39 = (bf16[72,2560]{1,0:T(8,128)(2,1)S(1)}, bf16[72,2560]{1,0:T(8,128)(2,1)S(1)}, u32[]{:S(2)}, u32[]{:S(2)}) collective-permute-start(bf16[72,2560]{1,0:T(8,128)(2,1)S(1)} %add_convert_fusion.2), channel_id=1, source_target_pairs={{0,64},{1,65},{2,66},{3,67},{4,68},{5,69},{6,70},{7,71},{8,72},{9,... | collective-permute-start | bytes 1105928 | tf_op jit(solution)/shard_map/ppermute | solution.py:39
  141.7 3.0 %collective-permute-start.42 = (bf16[72,2560]{1,0:T(8,128)(2,1)S(1)}, bf16[72,2560]{1,0:T(8,128)(2,1)S(1)}, u32[]{:S(2)}, u32[]{:S(2)}) collective-permute-start(bf16[72,2560]{1,0:T(8,128)(2,1)S(1)} %pad_maximum_fusion), channel_id=1, source_target_pairs={{0,48},{1,49},{2,50},{3,51},{4,52},{5,53},{6,54},{7,55},{8,56},{9,... | collective-permute-start | bytes 1105928 | tf_op jit(solution)/shard_map/ppermute | solution.py:39
  144.7 1.1 shard_map.73
  145.9 0.6 collective-permute-done.39
  146.4 3.4 %collective-permute-done.44 = bf16[72,2560]{1,0:T(8,128)(2,1)S(1)} collective-permute-done((bf16[72,2560]{1,0:T(8,128)(2,1)S(1)}, bf16[72,2560]{1,0:T(8,128)(2,1)S(1)}, u32[]{:S(2)}, u32[]{:S(2)}) %collective-permute-start.44) | collective-permute-done | bytes 368672 | tf_op jit(solution)/shard_map/ppermute | solution.py:39
  149.8 0.9 add_convert_fusion
  (71 shorter events, 4.1 us)
Async XLA Ops:
  0.6 11.2 %collective-permute-start.1 = (bf16[64,2560]{1,0:T(8,128)(2,1)}, bf16[64,2560]{1,0:T(8,128)(2,1)S(1)}, u32[]{:S(2)}, u32[]{:S(2)}) collective-permute-start(bf16[64,2560]{1,0:T(8,128)(2,1)} %refs_0_.1), channel_id=1, source_target_pairs={{0,2},{1,3},{2,4},{3,5},{4,6},{5,7},{6,0},{7,1},{8,10},{9,11},{10,... | collective-permute-start | bytes 983048 | tf_op jit(solution)/shard_map/ppermute | solution.py:39
  2.3 10.8 %collective-permute-start.4 = (bf16[64,2560]{1,0:T(8,128)(2,1)}, bf16[64,2560]{1,0:T(8,128)(2,1)S(1)}, u32[]{:S(2)}, u32[]{:S(2)}) collective-permute-start(bf16[64,2560]{1,0:T(8,128)(2,1)} %refs_0_.1), channel_id=1, source_target_pairs={{0,65},{1,64},{2,67},{3,66},{4,69},{5,68},{6,71},{7,70},{8,73},{9,... | collective-permute-start | bytes 983048 | tf_op jit(solution)/shard_map/ppermute | solution.py:39
  5.3 10.9 %collective-permute-start.5 = (bf16[64,2560]{1,0:T(8,128)(2,1)}, bf16[64,2560]{1,0:T(8,128)(2,1)S(1)}, u32[]{:S(2)}, u32[]{:S(2)}) collective-permute-start(bf16[64,2560]{1,0:T(8,128)(2,1)} %refs_0_.1), channel_id=1, source_target_pairs={{0,6},{1,7},{2,0},{3,1},{4,2},{5,3},{6,4},{7,5},{8,14},{9,15},{10,... | collective-permute-start | bytes 983048 | tf_op jit(solution)/shard_map/ppermute | solution.py:39
  8.2 11.9 %collective-permute-start.9 = (bf16[64,2560]{1,0:T(8,128)(2,1)S(1)}, bf16[64,2560]{1,0:T(8,128)(2,1)S(1)}, u32[]{:S(2)}, u32[]{:S(2)}) collective-permute-start(bf16[64,2560]{1,0:T(8,128)(2,1)S(1)} %get-tuple-element.98.refs_0_), channel_id=1, source_target_pairs={{0,2},{1,3},{2,4},{3,5},{4,6},{5,7},{6,0},{7,1},{8,10},{9,11},{10,... | collective-permute-start | bytes 983048 | tf_op jit(solution)/shard_map/ppermute | solution.py:39
  8.5 14.7 %collective-permute-start.18 = (bf16[64,2560]{1,0:T(8,128)(2,1)S(1)}, bf16[64,2560]{1,0:T(8,128)(2,1)S(1)}, u32[]{:S(2)}, u32[]{:S(2)}) collective-permute-start(bf16[64,2560]{1,0:T(8,128)(2,1)S(1)} %get-tuple-element.98.refs_0_), channel_id=1, source_target_pairs={{0,6},{1,7},{2,0},{3,1},{4,2},{5,3},{6,4},{7,5},{8,14},{9,15},{10,... | collective-permute-start | bytes 983048 | tf_op jit(solution)/shard_map/ppermute | solution.py:39
  11.8 15.3 %collective-permute-start.2 = (bf16[64,2560]{1,0:T(8,128)(2,1)S(1)}, bf16[64,2560]{1,0:T(8,128)(2,1)S(1)}, u32[]{:S(2)}, u32[]{:S(2)}) collective-permute-start(bf16[64,2560]{1,0:T(8,128)(2,1)S(1)} %collective-permute-done.1.refs_1_), channel_id=1, source_target_pairs={{0,2},{1,3},{2,4},{3,5},{4,6},{5,7},{6,0},{7,1},{8,10},{9,11},{10,... | collective-permute-start | bytes 983048 | tf_op jit(solution)/shard_map/ppermute | solution.py:39
  16.1 14.0 %collective-permute-start.6 = (bf16[64,2560]{1,0:T(8,128)(2,1)S(1)}, bf16[64,2560]{1,0:T(8,128)(2,1)S(1)}, u32[]{:S(2)}, u32[]{:S(2)}) collective-permute-start(bf16[64,2560]{1,0:T(8,128)(2,1)S(1)} %collective-permute-done.4.refs_4_), channel_id=1, source_target_pairs={{0,6},{1,7},{2,0},{3,1},{4,2},{5,3},{6,4},{7,5},{8,14},{9,15},{10,... | collective-permute-start | bytes 983048 | tf_op jit(solution)/shard_map/ppermute | solution.py:39
  19.1 12.6 %collective-permute-start.11 = (bf16[64,2560]{1,0:T(8,128)(2,1)S(1)}, bf16[64,2560]{1,0:T(8,128)(2,1)S(1)}, u32[]{:S(2)}, u32[]{:S(2)}) collective-permute-start(bf16[64,2560]{1,0:T(8,128)(2,1)S(1)} %get-tuple-element.98.refs_0_), channel_id=1, source_target_pairs={{0,65},{1,64},{2,67},{3,66},{4,69},{5,68},{6,71},{7,70},{8,73},{9,... | collective-permute-start | bytes 983048 | tf_op jit(solution)/shard_map/ppermute | solution.py:39
  20.1 13.7 %collective-permute-start.10 = (bf16[64,2560]{1,0:T(8,128)(2,1)S(1)}, bf16[64,2560]{1,0:T(8,128)(2,1)S(1)}, u32[]{:S(2)}, u32[]{:S(2)}) collective-permute-start(bf16[64,2560]{1,0:T(8,128)(2,1)S(1)} %collective-permute-done.4.refs_4_), channel_id=1, source_target_pairs={{0,2},{1,3},{2,4},{3,5},{4,6},{5,7},{6,0},{7,1},{8,10},{9,11},{10,... | collective-permute-start | bytes 983048 | tf_op jit(solution)/shard_map/ppermute | solution.py:39
  23.2 14.0 %collective-permute-start.19 = (bf16[64,2560]{1,0:T(8,128)(2,1)S(1)}, bf16[64,2560]{1,0:T(8,128)(2,1)S(1)}, u32[]{:S(2)}, u32[]{:S(2)}) collective-permute-start(bf16[64,2560]{1,0:T(8,128)(2,1)S(1)} %collective-permute-done.18.refs_2_), channel_id=1, source_target_pairs={{0,6},{1,7},{2,0},{3,1},{4,2},{5,3},{6,4},{7,5},{8,14},{9,15},{10,... | collective-permute-start | bytes 983048 | tf_op jit(solution)/shard_map/ppermute | solution.py:39
  26.1 39.3 %slice-start = ((s8[11796480]{0:T(1024)(128)(4,1)}), s8[4194304]{0:T(1024)(128)(4,1)S(1)}, s32[]{:S(2)}) async-start(s8[11796480]{0:T(1024)(128)(4,1)} %bitcast), calls=%async_computation | async-start | bytes 8388608
  26.1 39.3 %slice-start.1 = ((s8[11796480]{0:T(1024)(128)(4,1)}), s8[4194304]{0:T(1024)(128)(4,1)S(1)}, s32[]{:S(2)}) async-start(s8[11796480]{0:T(1024)(128)(4,1)} %bitcast), calls=%async_computation.1 | async-start | bytes 8388608
  26.1 39.3 %slice-start.2 = ((s8[11796480]{0:T(1024)(128)(4,1)}), s8[3407872]{0:T(1024)(128)(4,1)S(1)}, s32[]{:S(2)}) async-start(s8[11796480]{0:T(1024)(128)(4,1)} %bitcast), calls=%async_computation.2 | async-start | bytes 6815744
  27.1 10.3 %collective-permute-start.8 = (bf16[64,2560]{1,0:T(8,128)(2,1)S(1)}, bf16[64,2560]{1,0:T(8,128)(2,1)S(1)}, u32[]{:S(2)}, u32[]{:S(2)}) collective-permute-start(bf16[64,2560]{1,0:T(8,128)(2,1)S(1)} %get-tuple-element.54.refs_0_), channel_id=1, source_target_pairs={{0,65},{1,64},{2,67},{3,66},{4,69},{5,68},{6,71},{7,70},{8,73},{9,... | collective-permute-start | bytes 983048 | tf_op jit(solution)/shard_map/ppermute | solution.py:39
  30.2 15.0 %collective-permute-start.3 = (bf16[64,2560]{1,0:T(8,128)(2,1)S(1)}, bf16[64,2560]{1,0:T(8,128)(2,1)S(1)}, u32[]{:S(2)}, u32[]{:S(2)}) collective-permute-start(bf16[64,2560]{1,0:T(8,128)(2,1)S(1)} %get-tuple-element.54.refs_0_), channel_id=1, source_target_pairs={{0,2},{1,3},{2,4},{3,5},{4,6},{5,7},{6,0},{7,1},{8,10},{9,11},{10,... | collective-permute-start | bytes 983048 | tf_op jit(solution)/shard_map/ppermute | solution.py:39
  31.7 15.4 %collective-permute-start.7 = (bf16[64,2560]{1,0:T(8,128)(2,1)S(1)}, bf16[64,2560]{1,0:T(8,128)(2,1)S(1)}, u32[]{:S(2)}, u32[]{:S(2)}) collective-permute-start(bf16[64,2560]{1,0:T(8,128)(2,1)S(1)} %get-tuple-element.54.refs_0_), channel_id=1, source_target_pairs={{0,6},{1,7},{2,0},{3,1},{4,2},{5,3},{6,4},{7,5},{8,14},{9,15},{10,... | collective-permute-start | bytes 983048 | tf_op jit(solution)/shard_map/ppermute | solution.py:39
  33.8 13.3 %collective-permute-start.12 = (bf16[64,2560]{1,0:T(8,128)(2,1)S(1)}, bf16[64,2560]{1,0:T(8,128)(2,1)S(1)}, u32[]{:S(2)}, u32[]{:S(2)}) collective-permute-start(bf16[64,2560]{1,0:T(8,128)(2,1)S(1)} %collective-permute-done.2.refs_3_), channel_id=1, source_target_pairs={{0,65},{1,64},{2,67},{3,66},{4,69},{5,68},{6,71},{7,70},{8,73},{9,... | collective-permute-start | bytes 983048 | tf_op jit(solution)/shard_map/ppermute | solution.py:39
  37.2 5.4 %collective-permute-start = (s32[512]{0:T(512)}, s32[512]{0:T(512)S(1)}, u32[]{:S(2)}, u32[]{:S(2)}) collective-permute-start(s32[512]{0:T(512)} %ids_own.7), channel_id=1, source_target_pairs={{0,65},{1,64},{2,67},{3,66},{4,69},{5,68},{6,71},{7,70},{8,73},{9,... | collective-permute-start | bytes 6152 | tf_op jit(solution)/shard_map/ppermute | solution.py:39
  37.4 20.8 %collective-permute-start.17 = (bf16[64,2560]{1,0:T(8,128)(2,1)S(1)}, bf16[64,2560]{1,0:T(8,128)(2,1)S(1)}, u32[]{:S(2)}, u32[]{:S(2)}) collective-permute-start(bf16[64,2560]{1,0:T(8,128)(2,1)S(1)} %collective-permute-done.11.refs_4_), channel_id=1, source_target_pairs={{0,2},{1,3},{2,4},{3,5},{4,6},{5,7},{6,0},{7,1},{8,10},{9,11},{10,... | collective-permute-start | bytes 983048 | tf_op jit(solution)/shard_map/ppermute | solution.py:39
  42.6 21.6 %collective-permute-start.20 = (bf16[64,2560]{1,0:T(8,128)(2,1)S(1)}, bf16[64,2560]{1,0:T(8,128)(2,1)S(1)}, u32[]{:S(2)}, u32[]{:S(2)}) collective-permute-start(bf16[64,2560]{1,0:T(8,128)(2,1)S(1)} %collective-permute-done.11.refs_4_), channel_id=1, source_target_pairs={{0,6},{1,7},{2,0},{3,1},{4,2},{5,3},{6,4},{7,5},{8,14},{9,15},{10,... | collective-permute-start | bytes 983048 | tf_op jit(solution)/shard_map/ppermute | solution.py:39
  45.2 20.3 %collective-permute-start.22 = (bf16[64,2560]{1,0:T(8,128)(2,1)S(1)}, bf16[64,2560]{1,0:T(8,128)(2,1)S(1)}, u32[]{:S(2)}, u32[]{:S(2)}) collective-permute-start(bf16[64,2560]{1,0:T(8,128)(2,1)S(1)} %collective-permute-done.19.refs_3_), channel_id=1, source_target_pairs={{0,65},{1,64},{2,67},{3,66},{4,69},{5,68},{6,71},{7,70},{8,73},{9,... | collective-permute-start | bytes 983048 | tf_op jit(solution)/shard_map/ppermute | solution.py:39
  47.1 2.7 %copy-start = (bf16[1152,2560]{1,0:T(8,128)(2,1)S(1)}, bf16[1152,2560]{1,0:T(8,128)(2,1)}, u32[]{:S(2)}) copy-start(bf16[1152,2560]{1,0:T(8,128)(2,1)} %head.6) | copy-start | bytes 17694724
  49.8 1.0 copy-start.1
  50.8 0.7 copy-start.2
  55.0 5.5 %collective-permute-start.15 = (f32[8,512]{1,0:T(8,128)S(1)}, f32[8,512]{1,0:T(8,128)S(1)}, u32[]{:S(2)}, u32[]{:S(2)}) collective-permute-start(f32[8,512]{1,0:T(8,128)S(1)} %get-tuple-element.58), channel_id=1, source_target_pairs={{0,4},{1,5},{2,6},{3,7},{4,0},{5,1},{6,2},{7,3},{8,12},{9,13},{10,... | collective-permute-start | bytes 49160 | tf_op jit(solution)/shard_map/ppermute | solution.py:39
  55.9 5.0 %collective-permute-start.14 = (f32[8,512]{1,0:T(8,128)S(1)}, f32[8,512]{1,0:T(8,128)S(1)}, u32[]{:S(2)}, u32[]{:S(2)}) collective-permute-start(f32[8,512]{1,0:T(8,128)S(1)} %get-tuple-element.58), channel_id=1, source_target_pairs={{0,6},{1,7},{2,0},{3,1},{4,2},{5,3},{6,4},{7,5},{8,14},{9,15},{10,... | collective-permute-start | bytes 49160 | tf_op jit(solution)/shard_map/ppermute | solution.py:39
  58.2 5.2 %collective-permute-start.13 = (f32[8,512]{1,0:T(8,128)S(1)}, f32[8,512]{1,0:T(8,128)S(1)}, u32[]{:S(2)}, u32[]{:S(2)}) collective-permute-start(f32[8,512]{1,0:T(8,128)S(1)} %get-tuple-element.58), channel_id=1, source_target_pairs={{0,2},{1,3},{2,4},{3,5},{4,6},{5,7},{6,0},{7,1},{8,10},{9,11},{10,... | collective-permute-start | bytes 49160 | tf_op jit(solution)/shard_map/ppermute | solution.py:39
  60.5 9.7 %collective-permute-start.21 = (bf16[64,2560]{1,0:T(8,128)(2,1)S(1)}, bf16[64,2560]{1,0:T(8,128)(2,1)S(1)}, u32[]{:S(2)}, u32[]{:S(2)}) collective-permute-start(bf16[64,2560]{1,0:T(8,128)(2,1)S(1)} %collective-permute-done.3.refs_1_), channel_id=1, source_target_pairs={{0,2},{1,3},{2,4},{3,5},{4,6},{5,7},{6,0},{7,1},{8,10},{9,11},{10,... | collective-permute-start | bytes 983048 | tf_op jit(solution)/shard_map/ppermute | solution.py:39
  60.9 14.4 %collective-permute-start.23 = (bf16[64,2560]{1,0:T(8,128)(2,1)S(1)}, bf16[64,2560]{1,0:T(8,128)(2,1)S(1)}, u32[]{:S(2)}, u32[]{:S(2)}) collective-permute-start(bf16[64,2560]{1,0:T(8,128)(2,1)S(1)} %collective-permute-done.8.refs_4_), channel_id=1, source_target_pairs={{0,2},{1,3},{2,4},{3,5},{4,6},{5,7},{6,0},{7,1},{8,10},{9,11},{10,... | collective-permute-start | bytes 983048 | tf_op jit(solution)/shard_map/ppermute | solution.py:39
  63.4 11.9 %collective-permute-start.24 = (bf16[64,2560]{1,0:T(8,128)(2,1)S(1)}, bf16[64,2560]{1,0:T(8,128)(2,1)S(1)}, u32[]{:S(2)}, u32[]{:S(2)}) collective-permute-start(bf16[64,2560]{1,0:T(8,128)(2,1)S(1)} %collective-permute-done.8.refs_4_), channel_id=1, source_target_pairs={{0,6},{1,7},{2,0},{3,1},{4,2},{5,3},{6,4},{7,5},{8,14},{9,15},{10,... | collective-permute-start | bytes 983048 | tf_op jit(solution)/shard_map/ppermute | solution.py:39
  64.1 7.1 %slice-start.3 = ((s8[5898240]{0:T(1024)(128)(4,1)}), s8[4194304]{0:T(1024)(128)(4,1)S(1)}, s32[]{:S(2)}) async-start(s8[5898240]{0:T(1024)(128)(4,1)} %bitcast.2), calls=%async_computation.3 | async-start | bytes 8388608
  64.1 7.1 %slice-start.4 = ((s8[5898240]{0:T(1024)(128)(4,1)}), s8[1703936]{0:T(1024)(128)(4,1)S(1)}, s32[]{:S(2)}) async-start(s8[5898240]{0:T(1024)(128)(4,1)} %bitcast.2), calls=%async_computation.4 | async-start | bytes 3407872
  64.2 7.1 %copy-start.3 = (s32[512]{0:T(512)S(1)}, s32[512]{0:T(512)}, u32[]{:S(2)}) copy-start(s32[512]{0:T(512)} %ids_own.7) | copy-start | bytes 6148
  64.2 5.4 %collective-permute-start.16 = (f32[8,512]{1,0:T(8,128)S(1)}, f32[8,512]{1,0:T(8,128)S(1)}, u32[]{:S(2)}, u32[]{:S(2)}) collective-permute-start(f32[8,512]{1,0:T(8,128)S(1)} %add_add_fusion.1), channel_id=1, source_target_pairs={{0,65},{1,64},{2,67},{3,66},{4,69},{5,68},{6,71},{7,70},{8,73},{9,... | collective-permute-start | bytes 49160 | tf_op jit(solution)/shard_map/ppermute | solution.py:39
  70.2 8.3 %collective-permute-start.25 = (bf16[64,2560]{1,0:T(8,128)(2,1)S(1)}, bf16[64,2560]{1,0:T(8,128)(2,1)S(1)}, u32[]{:S(2)}, u32[]{:S(2)}) collective-permute-start(bf16[64,2560]{1,0:T(8,128)(2,1)S(1)} %collective-permute-done.21.refs_3_), channel_id=1, source_target_pairs={{0,65},{1,64},{2,67},{3,66},{4,69},{5,68},{6,71},{7,70},{8,73},{9,... | collective-permute-start | bytes 983048 | tf_op jit(solution)/shard_map/ppermute | solution.py:39
  82.2 5.3 %collective-permute-start.28 = (f32[8,512]{1,0:T(8,128)S(1)}, f32[8,512]{1,0:T(8,128)S(1)}, u32[]{:S(2)}, u32[]{:S(2)}) collective-permute-start(f32[8,512]{1,0:T(8,128)S(1)} %shard_map.71), channel_id=1, source_target_pairs={{0,4},{1,5},{2,6},{3,7},{4,0},{5,1},{6,2},{7,3},{8,12},{9,13},{10,... | collective-permute-start | bytes 49160 | tf_op jit(solution)/shard_map/ppermute | solution.py:39
  82.9 4.6 %collective-permute-start.27 = (f32[8,512]{1,0:T(8,128)S(1)}, f32[8,512]{1,0:T(8,128)S(1)}, u32[]{:S(2)}, u32[]{:S(2)}) collective-permute-start(f32[8,512]{1,0:T(8,128)S(1)} %shard_map.71), channel_id=1, source_target_pairs={{0,6},{1,7},{2,0},{3,1},{4,2},{5,3},{6,4},{7,5},{8,14},{9,15},{10,... | collective-permute-start | bytes 49160 | tf_op jit(solution)/shard_map/ppermute | solution.py:39
  85.8 4.9 %collective-permute-start.26 = (f32[8,512]{1,0:T(8,128)S(1)}, f32[8,512]{1,0:T(8,128)S(1)}, u32[]{:S(2)}, u32[]{:S(2)}) collective-permute-start(f32[8,512]{1,0:T(8,128)S(1)} %shard_map.71), channel_id=1, source_target_pairs={{0,2},{1,3},{2,4},{3,5},{4,6},{5,7},{6,0},{7,1},{8,10},{9,11},{10,... | collective-permute-start | bytes 49160 | tf_op jit(solution)/shard_map/ppermute | solution.py:39
  90.8 5.3 %collective-permute-start.29 = (f32[8,512]{1,0:T(8,128)S(1)}, f32[8,512]{1,0:T(8,128)S(1)}, u32[]{:S(2)}, u32[]{:S(2)}) collective-permute-start(f32[8,512]{1,0:T(8,128)S(1)} %add_add_fusion), channel_id=1, source_target_pairs={{0,65},{1,64},{2,67},{3,66},{4,69},{5,68},{6,71},{7,70},{8,73},{9,... | collective-permute-start | bytes 49160 | tf_op jit(solution)/shard_map/ppermute | solution.py:39
  92.3 27.5 %collective-permute-start.36 = (bf16[512,2560]{1,0:T(8,128)(2,1)S(1)}, bf16[512,2560]{1,0:T(8,128)(2,1)S(1)}, u32[]{:S(2)}, u32[]{:S(2)}) collective-permute-start(bf16[512,2560]{1,0:T(8,128)(2,1)S(1)} %get-tuple-element.89.hidden), channel_id=1, source_target_pairs={{0,8},{1,9},{2,10},{3,11},{4,12},{5,13},{6,14},{7,15},{8,0},{9,1},... | collective-permute-start | bytes 7864328 | tf_op jit(solution)/shard_map/ppermute | solution.py:39
  92.3 17.5 %collective-permute-start.30 = (bf16[128,2560]{1,0:T(8,128)(2,1)S(1)}, bf16[128,2560]{1,0:T(8,128)(2,1)S(1)}, u32[]{:S(2)}, u32[]{:S(2)}) collective-permute-start(bf16[128,2560]{1,0:T(8,128)(2,1)S(1)} %get-tuple-element.79), channel_id=1, source_target_pairs={{0,6},{1,7},{2,0},{3,1},{4,2},{5,3},{6,4},{7,5},{8,14},{9,15},{10,... | collective-permute-start | bytes 1966088 | tf_op jit(solution)/shard_map/ppermute | solution.py:39
  92.4 25.3 %collective-permute-start.31 = (bf16[128,2560]{1,0:T(8,128)(2,1)S(1)}, bf16[128,2560]{1,0:T(8,128)(2,1)S(1)}, u32[]{:S(2)}, u32[]{:S(2)}) collective-permute-start(bf16[128,2560]{1,0:T(8,128)(2,1)S(1)} %get-tuple-element.81), channel_id=1, source_target_pairs={{0,2},{1,3},{2,4},{3,5},{4,6},{5,7},{6,0},{7,1},{8,10},{9,11},{10,... | collective-permute-start | bytes 1966088 | tf_op jit(solution)/shard_map/ppermute | solution.py:39
  94.3 10.8 %collective-permute-start.32 = (bf16[64,2560]{1,0:T(8,128)(2,1)S(1)}, bf16[64,2560]{1,0:T(8,128)(2,1)S(1)}, u32[]{:S(2)}, u32[]{:S(2)}) collective-permute-start(bf16[64,2560]{1,0:T(8,128)(2,1)S(1)} %get-tuple-element.84), channel_id=1, source_target_pairs={{0,65},{1,64},{2,67},{3,66},{4,69},{5,68},{6,71},{7,70},{8,73},{9,... | collective-permute-start | bytes 983048 | tf_op jit(solution)/shard_map/ppermute | solution.py:39
  96.8 23.1 %collective-permute-start.35 = (bf16[576,512]{1,0:T(8,128)(2,1)S(1)}, bf16[576,512]{1,0:T(8,128)(2,1)S(1)}, u32[]{:S(2)}, u32[]{:S(2)}) collective-permute-start(bf16[576,512]{1,0:T(8,128)(2,1)S(1)} %get-tuple-element.88), channel_id=1, source_target_pairs={{0,8},{1,9},{2,10},{3,11},{4,12},{5,13},{6,14},{7,15},{8,0},{9,1},... | collective-permute-start | bytes 1769480 | tf_op jit(solution)/shard_map/ppermute | solution.py:39
  105.2 39.6 %collective-permute-start.33 = (bf16[64,2560]{1,0:T(8,128)(2,1)S(1)}, bf16[64,2560]{1,0:T(8,128)(2,1)S(1)}, u32[]{:S(2)}, u32[]{:S(2)}) collective-permute-start(bf16[64,2560]{1,0:T(8,128)(2,1)S(1)} %add_convert_fusion.4), channel_id=1, source_target_pairs={{0,4},{1,5},{2,6},{3,7},{4,0},{5,1},{6,2},{7,3},{8,12},{9,13},{10,... | collective-permute-start | bytes 983048 | tf_op jit(solution)/shard_map/ppermute | solution.py:39
  117.8 26.9 %collective-permute-start.34 = (bf16[64,2560]{1,0:T(8,128)(2,1)S(1)}, bf16[64,2560]{1,0:T(8,128)(2,1)S(1)}, u32[]{:S(2)}, u32[]{:S(2)}) collective-permute-start(bf16[64,2560]{1,0:T(8,128)(2,1)S(1)} %add_convert_fusion.3), channel_id=1, source_target_pairs={{0,65},{1,64},{2,67},{3,66},{4,69},{5,68},{6,71},{7,70},{8,73},{9,... | collective-permute-start | bytes 983048 | tf_op jit(solution)/shard_map/ppermute | solution.py:39
  121.5 9.9 %collective-permute-start.40 = (bf16[72,2560]{1,0:T(8,128)(2,1)S(1)}, bf16[72,2560]{1,0:T(8,128)(2,1)S(1)}, u32[]{:S(2)}, u32[]{:S(2)}) collective-permute-start(bf16[72,2560]{1,0:T(8,128)(2,1)S(1)} %get-tuple-element.96), channel_id=1, source_target_pairs={{0,64},{1,65},{2,66},{3,67},{4,68},{5,69},{6,70},{7,71},{8,72},{9,... | collective-permute-start | bytes 1105928 | tf_op jit(solution)/shard_map/ppermute | solution.py:39
  123.4 12.8 %collective-permute-start.38 = (bf16[72,2560]{1,0:T(8,128)(2,1)S(1)}, bf16[72,2560]{1,0:T(8,128)(2,1)S(1)}, u32[]{:S(2)}, u32[]{:S(2)}) collective-permute-start(bf16[72,2560]{1,0:T(8,128)(2,1)S(1)} %get-tuple-element.93), channel_id=1, source_target_pairs={{0,16},{1,17},{2,18},{3,19},{4,20},{5,21},{6,22},{7,23},{8,24},{9,... | collective-permute-start | bytes 1105928 | tf_op jit(solution)/shard_map/ppermute | solution.py:39
  125.3 12.5 %collective-permute-start.37 = (bf16[72,2560]{1,0:T(8,128)(2,1)S(1)}, bf16[72,2560]{1,0:T(8,128)(2,1)S(1)}, u32[]{:S(2)}, u32[]{:S(2)}) collective-permute-start(bf16[72,2560]{1,0:T(8,128)(2,1)S(1)} %get-tuple-element.92), channel_id=1, source_target_pairs={{0,48},{1,49},{2,50},{3,51},{4,52},{5,53},{6,54},{7,55},{8,56},{9,... | collective-permute-start | bytes 1105928 | tf_op jit(solution)/shard_map/ppermute | solution.py:39
  131.6 9.4 %collective-permute-start.43 = (bf16[72,1280]{1,0:T(8,128)(2,1)S(1)}, bf16[72,1280]{1,0:T(8,128)(2,1)S(1)}, u32[]{:S(2)}, u32[]{:S(2)}) collective-permute-start(bf16[72,1280]{1,0:T(8,128)(2,1)S(1)} %get-tuple-element.101), channel_id=1, source_target_pairs={{0,16},{1,17},{2,18},{3,19},{4,20},{5,21},{6,22},{7,23},{8,24},{9,... | collective-permute-start | bytes 552968 | tf_op jit(solution)/shard_map/ppermute | solution.py:39
  136.1 5.5 %collective-permute-start.41 = (bf16[72,1280]{1,0:T(8,128)(2,1)S(1)}, bf16[72,1280]{1,0:T(8,128)(2,1)S(1)}, u32[]{:S(2)}, u32[]{:S(2)}) collective-permute-start(bf16[72,1280]{1,0:T(8,128)(2,1)S(1)} %get-tuple-element.100), channel_id=1, source_target_pairs={{0,48},{1,49},{2,50},{3,51},{4,52},{5,53},{6,54},{7,55},{8,56},{9,... | collective-permute-start | bytes 552968 | tf_op jit(solution)/shard_map/ppermute | solution.py:39
  138.0 8.4 %collective-permute-start.39 = (bf16[72,2560]{1,0:T(8,128)(2,1)S(1)}, bf16[72,2560]{1,0:T(8,128)(2,1)S(1)}, u32[]{:S(2)}, u32[]{:S(2)}) collective-permute-start(bf16[72,2560]{1,0:T(8,128)(2,1)S(1)} %add_convert_fusion.2), channel_id=1, source_target_pairs={{0,64},{1,65},{2,66},{3,67},{4,68},{5,69},{6,70},{7,71},{8,72},{9,... | collective-permute-start | bytes 1105928 | tf_op jit(solution)/shard_map/ppermute | solution.py:39
  141.0 8.8 %collective-permute-start.44 = (bf16[72,2560]{1,0:T(8,128)(2,1)S(1)}, bf16[72,2560]{1,0:T(8,128)(2,1)S(1)}, u32[]{:S(2)}, u32[]{:S(2)}) collective-permute-start(bf16[72,2560]{1,0:T(8,128)(2,1)S(1)} %pad_maximum_fusion.1), channel_id=1, source_target_pairs={{0,16},{1,17},{2,18},{3,19},{4,20},{5,21},{6,22},{7,23},{8,24},{9,... | collective-permute-start | bytes 1105928 | tf_op jit(solution)/shard_map/ppermute | solution.py:39
  141.7 8.1 %collective-permute-start.42 = (bf16[72,2560]{1,0:T(8,128)(2,1)S(1)}, bf16[72,2560]{1,0:T(8,128)(2,1)S(1)}, u32[]{:S(2)}, u32[]{:S(2)}) collective-permute-start(bf16[72,2560]{1,0:T(8,128)(2,1)S(1)} %pad_maximum_fusion), channel_id=1, source_target_pairs={{0,48},{1,49},{2,50},{3,51},{4,52},{5,53},{6,54},{7,55},{8,56},{9,... | collective-permute-start | bytes 1105928 | tf_op jit(solution)/shard_map/ppermute | solution.py:39

commit v3 on v2

v3 whole, which is shorter than its diff:
```python
import functools

import jax
import jax.numpy as jnp
from jax import lax
from jax.experimental import pallas as pl
from jax.experimental.pallas import tpu as pltpu
from jax.sharding import PartitionSpec as P

BF16 = jnp.bfloat16
F32 = jnp.float32
AXES = ("dp", "vocab")

REL = ((0, 0), (-1, 0), (1, 0), (2, 0), (0, 1), (-1, 1), (1, 1), (2, 1))


def pairs(move):
    out = []
    for i in range(128):
        dp, v = i // 8, i % 8
        y_lo, z, core, x, y_hi = dp // 8, (dp // 2) % 4, dp % 2, v // 2, v % 2
        x, y, z, core = move(x, y_hi * 2 + y_lo, z, core)
        x, y, z = x % 4, y % 4, z % 4
        out.append((i, (((y % 2) * 4 + z) * 2 + core) * 8 + x * 2 + y // 2))
    return out


X_UP = pairs(lambda x, y, z, c: (x + 1, y, z, c))
X_DOWN = pairs(lambda x, y, z, c: (x - 1, y, z, c))
X_FAR = pairs(lambda x, y, z, c: (x + 2, y, z, c))
Y_HI = pairs(lambda x, y, z, c: (x, 3 - y, z, c))
Z_UP = pairs(lambda x, y, z, c: (x, y, z + 1, c))
Z_DOWN = pairs(lambda x, y, z, c: (x, y, z - 1, c))
Z_FAR = pairs(lambda x, y, z, c: (x, y, z + 2, c))
Y_LO = pairs(lambda x, y, z, c: (x, y ^ 1, z, c))
CORE = pairs(lambda x, y, z, c: (x, y, z, 1 - c))


def send(a, to):
    return lax.ppermute(a, AXES, to)


class Link:
    def __init__(self, to, ahead=2):
        self.to, self.ahead, self.sent = to, ahead, []

    def __call__(self, a):
        if len(self.sent) >= self.ahead:
            a = after(a, self.sent[-self.ahead])
        self.sent.append(send(a, self.to))
        return self.sent[-1]


def after(a, *others):
    return lax.optimization_barrier((a, *others))[0]


def params(mib):
    return pltpu.CompilerParams(vmem_limit_bytes=mib * 2**20)


LONG, SHORT = 20, 1


VMEM = pl.BlockSpec(memory_space=pltpu.VMEM)


def kernel_call(body, arrays, outs, scratch, mib, said=SHORT):
    return pl.pallas_call(
        body,
        in_specs=[VMEM] * len(arrays),
        out_specs=[VMEM] * len(outs),
        out_shape=[jax.ShapeDtypeStruct(shape, dtype) for shape, dtype in outs],
        scratch_shapes=[pltpu.VMEM(shape, dtype) for shape, dtype in scratch],
        compiler_params=params(mib),
        cost_estimate=pl.CostEstimate(flops=said * 10**9, bytes_accessed=said * 10**6, transcendentals=0),
    )(*arrays)


class Place:
    def __init__(self):
        dp, v = lax.axis_index("dp"), lax.axis_index("vocab")
        self.y_lo, self.z, self.core = lax.div(dp, 8), lax.rem(lax.div(dp, 2), 4), lax.rem(dp, 2)
        self.vocab, self.x, self.y_hi = v, lax.div(v, 2), lax.rem(v, 2)

    def block(self, r):
        dx, dy = REL[r]
        owner = lax.rem(self.x + (dx + 4), 4) * 2 + lax.rem(self.y_hi + dy, 2)
        return pl.multiple_of(owner * 64, 64)

    def chip(self, dz, dy):
        return lax.rem(self.y_lo + dy, 2) * 4 + lax.rem(self.z + (dz + 4), 4)


def ids_kernel(own, near, ids):
    half = lax.rem(lax.div(lax.broadcasted_iota(jnp.int32, (1, 512), 1), 64), 2)
    ids[...] = jnp.where(half == Place().y_hi, own[...].reshape(1, 512), near[...].reshape(1, 512))


def fold(a):
    return jnp.sum(a.reshape(a.shape[0] // 8, 8, a.shape[1]), axis=0)


NT = (((1,), (1,)), ((), ()))
NN = (((1,), (0,)), ((), ()))
TILE = 384
WIDE = 512
STATS = (8, 512)


def put_blocks(place, blocks, hidden):
    for r, block in enumerate(blocks):
        hidden[pl.ds(place.block(r), 64), :] = block[...]


def put_stats(stats, first, sums, picks):
    stats[first:first + 1, :] = jnp.sum(sums, axis=0, keepdims=True)
    stats[first + 1:first + 2, :] = jnp.sum(picks, axis=0, keepdims=True)


def advantage(total):
    norm = jnp.log(total[0:1, :])
    return (total[3:4, :] - jnp.log(total[2:3, :])) - (total[1:2, :] - norm), norm


def student_kernel(ids, head, *refs):
    blocks, (logits, hidden, stats) = refs[:8], refs[8:]
    place = Place()
    put_blocks(place, blocks, hidden)
    sums = picks = 0.0
    for j in range(head.shape[0] // TILE):
        tile = slice(j * TILE, (j + 1) * TILE)
        out = lax.dot_general(head[tile, :], hidden[...], NT, preferred_element_type=F32)
        logits[tile, :] = out
        rows = lax.broadcasted_iota(jnp.int32, out.shape, 0) + (place.vocab * head.shape[0] + j * TILE)
        sums += fold(jnp.exp(out))
        picks += fold(jnp.where(rows == ids[...], out, 0.0))
    stats[...] = jnp.zeros_like(stats)
    put_stats(stats, 0, sums, picks)


def student_logits(ids, blocks, head):
    v, d = head.shape
    outs = [((v, 512), F32), ((512, d), BF16), (STATS, F32)]
    return kernel_call(student_kernel, (ids, head, *blocks), outs, [], 6, LONG)


def teacher_first_kernel(head, *refs):
    blocks, (logits, hidden) = refs[:8], refs[8:]
    put_blocks(Place(), blocks, hidden)
    for j in range(head.shape[0] // TILE):
        tile = slice(j * TILE, (j + 1) * TILE)
        logits[tile, :] = lax.dot_general(
            head[tile, 0:hidden.shape[1]], hidden[...], NT, preferred_element_type=F32
        )


def teacher_first(blocks, head):
    v, d = head.shape
    return kernel_call(teacher_first_kernel, (head, *blocks), [((v, 512), F32)], [((512, d // 2), BF16)], 8, LONG)[0]


def teacher_second_kernel(ids, student_stats, head, logits, *refs):
    blocks, (stats, hidden) = refs[:8], refs[8:]
    place = Place()
    put_blocks(place, blocks, hidden)
    sums = picks = 0.0
    for j in range(head.shape[0] // TILE):
        tile = slice(j * TILE, (j + 1) * TILE)
        out = logits[tile, :] + lax.dot_general(
            head[tile, hidden.shape[1]:], hidden[...], NT, preferred_element_type=F32
        )
        rows = lax.broadcasted_iota(jnp.int32, out.shape, 0) + (place.vocab * head.shape[0] + j * TILE)
        sums += fold(jnp.exp(out))
        picks += fold(jnp.where(rows == ids[...], out, 0.0))
    stats[...] = student_stats[...]
    put_stats(stats, 2, sums, picks)


def teacher_second(ids, student_stats, blocks, head, logits):
    scratch = [((512, head.shape[1] // 2), BF16)]
    return kernel_call(teacher_second_kernel, (ids, student_stats, head, logits, *blocks), [(STATS, F32)], scratch, 8, LONG)[0]


def hidden_kernel(ids, total, logits, head, own, near, far, far_near, lefts, rights, grad_t, product):
    place = Place()
    adv, norm = advantage(total)
    for k in range(head.shape[0] // 128):
        part = slice(k * 128, (k + 1) * 128)
        rows = lax.broadcasted_iota(jnp.int32, (128, 512), 0) + (place.vocab * head.shape[0] + k * 128)
        onehot = jnp.where(rows == ids[...], 1.0, 0.0)
        grad_t[:, part] = (adv * (jnp.exp(logits[part, :] - norm) - onehot)).T.astype(BF16)

    outs = ((own, 0), (lefts, 0), (rights, 0), (far, 0), (near, 0), (lefts, 64), (rights, 64), (far_near, 0))
    for j in range(head.shape[1] // WIDE):
        tile = slice(j * WIDE, (j + 1) * WIDE)
        product[...] = lax.dot_general(grad_t[...], head[:, tile], NN, preferred_element_type=F32)
        for r, (out, row) in enumerate(outs):
            out[row:row + 64, tile] = product[pl.ds(place.block(r), 64), :].astype(out.dtype)


def hidden_parts(ids, total, logits, head):
    v, d = head.shape
    outs = [((64, d), F32)] * 3 + [((64, d), BF16)] + [((128, d), BF16)] * 2
    scratch = [((512, v), BF16), ((512, WIDE), F32)]
    return kernel_call(hidden_kernel, (ids, total, logits, head), outs, scratch, 6, LONG)


CHIPS = ((-1, 0), (-1, 1), (1, 0), (1, 1), (2, 1), (2, 0), (0, 1), (0, 0))


def grad_kernel(ids, total, logits, mine, other, mine_f, other_f):
    place = Place()
    adv, norm = advantage(total)
    for r, chip in enumerate(CHIPS):
        for out, core in ((mine_f, place.core), (other_f, 1 - place.core)):
            start = pl.multiple_of(place.chip(*chip) * 144 + core * 72, 8)
            rows = lax.broadcasted_iota(jnp.int32, (72, 512), 0) + (place.vocab * logits.shape[0] + start)
            onehot = jnp.where(rows == ids[...], 1.0, 0.0)
            probs = jnp.exp(logits[pl.ds(start, 72), :] - norm)
            out[r * 72:(r + 1) * 72, :] = adv * (probs - onehot)
    mine[...] = mine_f[...].astype(BF16)
    other[...] = other_f[...].astype(BF16)


def logit_grads(ids, total, logits):
    half = logits.shape[0] // 2
    outs = [((half, 512), BF16)] * 2
    return kernel_call(grad_kernel, (ids, total, logits), outs, [((half, 512), F32)] * 2, 5, LONG)


def head_kernel(first, grad_mine, grad_from, hidden, hidden_from, *outs):
    n = sum(out.shape[0] for out in outs)
    rows = slice(first, first + n)
    for j in range(hidden.shape[1] // WIDE):
        tile = slice(j * WIDE, (j + 1) * WIDE)
        product = lax.dot_general(grad_mine[rows, :], hidden[:, tile], NN, preferred_element_type=F32)
        product += lax.dot_general(grad_from[rows, :], hidden_from[:, tile], NN, preferred_element_type=F32)
        start = 0
        for out in outs:
            out[:, tile] = product[start:start + out.shape[0], :].astype(out.dtype)
            start += out.shape[0]


def head_parts(first, outs, said, grad_mine, grad_from, hidden, hidden_from):
    outs = [((n, hidden.shape[1]), t) for n, t in outs]
    arrays = (grad_mine, grad_from, hidden, hidden_from)
    return kernel_call(functools.partial(head_kernel, first), arrays, outs, [], 4, said)


def finish_kernel(own, lefts, rights, far, near, out):
    total = own[...] + lefts[0:64, :].astype(F32) + rights[0:64, :].astype(F32)
    out[...] = (total + far[...].astype(F32) + near[...].astype(F32)).astype(out.dtype)


def group_sum(a):
    around = a + send(a, X_UP) + send(a, X_DOWN) + send(a, X_FAR)
    return around + send(around, Y_HI)


def on_device(student_hidden, teacher_hidden, student_head, teacher_head, sampled_ids):
    up, down, over = Link(X_UP), Link(X_DOWN), Link(Y_HI)
    half = teacher_hidden.shape[1] // 2
    t_a, t_b = teacher_hidden[:, :half], teacher_hidden[:, half:]
    left, right, near = up(student_hidden), down(student_hidden), over(student_hidden)
    ids_near = send(sampled_ids, Y_HI)
    l_a, r_a, near_a = up(t_a), down(t_a), over(after(t_a, ids_near))
    near_b = over(t_b)
    ids = kernel_call(ids_kernel, (sampled_ids, ids_near), [((1, 512), jnp.int32)], [], 1, LONG)[0]
    t_b = after(t_b, ids)
    far, right_near = up(left), down(near)
    left_near, f_a, far_near = up(near), down(r_a), over(far)
    l_b, r_b = up(t_b), down(t_b)
    ln_a, rn_a, fn_a = up(near_a), down(near_a), over(f_a)
    f_b = up(l_b)
    fn_b = over(f_b)
    ln_b, rn_b = up(near_b), down(near_b)

    blocks = (student_hidden, left, right, far, near, left_near, right_near, far_near)
    logits, hidden, student_stats = student_logits(ids, blocks, student_head)
    hidden_from = send(hidden, CORE)
    teacher_logits = teacher_first((t_a, l_a, r_a, f_a, near_a, ln_a, rn_a, fn_a), teacher_head)
    blocks = (t_b, l_b, r_b, f_b, near_b, ln_b, rn_b, fn_b)
    total = group_sum(teacher_second(ids, student_stats, blocks, teacher_head, teacher_logits))

    mine, other = logit_grads(ids, total, logits)
    grads = (mine, send(other, CORE), hidden, hidden_from)
    h_lefts, h_rights = head_parts(0, ((144, BF16), (144, BF16)), SHORT, *grads)
    grads = (after(mine, h_lefts), *grads[1:])
    h_fl, h_f, h_y, h_own = head_parts(288, ((72, BF16), (72, F32), (72, F32), (72, F32)), LONG, *grads)
    from_lefts, from_rights, from_fl = send(h_lefts, Z_DOWN), send(h_rights, Z_UP), send(h_fl, Y_LO)
    from_f = send(after((h_f + from_fl.astype(F32)).astype(BF16), from_lefts), Z_FAR)
    h_y = h_y + from_lefts[72:].astype(F32) + from_rights[72:].astype(F32)
    from_y = send(h_y.astype(BF16), Y_LO)
    head_sum = h_own + from_lefts[:72].astype(F32) + from_rights[:72].astype(F32)
    head_sum = head_sum + from_f.astype(F32) + from_y.astype(F32)

    g_own, g_near, g_far, g_far_near, g_lefts, g_rights = hidden_parts(ids, after(total, h_fl), logits, student_head)
    from_lefts, from_rights, from_fn = send(g_lefts, X_DOWN), send(g_rights, X_UP), send(after(g_far_near, from_fl), Y_HI)
    from_far = send((g_far + from_fn.astype(F32)).astype(BF16), X_FAR)
    g_near = g_near + from_lefts[64:].astype(F32) + from_rights[64:].astype(F32)
    from_near = send(g_near.astype(BF16), Y_HI)
    pieces = (g_own, from_lefts, from_rights, from_far, from_near)
    return kernel_call(finish_kernel, pieces, [(student_hidden.shape, BF16)], [], 4)[0], head_sum.astype(BF16)


def solution(mesh):
    in_specs = (
        P(("dp", "vocab"), None),
        P(("dp", "vocab"), None),
        P("vocab", None),
        P("vocab", None),
        P("dp"),
    )
    out_specs = (P(("dp", "vocab"), None), P(("vocab", "dp"), None))
    return jax.shard_map(
        on_device, mesh=mesh, in_specs=in_specs, out_specs=out_specs, check_vma=False
    )
```

time: 153 us -> 131 us (0.86); the launches traced: 151 us -> 131 us
  starting transfers between devices: 64.7 us -> 52.3 us
  local copies, waits for them, and re-layouts: 5.54 us -> 1.82 us
  waiting for transfers between devices: 58.2 us -> 54.5 us
    ppermute x45 -> x38, starting transfers between devices: 64.7 us -> 52.3 us  [send(): return lax.ppermute(a, AXES, to)]
    ppermute x45 -> x38, waiting for transfers between devices: 58.2 us -> 54.5 us  [send(): return lax.ppermute(a, AXES, to)]
    unnamed x18 -> x14, local copies, waits for them, and re-layouts: 4.35 us -> 0.71 us
    pallas_call x8 -> x9, Pallas kernels: 19.9 us -> 19.9 us  [kernel_call(): pl.pallas_call(body, in_specs=[VMEM] * len(arrays), out_specs=[VMEM] * le...]
  transfers between devices with their start and end apart: 45 -> 38, of which waited for: 24 -> 19; matrix products, arithmetic and copies ran while one was open for 1% -> 1% of each run, Pallas kernels for 11% -> 10%
where the time goes in v3:
time: 131 us
  waiting for transfers between devices  54.5 us (42%)
  starting transfers between devices  52.3 us (40%)
  Pallas kernels  19.9 us (15%)
  local copies, waits for them, and re-layouts  1.82 us (1%)
  other arithmetic  1.36 us (1%)
    ppermute x38, waiting for transfers between devices, send(): return lax.ppermute(a, AXES, to)  54.5 us
    ppermute x38, starting transfers between devices, send(): return lax.ppermute(a, AXES, to)  52.3 us
    pallas_call x9, Pallas kernels, kernel_call(): pl.pallas_call(body, in_specs=[VMEM] * len(arrays), out_specs=[VMEM] * le...  19.9 us
  transfers between devices with their start and end apart: 38, of which 19 were waited for; matrix products, arithmetic and copies ran while one was open for 1% of the time, Pallas kernels for 10%

profile of v3, /device:TPU:0, one launch (start us, length us, event | category | flops | bytes accessed | tf_op | source)
XLA Modules:
  0.0 130.7 jit_solution(2534129063755715743)
XLA Ops:
  0.6 2.9 %collective-permute-start.2 = (bf16[64,2560]{1,0:T(8,128)(2,1)}, bf16[64,2560]{1,0:T(8,128)(2,1)S(1)}, u32[]{:S(2)}, u32[]{:S(2)}) collective-permute-start(bf16[64,2560]{1,0:T(8,128)(2,1)} %refs_0_.1), channel_id=1, source_target_pairs={{0,6},{1,7},{2,0},{3,1},{4,2},{5,3},{6,4},{7,5},{8,14},{9,15},{10,... | collective-permute-start | bytes 983048 | tf_op jit(solution)/shard_map/ppermute | solution.py:40
  3.5 3.0 %collective-permute-start.4 = (bf16[64,2560]{1,0:T(8,128)(2,1)}, bf16[64,2560]{1,0:T(8,128)(2,1)S(1)}, u32[]{:S(2)}, u32[]{:S(2)}) collective-permute-start(bf16[64,2560]{1,0:T(8,128)(2,1)} %refs_0_.1), channel_id=1, source_target_pairs={{0,65},{1,64},{2,67},{3,66},{4,69},{5,68},{6,71},{7,70},{8,73},{9,... | collective-permute-start | bytes 983048 | tf_op jit(solution)/shard_map/ppermute | solution.py:40
  6.6 0.2 collective-permute-start
  6.8 1.1 fusion
  7.9 0.8 collective-permute-start.5
  8.7 5.6 %collective-permute-done.near = s32[512]{0:T(512)S(1)} collective-permute-done((s32[512]{0:T(512)}, s32[512]{0:T(512)S(1)}, u32[]{:S(2)}, u32[]{:S(2)}) %collective-permute-start) | collective-permute-done | bytes 2080 | tf_op jit(solution)/shard_map/ppermute | solution.py:40
  14.3 2.9 %collective-permute-start.10 = (bf16[64,2560]{1,0:T(8,128)(2,1)S(1)}, bf16[64,2560]{1,0:T(8,128)(2,1)S(1)}, u32[]{:S(2)}, u32[]{:S(2)}) collective-permute-start(bf16[64,2560]{1,0:T(8,128)(2,1)S(1)} %get-tuple-element.43.refs_0_), channel_id=1, source_target_pairs={{0,6},{1,7},{2,0},{3,1},{4,2},{5,3},{6,4},{7,5},{8,14},{9,15},{10,... | collective-permute-start | bytes 983048 | tf_op jit(solution)/shard_map/ppermute | solution.py:40
  17.2 2.9 %collective-permute-start.8 = (bf16[64,2560]{1,0:T(8,128)(2,1)S(1)}, bf16[64,2560]{1,0:T(8,128)(2,1)S(1)}, u32[]{:S(2)}, u32[]{:S(2)}) collective-permute-start(bf16[64,2560]{1,0:T(8,128)(2,1)S(1)} %get-tuple-element.43.refs_0_), channel_id=1, source_target_pairs={{0,65},{1,64},{2,67},{3,66},{4,69},{5,68},{6,71},{7,70},{8,73},{9,... | collective-permute-start | bytes 983048 | tf_op jit(solution)/shard_map/ppermute | solution.py:40
  20.2 3.2 %collective-permute-start.7 = (bf16[64,2560]{1,0:T(8,128)(2,1)S(1)}, bf16[64,2560]{1,0:T(8,128)(2,1)S(1)}, u32[]{:S(2)}, u32[]{:S(2)}) collective-permute-start(bf16[64,2560]{1,0:T(8,128)(2,1)S(1)} %collective-permute-done.4.refs_4_), channel_id=1, source_target_pairs={{0,6},{1,7},{2,0},{3,1},{4,2},{5,3},{6,4},{7,5},{8,14},{9,15},{10,... | collective-permute-start | bytes 983048 | tf_op jit(solution)/shard_map/ppermute | solution.py:40
  23.4 2.2 %collective-permute-start.14 = (bf16[64,2560]{1,0:T(8,128)(2,1)S(1)}, bf16[64,2560]{1,0:T(8,128)(2,1)S(1)}, u32[]{:S(2)}, u32[]{:S(2)}) collective-permute-start(bf16[64,2560]{1,0:T(8,128)(2,1)S(1)} %get-tuple-element.53.refs_0_), channel_id=1, source_target_pairs={{0,65},{1,64},{2,67},{3,66},{4,69},{5,68},{6,71},{7,70},{8,73},{9,... | collective-permute-start | bytes 983048 | tf_op jit(solution)/shard_map/ppermute | solution.py:40
  25.6 0.7 copy-done.1
  26.4 4.8 %collective-permute-done.3.refs_3_ = bf16[64,2560]{1,0:T(8,128)(2,1)S(1)} collective-permute-done((bf16[64,2560]{1,0:T(8,128)(2,1)S(1)}, bf16[64,2560]{1,0:T(8,128)(2,1)S(1)}, u32[]{:S(2)}, u32[]{:S(2)}) %collective-permute-start.3) | collective-permute-done | bytes 327712 | tf_op jit(solution)/shard_map/ppermute | solution.py:40
  31.1 0.4 collective-permute-done.7.refs_6_
  31.5 1.6 %collective-permute-start.16 = (bf16[64,2560]{1,0:T(8,128)(2,1)S(1)}, bf16[64,2560]{1,0:T(8,128)(2,1)S(1)}, u32[]{:S(2)}, u32[]{:S(2)}) collective-permute-start(bf16[64,2560]{1,0:T(8,128)(2,1)S(1)} %get-tuple-element.53.refs_0_), channel_id=1, source_target_pairs={{0,2},{1,3},{2,4},{3,5},{4,6},{5,7},{6,0},{7,1},{8,10},{9,11},{10,... | collective-permute-start | bytes 983048 | tf_op jit(solution)/shard_map/ppermute | solution.py:40
  33.2 2.1 %collective-permute-start.17 = (bf16[64,2560]{1,0:T(8,128)(2,1)S(1)}, bf16[64,2560]{1,0:T(8,128)(2,1)S(1)}, u32[]{:S(2)}, u32[]{:S(2)}) collective-permute-start(bf16[64,2560]{1,0:T(8,128)(2,1)S(1)} %get-tuple-element.53.refs_0_), channel_id=1, source_target_pairs={{0,6},{1,7},{2,0},{3,1},{4,2},{5,3},{6,4},{7,5},{8,14},{9,15},{10,... | collective-permute-start | bytes 983048 | tf_op jit(solution)/shard_map/ppermute | solution.py:40
  35.2 2.9 %collective-permute-done.6.refs_5_ = bf16[64,2560]{1,0:T(8,128)(2,1)S(1)} collective-permute-done((bf16[64,2560]{1,0:T(8,128)(2,1)S(1)}, bf16[64,2560]{1,0:T(8,128)(2,1)S(1)}, u32[]{:S(2)}, u32[]{:S(2)}) %collective-permute-start.6) | collective-permute-done | bytes 327712 | tf_op jit(solution)/shard_map/ppermute | solution.py:40
  38.2 2.5 %collective-permute-start.9 = (bf16[64,2560]{1,0:T(8,128)(2,1)S(1)}, bf16[64,2560]{1,0:T(8,128)(2,1)S(1)}, u32[]{:S(2)}, u32[]{:S(2)}) collective-permute-start(bf16[64,2560]{1,0:T(8,128)(2,1)S(1)} %collective-permute-done.3.refs_3_), channel_id=1, source_target_pairs={{0,65},{1,64},{2,67},{3,66},{4,69},{5,68},{6,71},{7,70},{8,73},{9,... | collective-permute-start | bytes 983048 | tf_op jit(solution)/shard_map/ppermute | solution.py:40
  40.6 1.1 collective-permute-done.11.refs_3_
  41.8 2.1 %collective-permute-start.13 = (bf16[64,2560]{1,0:T(8,128)(2,1)S(1)}, bf16[64,2560]{1,0:T(8,128)(2,1)S(1)}, u32[]{:S(2)}, u32[]{:S(2)}) collective-permute-start(bf16[64,2560]{1,0:T(8,128)(2,1)S(1)} %collective-permute-done.8.refs_4_), channel_id=1, source_target_pairs={{0,6},{1,7},{2,0},{3,1},{4,2},{5,3},{6,4},{7,5},{8,14},{9,15},{10,... | collective-permute-start | bytes 983048 | tf_op jit(solution)/shard_map/ppermute | solution.py:40
  43.9 1.3 %collective-permute-done.16.refs_1_ = bf16[64,2560]{1,0:T(8,128)(2,1)S(1)} collective-permute-done((bf16[64,2560]{1,0:T(8,128)(2,1)S(1)}, bf16[64,2560]{1,0:T(8,128)(2,1)S(1)}, u32[]{:S(2)}, u32[]{:S(2)}) %collective-permute-start.16) | collective-permute-done | bytes 327712 | tf_op jit(solution)/shard_map/ppermute | solution.py:40
  45.2 2.5 %collective-permute-start.15 = (bf16[64,2560]{1,0:T(8,128)(2,1)S(1)}, bf16[64,2560]{1,0:T(8,128)(2,1)S(1)}, u32[]{:S(2)}, u32[]{:S(2)}) collective-permute-start(bf16[64,2560]{1,0:T(8,128)(2,1)S(1)} %collective-permute-done.11.refs_3_), channel_id=1, source_target_pairs={{0,65},{1,64},{2,67},{3,66},{4,69},{5,68},{6,71},{7,70},{8,73},{9,... | collective-permute-start | bytes 983048 | tf_op jit(solution)/shard_map/ppermute | solution.py:40
  47.7 4.5 %collective-permute-done.12.refs_5_ = bf16[64,2560]{1,0:T(8,128)(2,1)S(1)} collective-permute-done((bf16[64,2560]{1,0:T(8,128)(2,1)S(1)}, bf16[64,2560]{1,0:T(8,128)(2,1)S(1)}, u32[]{:S(2)}, u32[]{:S(2)}) %collective-permute-start.12) | collective-permute-done | bytes 327712 | tf_op jit(solution)/shard_map/ppermute | solution.py:40
  52.2 2.0 %collective-permute-start.19 = (bf16[64,2560]{1,0:T(8,128)(2,1)S(1)}, bf16[64,2560]{1,0:T(8,128)(2,1)S(1)}, u32[]{:S(2)}, u32[]{:S(2)}) collective-permute-start(bf16[64,2560]{1,0:T(8,128)(2,1)S(1)} %collective-permute-done.14.refs_4_), channel_id=1, source_target_pairs={{0,2},{1,3},{2,4},{3,5},{4,6},{5,7},{6,0},{7,1},{8,10},{9,11},{10,... | collective-permute-start | bytes 983048 | tf_op jit(solution)/shard_map/ppermute | solution.py:40
  54.2 3.5 %shard_map.69 = (f32[1152,512]{1,0:T(8,128)S(1)}, bf16[512,2560]{1,0:T(8,128)(2,1)S(1)}, f32[8,512]{1,0:T(8,128)S(1)}) custom-call(s32[1,512]{1,0:T(1,128)S(1)} %shard_map.68.ids, bf16[1152,2560]{1,0:T(8,128)(2,1)S(1)} %bitcast.3, bf16[64,2560]{1,0:T(8,128)(2,1)S(1)} %copy-done, bf16[64,2560]{1,0:T(8,128)(2,1)S(1)} %collective-permute-done.1.refs_1_, ...), custom_call_target="tpu_custom_call" | custom-call | flops 20000000000 | bytes 20000000 | tf_op jit(solution)/shard_map/pallas_call | solution.py:69
  57.8 1.7 %collective-permute-done.18.refs_3_ = bf16[64,2560]{1,0:T(8,128)(2,1)S(1)} collective-permute-done((bf16[64,2560]{1,0:T(8,128)(2,1)S(1)}, bf16[64,2560]{1,0:T(8,128)(2,1)S(1)}, u32[]{:S(2)}, u32[]{:S(2)}) %collective-permute-start.18) | collective-permute-done | bytes 327712 | tf_op jit(solution)/shard_map/ppermute | solution.py:40
  59.5 2.4 %collective-permute-start.21 = (bf16[64,2560]{1,0:T(8,128)(2,1)S(1)}, bf16[64,2560]{1,0:T(8,128)(2,1)S(1)}, u32[]{:S(2)}, u32[]{:S(2)}) collective-permute-start(bf16[64,2560]{1,0:T(8,128)(2,1)S(1)} %collective-permute-done.18.refs_3_), channel_id=1, source_target_pairs={{0,65},{1,64},{2,67},{3,66},{4,69},{5,68},{6,71},{7,70},{8,73},{9,... | collective-permute-start | bytes 983048 | tf_op jit(solution)/shard_map/ppermute | solution.py:40
  61.9 3.5 %shard_map.70.logits = f32[1152,512]{1,0:T(8,128)S(1)} custom-call(bf16[1152,5120]{1,0:T(8,128)(2,1)S(1)} %bitcast.1, bf16[64,2560]{1,0:T(8,128)(2,1)S(1)} %get-tuple-element.43.refs_0_, bf16[64,2560]{1,0:T(8,128)(2,1)S(1)} %collective-permute-done.5.refs_1_, bf16[64,2560]{1,0:T(8,128)(2,1)S(1)} %collective-permute-done.10.refs_2_, ...), custom_call_target="tpu_custom_call" | custom-call | flops 20000000000 | bytes 20000000 | tf_op jit(solution)/shard_map/pallas_call | solution.py:69
  65.4 2.4 %collective-permute-done.21.refs_7_ = bf16[64,2560]{1,0:T(8,128)(2,1)S(1)} collective-permute-done((bf16[64,2560]{1,0:T(8,128)(2,1)S(1)}, bf16[64,2560]{1,0:T(8,128)(2,1)S(1)}, u32[]{:S(2)}, u32[]{:S(2)}) %collective-permute-start.21) | collective-permute-done | bytes 327712 | tf_op jit(solution)/shard_map/ppermute | solution.py:40
  67.8 3.8 %shard_map.71 = f32[8,512]{1,0:T(8,128)S(1)} custom-call(s32[1,512]{1,0:T(1,128)S(1)} %shard_map.68.ids, f32[8,512]{1,0:T(8,128)S(1)} %get-tuple-element.45.student_stats, bf16[1152,5120]{1,0:T(8,128)(2,1)S(1)} %bitcast.1, f32[1152,512]{1,0:T(8,128)S(1)} %shard_map.70.logits, bf16[64,2560]{1,0:T(8,128)(2,1)S(1)} %get-tuple-element.53.refs_0_, ...), custom_call_target="tpu_custom_call" | custom-call | flops 20000000000 | bytes 20000000 | tf_op jit(solution)/shard_map/pallas_call | solution.py:69
  71.6 0.1 collective-permute-start.24
  71.7 1.4 %collective-permute-start.23 = (f32[8,512]{1,0:T(8,128)S(1)}, f32[8,512]{1,0:T(8,128)S(1)}, u32[]{:S(2)}, u32[]{:S(2)}) collective-permute-start(f32[8,512]{1,0:T(8,128)S(1)} %shard_map.71), channel_id=1, source_target_pairs={{0,6},{1,7},{2,0},{3,1},{4,2},{5,3},{6,4},{7,5},{8,14},{9,15},{10,... | collective-permute-start | bytes 49160 | tf_op jit(solution)/shard_map/ppermute | solution.py:40
  73.1 0.7 collective-permute-start.22
  73.8 3.1 %collective-permute-done.24 = f32[8,512]{1,0:T(8,128)S(1)} collective-permute-done((f32[8,512]{1,0:T(8,128)S(1)}, f32[8,512]{1,0:T(8,128)S(1)}, u32[]{:S(2)}, u32[]{:S(2)}) %collective-permute-start.24) | collective-permute-done | bytes 16416 | tf_op jit(solution)/shard_map/ppermute | solution.py:40
  76.9 1.1 collective-permute-done.22
  78.0 2.5 %collective-permute-start.25 = (f32[8,512]{1,0:T(8,128)S(1)}, f32[8,512]{1,0:T(8,128)S(1)}, u32[]{:S(2)}, u32[]{:S(2)}) collective-permute-start(f32[8,512]{1,0:T(8,128)S(1)} %add_add_fusion), channel_id=1, source_target_pairs={{0,65},{1,64},{2,67},{3,66},{4,69},{5,68},{6,71},{7,70},{8,73},{9,... | collective-permute-start | bytes 49160 | tf_op jit(solution)/shard_map/ppermute | solution.py:40
  80.6 2.4 %collective-permute-done.25 = f32[8,512]{1,0:T(8,128)S(1)} collective-permute-done((f32[8,512]{1,0:T(8,128)S(1)}, f32[8,512]{1,0:T(8,128)S(1)}, u32[]{:S(2)}, u32[]{:S(2)}) %collective-permute-start.25) | collective-permute-done | bytes 16416 | tf_op jit(solution)/shard_map/ppermute | solution.py:40
  83.0 0.6 shard_map.72
  83.6 0.1 collective-permute-start.26
  83.7 2.0 %collective-permute-done.26.grad_from = bf16[576,512]{1,0:T(8,128)(2,1)S(1)} collective-permute-done((bf16[576,512]{1,0:T(8,128)(2,1)S(1)}, bf16[576,512]{1,0:T(8,128)(2,1)S(1)}, u32[]{:S(2)}, u32[]{:S(2)}) %collective-permute-start.26) | collective-permute-done | bytes 589856 | tf_op jit(solution)/shard_map/ppermute | solution.py:40
  85.7 1.7 %shard_map.73 = (bf16[144,2560]{1,0:T(8,128)(2,1)S(1)}, bf16[144,2560]{1,0:T(8,128)(2,1)S(1)}) custom-call(bf16[576,512]{1,0:T(8,128)(2,1)S(1)} %get-tuple-element.63.grad_mine, bf16[576,512]{1,0:T(8,128)(2,1)S(1)} %collective-permute-done.26.grad_from, bf16[512,2560]{1,0:T(8,128)(2,1)S(1)} %get-tuple-element.61.hidden, ...), custom_call_target="tpu_custom_call" | custom-call | flops 1000000000 | bytes 1000000 | tf_op jit(solution)/shard_map/pallas_call | solution.py:69
  87.4 1.7 %shard_map.74 = (bf16[72,2560]{1,0:T(8,128)(2,1)S(1)}, f32[72,2560]{1,0:T(8,128)S(1)}, f32[72,2560]{1,0:T(8,128)S(1)}, f32[72,2560]{1,0:T(8,128)S(1)}) custom-call(bf16[576,512]{1,0:T(8,128)(2,1)S(1)} %get-tuple-element.63.grad_mine, bf16[576,512]{1,0:T(8,128)(2,1)S(1)} %collective-permute-done.26.grad_from, bf16[512,2560]{1,0:T(8,128)(2,1)S(1)} %get-tuple-element.61.hidden, ...), custom_call_target="tpu_custom_call" | custom-call | flops 20000000000 | bytes 20000000 | tf_op jit(solution)/shard_map/pallas_call | solution.py:69
  89.1 0.1 collective-permute-start.30
  89.2 4.1 %collective-permute-start.34 = (bf16[144,2560]{1,0:T(8,128)(2,1)S(1)}, bf16[144,2560]{1,0:T(8,128)(2,1)S(1)}, u32[]{:S(2)}, u32[]{:S(2)}) collective-permute-start(bf16[144,2560]{1,0:T(8,128)(2,1)S(1)} %get-tuple-element.62), channel_id=1, source_target_pairs={{0,48},{1,49},{2,50},{3,51},{4,52},{5,53},{6,54},{7,55},{8,56},{9,... | collective-permute-start | bytes 2211848 | tf_op jit(solution)/shard_map/ppermute | solution.py:40
  93.3 4.2 %shard_map.75 = (f32[64,2560]{1,0:T(8,128)S(1)}, f32[64,2560]{1,0:T(8,128)S(1)}, f32[64,2560]{1,0:T(8,128)S(1)}, bf16[64,2560]{1,0:T(8,128)(2,1)S(1)}, bf16[128,...) custom-call(s32[1,512]{1,0:T(1,128)S(1)} %shard_map.68.ids, f32[8,512]{1,0:T(8,128)S(1)} %add.45.total, ...), custom_call_target="tpu_custom_call" | custom-call | flops 20000000000 | bytes 20000000 | tf_op jit(solution)/shard_map/pallas_call | solution.py:69
  97.5 1.5 %collective-permute-start.28 = (bf16[128,2560]{1,0:T(8,128)(2,1)S(1)}, bf16[128,2560]{1,0:T(8,128)(2,1)S(1)}, u32[]{:S(2)}, u32[]{:S(2)}) collective-permute-start(bf16[128,2560]{1,0:T(8,128)(2,1)S(1)} %get-tuple-element.67), channel_id=1, source_target_pairs={{0,6},{1,7},{2,0},{3,1},{4,2},{5,3},{6,4},{7,5},{8,14},{9,15},{10,... | collective-permute-start | bytes 1966088 | tf_op jit(solution)/shard_map/ppermute | solution.py:40
  99.0 0.6 collective-permute-start.29
  99.6 0.2 collective-permute-done.30
  99.8 2.5 %collective-permute-start.31 = (bf16[64,2560]{1,0:T(8,128)(2,1)S(1)}, bf16[64,2560]{1,0:T(8,128)(2,1)S(1)}, u32[]{:S(2)}, u32[]{:S(2)}) collective-permute-start(bf16[64,2560]{1,0:T(8,128)(2,1)S(1)} %get-tuple-element.71), channel_id=1, source_target_pairs={{0,65},{1,64},{2,67},{3,66},{4,69},{5,68},{6,71},{7,70},{8,73},{9,... | collective-permute-start | bytes 983048 | tf_op jit(solution)/shard_map/ppermute | solution.py:40
  102.3 0.1 add_convert_fusion.2
  102.4 11.6 %collective-permute-done.28.lefts = bf16[128,2560]{1,0:T(8,128)(2,1)S(1)} collective-permute-done((bf16[128,2560]{1,0:T(8,128)(2,1)S(1)}, bf16[128,2560]{1,0:T(8,128)(2,1)S(1)}, u32[]{:S(2)}, u32[]{:S(2)}) %collective-permute-start.28) | collective-permute-done | bytes 655392 | tf_op jit(solution)/shard_map/ppermute | solution.py:40
  114.0 2.4 %collective-permute-done.29.rights = bf16[128,2560]{1,0:T(8,128)(2,1)S(1)} collective-permute-done((bf16[128,2560]{1,0:T(8,128)(2,1)S(1)}, bf16[128,2560]{1,0:T(8,128)(2,1)S(1)}, u32[]{:S(2)}, u32[]{:S(2)}) %collective-permute-start.29) | collective-permute-done | bytes 655392 | tf_op jit(solution)/shard_map/ppermute | solution.py:40
  116.4 0.1 add_convert_fusion.3
  116.5 2.5 %collective-permute-start.33 = (bf16[64,2560]{1,0:T(8,128)(2,1)S(1)}, bf16[64,2560]{1,0:T(8,128)(2,1)S(1)}, u32[]{:S(2)}, u32[]{:S(2)}) collective-permute-start(bf16[64,2560]{1,0:T(8,128)(2,1)S(1)} %add_convert_fusion.3), channel_id=1, source_target_pairs={{0,65},{1,64},{2,67},{3,66},{4,69},{5,68},{6,71},{7,70},{8,73},{9,... | collective-permute-start | bytes 983048 | tf_op jit(solution)/shard_map/ppermute | solution.py:40
  119.0 0.1 add_convert_fusion.4
  119.0 0.1 collective-permute-start.32
  119.1 1.8 %collective-permute-start.36 = (bf16[72,2560]{1,0:T(8,128)(2,1)S(1)}, bf16[72,2560]{1,0:T(8,128)(2,1)S(1)}, u32[]{:S(2)}, u32[]{:S(2)}) collective-permute-start(bf16[72,2560]{1,0:T(8,128)(2,1)S(1)} %add_convert_fusion.2), channel_id=1, source_target_pairs={{0,32},{1,33},{2,34},{3,35},{4,36},{5,37},{6,38},{7,39},{8,40},{9,... | collective-permute-start | bytes 1105928 | tf_op jit(solution)/shard_map/ppermute | solution.py:40
  121.0 0.1 add_convert_fusion.1
  121.1 1.0 collective-permute-start.37
  122.1 4.0 %collective-permute-done.33.near = bf16[64,2560]{1,0:T(8,128)(2,1)S(1)} collective-permute-done((bf16[64,2560]{1,0:T(8,128)(2,1)S(1)}, bf16[64,2560]{1,0:T(8,128)(2,1)S(1)}, u32[]{:S(2)}, u32[]{:S(2)}) %collective-permute-start.33) | collective-permute-done | bytes 327712 | tf_op jit(solution)/shard_map/ppermute | solution.py:40
  126.1 2.5 %collective-permute-done.32.far = bf16[64,2560]{1,0:T(8,128)(2,1)S(1)} collective-permute-done((bf16[64,2560]{1,0:T(8,128)(2,1)S(1)}, bf16[64,2560]{1,0:T(8,128)(2,1)S(1)}, u32[]{:S(2)}, u32[]{:S(2)}) %collective-permute-start.32) | collective-permute-done | bytes 327712 | tf_op jit(solution)/shard_map/ppermute | solution.py:40
  128.6 0.9 shard_map.76
  129.6 0.0 collective-permute-done.36
  129.6 0.1 collective-permute-done.37
  129.7 1.0 add_convert_fusion
  (45 shorter events, 0.1 us)
Async XLA Ops:
  0.6 19.5 %collective-permute-start.2 = (bf16[64,2560]{1,0:T(8,128)(2,1)}, bf16[64,2560]{1,0:T(8,128)(2,1)S(1)}, u32[]{:S(2)}, u32[]{:S(2)}) collective-permute-start(bf16[64,2560]{1,0:T(8,128)(2,1)} %refs_0_.1), channel_id=1, source_target_pairs={{0,6},{1,7},{2,0},{3,1},{4,2},{5,3},{6,4},{7,5},{8,14},{9,15},{10,... | collective-permute-start | bytes 983048 | tf_op jit(solution)/shard_map/ppermute | solution.py:40
  3.5 13.7 %collective-permute-start.1 = (bf16[64,2560]{1,0:T(8,128)(2,1)}, bf16[64,2560]{1,0:T(8,128)(2,1)S(1)}, u32[]{:S(2)}, u32[]{:S(2)}) collective-permute-start(bf16[64,2560]{1,0:T(8,128)(2,1)} %refs_0_.1), channel_id=1, source_target_pairs={{0,2},{1,3},{2,4},{3,5},{4,6},{5,7},{6,0},{7,1},{8,10},{9,11},{10,... | collective-permute-start | bytes 983048 | tf_op jit(solution)/shard_map/ppermute | solution.py:40
  3.5 16.6 %collective-permute-start.4 = (bf16[64,2560]{1,0:T(8,128)(2,1)}, bf16[64,2560]{1,0:T(8,128)(2,1)S(1)}, u32[]{:S(2)}, u32[]{:S(2)}) collective-permute-start(bf16[64,2560]{1,0:T(8,128)(2,1)} %refs_0_.1), channel_id=1, source_target_pairs={{0,65},{1,64},{2,67},{3,66},{4,69},{5,68},{6,71},{7,70},{8,73},{9,... | collective-permute-start | bytes 983048 | tf_op jit(solution)/shard_map/ppermute | solution.py:40
  6.6 7.7 %collective-permute-start = (s32[512]{0:T(512)}, s32[512]{0:T(512)S(1)}, u32[]{:S(2)}, u32[]{:S(2)}) collective-permute-start(s32[512]{0:T(512)} %own.1), channel_id=1, source_target_pairs={{0,65},{1,64},{2,67},{3,66},{4,69},{5,68},{6,71},{7,70},{8,73},{9,... | collective-permute-start | bytes 6152 | tf_op jit(solution)/shard_map/ppermute | solution.py:40
  7.9 15.5 %collective-permute-start.5 = (bf16[64,2560]{1,0:T(8,128)(2,1)S(1)}, bf16[64,2560]{1,0:T(8,128)(2,1)S(1)}, u32[]{:S(2)}, u32[]{:S(2)}) collective-permute-start(bf16[64,2560]{1,0:T(8,128)(2,1)S(1)} %get-tuple-element.43.refs_0_), channel_id=1, source_target_pairs={{0,2},{1,3},{2,4},{3,5},{4,6},{5,7},{6,0},{7,1},{8,10},{9,11},{10,... | collective-permute-start | bytes 983048 | tf_op jit(solution)/shard_map/ppermute | solution.py:40
  14.3 11.3 %collective-permute-start.10 = (bf16[64,2560]{1,0:T(8,128)(2,1)S(1)}, bf16[64,2560]{1,0:T(8,128)(2,1)S(1)}, u32[]{:S(2)}, u32[]{:S(2)}) collective-permute-start(bf16[64,2560]{1,0:T(8,128)(2,1)S(1)} %get-tuple-element.43.refs_0_), channel_id=1, source_target_pairs={{0,6},{1,7},{2,0},{3,1},{4,2},{5,3},{6,4},{7,5},{8,14},{9,15},{10,... | collective-permute-start | bytes 983048 | tf_op jit(solution)/shard_map/ppermute | solution.py:40
  17.2 15.9 %collective-permute-start.8 = (bf16[64,2560]{1,0:T(8,128)(2,1)S(1)}, bf16[64,2560]{1,0:T(8,128)(2,1)S(1)}, u32[]{:S(2)}, u32[]{:S(2)}) collective-permute-start(bf16[64,2560]{1,0:T(8,128)(2,1)S(1)} %get-tuple-element.43.refs_0_), channel_id=1, source_target_pairs={{0,65},{1,64},{2,67},{3,66},{4,69},{5,68},{6,71},{7,70},{8,73},{9,... | collective-permute-start | bytes 983048 | tf_op jit(solution)/shard_map/ppermute | solution.py:40
  20.2 11.0 %collective-permute-start.3 = (bf16[64,2560]{1,0:T(8,128)(2,1)S(1)}, bf16[64,2560]{1,0:T(8,128)(2,1)S(1)}, u32[]{:S(2)}, u32[]{:S(2)}) collective-permute-start(bf16[64,2560]{1,0:T(8,128)(2,1)S(1)} %collective-permute-done.1.refs_1_), channel_id=1, source_target_pairs={{0,2},{1,3},{2,4},{3,5},{4,6},{5,7},{6,0},{7,1},{8,10},{9,11},{10,... | collective-permute-start | bytes 983048 | tf_op jit(solution)/shard_map/ppermute | solution.py:40
  20.2 11.4 %collective-permute-start.7 = (bf16[64,2560]{1,0:T(8,128)(2,1)S(1)}, bf16[64,2560]{1,0:T(8,128)(2,1)S(1)}, u32[]{:S(2)}, u32[]{:S(2)}) collective-permute-start(bf16[64,2560]{1,0:T(8,128)(2,1)S(1)} %collective-permute-done.4.refs_4_), channel_id=1, source_target_pairs={{0,6},{1,7},{2,0},{3,1},{4,2},{5,3},{6,4},{7,5},{8,14},{9,15},{10,... | collective-permute-start | bytes 983048 | tf_op jit(solution)/shard_map/ppermute | solution.py:40
  23.4 30.8 %slice-start.3 = ((s8[5898240]{0:T(1024)(128)(4,1)}), s8[4194304]{0:T(1024)(128)(4,1)S(1)}, s32[]{:S(2)}) async-start(s8[5898240]{0:T(1024)(128)(4,1)} %bitcast.2), calls=%async_computation.3 | async-start | bytes 8388608
  23.4 30.8 %slice-start.4 = ((s8[5898240]{0:T(1024)(128)(4,1)}), s8[1703936]{0:T(1024)(128)(4,1)S(1)}, s32[]{:S(2)}) async-start(s8[5898240]{0:T(1024)(128)(4,1)} %bitcast.2), calls=%async_computation.4 | async-start | bytes 3407872
  23.4 30.8 %copy-start = (bf16[64,2560]{1,0:T(8,128)(2,1)S(1)}, bf16[64,2560]{1,0:T(8,128)(2,1)}, u32[]{:S(2)}) copy-start(bf16[64,2560]{1,0:T(8,128)(2,1)} %refs_0_.1) | copy-start | bytes 983044
  23.4 14.8 %collective-permute-start.14 = (bf16[64,2560]{1,0:T(8,128)(2,1)S(1)}, bf16[64,2560]{1,0:T(8,128)(2,1)S(1)}, u32[]{:S(2)}, u32[]{:S(2)}) collective-permute-start(bf16[64,2560]{1,0:T(8,128)(2,1)S(1)} %get-tuple-element.53.refs_0_), channel_id=1, source_target_pairs={{0,65},{1,64},{2,67},{3,66},{4,69},{5,68},{6,71},{7,70},{8,73},{9,... | collective-permute-start | bytes 983048 | tf_op jit(solution)/shard_map/ppermute | solution.py:40
  25.6 12.5 %collective-permute-start.6 = (bf16[64,2560]{1,0:T(8,128)(2,1)S(1)}, bf16[64,2560]{1,0:T(8,128)(2,1)S(1)}, u32[]{:S(2)}, u32[]{:S(2)}) collective-permute-start(bf16[64,2560]{1,0:T(8,128)(2,1)S(1)} %collective-permute-done.4.refs_4_), channel_id=1, source_target_pairs={{0,2},{1,3},{2,4},{3,5},{4,6},{5,7},{6,0},{7,1},{8,10},{9,11},{10,... | collective-permute-start | bytes 983048 | tf_op jit(solution)/shard_map/ppermute | solution.py:40
  25.6 0.7 copy-start.1
  26.3 35.6 %slice-start = ((s8[11796480]{0:T(1024)(128)(4,1)}), s8[4194304]{0:T(1024)(128)(4,1)S(1)}, s32[]{:S(2)}) async-start(s8[11796480]{0:T(1024)(128)(4,1)} %bitcast), calls=%async_computation | async-start | bytes 8388608
  26.3 35.6 %slice-start.1 = ((s8[11796480]{0:T(1024)(128)(4,1)}), s8[4194304]{0:T(1024)(128)(4,1)S(1)}, s32[]{:S(2)}) async-start(s8[11796480]{0:T(1024)(128)(4,1)} %bitcast), calls=%async_computation.1 | async-start | bytes 8388608
  26.3 35.6 %slice-start.2 = ((s8[11796480]{0:T(1024)(128)(4,1)}), s8[3407872]{0:T(1024)(128)(4,1)S(1)}, s32[]{:S(2)}) async-start(s8[11796480]{0:T(1024)(128)(4,1)} %bitcast), calls=%async_computation.2 | async-start | bytes 6815744
  31.1 10.6 %collective-permute-start.11 = (bf16[64,2560]{1,0:T(8,128)(2,1)S(1)}, bf16[64,2560]{1,0:T(8,128)(2,1)S(1)}, u32[]{:S(2)}, u32[]{:S(2)}) collective-permute-start(bf16[64,2560]{1,0:T(8,128)(2,1)S(1)} %collective-permute-done.10.refs_2_), channel_id=1, source_target_pairs={{0,6},{1,7},{2,0},{3,1},{4,2},{5,3},{6,4},{7,5},{8,14},{9,15},{10,... | collective-permute-start | bytes 983048 | tf_op jit(solution)/shard_map/ppermute | solution.py:40
  31.5 13.6 %collective-permute-start.16 = (bf16[64,2560]{1,0:T(8,128)(2,1)S(1)}, bf16[64,2560]{1,0:T(8,128)(2,1)S(1)}, u32[]{:S(2)}, u32[]{:S(2)}) collective-permute-start(bf16[64,2560]{1,0:T(8,128)(2,1)S(1)} %get-tuple-element.53.refs_0_), channel_id=1, source_target_pairs={{0,2},{1,3},{2,4},{3,5},{4,6},{5,7},{6,0},{7,1},{8,10},{9,11},{10,... | collective-permute-start | bytes 983048 | tf_op jit(solution)/shard_map/ppermute | solution.py:40
  33.2 14.5 %collective-permute-start.17 = (bf16[64,2560]{1,0:T(8,128)(2,1)S(1)}, bf16[64,2560]{1,0:T(8,128)(2,1)S(1)}, u32[]{:S(2)}, u32[]{:S(2)}) collective-permute-start(bf16[64,2560]{1,0:T(8,128)(2,1)S(1)} %get-tuple-element.53.refs_0_), channel_id=1, source_target_pairs={{0,6},{1,7},{2,0},{3,1},{4,2},{5,3},{6,4},{7,5},{8,14},{9,15},{10,... | collective-permute-start | bytes 983048 | tf_op jit(solution)/shard_map/ppermute | solution.py:40
  38.2 14.0 %collective-permute-start.12 = (bf16[64,2560]{1,0:T(8,128)(2,1)S(1)}, bf16[64,2560]{1,0:T(8,128)(2,1)S(1)}, u32[]{:S(2)}, u32[]{:S(2)}) collective-permute-start(bf16[64,2560]{1,0:T(8,128)(2,1)S(1)} %collective-permute-done.8.refs_4_), channel_id=1, source_target_pairs={{0,2},{1,3},{2,4},{3,5},{4,6},{5,7},{6,0},{7,1},{8,10},{9,11},{10,... | collective-permute-start | bytes 983048 | tf_op jit(solution)/shard_map/ppermute | solution.py:40
  38.2 14.0 %collective-permute-start.9 = (bf16[64,2560]{1,0:T(8,128)(2,1)S(1)}, bf16[64,2560]{1,0:T(8,128)(2,1)S(1)}, u32[]{:S(2)}, u32[]{:S(2)}) collective-permute-start(bf16[64,2560]{1,0:T(8,128)(2,1)S(1)} %collective-permute-done.3.refs_3_), channel_id=1, source_target_pairs={{0,65},{1,64},{2,67},{3,66},{4,69},{5,68},{6,71},{7,70},{8,73},{9,... | collective-permute-start | bytes 983048 | tf_op jit(solution)/shard_map/ppermute | solution.py:40
  41.8 20.1 %collective-permute-start.13 = (bf16[64,2560]{1,0:T(8,128)(2,1)S(1)}, bf16[64,2560]{1,0:T(8,128)(2,1)S(1)}, u32[]{:S(2)}, u32[]{:S(2)}) collective-permute-start(bf16[64,2560]{1,0:T(8,128)(2,1)S(1)} %collective-permute-done.8.refs_4_), channel_id=1, source_target_pairs={{0,6},{1,7},{2,0},{3,1},{4,2},{5,3},{6,4},{7,5},{8,14},{9,15},{10,... | collective-permute-start | bytes 983048 | tf_op jit(solution)/shard_map/ppermute | solution.py:40
  45.2 16.7 %collective-permute-start.15 = (bf16[64,2560]{1,0:T(8,128)(2,1)S(1)}, bf16[64,2560]{1,0:T(8,128)(2,1)S(1)}, u32[]{:S(2)}, u32[]{:S(2)}) collective-permute-start(bf16[64,2560]{1,0:T(8,128)(2,1)S(1)} %collective-permute-done.11.refs_3_), channel_id=1, source_target_pairs={{0,65},{1,64},{2,67},{3,66},{4,69},{5,68},{6,71},{7,70},{8,73},{9,... | collective-permute-start | bytes 983048 | tf_op jit(solution)/shard_map/ppermute | solution.py:40
  47.7 11.9 %collective-permute-start.18 = (bf16[64,2560]{1,0:T(8,128)(2,1)S(1)}, bf16[64,2560]{1,0:T(8,128)(2,1)S(1)}, u32[]{:S(2)}, u32[]{:S(2)}) collective-permute-start(bf16[64,2560]{1,0:T(8,128)(2,1)S(1)} %collective-permute-done.16.refs_1_), channel_id=1, source_target_pairs={{0,2},{1,3},{2,4},{3,5},{4,6},{5,7},{6,0},{7,1},{8,10},{9,11},{10,... | collective-permute-start | bytes 983048 | tf_op jit(solution)/shard_map/ppermute | solution.py:40
  52.2 13.2 %collective-permute-start.20 = (bf16[64,2560]{1,0:T(8,128)(2,1)S(1)}, bf16[64,2560]{1,0:T(8,128)(2,1)S(1)}, u32[]{:S(2)}, u32[]{:S(2)}) collective-permute-start(bf16[64,2560]{1,0:T(8,128)(2,1)S(1)} %collective-permute-done.14.refs_4_), channel_id=1, source_target_pairs={{0,6},{1,7},{2,0},{3,1},{4,2},{5,3},{6,4},{7,5},{8,14},{9,15},{10,... | collective-permute-start | bytes 983048 | tf_op jit(solution)/shard_map/ppermute | solution.py:40
  52.2 13.2 %collective-permute-start.19 = (bf16[64,2560]{1,0:T(8,128)(2,1)S(1)}, bf16[64,2560]{1,0:T(8,128)(2,1)S(1)}, u32[]{:S(2)}, u32[]{:S(2)}) collective-permute-start(bf16[64,2560]{1,0:T(8,128)(2,1)S(1)} %collective-permute-done.14.refs_4_), channel_id=1, source_target_pairs={{0,2},{1,3},{2,4},{3,5},{4,6},{5,7},{6,0},{7,1},{8,10},{9,11},{10,... | collective-permute-start | bytes 983048 | tf_op jit(solution)/shard_map/ppermute | solution.py:40
  59.5 8.3 %collective-permute-start.21 = (bf16[64,2560]{1,0:T(8,128)(2,1)S(1)}, bf16[64,2560]{1,0:T(8,128)(2,1)S(1)}, u32[]{:S(2)}, u32[]{:S(2)}) collective-permute-start(bf16[64,2560]{1,0:T(8,128)(2,1)S(1)} %collective-permute-done.18.refs_3_), channel_id=1, source_target_pairs={{0,65},{1,64},{2,67},{3,66},{4,69},{5,68},{6,71},{7,70},{8,73},{9,... | collective-permute-start | bytes 983048 | tf_op jit(solution)/shard_map/ppermute | solution.py:40
  71.6 5.3 %collective-permute-start.24 = (f32[8,512]{1,0:T(8,128)S(1)}, f32[8,512]{1,0:T(8,128)S(1)}, u32[]{:S(2)}, u32[]{:S(2)}) collective-permute-start(f32[8,512]{1,0:T(8,128)S(1)} %shard_map.71), channel_id=1, source_target_pairs={{0,4},{1,5},{2,6},{3,7},{4,0},{5,1},{6,2},{7,3},{8,12},{9,13},{10,... | collective-permute-start | bytes 49160 | tf_op jit(solution)/shard_map/ppermute | solution.py:40
  71.7 5.2 %collective-permute-start.23 = (f32[8,512]{1,0:T(8,128)S(1)}, f32[8,512]{1,0:T(8,128)S(1)}, u32[]{:S(2)}, u32[]{:S(2)}) collective-permute-start(f32[8,512]{1,0:T(8,128)S(1)} %shard_map.71), channel_id=1, source_target_pairs={{0,6},{1,7},{2,0},{3,1},{4,2},{5,3},{6,4},{7,5},{8,14},{9,15},{10,... | collective-permute-start | bytes 49160 | tf_op jit(solution)/shard_map/ppermute | solution.py:40
  73.1 4.9 %collective-permute-start.22 = (f32[8,512]{1,0:T(8,128)S(1)}, f32[8,512]{1,0:T(8,128)S(1)}, u32[]{:S(2)}, u32[]{:S(2)}) collective-permute-start(f32[8,512]{1,0:T(8,128)S(1)} %shard_map.71), channel_id=1, source_target_pairs={{0,2},{1,3},{2,4},{3,5},{4,6},{5,7},{6,0},{7,1},{8,10},{9,11},{10,... | collective-permute-start | bytes 49160 | tf_op jit(solution)/shard_map/ppermute | solution.py:40
  73.8 12.0 %collective-permute-start.27 = (bf16[512,2560]{1,0:T(8,128)(2,1)S(1)}, bf16[512,2560]{1,0:T(8,128)(2,1)S(1)}, u32[]{:S(2)}, u32[]{:S(2)}) collective-permute-start(bf16[512,2560]{1,0:T(8,128)(2,1)S(1)} %get-tuple-element.61.hidden), channel_id=1, source_target_pairs={{0,8},{1,9},{2,10},{3,11},{4,12},{5,13},{6,14},{7,15},{8,0},{9,1},... | collective-permute-start | bytes 7864328 | tf_op jit(solution)/shard_map/ppermute | solution.py:40
  78.0 4.9 %collective-permute-start.25 = (f32[8,512]{1,0:T(8,128)S(1)}, f32[8,512]{1,0:T(8,128)S(1)}, u32[]{:S(2)}, u32[]{:S(2)}) collective-permute-start(f32[8,512]{1,0:T(8,128)S(1)} %add_add_fusion), channel_id=1, source_target_pairs={{0,65},{1,64},{2,67},{3,66},{4,69},{5,68},{6,71},{7,70},{8,73},{9,... | collective-permute-start | bytes 49160 | tf_op jit(solution)/shard_map/ppermute | solution.py:40
  83.6 2.1 %collective-permute-start.26 = (bf16[576,512]{1,0:T(8,128)(2,1)S(1)}, bf16[576,512]{1,0:T(8,128)(2,1)S(1)}, u32[]{:S(2)}, u32[]{:S(2)}) collective-permute-start(bf16[576,512]{1,0:T(8,128)(2,1)S(1)} %get-tuple-element.60), channel_id=1, source_target_pairs={{0,8},{1,9},{2,10},{3,11},{4,12},{5,13},{6,14},{7,15},{8,0},{9,1},... | collective-permute-start | bytes 1769480 | tf_op jit(solution)/shard_map/ppermute | solution.py:40
  89.1 10.7 %collective-permute-start.30 = (bf16[72,2560]{1,0:T(8,128)(2,1)S(1)}, bf16[72,2560]{1,0:T(8,128)(2,1)S(1)}, u32[]{:S(2)}, u32[]{:S(2)}) collective-permute-start(bf16[72,2560]{1,0:T(8,128)(2,1)S(1)} %get-tuple-element.64), channel_id=1, source_target_pairs={{0,64},{1,65},{2,66},{3,67},{4,68},{5,69},{6,70},{7,71},{8,72},{9,... | collective-permute-start | bytes 1105928 | tf_op jit(solution)/shard_map/ppermute | solution.py:40
  89.2 30.0 %collective-permute-start.34 = (bf16[144,2560]{1,0:T(8,128)(2,1)S(1)}, bf16[144,2560]{1,0:T(8,128)(2,1)S(1)}, u32[]{:S(2)}, u32[]{:S(2)}) collective-permute-start(bf16[144,2560]{1,0:T(8,128)(2,1)S(1)} %get-tuple-element.62), channel_id=1, source_target_pairs={{0,48},{1,49},{2,50},{3,51},{4,52},{5,53},{6,54},{7,55},{8,56},{9,... | collective-permute-start | bytes 2211848 | tf_op jit(solution)/shard_map/ppermute | solution.py:40
  93.3 27.7 %collective-permute-start.35 = (bf16[144,2560]{1,0:T(8,128)(2,1)S(1)}, bf16[144,2560]{1,0:T(8,128)(2,1)S(1)}, u32[]{:S(2)}, u32[]{:S(2)}) collective-permute-start(bf16[144,2560]{1,0:T(8,128)(2,1)S(1)} %get-tuple-element.74), channel_id=1, source_target_pairs={{0,16},{1,17},{2,18},{3,19},{4,20},{5,21},{6,22},{7,23},{8,24},{9,... | collective-permute-start | bytes 2211848 | tf_op jit(solution)/shard_map/ppermute | solution.py:40
  97.5 16.6 %collective-permute-start.28 = (bf16[128,2560]{1,0:T(8,128)(2,1)S(1)}, bf16[128,2560]{1,0:T(8,128)(2,1)S(1)}, u32[]{:S(2)}, u32[]{:S(2)}) collective-permute-start(bf16[128,2560]{1,0:T(8,128)(2,1)S(1)} %get-tuple-element.67), channel_id=1, source_target_pairs={{0,6},{1,7},{2,0},{3,1},{4,2},{5,3},{6,4},{7,5},{8,14},{9,15},{10,... | collective-permute-start | bytes 1966088 | tf_op jit(solution)/shard_map/ppermute | solution.py:40
  99.0 17.4 %collective-permute-start.29 = (bf16[128,2560]{1,0:T(8,128)(2,1)S(1)}, bf16[128,2560]{1,0:T(8,128)(2,1)S(1)}, u32[]{:S(2)}, u32[]{:S(2)}) collective-permute-start(bf16[128,2560]{1,0:T(8,128)(2,1)S(1)} %get-tuple-element.68), channel_id=1, source_target_pairs={{0,2},{1,3},{2,4},{3,5},{4,6},{5,7},{6,0},{7,1},{8,10},{9,11},{10,... | collective-permute-start | bytes 1966088 | tf_op jit(solution)/shard_map/ppermute | solution.py:40
  99.8 19.2 %collective-permute-start.31 = (bf16[64,2560]{1,0:T(8,128)(2,1)S(1)}, bf16[64,2560]{1,0:T(8,128)(2,1)S(1)}, u32[]{:S(2)}, u32[]{:S(2)}) collective-permute-start(bf16[64,2560]{1,0:T(8,128)(2,1)S(1)} %get-tuple-element.71), channel_id=1, source_target_pairs={{0,65},{1,64},{2,67},{3,66},{4,69},{5,68},{6,71},{7,70},{8,73},{9,... | collective-permute-start | bytes 983048 | tf_op jit(solution)/shard_map/ppermute | solution.py:40
  116.5 9.6 %collective-permute-start.33 = (bf16[64,2560]{1,0:T(8,128)(2,1)S(1)}, bf16[64,2560]{1,0:T(8,128)(2,1)S(1)}, u32[]{:S(2)}, u32[]{:S(2)}) collective-permute-start(bf16[64,2560]{1,0:T(8,128)(2,1)S(1)} %add_convert_fusion.3), channel_id=1, source_target_pairs={{0,65},{1,64},{2,67},{3,66},{4,69},{5,68},{6,71},{7,70},{8,73},{9,... | collective-permute-start | bytes 983048 | tf_op jit(solution)/shard_map/ppermute | solution.py:40
  119.0 9.6 %collective-permute-start.32 = (bf16[64,2560]{1,0:T(8,128)(2,1)S(1)}, bf16[64,2560]{1,0:T(8,128)(2,1)S(1)}, u32[]{:S(2)}, u32[]{:S(2)}) collective-permute-start(bf16[64,2560]{1,0:T(8,128)(2,1)S(1)} %add_convert_fusion.4), channel_id=1, source_target_pairs={{0,4},{1,5},{2,6},{3,7},{4,0},{5,1},{6,2},{7,3},{8,12},{9,13},{10,... | collective-permute-start | bytes 983048 | tf_op jit(solution)/shard_map/ppermute | solution.py:40
  119.1 10.5 %collective-permute-start.36 = (bf16[72,2560]{1,0:T(8,128)(2,1)S(1)}, bf16[72,2560]{1,0:T(8,128)(2,1)S(1)}, u32[]{:S(2)}, u32[]{:S(2)}) collective-permute-start(bf16[72,2560]{1,0:T(8,128)(2,1)S(1)} %add_convert_fusion.2), channel_id=1, source_target_pairs={{0,32},{1,33},{2,34},{3,35},{4,36},{5,37},{6,38},{7,39},{8,40},{9,... | collective-permute-start | bytes 1105928 | tf_op jit(solution)/shard_map/ppermute | solution.py:40
  121.1 8.6 %collective-permute-start.37 = (bf16[72,2560]{1,0:T(8,128)(2,1)S(1)}, bf16[72,2560]{1,0:T(8,128)(2,1)S(1)}, u32[]{:S(2)}, u32[]{:S(2)}) collective-permute-start(bf16[72,2560]{1,0:T(8,128)(2,1)S(1)} %add_convert_fusion.1), channel_id=1, source_target_pairs={{0,64},{1,65},{2,66},{3,67},{4,68},{5,69},{6,70},{7,71},{8,72},{9,... | collective-permute-start | bytes 1105928 | tf_op jit(solution)/shard_map/ppermute | solution.py:40

commit v4 on v3

--- a/solution.py
+++ b/solution.py
@@ -248,9 +248,24 @@
     return kernel_call(functools.partial(head_kernel, first), arrays, outs, [], 4, said)
 
 
+def pass_on_kernel(near, far, lefts, rights, far_near, near_out, far_out):
+    n = near.shape[0]
+    near_out[...] = (near[...] + lefts[n:, :].astype(F32) + rights[n:, :].astype(F32)).astype(near_out.dtype)
+    far_out[...] = (far[...] + far_near[...].astype(F32)).astype(far_out.dtype)
+
+
+def pass_on(pieces):
+    return kernel_call(pass_on_kernel, pieces, [(pieces[0].shape, BF16)] * 2, [], 4, LONG)
+
+
 def finish_kernel(own, lefts, rights, far, near, out):
-    total = own[...] + lefts[0:64, :].astype(F32) + rights[0:64, :].astype(F32)
+    n = out.shape[0]
+    total = own[...] + lefts[0:n, :].astype(F32) + rights[0:n, :].astype(F32)
     out[...] = (total + far[...].astype(F32) + near[...].astype(F32)).astype(out.dtype)
+
+
+def finish(pieces, said):
+    return kernel_call(finish_kernel, pieces, [(pieces[0].shape, BF16)], [], 4, said)[0]
 
 
 def group_sum(a):
@@ -268,11 +283,10 @@
     near_b = over(t_b)
     ids = kernel_call(ids_kernel, (sampled_ids, ids_near), [((1, 512), jnp.int32)], [], 1, LONG)[0]
     t_b = after(t_b, ids)
-    far, right_near = up(left), down(near)
-    left_near, f_a, far_near = up(near), down(r_a), over(far)
-    l_b, r_b = up(t_b), down(t_b)
-    ln_a, rn_a, fn_a = up(near_a), down(near_a), over(f_a)
-    f_b = up(l_b)
+    far, right_near, left_near = up(left), down(near), over(left)
+    l_b, f_a, far_near = up(t_b), down(r_a), over(far)
+    ln_a, r_b, fn_a = up(near_a), down(t_b), over(f_a)
+    f_b, rn_a = up(l_b), down(near_a)
     fn_b = over(f_b)
     ln_b, rn_b = up(near_b), down(near_b)
 
@@ -285,23 +299,20 @@
 
     mine, other = logit_grads(ids, total, logits)
     grads = (mine, send(other, CORE), hidden, hidden_from)
-    h_lefts, h_rights = head_parts(0, ((144, BF16), (144, BF16)), SHORT, *grads)
-    grads = (after(mine, h_lefts), *grads[1:])
-    h_fl, h_f, h_y, h_own = head_parts(288, ((72, BF16), (72, F32), (72, F32), (72, F32)), LONG, *grads)
+    h_lefts, h_rights, h_fl = head_parts(0, ((144, BF16), (144, BF16), (72, BF16)), SHORT, *grads)
+    parts = hidden_parts(ids, after(total, h_fl), logits, student_head)
+    grads = (after(mine, parts[0]), *grads[1:])
+    h_f, h_y, h_own = head_parts(360, ((72, F32),) * 3, SHORT, *grads)
     from_lefts, from_rights, from_fl = send(h_lefts, Z_DOWN), send(h_rights, Z_UP), send(h_fl, Y_LO)
-    from_f = send(after((h_f + from_fl.astype(F32)).astype(BF16), from_lefts), Z_FAR)
-    h_y = h_y + from_lefts[72:].astype(F32) + from_rights[72:].astype(F32)
-    from_y = send(h_y.astype(BF16), Y_LO)
-    head_sum = h_own + from_lefts[:72].astype(F32) + from_rights[:72].astype(F32)
-    head_sum = head_sum + from_f.astype(F32) + from_y.astype(F32)
-
-    g_own, g_near, g_far, g_far_near, g_lefts, g_rights = hidden_parts(ids, after(total, h_fl), logits, student_head)
+    h_y, h_f = pass_on((h_y, h_f, from_lefts, from_rights, from_fl))
+    from_y, from_f = send(h_y, Y_LO), send(h_f, Z_FAR)
+    head_grad = finish((h_own, from_lefts, from_rights, from_f, from_y), SHORT)
+
+    g_own, g_near, g_far, g_far_near, g_lefts, g_rights = parts
     from_lefts, from_rights, from_fn = send(g_lefts, X_DOWN), send(g_rights, X_UP), send(after(g_far_near, from_fl), Y_HI)
-    from_far = send((g_far + from_fn.astype(F32)).astype(BF16), X_FAR)
-    g_near = g_near + from_lefts[64:].astype(F32) + from_rights[64:].astype(F32)
-    from_near = send(g_near.astype(BF16), Y_HI)
-    pieces = (g_own, from_lefts, from_rights, from_far, from_near)
-    return kernel_call(finish_kernel, pieces, [(student_hidden.shape, BF16)], [], 4)[0], head_sum.astype(BF16)
+    near_sum, far_sum = pass_on((after(g_near, h_y), g_far, from_lefts, from_rights, from_fn))
+    from_far, from_near = send(far_sum, X_FAR), send(near_sum, Y_HI)
+    return finish((after(g_own, head_grad), from_lefts, from_rights, from_far, from_near), SHORT), head_grad
 
 
 def solution(mesh):

time: 131 us -> 123 us (0.939)
  waiting for transfers between devices: 54.5 us -> 49.1 us
  starting transfers between devices: 52.3 us -> 49.6 us
  Pallas kernels: 19.9 us -> 21.3 us
  other arithmetic: 1.36 us -> 0.01 us
    ppermute x38, waiting for transfers between devices: 54.5 us -> 49.1 us  [send(): return lax.ppermute(a, AXES, to)]
    ppermute x38, starting transfers between devices: 52.3 us -> 49.6 us  [send(): return lax.ppermute(a, AXES, to)]
    pallas_call x9 -> x12, Pallas kernels: 19.9 us -> 21.3 us  [kernel_call(): pl.pallas_call(body, in_specs=[VMEM] * len(arrays), out_specs=[VMEM] * le...]
    convert_element_type x5 -> x0, other arithmetic: 1.35 us -> none  [the longest x1 0.97 us: on_device(): head_sum.astype(BF16)]
  transfers between devices with their start and end apart: 38 -> 38, of which waited for: 19 -> 16; matrix products, arithmetic and copies ran while one was open for 1% -> 1% of each run, Pallas kernels for 10% -> 12%
where the time goes in v4:
time: 123 us
  starting transfers between devices  49.6 us (40%)
  waiting for transfers between devices  49.1 us (40%)
  Pallas kernels  21.3 us (17%)
  local copies, waits for them, and re-layouts  1.83 us (1%)
    ppermute x38, starting transfers between devices, send(): return lax.ppermute(a, AXES, to)  49.6 us
    ppermute x38, waiting for transfers between devices, send(): return lax.ppermute(a, AXES, to)  49.1 us
    pallas_call x12, Pallas kernels, kernel_call(): pl.pallas_call(body, in_specs=[VMEM] * len(arrays), out_specs=[VMEM] * le...  21.3 us
  transfers between devices with their start and end apart: 38, of which 16 were waited for; matrix products, arithmetic and copies ran while one was open for 1% of the time, Pallas kernels for 12%

profile of v4, /device:TPU:0, one launch (start us, length us, event | category | flops | bytes accessed | tf_op | source)
XLA Modules:
  0.0 122.7 jit_solution(5885801345193309132)
XLA Ops:
  0.6 2.9 %collective-permute-start.2 = (bf16[64,2560]{1,0:T(8,128)(2,1)}, bf16[64,2560]{1,0:T(8,128)(2,1)S(1)}, u32[]{:S(2)}, u32[]{:S(2)}) collective-permute-start(bf16[64,2560]{1,0:T(8,128)(2,1)} %refs_0_.1), channel_id=1, source_target_pairs={{0,6},{1,7},{2,0},{3,1},{4,2},{5,3},{6,4},{7,5},{8,14},{9,15},{10,... | collective-permute-start | bytes 983048 | tf_op jit(solution)/shard_map/ppermute | solution.py:40
  3.5 3.0 %collective-permute-start.4 = (bf16[64,2560]{1,0:T(8,128)(2,1)}, bf16[64,2560]{1,0:T(8,128)(2,1)S(1)}, u32[]{:S(2)}, u32[]{:S(2)}) collective-permute-start(bf16[64,2560]{1,0:T(8,128)(2,1)} %refs_0_.1), channel_id=1, source_target_pairs={{0,65},{1,64},{2,67},{3,66},{4,69},{5,68},{6,71},{7,70},{8,73},{9,... | collective-permute-start | bytes 983048 | tf_op jit(solution)/shard_map/ppermute | solution.py:40
  6.6 0.2 collective-permute-start
  6.8 1.1 fusion
  7.9 0.0 slice-start.3
  7.9 0.0 slice-start.4
  7.9 0.0 copy-start
  7.9 3.3 %collective-permute-start.11 = (bf16[64,2560]{1,0:T(8,128)(2,1)S(1)}, bf16[64,2560]{1,0:T(8,128)(2,1)S(1)}, u32[]{:S(2)}, u32[]{:S(2)}) collective-permute-start(bf16[64,2560]{1,0:T(8,128)(2,1)S(1)} %get-tuple-element.46.refs_0_), channel_id=1, source_target_pairs={{0,6},{1,7},{2,0},{3,1},{4,2},{5,3},{6,4},{7,5},{8,14},{9,15},{10,... | collective-permute-start | bytes 983048 | tf_op jit(solution)/shard_map/ppermute | solution.py:40
  11.2 3.1 %collective-permute-done.near = s32[512]{0:T(512)S(1)} collective-permute-done((s32[512]{0:T(512)}, s32[512]{0:T(512)S(1)}, u32[]{:S(2)}, u32[]{:S(2)}) %collective-permute-start) | collective-permute-done | bytes 2080 | tf_op jit(solution)/shard_map/ppermute | solution.py:40
  14.3 0.4 collective-permute-start.10
  14.8 2.9 %collective-permute-start.5 = (bf16[64,2560]{1,0:T(8,128)(2,1)S(1)}, bf16[64,2560]{1,0:T(8,128)(2,1)S(1)}, u32[]{:S(2)}, u32[]{:S(2)}) collective-permute-start(bf16[64,2560]{1,0:T(8,128)(2,1)S(1)} %get-tuple-element.46.refs_0_), channel_id=1, source_target_pairs={{0,65},{1,64},{2,67},{3,66},{4,69},{5,68},{6,71},{7,70},{8,73},{9,... | collective-permute-start | bytes 983048 | tf_op jit(solution)/shard_map/ppermute | solution.py:40
  17.7 0.7 copy-done.1
  18.4 0.0 slice-start
  18.4 0.0 slice-start.1
  18.4 2.8 %collective-permute-start.7 = (bf16[64,2560]{1,0:T(8,128)(2,1)S(1)}, bf16[64,2560]{1,0:T(8,128)(2,1)S(1)}, u32[]{:S(2)}, u32[]{:S(2)}) collective-permute-start(bf16[64,2560]{1,0:T(8,128)(2,1)S(1)} %collective-permute-done.4.refs_4_), channel_id=1, source_target_pairs={{0,6},{1,7},{2,0},{3,1},{4,2},{5,3},{6,4},{7,5},{8,14},{9,15},{10,... | collective-permute-start | bytes 983048 | tf_op jit(solution)/shard_map/ppermute | solution.py:40
  21.2 3.7 %collective-permute-done.10.refs_1_ = bf16[64,2560]{1,0:T(8,128)(2,1)S(1)} collective-permute-done((bf16[64,2560]{1,0:T(8,128)(2,1)S(1)}, bf16[64,2560]{1,0:T(8,128)(2,1)S(1)}, u32[]{:S(2)}, u32[]{:S(2)}) %collective-permute-start.10) | collective-permute-done | bytes 327712 | tf_op jit(solution)/shard_map/ppermute | solution.py:40
  24.9 4.2 %collective-permute-start.8 = (bf16[64,2560]{1,0:T(8,128)(2,1)S(1)}, bf16[64,2560]{1,0:T(8,128)(2,1)S(1)}, u32[]{:S(2)}, u32[]{:S(2)}) collective-permute-start(bf16[64,2560]{1,0:T(8,128)(2,1)S(1)} %get-tuple-element.58.refs_0_), channel_id=1, source_target_pairs={{0,65},{1,64},{2,67},{3,66},{4,69},{5,68},{6,71},{7,70},{8,73},{9,... | collective-permute-start | bytes 983048 | tf_op jit(solution)/shard_map/ppermute | solution.py:40
  29.1 3.2 %collective-permute-start.12 = (bf16[64,2560]{1,0:T(8,128)(2,1)S(1)}, bf16[64,2560]{1,0:T(8,128)(2,1)S(1)}, u32[]{:S(2)}, u32[]{:S(2)}) collective-permute-start(bf16[64,2560]{1,0:T(8,128)(2,1)S(1)} %collective-permute-done.11.refs_2_), channel_id=1, source_target_pairs={{0,6},{1,7},{2,0},{3,1},{4,2},{5,3},{6,4},{7,5},{8,14},{9,15},{10,... | collective-permute-start | bytes 983048 | tf_op jit(solution)/shard_map/ppermute | solution.py:40
  32.3 0.0 collective-permute-start.6
  32.3 0.8 collective-permute-done.3.refs_3_
  33.1 4.5 %collective-permute-done.8.refs_4_ = bf16[64,2560]{1,0:T(8,128)(2,1)S(1)} collective-permute-done((bf16[64,2560]{1,0:T(8,128)(2,1)S(1)}, bf16[64,2560]{1,0:T(8,128)(2,1)S(1)}, u32[]{:S(2)}, u32[]{:S(2)}) %collective-permute-start.8) | collective-permute-done | bytes 327712 | tf_op jit(solution)/shard_map/ppermute | solution.py:40
  37.6 0.5 collective-permute-start.17
  38.1 2.8 %collective-permute-done.16.refs_1_ = bf16[64,2560]{1,0:T(8,128)(2,1)S(1)} collective-permute-done((bf16[64,2560]{1,0:T(8,128)(2,1)S(1)}, bf16[64,2560]{1,0:T(8,128)(2,1)S(1)}, u32[]{:S(2)}, u32[]{:S(2)}) %collective-permute-start.16) | collective-permute-done | bytes 327712 | tf_op jit(solution)/shard_map/ppermute | solution.py:40
  40.9 2.2 %collective-permute-start.9 = (bf16[64,2560]{1,0:T(8,128)(2,1)S(1)}, bf16[64,2560]{1,0:T(8,128)(2,1)S(1)}, u32[]{:S(2)}, u32[]{:S(2)}) collective-permute-start(bf16[64,2560]{1,0:T(8,128)(2,1)S(1)} %collective-permute-done.3.refs_3_), channel_id=1, source_target_pairs={{0,65},{1,64},{2,67},{3,66},{4,69},{5,68},{6,71},{7,70},{8,73},{9,... | collective-permute-start | bytes 983048 | tf_op jit(solution)/shard_map/ppermute | solution.py:40
  43.1 3.2 %collective-permute-start.14 = (bf16[64,2560]{1,0:T(8,128)(2,1)S(1)}, bf16[64,2560]{1,0:T(8,128)(2,1)S(1)}, u32[]{:S(2)}, u32[]{:S(2)}) collective-permute-start(bf16[64,2560]{1,0:T(8,128)(2,1)S(1)} %collective-permute-done.5.refs_4_), channel_id=1, source_target_pairs={{0,6},{1,7},{2,0},{3,1},{4,2},{5,3},{6,4},{7,5},{8,14},{9,15},{10,... | collective-permute-start | bytes 983048 | tf_op jit(solution)/shard_map/ppermute | solution.py:40
  46.3 1.6 %collective-permute-done.13.refs_5_ = bf16[64,2560]{1,0:T(8,128)(2,1)S(1)} collective-permute-done((bf16[64,2560]{1,0:T(8,128)(2,1)S(1)}, bf16[64,2560]{1,0:T(8,128)(2,1)S(1)}, u32[]{:S(2)}, u32[]{:S(2)}) %collective-permute-start.13) | collective-permute-done | bytes 327712 | tf_op jit(solution)/shard_map/ppermute | solution.py:40
  47.9 2.2 %collective-permute-start.15 = (bf16[64,2560]{1,0:T(8,128)(2,1)S(1)}, bf16[64,2560]{1,0:T(8,128)(2,1)S(1)}, u32[]{:S(2)}, u32[]{:S(2)}) collective-permute-start(bf16[64,2560]{1,0:T(8,128)(2,1)S(1)} %collective-permute-done.12.refs_3_), channel_id=1, source_target_pairs={{0,65},{1,64},{2,67},{3,66},{4,69},{5,68},{6,71},{7,70},{8,73},{9,... | collective-permute-start | bytes 983048 | tf_op jit(solution)/shard_map/ppermute | solution.py:40
  50.1 2.0 %collective-permute-done.9.refs_7_ = bf16[64,2560]{1,0:T(8,128)(2,1)S(1)} collective-permute-done((bf16[64,2560]{1,0:T(8,128)(2,1)S(1)}, bf16[64,2560]{1,0:T(8,128)(2,1)S(1)}, u32[]{:S(2)}, u32[]{:S(2)}) %collective-permute-start.9) | collective-permute-done | bytes 327712 | tf_op jit(solution)/shard_map/ppermute | solution.py:40
  52.1 1.2 collective-permute-start.20
  53.4 1.6 %collective-permute-done.18.refs_3_ = bf16[64,2560]{1,0:T(8,128)(2,1)S(1)} collective-permute-done((bf16[64,2560]{1,0:T(8,128)(2,1)S(1)}, bf16[64,2560]{1,0:T(8,128)(2,1)S(1)}, u32[]{:S(2)}, u32[]{:S(2)}) %collective-permute-start.18) | collective-permute-done | bytes 327712 | tf_op jit(solution)/shard_map/ppermute | solution.py:40
  55.0 2.2 %collective-permute-start.21 = (bf16[64,2560]{1,0:T(8,128)(2,1)S(1)}, bf16[64,2560]{1,0:T(8,128)(2,1)S(1)}, u32[]{:S(2)}, u32[]{:S(2)}) collective-permute-start(bf16[64,2560]{1,0:T(8,128)(2,1)S(1)} %collective-permute-done.18.refs_3_), channel_id=1, source_target_pairs={{0,65},{1,64},{2,67},{3,66},{4,69},{5,68},{6,71},{7,70},{8,73},{9,... | collective-permute-start | bytes 983048 | tf_op jit(solution)/shard_map/ppermute | solution.py:40
  57.2 3.5 %shard_map.69 = (f32[1152,512]{1,0:T(8,128)S(1)}, bf16[512,2560]{1,0:T(8,128)(2,1)S(1)}, f32[8,512]{1,0:T(8,128)S(1)}) custom-call(s32[1,512]{1,0:T(1,128)S(1)} %shard_map.68.ids, bf16[1152,2560]{1,0:T(8,128)(2,1)S(1)} %bitcast.3, bf16[64,2560]{1,0:T(8,128)(2,1)S(1)} %copy-done, bf16[64,2560]{1,0:T(8,128)(2,1)S(1)} %collective-permute-done.1.refs_1_, ...), custom_call_target="tpu_custom_call" | custom-call | flops 20000000000 | bytes 20000000 | tf_op jit(solution)/shard_map/pallas_call | solution.py:69
  60.8 3.5 %shard_map.70.logits = f32[1152,512]{1,0:T(8,128)S(1)} custom-call(bf16[1152,5120]{1,0:T(8,128)(2,1)S(1)} %bitcast.1, bf16[64,2560]{1,0:T(8,128)(2,1)S(1)} %get-tuple-element.46.refs_0_, bf16[64,2560]{1,0:T(8,128)(2,1)S(1)} %collective-permute-done.10.refs_1_, bf16[64,2560]{1,0:T(8,128)(2,1)S(1)} %collective-permute-done.11.refs_2_, ...), custom_call_target="tpu_custom_call" | custom-call | flops 20000000000 | bytes 20000000 | tf_op jit(solution)/shard_map/pallas_call | solution.py:69
  64.2 3.8 %shard_map.71 = f32[8,512]{1,0:T(8,128)S(1)} custom-call(s32[1,512]{1,0:T(1,128)S(1)} %shard_map.68.ids, f32[8,512]{1,0:T(8,128)S(1)} %get-tuple-element.51.student_stats, bf16[1152,5120]{1,0:T(8,128)(2,1)S(1)} %bitcast.1, f32[1152,512]{1,0:T(8,128)S(1)} %shard_map.70.logits, bf16[64,2560]{1,0:T(8,128)(2,1)S(1)} %get-tuple-element.58.refs_0_, ...), custom_call_target="tpu_custom_call" | custom-call | flops 20000000000 | bytes 20000000 | tf_op jit(solution)/shard_map/pallas_call | solution.py:69
  68.0 0.9 collective-permute-start.24
  68.9 1.1 collective-permute-start.23
  70.1 0.9 collective-permute-start.22
  70.9 2.4 %collective-permute-done.24 = f32[8,512]{1,0:T(8,128)S(1)} collective-permute-done((f32[8,512]{1,0:T(8,128)S(1)}, f32[8,512]{1,0:T(8,128)S(1)}, u32[]{:S(2)}, u32[]{:S(2)}) %collective-permute-start.24) | collective-permute-done | bytes 16416 | tf_op jit(solution)/shard_map/ppermute | solution.py:40
  73.4 1.6 %collective-permute-done.22 = f32[8,512]{1,0:T(8,128)S(1)} collective-permute-done((f32[8,512]{1,0:T(8,128)S(1)}, f32[8,512]{1,0:T(8,128)S(1)}, u32[]{:S(2)}, u32[]{:S(2)}) %collective-permute-start.22) | collective-permute-done | bytes 16416 | tf_op jit(solution)/shard_map/ppermute | solution.py:40
  75.0 1.2 collective-permute-start.25
  76.2 3.8 %collective-permute-done.25 = f32[8,512]{1,0:T(8,128)S(1)} collective-permute-done((f32[8,512]{1,0:T(8,128)S(1)}, f32[8,512]{1,0:T(8,128)S(1)}, u32[]{:S(2)}, u32[]{:S(2)}) %collective-permute-start.25) | collective-permute-done | bytes 16416 | tf_op jit(solution)/shard_map/ppermute | solution.py:40
  80.0 0.6 shard_map.72
  80.6 0.1 collective-permute-start.26
  80.7 2.0 %collective-permute-done.26.grad_from = bf16[576,512]{1,0:T(8,128)(2,1)S(1)} collective-permute-done((bf16[576,512]{1,0:T(8,128)(2,1)S(1)}, bf16[576,512]{1,0:T(8,128)(2,1)S(1)}, u32[]{:S(2)}, u32[]{:S(2)}) %collective-permute-start.26) | collective-permute-done | bytes 589856 | tf_op jit(solution)/shard_map/ppermute | solution.py:40
  82.7 2.1 %shard_map.73 = (bf16[144,2560]{1,0:T(8,128)(2,1)S(1)}, bf16[144,2560]{1,0:T(8,128)(2,1)S(1)}, bf16[72,2560]{1,0:T(8,128)(2,1)S(1)}) custom-call(bf16[576,512]{1,0:T(8,128)(2,1)S(1)} %get-tuple-element.70.grad_mine, bf16[576,512]{1,0:T(8,128)(2,1)S(1)} %collective-permute-done.26.grad_from, bf16[512,2560]{1,0:T(8,128)(2,1)S(1)} %get-tuple-element.66.hidden, ...), custom_call_target="tpu_custom_call" | custom-call | flops 1000000000 | bytes 1000000 | tf_op jit(solution)/shard_map/pallas_call | solution.py:69
  84.8 0.1 collective-permute-start.30
  84.9 4.1 %collective-permute-start.28 = (bf16[144,2560]{1,0:T(8,128)(2,1)S(1)}, bf16[144,2560]{1,0:T(8,128)(2,1)S(1)}, u32[]{:S(2)}, u32[]{:S(2)}) collective-permute-start(bf16[144,2560]{1,0:T(8,128)(2,1)S(1)} %get-tuple-element.72), channel_id=1, source_target_pairs={{0,48},{1,49},{2,50},{3,51},{4,52},{5,53},{6,54},{7,55},{8,56},{9,... | collective-permute-start | bytes 2211848 | tf_op jit(solution)/shard_map/ppermute | solution.py:40
  89.0 0.0 collective-permute-start.29
  89.0 4.2 %shard_map.74 = (f32[64,2560]{1,0:T(8,128)S(1)}, f32[64,2560]{1,0:T(8,128)S(1)}, f32[64,2560]{1,0:T(8,128)S(1)}, bf16[64,2560]{1,0:T(8,128)(2,1)S(1)}, bf16[128,...) custom-call(s32[1,512]{1,0:T(1,128)S(1)} %shard_map.68.ids, f32[8,512]{1,0:T(8,128)S(1)} %add.15.total, ...), custom_call_target="tpu_custom_call" | custom-call | flops 20000000000 | bytes 20000000 | tf_op jit(solution)/shard_map/pallas_call | solution.py:69
  93.2 1.0 collective-permute-start.33
  94.2 1.1 collective-permute-start.34
  95.3 1.3 %shard_map.75 = (f32[72,2560]{1,0:T(8,128)S(1)}, f32[72,2560]{1,0:T(8,128)S(1)}, f32[72,2560]{1,0:T(8,128)S(1)}) custom-call(bf16[576,512]{1,0:T(8,128)(2,1)S(1)} %get-tuple-element.70.grad_mine, bf16[576,512]{1,0:T(8,128)(2,1)S(1)} %collective-permute-done.26.grad_from, bf16[512,2560]{1,0:T(8,128)(2,1)S(1)} %get-tuple-element.66.hidden, ...), custom_call_target="tpu_custom_call" | custom-call | flops 1000000000 | bytes 1000000 | tf_op jit(solution)/shard_map/pallas_call | solution.py:69
  96.6 1.3 %collective-permute-start.35 = (bf16[64,2560]{1,0:T(8,128)(2,1)S(1)}, bf16[64,2560]{1,0:T(8,128)(2,1)S(1)}, u32[]{:S(2)}, u32[]{:S(2)}) collective-permute-start(bf16[64,2560]{1,0:T(8,128)(2,1)S(1)} %get-tuple-element.85), channel_id=1, source_target_pairs={{0,65},{1,64},{2,67},{3,66},{4,69},{5,68},{6,71},{7,70},{8,73},{9,... | collective-permute-start | bytes 983048 | tf_op jit(solution)/shard_map/ppermute | solution.py:40
  97.9 7.2 %collective-permute-done.28.lefts = bf16[144,2560]{1,0:T(8,128)(2,1)S(1)} collective-permute-done((bf16[144,2560]{1,0:T(8,128)(2,1)S(1)}, bf16[144,2560]{1,0:T(8,128)(2,1)S(1)}, u32[]{:S(2)}, u32[]{:S(2)}) %collective-permute-start.28) | collective-permute-done | bytes 737312 | tf_op jit(solution)/shard_map/ppermute | solution.py:40
  105.0 3.4 %collective-permute-done.29.rights = bf16[144,2560]{1,0:T(8,128)(2,1)S(1)} collective-permute-done((bf16[144,2560]{1,0:T(8,128)(2,1)S(1)}, bf16[144,2560]{1,0:T(8,128)(2,1)S(1)}, u32[]{:S(2)}, u32[]{:S(2)}) %collective-permute-start.29) | collective-permute-done | bytes 737312 | tf_op jit(solution)/shard_map/ppermute | solution.py:40
  108.4 0.2 shard_map.76
  108.6 1.7 %collective-permute-start.32 = (bf16[72,2560]{1,0:T(8,128)(2,1)S(1)}, bf16[72,2560]{1,0:T(8,128)(2,1)S(1)}, u32[]{:S(2)}, u32[]{:S(2)}) collective-permute-start(bf16[72,2560]{1,0:T(8,128)(2,1)S(1)} %get-tuple-element.77), channel_id=1, source_target_pairs={{0,64},{1,65},{2,66},{3,67},{4,68},{5,69},{6,70},{7,71},{8,72},{9,... | collective-permute-start | bytes 1105928 | tf_op jit(solution)/shard_map/ppermute | solution.py:40
  110.4 1.2 collective-permute-done.34.rights
  111.6 0.2 shard_map.78
  111.8 0.4 collective-permute-start.36
  112.2 1.2 collective-permute-start.37
  113.4 7.4 %collective-permute-done.31.far = bf16[72,2560]{1,0:T(8,128)(2,1)S(1)} collective-permute-done((bf16[72,2560]{1,0:T(8,128)(2,1)S(1)}, bf16[72,2560]{1,0:T(8,128)(2,1)S(1)}, u32[]{:S(2)}, u32[]{:S(2)}) %collective-permute-start.31) | collective-permute-done | bytes 368672 | tf_op jit(solution)/shard_map/ppermute | solution.py:40
  120.8 0.9 shard_map.77
  121.7 0.9 shard_map.79
  (43 shorter events, 0.1 us)
Async XLA Ops:
  0.6 14.1 %collective-permute-start.2 = (bf16[64,2560]{1,0:T(8,128)(2,1)}, bf16[64,2560]{1,0:T(8,128)(2,1)S(1)}, u32[]{:S(2)}, u32[]{:S(2)}) collective-permute-start(bf16[64,2560]{1,0:T(8,128)(2,1)} %refs_0_.1), channel_id=1, source_target_pairs={{0,6},{1,7},{2,0},{3,1},{4,2},{5,3},{6,4},{7,5},{8,14},{9,15},{10,... | collective-permute-start | bytes 983048 | tf_op jit(solution)/shard_map/ppermute | solution.py:40
  3.5 17.7 %collective-permute-start.1 = (bf16[64,2560]{1,0:T(8,128)(2,1)}, bf16[64,2560]{1,0:T(8,128)(2,1)S(1)}, u32[]{:S(2)}, u32[]{:S(2)}) collective-permute-start(bf16[64,2560]{1,0:T(8,128)(2,1)} %refs_0_.1), channel_id=1, source_target_pairs={{0,2},{1,3},{2,4},{3,5},{4,6},{5,7},{6,0},{7,1},{8,10},{9,11},{10,... | collective-permute-start | bytes 983048 | tf_op jit(solution)/shard_map/ppermute | solution.py:40
  3.5 14.9 %collective-permute-start.4 = (bf16[64,2560]{1,0:T(8,128)(2,1)}, bf16[64,2560]{1,0:T(8,128)(2,1)S(1)}, u32[]{:S(2)}, u32[]{:S(2)}) collective-permute-start(bf16[64,2560]{1,0:T(8,128)(2,1)} %refs_0_.1), channel_id=1, source_target_pairs={{0,65},{1,64},{2,67},{3,66},{4,69},{5,68},{6,71},{7,70},{8,73},{9,... | collective-permute-start | bytes 983048 | tf_op jit(solution)/shard_map/ppermute | solution.py:40
  6.6 7.7 %collective-permute-start = (s32[512]{0:T(512)}, s32[512]{0:T(512)S(1)}, u32[]{:S(2)}, u32[]{:S(2)}) collective-permute-start(s32[512]{0:T(512)} %own.1), channel_id=1, source_target_pairs={{0,65},{1,64},{2,67},{3,66},{4,69},{5,68},{6,71},{7,70},{8,73},{9,... | collective-permute-start | bytes 6152 | tf_op jit(solution)/shard_map/ppermute | solution.py:40
  7.9 49.2 %slice-start.3 = ((s8[5898240]{0:T(1024)(128)(4,1)}), s8[4194304]{0:T(1024)(128)(4,1)S(1)}, s32[]{:S(2)}) async-start(s8[5898240]{0:T(1024)(128)(4,1)} %bitcast.2), calls=%async_computation.3 | async-start | bytes 8388608
  7.9 49.2 %slice-start.4 = ((s8[5898240]{0:T(1024)(128)(4,1)}), s8[1703936]{0:T(1024)(128)(4,1)S(1)}, s32[]{:S(2)}) async-start(s8[5898240]{0:T(1024)(128)(4,1)} %bitcast.2), calls=%async_computation.4 | async-start | bytes 3407872
  7.9 49.2 %copy-start = (bf16[64,2560]{1,0:T(8,128)(2,1)S(1)}, bf16[64,2560]{1,0:T(8,128)(2,1)}, u32[]{:S(2)}) copy-start(bf16[64,2560]{1,0:T(8,128)(2,1)} %refs_0_.1) | copy-start | bytes 983044
  7.9 21.1 %collective-permute-start.11 = (bf16[64,2560]{1,0:T(8,128)(2,1)S(1)}, bf16[64,2560]{1,0:T(8,128)(2,1)S(1)}, u32[]{:S(2)}, u32[]{:S(2)}) collective-permute-start(bf16[64,2560]{1,0:T(8,128)(2,1)S(1)} %get-tuple-element.46.refs_0_), channel_id=1, source_target_pairs={{0,6},{1,7},{2,0},{3,1},{4,2},{5,3},{6,4},{7,5},{8,14},{9,15},{10,... | collective-permute-start | bytes 983048 | tf_op jit(solution)/shard_map/ppermute | solution.py:40
  14.3 10.6 %collective-permute-start.10 = (bf16[64,2560]{1,0:T(8,128)(2,1)S(1)}, bf16[64,2560]{1,0:T(8,128)(2,1)S(1)}, u32[]{:S(2)}, u32[]{:S(2)}) collective-permute-start(bf16[64,2560]{1,0:T(8,128)(2,1)S(1)} %get-tuple-element.46.refs_0_), channel_id=1, source_target_pairs={{0,2},{1,3},{2,4},{3,5},{4,6},{5,7},{6,0},{7,1},{8,10},{9,11},{10,... | collective-permute-start | bytes 983048 | tf_op jit(solution)/shard_map/ppermute | solution.py:40
  14.8 14.3 %collective-permute-start.5 = (bf16[64,2560]{1,0:T(8,128)(2,1)S(1)}, bf16[64,2560]{1,0:T(8,128)(2,1)S(1)}, u32[]{:S(2)}, u32[]{:S(2)}) collective-permute-start(bf16[64,2560]{1,0:T(8,128)(2,1)S(1)} %get-tuple-element.46.refs_0_), channel_id=1, source_target_pairs={{0,65},{1,64},{2,67},{3,66},{4,69},{5,68},{6,71},{7,70},{8,73},{9,... | collective-permute-start | bytes 983048 | tf_op jit(solution)/shard_map/ppermute | solution.py:40
  17.7 0.7 copy-start.1
  18.4 42.3 %slice-start = ((s8[11796480]{0:T(1024)(128)(4,1)}), s8[4194304]{0:T(1024)(128)(4,1)S(1)}, s32[]{:S(2)}) async-start(s8[11796480]{0:T(1024)(128)(4,1)} %bitcast), calls=%async_computation | async-start | bytes 8388608
  18.4 42.3 %slice-start.1 = ((s8[11796480]{0:T(1024)(128)(4,1)}), s8[4194304]{0:T(1024)(128)(4,1)S(1)}, s32[]{:S(2)}) async-start(s8[11796480]{0:T(1024)(128)(4,1)} %bitcast), calls=%async_computation.1 | async-start | bytes 8388608
  18.4 42.3 %slice-start.2 = ((s8[11796480]{0:T(1024)(128)(4,1)}), s8[3407872]{0:T(1024)(128)(4,1)S(1)}, s32[]{:S(2)}) async-start(s8[11796480]{0:T(1024)(128)(4,1)} %bitcast), calls=%async_computation.2 | async-start | bytes 6815744
  18.4 13.9 %collective-permute-start.7 = (bf16[64,2560]{1,0:T(8,128)(2,1)S(1)}, bf16[64,2560]{1,0:T(8,128)(2,1)S(1)}, u32[]{:S(2)}, u32[]{:S(2)}) collective-permute-start(bf16[64,2560]{1,0:T(8,128)(2,1)S(1)} %collective-permute-done.4.refs_4_), channel_id=1, source_target_pairs={{0,6},{1,7},{2,0},{3,1},{4,2},{5,3},{6,4},{7,5},{8,14},{9,15},{10,... | collective-permute-start | bytes 983048 | tf_op jit(solution)/shard_map/ppermute | solution.py:40
  21.2 11.9 %collective-permute-start.3 = (bf16[64,2560]{1,0:T(8,128)(2,1)S(1)}, bf16[64,2560]{1,0:T(8,128)(2,1)S(1)}, u32[]{:S(2)}, u32[]{:S(2)}) collective-permute-start(bf16[64,2560]{1,0:T(8,128)(2,1)S(1)} %collective-permute-done.1.refs_1_), channel_id=1, source_target_pairs={{0,2},{1,3},{2,4},{3,5},{4,6},{5,7},{6,0},{7,1},{8,10},{9,11},{10,... | collective-permute-start | bytes 983048 | tf_op jit(solution)/shard_map/ppermute | solution.py:40
  24.9 12.7 %collective-permute-start.8 = (bf16[64,2560]{1,0:T(8,128)(2,1)S(1)}, bf16[64,2560]{1,0:T(8,128)(2,1)S(1)}, u32[]{:S(2)}, u32[]{:S(2)}) collective-permute-start(bf16[64,2560]{1,0:T(8,128)(2,1)S(1)} %get-tuple-element.58.refs_0_), channel_id=1, source_target_pairs={{0,65},{1,64},{2,67},{3,66},{4,69},{5,68},{6,71},{7,70},{8,73},{9,... | collective-permute-start | bytes 983048 | tf_op jit(solution)/shard_map/ppermute | solution.py:40
  29.1 11.9 %collective-permute-start.16 = (bf16[64,2560]{1,0:T(8,128)(2,1)S(1)}, bf16[64,2560]{1,0:T(8,128)(2,1)S(1)}, u32[]{:S(2)}, u32[]{:S(2)}) collective-permute-start(bf16[64,2560]{1,0:T(8,128)(2,1)S(1)} %get-tuple-element.58.refs_0_), channel_id=1, source_target_pairs={{0,2},{1,3},{2,4},{3,5},{4,6},{5,7},{6,0},{7,1},{8,10},{9,11},{10,... | collective-permute-start | bytes 983048 | tf_op jit(solution)/shard_map/ppermute | solution.py:40
  29.1 14.0 %collective-permute-start.12 = (bf16[64,2560]{1,0:T(8,128)(2,1)S(1)}, bf16[64,2560]{1,0:T(8,128)(2,1)S(1)}, u32[]{:S(2)}, u32[]{:S(2)}) collective-permute-start(bf16[64,2560]{1,0:T(8,128)(2,1)S(1)} %collective-permute-done.11.refs_2_), channel_id=1, source_target_pairs={{0,6},{1,7},{2,0},{3,1},{4,2},{5,3},{6,4},{7,5},{8,14},{9,15},{10,... | collective-permute-start | bytes 983048 | tf_op jit(solution)/shard_map/ppermute | solution.py:40
  32.3 10.8 %collective-permute-start.6 = (bf16[64,2560]{1,0:T(8,128)(2,1)S(1)}, bf16[64,2560]{1,0:T(8,128)(2,1)S(1)}, u32[]{:S(2)}, u32[]{:S(2)}) collective-permute-start(bf16[64,2560]{1,0:T(8,128)(2,1)S(1)} %collective-permute-done.1.refs_1_), channel_id=1, source_target_pairs={{0,65},{1,64},{2,67},{3,66},{4,69},{5,68},{6,71},{7,70},{8,73},{9,... | collective-permute-start | bytes 983048 | tf_op jit(solution)/shard_map/ppermute | solution.py:40
  33.1 14.8 %collective-permute-start.13 = (bf16[64,2560]{1,0:T(8,128)(2,1)S(1)}, bf16[64,2560]{1,0:T(8,128)(2,1)S(1)}, u32[]{:S(2)}, u32[]{:S(2)}) collective-permute-start(bf16[64,2560]{1,0:T(8,128)(2,1)S(1)} %collective-permute-done.5.refs_4_), channel_id=1, source_target_pairs={{0,2},{1,3},{2,4},{3,5},{4,6},{5,7},{6,0},{7,1},{8,10},{9,11},{10,... | collective-permute-start | bytes 983048 | tf_op jit(solution)/shard_map/ppermute | solution.py:40
  37.6 12.5 %collective-permute-start.17 = (bf16[64,2560]{1,0:T(8,128)(2,1)S(1)}, bf16[64,2560]{1,0:T(8,128)(2,1)S(1)}, u32[]{:S(2)}, u32[]{:S(2)}) collective-permute-start(bf16[64,2560]{1,0:T(8,128)(2,1)S(1)} %get-tuple-element.58.refs_0_), channel_id=1, source_target_pairs={{0,6},{1,7},{2,0},{3,1},{4,2},{5,3},{6,4},{7,5},{8,14},{9,15},{10,... | collective-permute-start | bytes 983048 | tf_op jit(solution)/shard_map/ppermute | solution.py:40
  40.9 11.2 %collective-permute-start.9 = (bf16[64,2560]{1,0:T(8,128)(2,1)S(1)}, bf16[64,2560]{1,0:T(8,128)(2,1)S(1)}, u32[]{:S(2)}, u32[]{:S(2)}) collective-permute-start(bf16[64,2560]{1,0:T(8,128)(2,1)S(1)} %collective-permute-done.3.refs_3_), channel_id=1, source_target_pairs={{0,65},{1,64},{2,67},{3,66},{4,69},{5,68},{6,71},{7,70},{8,73},{9,... | collective-permute-start | bytes 983048 | tf_op jit(solution)/shard_map/ppermute | solution.py:40
  43.1 11.9 %collective-permute-start.18 = (bf16[64,2560]{1,0:T(8,128)(2,1)S(1)}, bf16[64,2560]{1,0:T(8,128)(2,1)S(1)}, u32[]{:S(2)}, u32[]{:S(2)}) collective-permute-start(bf16[64,2560]{1,0:T(8,128)(2,1)S(1)} %collective-permute-done.16.refs_1_), channel_id=1, source_target_pairs={{0,2},{1,3},{2,4},{3,5},{4,6},{5,7},{6,0},{7,1},{8,10},{9,11},{10,... | collective-permute-start | bytes 983048 | tf_op jit(solution)/shard_map/ppermute | solution.py:40
  43.1 17.6 %collective-permute-start.14 = (bf16[64,2560]{1,0:T(8,128)(2,1)S(1)}, bf16[64,2560]{1,0:T(8,128)(2,1)S(1)}, u32[]{:S(2)}, u32[]{:S(2)}) collective-permute-start(bf16[64,2560]{1,0:T(8,128)(2,1)S(1)} %collective-permute-done.5.refs_4_), channel_id=1, source_target_pairs={{0,6},{1,7},{2,0},{3,1},{4,2},{5,3},{6,4},{7,5},{8,14},{9,15},{10,... | collective-permute-start | bytes 983048 | tf_op jit(solution)/shard_map/ppermute | solution.py:40
  47.9 12.8 %collective-permute-start.15 = (bf16[64,2560]{1,0:T(8,128)(2,1)S(1)}, bf16[64,2560]{1,0:T(8,128)(2,1)S(1)}, u32[]{:S(2)}, u32[]{:S(2)}) collective-permute-start(bf16[64,2560]{1,0:T(8,128)(2,1)S(1)} %collective-permute-done.12.refs_3_), channel_id=1, source_target_pairs={{0,65},{1,64},{2,67},{3,66},{4,69},{5,68},{6,71},{7,70},{8,73},{9,... | collective-permute-start | bytes 983048 | tf_op jit(solution)/shard_map/ppermute | solution.py:40
  50.1 14.1 %collective-permute-start.19 = (bf16[64,2560]{1,0:T(8,128)(2,1)S(1)}, bf16[64,2560]{1,0:T(8,128)(2,1)S(1)}, u32[]{:S(2)}, u32[]{:S(2)}) collective-permute-start(bf16[64,2560]{1,0:T(8,128)(2,1)S(1)} %collective-permute-done.8.refs_4_), channel_id=1, source_target_pairs={{0,2},{1,3},{2,4},{3,5},{4,6},{5,7},{6,0},{7,1},{8,10},{9,11},{10,... | collective-permute-start | bytes 983048 | tf_op jit(solution)/shard_map/ppermute | solution.py:40
  52.1 12.1 %collective-permute-start.20 = (bf16[64,2560]{1,0:T(8,128)(2,1)S(1)}, bf16[64,2560]{1,0:T(8,128)(2,1)S(1)}, u32[]{:S(2)}, u32[]{:S(2)}) collective-permute-start(bf16[64,2560]{1,0:T(8,128)(2,1)S(1)} %collective-permute-done.8.refs_4_), channel_id=1, source_target_pairs={{0,6},{1,7},{2,0},{3,1},{4,2},{5,3},{6,4},{7,5},{8,14},{9,15},{10,... | collective-permute-start | bytes 983048 | tf_op jit(solution)/shard_map/ppermute | solution.py:40
  55.0 9.3 %collective-permute-start.21 = (bf16[64,2560]{1,0:T(8,128)(2,1)S(1)}, bf16[64,2560]{1,0:T(8,128)(2,1)S(1)}, u32[]{:S(2)}, u32[]{:S(2)}) collective-permute-start(bf16[64,2560]{1,0:T(8,128)(2,1)S(1)} %collective-permute-done.18.refs_3_), channel_id=1, source_target_pairs={{0,65},{1,64},{2,67},{3,66},{4,69},{5,68},{6,71},{7,70},{8,73},{9,... | collective-permute-start | bytes 983048 | tf_op jit(solution)/shard_map/ppermute | solution.py:40
  68.0 5.3 %collective-permute-start.24 = (f32[8,512]{1,0:T(8,128)S(1)}, f32[8,512]{1,0:T(8,128)S(1)}, u32[]{:S(2)}, u32[]{:S(2)}) collective-permute-start(f32[8,512]{1,0:T(8,128)S(1)} %shard_map.71), channel_id=1, source_target_pairs={{0,4},{1,5},{2,6},{3,7},{4,0},{5,1},{6,2},{7,3},{8,12},{9,13},{10,... | collective-permute-start | bytes 49160 | tf_op jit(solution)/shard_map/ppermute | solution.py:40
  68.9 4.4 %collective-permute-start.23 = (f32[8,512]{1,0:T(8,128)S(1)}, f32[8,512]{1,0:T(8,128)S(1)}, u32[]{:S(2)}, u32[]{:S(2)}) collective-permute-start(f32[8,512]{1,0:T(8,128)S(1)} %shard_map.71), channel_id=1, source_target_pairs={{0,6},{1,7},{2,0},{3,1},{4,2},{5,3},{6,4},{7,5},{8,14},{9,15},{10,... | collective-permute-start | bytes 49160 | tf_op jit(solution)/shard_map/ppermute | solution.py:40
  70.1 4.9 %collective-permute-start.22 = (f32[8,512]{1,0:T(8,128)S(1)}, f32[8,512]{1,0:T(8,128)S(1)}, u32[]{:S(2)}, u32[]{:S(2)}) collective-permute-start(f32[8,512]{1,0:T(8,128)S(1)} %shard_map.71), channel_id=1, source_target_pairs={{0,2},{1,3},{2,4},{3,5},{4,6},{5,7},{6,0},{7,1},{8,10},{9,11},{10,... | collective-permute-start | bytes 49160 | tf_op jit(solution)/shard_map/ppermute | solution.py:40
  70.9 11.7 %collective-permute-start.27 = (bf16[512,2560]{1,0:T(8,128)(2,1)S(1)}, bf16[512,2560]{1,0:T(8,128)(2,1)S(1)}, u32[]{:S(2)}, u32[]{:S(2)}) collective-permute-start(bf16[512,2560]{1,0:T(8,128)(2,1)S(1)} %get-tuple-element.66.hidden), channel_id=1, source_target_pairs={{0,8},{1,9},{2,10},{3,11},{4,12},{5,13},{6,14},{7,15},{8,0},{9,1},... | collective-permute-start | bytes 7864328 | tf_op jit(solution)/shard_map/ppermute | solution.py:40
  75.0 4.9 %collective-permute-start.25 = (f32[8,512]{1,0:T(8,128)S(1)}, f32[8,512]{1,0:T(8,128)S(1)}, u32[]{:S(2)}, u32[]{:S(2)}) collective-permute-start(f32[8,512]{1,0:T(8,128)S(1)} %add_add_fusion), channel_id=1, source_target_pairs={{0,65},{1,64},{2,67},{3,66},{4,69},{5,68},{6,71},{7,70},{8,73},{9,... | collective-permute-start | bytes 49160 | tf_op jit(solution)/shard_map/ppermute | solution.py:40
  80.6 2.1 %collective-permute-start.26 = (bf16[576,512]{1,0:T(8,128)(2,1)S(1)}, bf16[576,512]{1,0:T(8,128)(2,1)S(1)}, u32[]{:S(2)}, u32[]{:S(2)}) collective-permute-start(bf16[576,512]{1,0:T(8,128)(2,1)S(1)} %get-tuple-element.65), channel_id=1, source_target_pairs={{0,8},{1,9},{2,10},{3,11},{4,12},{5,13},{6,14},{7,15},{8,0},{9,1},... | collective-permute-start | bytes 1769480 | tf_op jit(solution)/shard_map/ppermute | solution.py:40
  84.8 11.8 %collective-permute-start.30 = (bf16[72,2560]{1,0:T(8,128)(2,1)S(1)}, bf16[72,2560]{1,0:T(8,128)(2,1)S(1)}, u32[]{:S(2)}, u32[]{:S(2)}) collective-permute-start(bf16[72,2560]{1,0:T(8,128)(2,1)S(1)} %get-tuple-element.67), channel_id=1, source_target_pairs={{0,64},{1,65},{2,66},{3,67},{4,68},{5,69},{6,70},{7,71},{8,72},{9,... | collective-permute-start | bytes 1105928 | tf_op jit(solution)/shard_map/ppermute | solution.py:40
  84.9 20.2 %collective-permute-start.28 = (bf16[144,2560]{1,0:T(8,128)(2,1)S(1)}, bf16[144,2560]{1,0:T(8,128)(2,1)S(1)}, u32[]{:S(2)}, u32[]{:S(2)}) collective-permute-start(bf16[144,2560]{1,0:T(8,128)(2,1)S(1)} %get-tuple-element.72), channel_id=1, source_target_pairs={{0,48},{1,49},{2,50},{3,51},{4,52},{5,53},{6,54},{7,55},{8,56},{9,... | collective-permute-start | bytes 2211848 | tf_op jit(solution)/shard_map/ppermute | solution.py:40
  89.0 19.5 %collective-permute-start.29 = (bf16[144,2560]{1,0:T(8,128)(2,1)S(1)}, bf16[144,2560]{1,0:T(8,128)(2,1)S(1)}, u32[]{:S(2)}, u32[]{:S(2)}) collective-permute-start(bf16[144,2560]{1,0:T(8,128)(2,1)S(1)} %get-tuple-element.73), channel_id=1, source_target_pairs={{0,16},{1,17},{2,18},{3,19},{4,20},{5,21},{6,22},{7,23},{8,24},{9,... | collective-permute-start | bytes 2211848 | tf_op jit(solution)/shard_map/ppermute | solution.py:40
  93.2 17.2 %collective-permute-start.33 = (bf16[128,2560]{1,0:T(8,128)(2,1)S(1)}, bf16[128,2560]{1,0:T(8,128)(2,1)S(1)}, u32[]{:S(2)}, u32[]{:S(2)}) collective-permute-start(bf16[128,2560]{1,0:T(8,128)(2,1)S(1)} %get-tuple-element.79), channel_id=1, source_target_pairs={{0,6},{1,7},{2,0},{3,1},{4,2},{5,3},{6,4},{7,5},{8,14},{9,15},{10,... | collective-permute-start | bytes 1966088 | tf_op jit(solution)/shard_map/ppermute | solution.py:40
  94.2 17.4 %collective-permute-start.34 = (bf16[128,2560]{1,0:T(8,128)(2,1)S(1)}, bf16[128,2560]{1,0:T(8,128)(2,1)S(1)}, u32[]{:S(2)}, u32[]{:S(2)}) collective-permute-start(bf16[128,2560]{1,0:T(8,128)(2,1)S(1)} %get-tuple-element.80), channel_id=1, source_target_pairs={{0,2},{1,3},{2,4},{3,5},{4,6},{5,7},{6,0},{7,1},{8,10},{9,11},{10,... | collective-permute-start | bytes 1966088 | tf_op jit(solution)/shard_map/ppermute | solution.py:40
  96.6 15.0 %collective-permute-start.35 = (bf16[64,2560]{1,0:T(8,128)(2,1)S(1)}, bf16[64,2560]{1,0:T(8,128)(2,1)S(1)}, u32[]{:S(2)}, u32[]{:S(2)}) collective-permute-start(bf16[64,2560]{1,0:T(8,128)(2,1)S(1)} %get-tuple-element.85), channel_id=1, source_target_pairs={{0,65},{1,64},{2,67},{3,66},{4,69},{5,68},{6,71},{7,70},{8,73},{9,... | collective-permute-start | bytes 983048 | tf_op jit(solution)/shard_map/ppermute | solution.py:40
  108.6 12.1 %collective-permute-start.32 = (bf16[72,2560]{1,0:T(8,128)(2,1)S(1)}, bf16[72,2560]{1,0:T(8,128)(2,1)S(1)}, u32[]{:S(2)}, u32[]{:S(2)}) collective-permute-start(bf16[72,2560]{1,0:T(8,128)(2,1)S(1)} %get-tuple-element.77), channel_id=1, source_target_pairs={{0,64},{1,65},{2,66},{3,67},{4,68},{5,69},{6,70},{7,71},{8,72},{9,... | collective-permute-start | bytes 1105928 | tf_op jit(solution)/shard_map/ppermute | solution.py:40
  110.4 10.4 %collective-permute-start.31 = (bf16[72,2560]{1,0:T(8,128)(2,1)S(1)}, bf16[72,2560]{1,0:T(8,128)(2,1)S(1)}, u32[]{:S(2)}, u32[]{:S(2)}) collective-permute-start(bf16[72,2560]{1,0:T(8,128)(2,1)S(1)} %get-tuple-element.76), channel_id=1, source_target_pairs={{0,32},{1,33},{2,34},{3,35},{4,36},{5,37},{6,38},{7,39},{8,40},{9,... | collective-permute-start | bytes 1105928 | tf_op jit(solution)/shard_map/ppermute | solution.py:40
  111.8 10.0 %collective-permute-start.36 = (bf16[64,2560]{1,0:T(8,128)(2,1)S(1)}, bf16[64,2560]{1,0:T(8,128)(2,1)S(1)}, u32[]{:S(2)}, u32[]{:S(2)}) collective-permute-start(bf16[64,2560]{1,0:T(8,128)(2,1)S(1)} %get-tuple-element.86), channel_id=1, source_target_pairs={{0,4},{1,5},{2,6},{3,7},{4,0},{5,1},{6,2},{7,3},{8,12},{9,13},{10,... | collective-permute-start | bytes 983048 | tf_op jit(solution)/shard_map/ppermute | solution.py:40
  112.2 9.6 %collective-permute-start.37 = (bf16[64,2560]{1,0:T(8,128)(2,1)S(1)}, bf16[64,2560]{1,0:T(8,128)(2,1)S(1)}, u32[]{:S(2)}, u32[]{:S(2)}) collective-permute-start(bf16[64,2560]{1,0:T(8,128)(2,1)S(1)} %get-tuple-element.87), channel_id=1, source_target_pairs={{0,65},{1,64},{2,67},{3,66},{4,69},{5,68},{6,71},{7,70},{8,73},{9,... | collective-permute-start | bytes 983048 | tf_op jit(solution)/shard_map/ppermute | solution.py:40

commit v5 on v4

--- a/solution.py
+++ b/solution.py
@@ -11,7 +11,7 @@
 F32 = jnp.float32
 AXES = ("dp", "vocab")
 
-REL = ((0, 0), (-1, 0), (1, 0), (2, 0), (0, 1), (-1, 1), (1, 1), (2, 1))
+REL = ((0, 0), (0, 1), (-1, 0), (1, 0), (-1, 1), (1, 1), (2, 0), (2, 1))
 
 
 def pairs(move):
@@ -83,18 +83,24 @@
         self.y_lo, self.z, self.core = lax.div(dp, 8), lax.rem(lax.div(dp, 2), 4), lax.rem(dp, 2)
         self.vocab, self.x, self.y_hi = v, lax.div(v, 2), lax.rem(v, 2)
 
-    def block(self, r):
+    def owner(self, r):
         dx, dy = REL[r]
-        owner = lax.rem(self.x + (dx + 4), 4) * 2 + lax.rem(self.y_hi + dy, 2)
-        return pl.multiple_of(owner * 64, 64)
+        return lax.rem(self.x + (dx + 4), 4) * 2 + lax.rem(self.y_hi + dy, 2)
 
     def chip(self, dz, dy):
         return lax.rem(self.y_lo + dy, 2) * 4 + lax.rem(self.z + (dz + 4), 4)
 
 
+def block(r):
+    return slice(r * 64, (r + 1) * 64)
+
+
 def ids_kernel(own, near, ids):
+    place = Place()
     half = lax.rem(lax.div(lax.broadcasted_iota(jnp.int32, (1, 512), 1), 64), 2)
-    ids[...] = jnp.where(half == Place().y_hi, own[...].reshape(1, 512), near[...].reshape(1, 512))
+    held = jnp.where(half == place.y_hi, own[...].reshape(1, 512), near[...].reshape(1, 512))
+    for r in range(8):
+        ids[:, block(r)] = sum(jnp.where(place.owner(r) == a, held[:, block(a)], 0) for a in range(8))
 
 
 def fold(a):
@@ -108,14 +114,22 @@
 STATS = (8, 512)
 
 
-def put_blocks(place, blocks, hidden):
-    for r, block in enumerate(blocks):
-        hidden[pl.ds(place.block(r), 64), :] = block[...]
-
-
-def put_stats(stats, first, sums, picks):
-    stats[first:first + 1, :] = jnp.sum(sums, axis=0, keepdims=True)
-    stats[first + 1:first + 2, :] = jnp.sum(picks, axis=0, keepdims=True)
+EARLY, LATE = slice(0, 256), slice(256, 512)
+
+
+def put_blocks(blocks, hidden):
+    for r, rows in enumerate(blocks):
+        hidden[block(r), :] = rows[...]
+
+
+def sums_of(out, ids, first):
+    rows = lax.broadcasted_iota(jnp.int32, out.shape, 0) + first
+    return fold(jnp.exp(out)), fold(jnp.where(rows == ids, out, 0.0))
+
+
+def put_stats(stats, first, tokens, sums, picks):
+    stats[first:first + 1, tokens] = jnp.sum(sums, axis=0, keepdims=True)
+    stats[first + 1:first + 2, tokens] = jnp.sum(picks, axis=0, keepdims=True)
 
 
 def advantage(total):
@@ -123,20 +137,22 @@
     return (total[3:4, :] - jnp.log(total[2:3, :])) - (total[1:2, :] - norm), norm
 
 
+def tiles(head):
+    return [slice(j, j + TILE) for j in range(0, head.shape[0], TILE)]
+
+
 def student_kernel(ids, head, *refs):
     blocks, (logits, hidden, stats) = refs[:8], refs[8:]
-    place = Place()
-    put_blocks(place, blocks, hidden)
+    put_blocks(blocks, hidden)
+    first = Place().vocab * head.shape[0]
     sums = picks = 0.0
-    for j in range(head.shape[0] // TILE):
-        tile = slice(j * TILE, (j + 1) * TILE)
+    for tile in tiles(head):
         out = lax.dot_general(head[tile, :], hidden[...], NT, preferred_element_type=F32)
         logits[tile, :] = out
-        rows = lax.broadcasted_iota(jnp.int32, out.shape, 0) + (place.vocab * head.shape[0] + j * TILE)
-        sums += fold(jnp.exp(out))
-        picks += fold(jnp.where(rows == ids[...], out, 0.0))
+        some, pick = sums_of(out, ids[...], first + tile.start)
+        sums, picks = sums + some, picks + pick
     stats[...] = jnp.zeros_like(stats)
-    put_stats(stats, 0, sums, picks)
+    put_stats(stats, 0, slice(0, 512), sums, picks)
 
 
 def student_logits(ids, blocks, head):
@@ -145,65 +161,93 @@
     return kernel_call(student_kernel, (ids, head, *blocks), outs, [], 6, LONG)
 
 
-def teacher_first_kernel(head, *refs):
-    blocks, (logits, hidden) = refs[:8], refs[8:]
-    put_blocks(Place(), blocks, hidden)
-    for j in range(head.shape[0] // TILE):
-        tile = slice(j * TILE, (j + 1) * TILE)
+def teacher_early_kernel(head, *refs):
+    blocks, (logits, hidden) = refs[:4], refs[4:]
+    put_blocks(blocks, hidden)
+    for tile in tiles(head):
         logits[tile, :] = lax.dot_general(
-            head[tile, 0:hidden.shape[1]], hidden[...], NT, preferred_element_type=F32
+            head[tile, hidden.shape[1]:], hidden[...], NT, preferred_element_type=F32
         )
 
 
-def teacher_first(blocks, head):
+def teacher_early(blocks, head):
     v, d = head.shape
-    return kernel_call(teacher_first_kernel, (head, *blocks), [((v, 512), F32)], [((512, d // 2), BF16)], 8, LONG)[0]
-
-
-def teacher_second_kernel(ids, student_stats, head, logits, *refs):
-    blocks, (stats, hidden) = refs[:8], refs[8:]
-    place = Place()
-    put_blocks(place, blocks, hidden)
+    return kernel_call(teacher_early_kernel, (head, *blocks), [((v, 256), F32)], [((256, d // 2), BF16)], 6, LONG)[0]
+
+
+def teacher_first_kernel(ids, student_stats, early, head, *refs):
+    blocks, (logits, stats, hidden) = refs[:8], refs[8:]
+    put_blocks(blocks, hidden)
+    first = Place().vocab * head.shape[0]
     sums = picks = 0.0
-    for j in range(head.shape[0] // TILE):
-        tile = slice(j * TILE, (j + 1) * TILE)
+    for tile in tiles(head):
+        out = lax.dot_general(head[tile, 0:hidden.shape[1]], hidden[...], NT, preferred_element_type=F32)
+        logits[tile, :] = out[:, LATE]
+        some, pick = sums_of(out[:, EARLY] + early[tile, :], ids[:, EARLY], first + tile.start)
+        sums, picks = sums + some, picks + pick
+    stats[...] = student_stats[...]
+    put_stats(stats, 2, EARLY, sums, picks)
+
+
+def teacher_first(ids, student_stats, early, blocks, head):
+    v, d = head.shape
+    arrays = (ids, student_stats, early, head, *blocks)
+    return kernel_call(teacher_first_kernel, arrays, [((v, 256), F32), (STATS, F32)], [((512, d // 2), BF16)], 8, LONG)
+
+
+def teacher_second_kernel(ids, first_stats, head, logits, *refs):
+    blocks, (stats, hidden) = refs[:4], refs[4:]
+    put_blocks(blocks, hidden)
+    first = Place().vocab * head.shape[0]
+    sums = picks = 0.0
+    for tile in tiles(head):
         out = logits[tile, :] + lax.dot_general(
             head[tile, hidden.shape[1]:], hidden[...], NT, preferred_element_type=F32
         )
-        rows = lax.broadcasted_iota(jnp.int32, out.shape, 0) + (place.vocab * head.shape[0] + j * TILE)
-        sums += fold(jnp.exp(out))
-        picks += fold(jnp.where(rows == ids[...], out, 0.0))
-    stats[...] = student_stats[...]
-    put_stats(stats, 2, sums, picks)
-
-
-def teacher_second(ids, student_stats, blocks, head, logits):
-    scratch = [((512, head.shape[1] // 2), BF16)]
-    return kernel_call(teacher_second_kernel, (ids, student_stats, head, logits, *blocks), [(STATS, F32)], scratch, 8, LONG)[0]
-
-
-def hidden_kernel(ids, total, logits, head, own, near, far, far_near, lefts, rights, grad_t, product):
-    place = Place()
+        some, pick = sums_of(out, ids[:, LATE], first + tile.start)
+        sums, picks = sums + some, picks + pick
+    stats[...] = first_stats[...]
+    put_stats(stats, 2, LATE, sums, picks)
+
+
+def teacher_second(ids, stats, blocks, head, logits):
+    scratch = [((256, head.shape[1] // 2), BF16)]
+    return kernel_call(teacher_second_kernel, (ids, stats, head, logits, *blocks), [(STATS, F32)], scratch, 6, LONG)[0]
+
+
+def hidden_kernel(groups, places, ids, total, logits, head, *refs):
+    outs, grad_t = refs[:-1], refs[-1]
+    first = Place().vocab * head.shape[0]
     adv, norm = advantage(total)
-    for k in range(head.shape[0] // 128):
-        part = slice(k * 128, (k + 1) * 128)
-        rows = lax.broadcasted_iota(jnp.int32, (128, 512), 0) + (place.vocab * head.shape[0] + k * 128)
-        onehot = jnp.where(rows == ids[...], 1.0, 0.0)
-        grad_t[:, part] = (adv * (jnp.exp(logits[part, :] - norm) - onehot)).T.astype(BF16)
-
-    outs = ((own, 0), (lefts, 0), (rights, 0), (far, 0), (near, 0), (lefts, 64), (rights, 64), (far_near, 0))
-    for j in range(head.shape[1] // WIDE):
-        tile = slice(j * WIDE, (j + 1) * WIDE)
-        product[...] = lax.dot_general(grad_t[...], head[:, tile], NN, preferred_element_type=F32)
-        for r, (out, row) in enumerate(outs):
-            out[row:row + 64, tile] = product[pl.ds(place.block(r), 64), :].astype(out.dtype)
-
-
-def hidden_parts(ids, total, logits, head):
+    for i, start in enumerate(groups):
+        tokens = slice(start, start + 128)
+        for k in range(0, head.shape[0], 128):
+            rows = lax.broadcasted_iota(jnp.int32, (128, 128), 0) + (first + k)
+            onehot = jnp.where(rows == ids[:, tokens], 1.0, 0.0)
+            part = adv[:, tokens] * (jnp.exp(logits[k:k + 128, tokens] - norm[:, tokens]) - onehot)
+            grad_t[i * 128:(i + 1) * 128, k:k + 128] = part.T.astype(BF16)
+    for j in range(0, head.shape[1], WIDE):
+        tile = slice(j, j + WIDE)
+        product = lax.dot_general(grad_t[...], head[:, tile], NN, preferred_element_type=F32)
+        for r, (out, row) in enumerate(places):
+            outs[out][row:row + 64, tile] = product[block(r), :].astype(outs[out].dtype)
+
+
+def hidden_parts(ids, total, logits, head, groups, places, outs, said):
     v, d = head.shape
-    outs = [((64, d), F32)] * 3 + [((64, d), BF16)] + [((128, d), BF16)] * 2
-    scratch = [((512, v), BF16), ((512, WIDE), F32)]
-    return kernel_call(hidden_kernel, (ids, total, logits, head), outs, scratch, 6, LONG)
+    outs = [((n, d), t) for n, t in outs]
+    body = functools.partial(hidden_kernel, groups, places)
+    return kernel_call(body, (ids, total, logits, head), outs, [((256, v), BF16)], 6, said)
+
+
+def hidden_outer(*arrays):
+    places = ((0, 0), (1, 0), (0, 64), (1, 64))
+    return hidden_parts(*arrays, (128, 256), places, ((128, BF16),) * 2, LONG)
+
+
+def hidden_inner(*arrays):
+    places = ((0, 0), (1, 0), (2, 0), (3, 0))
+    return hidden_parts(*arrays, (0, 384), places, ((64, F32),) * 3 + ((64, BF16),), SHORT)
 
 
 CHIPS = ((-1, 0), (-1, 1), (1, 0), (1, 1), (2, 1), (2, 0), (0, 1), (0, 0))
@@ -268,9 +312,23 @@
     return kernel_call(finish_kernel, pieces, [(pieces[0].shape, BF16)], [], 4, said)[0]
 
 
+def merge_kernel(shifts, *refs):
+    arrays, out = refs[:-1], refs[-1]
+    for r, (dx, dy) in enumerate(REL):
+        total = 0.0
+        for (sx, sy), a in zip(shifts, arrays):
+            there = [i for i, (ox, oy) in enumerate(REL) if (ox + sx - dx) % 4 == 0 and (oy + sy - dy) % 2 == 0][0]
+            total += a[:, block(there)]
+        out[:, block(r)] = total
+
+
+def merge(shifts, arrays):
+    return kernel_call(functools.partial(merge_kernel, shifts), arrays, [(STATS, F32)], [], 2)[0]
+
+
 def group_sum(a):
-    around = a + send(a, X_UP) + send(a, X_DOWN) + send(a, X_FAR)
-    return around + send(around, Y_HI)
+    around = merge(((0, 0), (-1, 0), (1, 0), (2, 0)), (a, send(a, X_UP), send(a, X_DOWN), send(a, X_FAR)))
+    return merge(((0, 0), (0, 1)), (around, send(around, Y_HI)))
 
 
 def on_device(student_hidden, teacher_hidden, student_head, teacher_head, sampled_ids):
@@ -287,28 +345,30 @@
     l_b, f_a, far_near = up(t_b), down(r_a), over(far)
     ln_a, r_b, fn_a = up(near_a), down(t_b), over(f_a)
     f_b, rn_a = up(l_b), down(near_a)
-    fn_b = over(f_b)
+    blocks = (student_hidden, near, left, right, left_near, right_near, far, far_near)
+    logits, hidden, student_stats = student_logits(ids, blocks, student_head)
+    fn_b = over(after(f_b, student_stats))
     ln_b, rn_b = up(near_b), down(near_b)
 
-    blocks = (student_hidden, left, right, far, near, left_near, right_near, far_near)
-    logits, hidden, student_stats = student_logits(ids, blocks, student_head)
     hidden_from = send(hidden, CORE)
-    teacher_logits = teacher_first((t_a, l_a, r_a, f_a, near_a, ln_a, rn_a, fn_a), teacher_head)
-    blocks = (t_b, l_b, r_b, f_b, near_b, ln_b, rn_b, fn_b)
-    total = group_sum(teacher_second(ids, student_stats, blocks, teacher_head, teacher_logits))
+    early = teacher_early((t_b, near_b, l_b, r_b), teacher_head)
+    blocks = (t_a, near_a, l_a, r_a, ln_a, rn_a, f_a, fn_a)
+    teacher_logits, stats = teacher_first(ids, student_stats, early, blocks, teacher_head)
+    total = group_sum(teacher_second(ids, stats, (ln_b, rn_b, f_b, fn_b), teacher_head, teacher_logits))
 
     mine, other = logit_grads(ids, total, logits)
     grads = (mine, send(other, CORE), hidden, hidden_from)
     h_lefts, h_rights, h_fl = head_parts(0, ((144, BF16), (144, BF16), (72, BF16)), SHORT, *grads)
-    parts = hidden_parts(ids, after(total, h_fl), logits, student_head)
-    grads = (after(mine, parts[0]), *grads[1:])
+    g_lefts, g_rights = hidden_outer(ids, after(total, h_fl), logits, student_head)
+    from_fl = send(h_fl, Y_LO)
+    g_own, g_near, g_far, g_far_near = hidden_inner(ids, after(total, from_fl), logits, student_head)
+    grads = (after(mine, g_lefts), *grads[1:])
     h_f, h_y, h_own = head_parts(360, ((72, F32),) * 3, SHORT, *grads)
-    from_lefts, from_rights, from_fl = send(h_lefts, Z_DOWN), send(h_rights, Z_UP), send(h_fl, Y_LO)
+    from_lefts, from_rights = send(h_lefts, Z_DOWN), send(h_rights, Z_UP)
     h_y, h_f = pass_on((h_y, h_f, from_lefts, from_rights, from_fl))
     from_y, from_f = send(h_y, Y_LO), send(h_f, Z_FAR)
     head_grad = finish((h_own, from_lefts, from_rights, from_f, from_y), SHORT)
 
-    g_own, g_near, g_far, g_far_near, g_lefts, g_rights = parts
     from_lefts, from_rights, from_fn = send(g_lefts, X_DOWN), send(g_rights, X_UP), send(after(g_far_near, from_fl), Y_HI)
     near_sum, far_sum = pass_on((after(g_near, h_y), g_far, from_lefts, from_rights, from_fn))
     from_far, from_near = send(far_sum, X_FAR), send(near_sum, Y_HI)

time: 123 us -> 121 us (0.984)
    pallas_call x12 -> x16, Pallas kernels: 21.3 us -> 21.1 us  [kernel_call(): pl.pallas_call(body, in_specs=[VMEM] * len(arrays), out_specs=[VMEM] * le...]
  transfers between devices with their start and end apart: 38 -> 38, of which waited for: 16 -> 17; matrix products, arithmetic and copies ran while one was open for 1% -> 1% of each run, Pallas kernels for 12% -> 13%
where the time goes in v5:
time: 121 us
  starting transfers between devices  49.2 us (41%)
  waiting for transfers between devices  48 us (40%)
  Pallas kernels  21.1 us (17%)
  local copies, waits for them, and re-layouts  1.82 us (2%)
    ppermute x38, starting transfers between devices, send(): return lax.ppermute(a, AXES, to)  49.2 us
    ppermute x38, waiting for transfers between devices, send(): return lax.ppermute(a, AXES, to)  48 us
    pallas_call x16, Pallas kernels, kernel_call(): pl.pallas_call(body, in_specs=[VMEM] * len(arrays), out_specs=[VMEM] * le...  21.1 us
  transfers between devices with their start and end apart: 38, of which 17 were waited for; matrix products, arithmetic and copies ran while one was open for 1% of the time, Pallas kernels for 13%

profile of v5, /device:TPU:0, one launch (start us, length us, event | category | flops | bytes accessed | tf_op | source)
XLA Modules:
  0.0 121.0 jit_solution(10111195787632556490)
XLA Ops:
  0.6 1.6 %collective-permute-start.2 = (bf16[64,2560]{1,0:T(8,128)(2,1)}, bf16[64,2560]{1,0:T(8,128)(2,1)S(1)}, u32[]{:S(2)}, u32[]{:S(2)}) collective-permute-start(bf16[64,2560]{1,0:T(8,128)(2,1)} %refs_0_.1), channel_id=1, source_target_pairs={{0,2},{1,3},{2,4},{3,5},{4,6},{5,7},{6,0},{7,1},{8,10},{9,11},{10,... | collective-permute-start | bytes 983048 | tf_op jit(solution)/shard_map/ppermute | solution.py:40
  2.3 3.0 %collective-permute-start.1 = (bf16[64,2560]{1,0:T(8,128)(2,1)}, bf16[64,2560]{1,0:T(8,128)(2,1)S(1)}, u32[]{:S(2)}, u32[]{:S(2)}) collective-permute-start(bf16[64,2560]{1,0:T(8,128)(2,1)} %refs_0_.1), channel_id=1, source_target_pairs={{0,65},{1,64},{2,67},{3,66},{4,69},{5,68},{6,71},{7,70},{8,73},{9,... | collective-permute-start | bytes 983048 | tf_op jit(solution)/shard_map/ppermute | solution.py:40
  5.3 1.7 %collective-permute-start.3 = (bf16[64,2560]{1,0:T(8,128)(2,1)}, bf16[64,2560]{1,0:T(8,128)(2,1)S(1)}, u32[]{:S(2)}, u32[]{:S(2)}) collective-permute-start(bf16[64,2560]{1,0:T(8,128)(2,1)} %refs_0_.1), channel_id=1, source_target_pairs={{0,6},{1,7},{2,0},{3,1},{4,2},{5,3},{6,4},{7,5},{8,14},{9,15},{10,... | collective-permute-start | bytes 983048 | tf_op jit(solution)/shard_map/ppermute | solution.py:40
  7.0 0.1 collective-permute-start
  7.2 1.1 fusion
  8.3 1.7 %collective-permute-start.13 = (bf16[64,2560]{1,0:T(8,128)(2,1)S(1)}, bf16[64,2560]{1,0:T(8,128)(2,1)S(1)}, u32[]{:S(2)}, u32[]{:S(2)}) collective-permute-start(bf16[64,2560]{1,0:T(8,128)(2,1)S(1)} %get-tuple-element.49.refs_0_), channel_id=1, source_target_pairs={{0,6},{1,7},{2,0},{3,1},{4,2},{5,3},{6,4},{7,5},{8,14},{9,15},{10,... | collective-permute-start | bytes 983048 | tf_op jit(solution)/shard_map/ppermute | solution.py:40
  10.0 3.0 %collective-permute-done.near = s32[512]{0:T(512)S(1)} collective-permute-done((s32[512]{0:T(512)}, s32[512]{0:T(512)S(1)}, u32[]{:S(2)}, u32[]{:S(2)}) %collective-permute-start) | collective-permute-done | bytes 2080 | tf_op jit(solution)/shard_map/ppermute | solution.py:40
  13.0 1.5 %collective-permute-start.10 = (bf16[64,2560]{1,0:T(8,128)(2,1)S(1)}, bf16[64,2560]{1,0:T(8,128)(2,1)S(1)}, u32[]{:S(2)}, u32[]{:S(2)}) collective-permute-start(bf16[64,2560]{1,0:T(8,128)(2,1)S(1)} %get-tuple-element.49.refs_0_), channel_id=1, source_target_pairs={{0,2},{1,3},{2,4},{3,5},{4,6},{5,7},{6,0},{7,1},{8,10},{9,11},{10,... | collective-permute-start | bytes 983048 | tf_op jit(solution)/shard_map/ppermute | solution.py:40
  14.5 2.9 %collective-permute-start.4 = (bf16[64,2560]{1,0:T(8,128)(2,1)S(1)}, bf16[64,2560]{1,0:T(8,128)(2,1)S(1)}, u32[]{:S(2)}, u32[]{:S(2)}) collective-permute-start(bf16[64,2560]{1,0:T(8,128)(2,1)S(1)} %get-tuple-element.49.refs_0_), channel_id=1, source_target_pairs={{0,65},{1,64},{2,67},{3,66},{4,69},{5,68},{6,71},{7,70},{8,73},{9,... | collective-permute-start | bytes 983048 | tf_op jit(solution)/shard_map/ppermute | solution.py:40
  17.4 1.2 collective-permute-start.7
  18.6 2.0 %collective-permute-start.6 = (bf16[64,2560]{1,0:T(8,128)(2,1)S(1)}, bf16[64,2560]{1,0:T(8,128)(2,1)S(1)}, u32[]{:S(2)}, u32[]{:S(2)}) collective-permute-start(bf16[64,2560]{1,0:T(8,128)(2,1)S(1)} %collective-permute-done.1.refs_1_), channel_id=1, source_target_pairs={{0,6},{1,7},{2,0},{3,1},{4,2},{5,3},{6,4},{7,5},{8,14},{9,15},{10,... | collective-permute-start | bytes 983048 | tf_op jit(solution)/shard_map/ppermute | solution.py:40
  20.7 2.5 %collective-permute-done.13.refs_3_ = bf16[64,2560]{1,0:T(8,128)(2,1)S(1)} collective-permute-done((bf16[64,2560]{1,0:T(8,128)(2,1)S(1)}, bf16[64,2560]{1,0:T(8,128)(2,1)S(1)}, u32[]{:S(2)}, u32[]{:S(2)}) %collective-permute-start.13) | collective-permute-done | bytes 327712 | tf_op jit(solution)/shard_map/ppermute | solution.py:40
  23.2 0.2 collective-permute-start.8
  23.4 1.5 %collective-permute-done.10.refs_2_ = bf16[64,2560]{1,0:T(8,128)(2,1)S(1)} collective-permute-done((bf16[64,2560]{1,0:T(8,128)(2,1)S(1)}, bf16[64,2560]{1,0:T(8,128)(2,1)S(1)}, u32[]{:S(2)}, u32[]{:S(2)}) %collective-permute-start.10) | collective-permute-done | bytes 327712 | tf_op jit(solution)/shard_map/ppermute | solution.py:40
  24.9 1.4 %collective-permute-start.15 = (bf16[64,2560]{1,0:T(8,128)(2,1)S(1)}, bf16[64,2560]{1,0:T(8,128)(2,1)S(1)}, u32[]{:S(2)}, u32[]{:S(2)}) collective-permute-start(bf16[64,2560]{1,0:T(8,128)(2,1)S(1)} %collective-permute-done.13.refs_3_), channel_id=1, source_target_pairs={{0,6},{1,7},{2,0},{3,1},{4,2},{5,3},{6,4},{7,5},{8,14},{9,15},{10,... | collective-permute-start | bytes 983048 | tf_op jit(solution)/shard_map/ppermute | solution.py:40
  26.3 0.7 copy-done.1
  27.0 0.2 shard_map.68.ids
  27.1 0.7 collective-permute-start.11
  27.8 4.0 %collective-permute-done.7.refs_6_ = bf16[64,2560]{1,0:T(8,128)(2,1)S(1)} collective-permute-done((bf16[64,2560]{1,0:T(8,128)(2,1)S(1)}, bf16[64,2560]{1,0:T(8,128)(2,1)S(1)}, u32[]{:S(2)}, u32[]{:S(2)}) %collective-permute-start.7) | collective-permute-done | bytes 327712 | tf_op jit(solution)/shard_map/ppermute | solution.py:40
  31.8 2.8 %collective-permute-start.5 = (bf16[64,2560]{1,0:T(8,128)(2,1)S(1)}, bf16[64,2560]{1,0:T(8,128)(2,1)S(1)}, u32[]{:S(2)}, u32[]{:S(2)}) collective-permute-start(bf16[64,2560]{1,0:T(8,128)(2,1)S(1)} %collective-permute-done.2.refs_2_), channel_id=1, source_target_pairs={{0,65},{1,64},{2,67},{3,66},{4,69},{5,68},{6,71},{7,70},{8,73},{9,... | collective-permute-start | bytes 983048 | tf_op jit(solution)/shard_map/ppermute | solution.py:40
  34.6 0.4 collective-permute-start.14
  35.1 2.8 %collective-permute-start.12 = (bf16[64,2560]{1,0:T(8,128)(2,1)S(1)}, bf16[64,2560]{1,0:T(8,128)(2,1)S(1)}, u32[]{:S(2)}, u32[]{:S(2)}) collective-permute-start(bf16[64,2560]{1,0:T(8,128)(2,1)S(1)} %get-tuple-element.58.refs_0_), channel_id=1, source_target_pairs={{0,6},{1,7},{2,0},{3,1},{4,2},{5,3},{6,4},{7,5},{8,14},{9,15},{10,... | collective-permute-start | bytes 983048 | tf_op jit(solution)/shard_map/ppermute | solution.py:40
  37.9 0.4 collective-permute-start.9
  38.3 0.8 collective-permute-done.11.refs_2_
  39.0 1.1 collective-permute-start.16
  40.2 2.4 %collective-permute-done.5.refs_4_ = bf16[64,2560]{1,0:T(8,128)(2,1)S(1)} collective-permute-done((bf16[64,2560]{1,0:T(8,128)(2,1)S(1)}, bf16[64,2560]{1,0:T(8,128)(2,1)S(1)}, u32[]{:S(2)}, u32[]{:S(2)}) %collective-permute-start.5) | collective-permute-done | bytes 327712 | tf_op jit(solution)/shard_map/ppermute | solution.py:40
  42.6 0.2 collective-permute-start.20
  42.8 3.7 %collective-permute-done.14.refs_4_ = bf16[64,2560]{1,0:T(8,128)(2,1)S(1)} collective-permute-done((bf16[64,2560]{1,0:T(8,128)(2,1)S(1)}, bf16[64,2560]{1,0:T(8,128)(2,1)S(1)}, u32[]{:S(2)}, u32[]{:S(2)}) %collective-permute-start.14) | collective-permute-done | bytes 327712 | tf_op jit(solution)/shard_map/ppermute | solution.py:40
  46.5 2.7 %collective-permute-start.17 = (bf16[64,2560]{1,0:T(8,128)(2,1)S(1)}, bf16[64,2560]{1,0:T(8,128)(2,1)S(1)}, u32[]{:S(2)}, u32[]{:S(2)}) collective-permute-start(bf16[64,2560]{1,0:T(8,128)(2,1)S(1)} %collective-permute-done.15.refs_6_), channel_id=1, source_target_pairs={{0,65},{1,64},{2,67},{3,66},{4,69},{5,68},{6,71},{7,70},{8,73},{9,... | collective-permute-start | bytes 983048 | tf_op jit(solution)/shard_map/ppermute | solution.py:40
  49.2 0.3 collective-permute-done.9.refs_7_
  49.5 3.0 %collective-permute-start.19 = (bf16[64,2560]{1,0:T(8,128)(2,1)S(1)}, bf16[64,2560]{1,0:T(8,128)(2,1)S(1)}, u32[]{:S(2)}, u32[]{:S(2)}) collective-permute-start(bf16[64,2560]{1,0:T(8,128)(2,1)S(1)} %collective-permute-done.8.refs_1_), channel_id=1, source_target_pairs={{0,6},{1,7},{2,0},{3,1},{4,2},{5,3},{6,4},{7,5},{8,14},{9,15},{10,... | collective-permute-start | bytes 983048 | tf_op jit(solution)/shard_map/ppermute | solution.py:40
  52.4 3.4 %shard_map.69 = (f32[1152,512]{1,0:T(8,128)S(1)}, bf16[512,2560]{1,0:T(8,128)(2,1)S(1)}, f32[8,512]{1,0:T(8,128)S(1)}) custom-call(s32[1,512]{1,0:T(1,128)S(1)} %shard_map.68.ids, bf16[1152,2560]{1,0:T(8,128)(2,1)S(1)} %bitcast.1, bf16[64,2560]{1,0:T(8,128)(2,1)S(1)} %copy-done, bf16[64,2560]{1,0:T(8,128)(2,1)S(1)} %collective-permute-done.1.refs_1_, ...), custom_call_target="tpu_custom_call" | custom-call | flops 20000000000 | bytes 20000000 | tf_op jit(solution)/shard_map/pallas_call | solution.py:69
  55.8 1.0 collective-permute-start.21
  56.8 1.7 %shard_map.70.early = f32[1152,256]{1,0:T(8,128)S(1)} custom-call(bf16[1152,5120]{1,0:T(8,128)(2,1)S(1)} %bitcast.3, bf16[64,2560]{1,0:T(8,128)(2,1)S(1)} %get-tuple-element.58.refs_0_, bf16[64,2560]{1,0:T(8,128)(2,1)S(1)} %collective-permute-done.8.refs_1_, bf16[64,2560]{1,0:T(8,128)(2,1)S(1)} %collective-permute-done.11.refs_2_, ...), custom_call_target="tpu_custom_call" | custom-call | flops 20000000000 | bytes 20000000 | tf_op jit(solution)/shard_map/pallas_call | solution.py:69
  58.5 3.3 %shard_map.71 = (f32[1152,256]{1,0:T(8,128)S(1)}, f32[8,512]{1,0:T(8,128)S(1)}) custom-call(s32[1,512]{1,0:T(1,128)S(1)} %shard_map.68.ids, f32[8,512]{1,0:T(8,128)S(1)} %get-tuple-element.55.student_stats, f32[1152,256]{1,0:T(8,128)S(1)} %shard_map.70.early, bf16[1152,5120]{1,0:T(8,128)(2,1)S(1)} %bitcast.3, ...), custom_call_target="tpu_custom_call" | custom-call | flops 20000000000 | bytes 20000000 | tf_op jit(solution)/shard_map/pallas_call | solution.py:69
  61.8 2.5 %collective-permute-done.21.refs_3_ = bf16[64,2560]{1,0:T(8,128)(2,1)S(1)} collective-permute-done((bf16[64,2560]{1,0:T(8,128)(2,1)S(1)}, bf16[64,2560]{1,0:T(8,128)(2,1)S(1)}, u32[]{:S(2)}, u32[]{:S(2)}) %collective-permute-start.21) | collective-permute-done | bytes 327712 | tf_op jit(solution)/shard_map/ppermute | solution.py:40
  64.3 1.8 %shard_map.72.refs_0_ = f32[8,512]{1,0:T(8,128)S(1)} custom-call(s32[1,512]{1,0:T(1,128)S(1)} %shard_map.68.ids, f32[8,512]{1,0:T(8,128)S(1)} %get-tuple-element.63.first_stats, bf16[1152,5120]{1,0:T(8,128)(2,1)S(1)} %bitcast.3, f32[1152,256]{1,0:T(8,128)S(1)} %get-tuple-element.64.logits, bf16[64,2560]{1,0:T(8,128)(2,1)S(1)} %collective-permute-done.18.refs_0_, ...), custom_call_target="tpu_custom_call" | custom-call | flops 20000000000 | bytes 20000000 | tf_op jit(solution)/shard_map/pallas_call | solution.py:69
  66.3 1.7 %collective-permute-start.23 = (f32[8,512]{1,0:T(8,128)S(1)}, f32[8,512]{1,0:T(8,128)S(1)}, u32[]{:S(2)}, u32[]{:S(2)}) collective-permute-start(f32[8,512]{1,0:T(8,128)S(1)} %shard_map.72.refs_0_), channel_id=1, source_target_pairs={{0,6},{1,7},{2,0},{3,1},{4,2},{5,3},{6,4},{7,5},{8,14},{9,15},{10,... | collective-permute-start | bytes 49160 | tf_op jit(solution)/shard_map/ppermute | solution.py:40
  68.0 0.4 collective-permute-start.22
  68.4 3.1 %collective-permute-done.24.refs_3_ = f32[8,512]{1,0:T(8,128)S(1)} collective-permute-done((f32[8,512]{1,0:T(8,128)S(1)}, f32[8,512]{1,0:T(8,128)S(1)}, u32[]{:S(2)}, u32[]{:S(2)}) %collective-permute-start.24) | collective-permute-done | bytes 16416 | tf_op jit(solution)/shard_map/ppermute | solution.py:40
  71.5 1.4 %collective-permute-done.22.refs_1_ = f32[8,512]{1,0:T(8,128)S(1)} collective-permute-done((f32[8,512]{1,0:T(8,128)S(1)}, f32[8,512]{1,0:T(8,128)S(1)}, u32[]{:S(2)}, u32[]{:S(2)}) %collective-permute-start.22) | collective-permute-done | bytes 16416 | tf_op jit(solution)/shard_map/ppermute | solution.py:40
  73.1 2.1 %collective-permute-start.25 = (f32[8,512]{1,0:T(8,128)S(1)}, f32[8,512]{1,0:T(8,128)S(1)}, u32[]{:S(2)}, u32[]{:S(2)}) collective-permute-start(f32[8,512]{1,0:T(8,128)S(1)} %shard_map.73.refs_0_), channel_id=1, source_target_pairs={{0,65},{1,64},{2,67},{3,66},{4,69},{5,68},{6,71},{7,70},{8,73},{9,... | collective-permute-start | bytes 49160 | tf_op jit(solution)/shard_map/ppermute | solution.py:40
  75.1 3.0 %collective-permute-done.25.refs_1_ = f32[8,512]{1,0:T(8,128)S(1)} collective-permute-done((f32[8,512]{1,0:T(8,128)S(1)}, f32[8,512]{1,0:T(8,128)S(1)}, u32[]{:S(2)}, u32[]{:S(2)}) %collective-permute-start.25) | collective-permute-done | bytes 16416 | tf_op jit(solution)/shard_map/ppermute | solution.py:40
  78.2 0.6 shard_map.75
  78.9 2.0 %collective-permute-done.26.grad_from = bf16[576,512]{1,0:T(8,128)(2,1)S(1)} collective-permute-done((bf16[576,512]{1,0:T(8,128)(2,1)S(1)}, bf16[576,512]{1,0:T(8,128)(2,1)S(1)}, u32[]{:S(2)}, u32[]{:S(2)}) %collective-permute-start.26) | collective-permute-done | bytes 589856 | tf_op jit(solution)/shard_map/ppermute | solution.py:40
  80.9 2.1 %shard_map.76 = (bf16[144,2560]{1,0:T(8,128)(2,1)S(1)}, bf16[144,2560]{1,0:T(8,128)(2,1)S(1)}, bf16[72,2560]{1,0:T(8,128)(2,1)S(1)}) custom-call(bf16[576,512]{1,0:T(8,128)(2,1)S(1)} %get-tuple-element.79.grad_mine, bf16[576,512]{1,0:T(8,128)(2,1)S(1)} %collective-permute-done.26.grad_from, bf16[512,2560]{1,0:T(8,128)(2,1)S(1)} %get-tuple-element.73.hidden, ...), custom_call_target="tpu_custom_call" | custom-call | flops 1000000000 | bytes 1000000 | tf_op jit(solution)/shard_map/pallas_call | solution.py:69
  83.1 4.2 %collective-permute-start.29 = (bf16[144,2560]{1,0:T(8,128)(2,1)S(1)}, bf16[144,2560]{1,0:T(8,128)(2,1)S(1)}, u32[]{:S(2)}, u32[]{:S(2)}) collective-permute-start(bf16[144,2560]{1,0:T(8,128)(2,1)S(1)} %get-tuple-element.81), channel_id=1, source_target_pairs={{0,48},{1,49},{2,50},{3,51},{4,52},{5,53},{6,54},{7,55},{8,56},{9,... | collective-permute-start | bytes 2211848 | tf_op jit(solution)/shard_map/ppermute | solution.py:40
  87.3 2.1 %shard_map.78 = (bf16[128,2560]{1,0:T(8,128)(2,1)S(1)}, bf16[128,2560]{1,0:T(8,128)(2,1)S(1)}) custom-call(s32[1,512]{1,0:T(1,128)S(1)} %shard_map.68.ids, f32[8,512]{1,0:T(8,128)S(1)} %shard_map.74.total, f32[1152,512]{1,0:T(8,128)S(1)} %get-tuple-element.70.logits, bf16[1152,2560]{1,0:T(8,128)(2,1)S(1)} %bitcast.1), custom_call_target="tpu_custom_call" | custom-call | flops 20000000000 | bytes 20000000 | tf_op jit(solution)/shard_map/pallas_call | solution.py:69
  89.5 1.1 collective-permute-start.33
  90.6 1.0 collective-permute-start.34
  91.6 1.3 %shard_map.79 = (f32[72,2560]{1,0:T(8,128)S(1)}, f32[72,2560]{1,0:T(8,128)S(1)}, f32[72,2560]{1,0:T(8,128)S(1)}) custom-call(bf16[576,512]{1,0:T(8,128)(2,1)S(1)} %get-tuple-element.79.grad_mine, bf16[576,512]{1,0:T(8,128)(2,1)S(1)} %collective-permute-done.26.grad_from, bf16[512,2560]{1,0:T(8,128)(2,1)S(1)} %get-tuple-element.73.hidden, ...), custom_call_target="tpu_custom_call" | custom-call | flops 1000000000 | bytes 1000000 | tf_op jit(solution)/shard_map/pallas_call | solution.py:69
  92.9 0.8 collective-permute-done.28.far_near
  93.7 2.1 %shard_map.77 = (f32[64,2560]{1,0:T(8,128)S(1)}, f32[64,2560]{1,0:T(8,128)S(1)}, f32[64,2560]{1,0:T(8,128)S(1)}, bf16[64,2560]{1,0:T(8,128)(2,1)S(1)}) custom-call(s32[1,512]{1,0:T(1,128)S(1)} %shard_map.68.ids, f32[8,512]{1,0:T(8,128)S(1)} %shard_map.74.total, f32[1152,512]{1,0:T(8,128)S(1)} %get-tuple-element.70.logits, bf16[1152,2560]{1,0:T(8,128)(2,1)S(1)} %bitcast.1), custom_call_target="tpu_custom_call" | custom-call | flops 1000000000 | bytes 1000000 | tf_op jit(solution)/shard_map/pallas_call | solution.py:69
  95.8 2.1 %collective-permute-start.35 = (bf16[64,2560]{1,0:T(8,128)(2,1)S(1)}, bf16[64,2560]{1,0:T(8,128)(2,1)S(1)}, u32[]{:S(2)}, u32[]{:S(2)}) collective-permute-start(bf16[64,2560]{1,0:T(8,128)(2,1)S(1)} %get-tuple-element.93), channel_id=1, source_target_pairs={{0,65},{1,64},{2,67},{3,66},{4,69},{5,68},{6,71},{7,70},{8,73},{9,... | collective-permute-start | bytes 983048 | tf_op jit(solution)/shard_map/ppermute | solution.py:40
  97.9 5.4 %collective-permute-done.29.lefts = bf16[144,2560]{1,0:T(8,128)(2,1)S(1)} collective-permute-done((bf16[144,2560]{1,0:T(8,128)(2,1)S(1)}, bf16[144,2560]{1,0:T(8,128)(2,1)S(1)}, u32[]{:S(2)}, u32[]{:S(2)}) %collective-permute-start.29) | collective-permute-done | bytes 737312 | tf_op jit(solution)/shard_map/ppermute | solution.py:40
  103.4 3.4 %collective-permute-done.30.rights = bf16[144,2560]{1,0:T(8,128)(2,1)S(1)} collective-permute-done((bf16[144,2560]{1,0:T(8,128)(2,1)S(1)}, bf16[144,2560]{1,0:T(8,128)(2,1)S(1)}, u32[]{:S(2)}, u32[]{:S(2)}) %collective-permute-start.30) | collective-permute-done | bytes 737312 | tf_op jit(solution)/shard_map/ppermute | solution.py:40
  106.8 0.2 shard_map.80
  107.0 1.7 %collective-permute-start.32 = (bf16[72,2560]{1,0:T(8,128)(2,1)S(1)}, bf16[72,2560]{1,0:T(8,128)(2,1)S(1)}, u32[]{:S(2)}, u32[]{:S(2)}) collective-permute-start(bf16[72,2560]{1,0:T(8,128)(2,1)S(1)} %get-tuple-element.86), channel_id=1, source_target_pairs={{0,64},{1,65},{2,66},{3,67},{4,68},{5,69},{6,70},{7,71},{8,72},{9,... | collective-permute-start | bytes 1105928 | tf_op jit(solution)/shard_map/ppermute | solution.py:40
  108.7 0.2 shard_map.82
  108.9 0.5 collective-permute-start.36
  109.4 1.5 %collective-permute-start.37 = (bf16[64,2560]{1,0:T(8,128)(2,1)S(1)}, bf16[64,2560]{1,0:T(8,128)(2,1)S(1)}, u32[]{:S(2)}, u32[]{:S(2)}) collective-permute-start(bf16[64,2560]{1,0:T(8,128)(2,1)S(1)} %get-tuple-element.95), channel_id=1, source_target_pairs={{0,65},{1,64},{2,67},{3,66},{4,69},{5,68},{6,71},{7,70},{8,73},{9,... | collective-permute-start | bytes 983048 | tf_op jit(solution)/shard_map/ppermute | solution.py:40
  110.9 8.2 %collective-permute-done.31.far = bf16[72,2560]{1,0:T(8,128)(2,1)S(1)} collective-permute-done((bf16[72,2560]{1,0:T(8,128)(2,1)S(1)}, bf16[72,2560]{1,0:T(8,128)(2,1)S(1)}, u32[]{:S(2)}, u32[]{:S(2)}) %collective-permute-start.31) | collective-permute-done | bytes 368672 | tf_op jit(solution)/shard_map/ppermute | solution.py:40
  119.1 0.9 shard_map.81
  120.0 0.9 shard_map.83
  (45 shorter events, 0.5 us)
Async XLA Ops:
  0.6 13.9 %collective-permute-start.2 = (bf16[64,2560]{1,0:T(8,128)(2,1)}, bf16[64,2560]{1,0:T(8,128)(2,1)S(1)}, u32[]{:S(2)}, u32[]{:S(2)}) collective-permute-start(bf16[64,2560]{1,0:T(8,128)(2,1)} %refs_0_.1), channel_id=1, source_target_pairs={{0,2},{1,3},{2,4},{3,5},{4,6},{5,7},{6,0},{7,1},{8,10},{9,11},{10,... | collective-permute-start | bytes 983048 | tf_op jit(solution)/shard_map/ppermute | solution.py:40
  2.3 15.1 %collective-permute-start.1 = (bf16[64,2560]{1,0:T(8,128)(2,1)}, bf16[64,2560]{1,0:T(8,128)(2,1)S(1)}, u32[]{:S(2)}, u32[]{:S(2)}) collective-permute-start(bf16[64,2560]{1,0:T(8,128)(2,1)} %refs_0_.1), channel_id=1, source_target_pairs={{0,65},{1,64},{2,67},{3,66},{4,69},{5,68},{6,71},{7,70},{8,73},{9,... | collective-permute-start | bytes 983048 | tf_op jit(solution)/shard_map/ppermute | solution.py:40
  5.3 13.3 %collective-permute-start.3 = (bf16[64,2560]{1,0:T(8,128)(2,1)}, bf16[64,2560]{1,0:T(8,128)(2,1)S(1)}, u32[]{:S(2)}, u32[]{:S(2)}) collective-permute-start(bf16[64,2560]{1,0:T(8,128)(2,1)} %refs_0_.1), channel_id=1, source_target_pairs={{0,6},{1,7},{2,0},{3,1},{4,2},{5,3},{6,4},{7,5},{8,14},{9,15},{10,... | collective-permute-start | bytes 983048 | tf_op jit(solution)/shard_map/ppermute | solution.py:40
  7.0 6.0 %collective-permute-start = (s32[512]{0:T(512)}, s32[512]{0:T(512)S(1)}, u32[]{:S(2)}, u32[]{:S(2)}) collective-permute-start(s32[512]{0:T(512)} %own.1), channel_id=1, source_target_pairs={{0,65},{1,64},{2,67},{3,66},{4,69},{5,68},{6,71},{7,70},{8,73},{9,... | collective-permute-start | bytes 6152 | tf_op jit(solution)/shard_map/ppermute | solution.py:40
  8.3 14.9 %collective-permute-start.13 = (bf16[64,2560]{1,0:T(8,128)(2,1)S(1)}, bf16[64,2560]{1,0:T(8,128)(2,1)S(1)}, u32[]{:S(2)}, u32[]{:S(2)}) collective-permute-start(bf16[64,2560]{1,0:T(8,128)(2,1)S(1)} %get-tuple-element.49.refs_0_), channel_id=1, source_target_pairs={{0,6},{1,7},{2,0},{3,1},{4,2},{5,3},{6,4},{7,5},{8,14},{9,15},{10,... | collective-permute-start | bytes 983048 | tf_op jit(solution)/shard_map/ppermute | solution.py:40
  13.0 11.9 %collective-permute-start.10 = (bf16[64,2560]{1,0:T(8,128)(2,1)S(1)}, bf16[64,2560]{1,0:T(8,128)(2,1)S(1)}, u32[]{:S(2)}, u32[]{:S(2)}) collective-permute-start(bf16[64,2560]{1,0:T(8,128)(2,1)S(1)} %get-tuple-element.49.refs_0_), channel_id=1, source_target_pairs={{0,2},{1,3},{2,4},{3,5},{4,6},{5,7},{6,0},{7,1},{8,10},{9,11},{10,... | collective-permute-start | bytes 983048 | tf_op jit(solution)/shard_map/ppermute | solution.py:40
  14.5 12.6 %collective-permute-start.4 = (bf16[64,2560]{1,0:T(8,128)(2,1)S(1)}, bf16[64,2560]{1,0:T(8,128)(2,1)S(1)}, u32[]{:S(2)}, u32[]{:S(2)}) collective-permute-start(bf16[64,2560]{1,0:T(8,128)(2,1)S(1)} %get-tuple-element.49.refs_0_), channel_id=1, source_target_pairs={{0,65},{1,64},{2,67},{3,66},{4,69},{5,68},{6,71},{7,70},{8,73},{9,... | collective-permute-start | bytes 983048 | tf_op jit(solution)/shard_map/ppermute | solution.py:40
  17.4 14.4 %collective-permute-start.7 = (bf16[64,2560]{1,0:T(8,128)(2,1)S(1)}, bf16[64,2560]{1,0:T(8,128)(2,1)S(1)}, u32[]{:S(2)}, u32[]{:S(2)}) collective-permute-start(bf16[64,2560]{1,0:T(8,128)(2,1)S(1)} %collective-permute-done.2.refs_2_), channel_id=1, source_target_pairs={{0,2},{1,3},{2,4},{3,5},{4,6},{5,7},{6,0},{7,1},{8,10},{9,11},{10,... | collective-permute-start | bytes 983048 | tf_op jit(solution)/shard_map/ppermute | solution.py:40
  18.6 16.0 %collective-permute-start.6 = (bf16[64,2560]{1,0:T(8,128)(2,1)S(1)}, bf16[64,2560]{1,0:T(8,128)(2,1)S(1)}, u32[]{:S(2)}, u32[]{:S(2)}) collective-permute-start(bf16[64,2560]{1,0:T(8,128)(2,1)S(1)} %collective-permute-done.1.refs_1_), channel_id=1, source_target_pairs={{0,6},{1,7},{2,0},{3,1},{4,2},{5,3},{6,4},{7,5},{8,14},{9,15},{10,... | collective-permute-start | bytes 983048 | tf_op jit(solution)/shard_map/ppermute | solution.py:40
  20.7 31.8 %slice-start = ((s8[5898240]{0:T(1024)(128)(4,1)}), s8[4194304]{0:T(1024)(128)(4,1)S(1)}, s32[]{:S(2)}) async-start(s8[5898240]{0:T(1024)(128)(4,1)} %bitcast), calls=%async_computation | async-start | bytes 8388608
  20.7 31.8 %slice-start.1 = ((s8[5898240]{0:T(1024)(128)(4,1)}), s8[1703936]{0:T(1024)(128)(4,1)S(1)}, s32[]{:S(2)}) async-start(s8[5898240]{0:T(1024)(128)(4,1)} %bitcast), calls=%async_computation.1 | async-start | bytes 3407872
  20.7 31.8 %copy-start = (bf16[64,2560]{1,0:T(8,128)(2,1)S(1)}, bf16[64,2560]{1,0:T(8,128)(2,1)}, u32[]{:S(2)}) copy-start(bf16[64,2560]{1,0:T(8,128)(2,1)} %refs_0_.1) | copy-start | bytes 983044
  23.2 11.9 %collective-permute-start.8 = (bf16[64,2560]{1,0:T(8,128)(2,1)S(1)}, bf16[64,2560]{1,0:T(8,128)(2,1)S(1)}, u32[]{:S(2)}, u32[]{:S(2)}) collective-permute-start(bf16[64,2560]{1,0:T(8,128)(2,1)S(1)} %get-tuple-element.58.refs_0_), channel_id=1, source_target_pairs={{0,65},{1,64},{2,67},{3,66},{4,69},{5,68},{6,71},{7,70},{8,73},{9,... | collective-permute-start | bytes 983048 | tf_op jit(solution)/shard_map/ppermute | solution.py:40
  24.9 13.0 %collective-permute-start.15 = (bf16[64,2560]{1,0:T(8,128)(2,1)S(1)}, bf16[64,2560]{1,0:T(8,128)(2,1)S(1)}, u32[]{:S(2)}, u32[]{:S(2)}) collective-permute-start(bf16[64,2560]{1,0:T(8,128)(2,1)S(1)} %collective-permute-done.13.refs_3_), channel_id=1, source_target_pairs={{0,6},{1,7},{2,0},{3,1},{4,2},{5,3},{6,4},{7,5},{8,14},{9,15},{10,... | collective-permute-start | bytes 983048 | tf_op jit(solution)/shard_map/ppermute | solution.py:40
  26.3 0.7 copy-start.1
  26.9 29.8 %slice-start.2 = ((s8[11796480]{0:T(1024)(128)(4,1)}), s8[4194304]{0:T(1024)(128)(4,1)S(1)}, s32[]{:S(2)}) async-start(s8[11796480]{0:T(1024)(128)(4,1)} %bitcast.2), calls=%async_computation.2 | async-start | bytes 8388608
  27.0 29.8 %slice-start.3 = ((s8[11796480]{0:T(1024)(128)(4,1)}), s8[4194304]{0:T(1024)(128)(4,1)S(1)}, s32[]{:S(2)}) async-start(s8[11796480]{0:T(1024)(128)(4,1)} %bitcast.2), calls=%async_computation.3 | async-start | bytes 8388608
  27.1 29.7 %slice-start.4 = ((s8[11796480]{0:T(1024)(128)(4,1)}), s8[3407872]{0:T(1024)(128)(4,1)S(1)}, s32[]{:S(2)}) async-start(s8[11796480]{0:T(1024)(128)(4,1)} %bitcast.2), calls=%async_computation.4 | async-start | bytes 6815744
  27.1 11.9 %collective-permute-start.11 = (bf16[64,2560]{1,0:T(8,128)(2,1)S(1)}, bf16[64,2560]{1,0:T(8,128)(2,1)S(1)}, u32[]{:S(2)}, u32[]{:S(2)}) collective-permute-start(bf16[64,2560]{1,0:T(8,128)(2,1)S(1)} %get-tuple-element.58.refs_0_), channel_id=1, source_target_pairs={{0,2},{1,3},{2,4},{3,5},{4,6},{5,7},{6,0},{7,1},{8,10},{9,11},{10,... | collective-permute-start | bytes 983048 | tf_op jit(solution)/shard_map/ppermute | solution.py:40
  31.8 10.8 %collective-permute-start.5 = (bf16[64,2560]{1,0:T(8,128)(2,1)S(1)}, bf16[64,2560]{1,0:T(8,128)(2,1)S(1)}, u32[]{:S(2)}, u32[]{:S(2)}) collective-permute-start(bf16[64,2560]{1,0:T(8,128)(2,1)S(1)} %collective-permute-done.2.refs_2_), channel_id=1, source_target_pairs={{0,65},{1,64},{2,67},{3,66},{4,69},{5,68},{6,71},{7,70},{8,73},{9,... | collective-permute-start | bytes 983048 | tf_op jit(solution)/shard_map/ppermute | solution.py:40
  34.6 11.9 %collective-permute-start.14 = (bf16[64,2560]{1,0:T(8,128)(2,1)S(1)}, bf16[64,2560]{1,0:T(8,128)(2,1)S(1)}, u32[]{:S(2)}, u32[]{:S(2)}) collective-permute-start(bf16[64,2560]{1,0:T(8,128)(2,1)S(1)} %collective-permute-done.4.refs_1_), channel_id=1, source_target_pairs={{0,2},{1,3},{2,4},{3,5},{4,6},{5,7},{6,0},{7,1},{8,10},{9,11},{10,... | collective-permute-start | bytes 983048 | tf_op jit(solution)/shard_map/ppermute | solution.py:40
  35.1 14.1 %collective-permute-start.12 = (bf16[64,2560]{1,0:T(8,128)(2,1)S(1)}, bf16[64,2560]{1,0:T(8,128)(2,1)S(1)}, u32[]{:S(2)}, u32[]{:S(2)}) collective-permute-start(bf16[64,2560]{1,0:T(8,128)(2,1)S(1)} %get-tuple-element.58.refs_0_), channel_id=1, source_target_pairs={{0,6},{1,7},{2,0},{3,1},{4,2},{5,3},{6,4},{7,5},{8,14},{9,15},{10,... | collective-permute-start | bytes 983048 | tf_op jit(solution)/shard_map/ppermute | solution.py:40
  37.9 11.6 %collective-permute-start.9 = (bf16[64,2560]{1,0:T(8,128)(2,1)S(1)}, bf16[64,2560]{1,0:T(8,128)(2,1)S(1)}, u32[]{:S(2)}, u32[]{:S(2)}) collective-permute-start(bf16[64,2560]{1,0:T(8,128)(2,1)S(1)} %collective-permute-done.7.refs_6_), channel_id=1, source_target_pairs={{0,65},{1,64},{2,67},{3,66},{4,69},{5,68},{6,71},{7,70},{8,73},{9,... | collective-permute-start | bytes 983048 | tf_op jit(solution)/shard_map/ppermute | solution.py:40
  39.0 19.5 %collective-permute-start.16 = (bf16[64,2560]{1,0:T(8,128)(2,1)S(1)}, bf16[64,2560]{1,0:T(8,128)(2,1)S(1)}, u32[]{:S(2)}, u32[]{:S(2)}) collective-permute-start(bf16[64,2560]{1,0:T(8,128)(2,1)S(1)} %collective-permute-done.4.refs_1_), channel_id=1, source_target_pairs={{0,6},{1,7},{2,0},{3,1},{4,2},{5,3},{6,4},{7,5},{8,14},{9,15},{10,... | collective-permute-start | bytes 983048 | tf_op jit(solution)/shard_map/ppermute | solution.py:40
  42.6 13.2 %collective-permute-start.20 = (bf16[64,2560]{1,0:T(8,128)(2,1)S(1)}, bf16[64,2560]{1,0:T(8,128)(2,1)S(1)}, u32[]{:S(2)}, u32[]{:S(2)}) collective-permute-start(bf16[64,2560]{1,0:T(8,128)(2,1)S(1)} %collective-permute-done.11.refs_2_), channel_id=1, source_target_pairs={{0,2},{1,3},{2,4},{3,5},{4,6},{5,7},{6,0},{7,1},{8,10},{9,11},{10,... | collective-permute-start | bytes 983048 | tf_op jit(solution)/shard_map/ppermute | solution.py:40
  46.5 12.0 %collective-permute-start.17 = (bf16[64,2560]{1,0:T(8,128)(2,1)S(1)}, bf16[64,2560]{1,0:T(8,128)(2,1)S(1)}, u32[]{:S(2)}, u32[]{:S(2)}) collective-permute-start(bf16[64,2560]{1,0:T(8,128)(2,1)S(1)} %collective-permute-done.15.refs_6_), channel_id=1, source_target_pairs={{0,65},{1,64},{2,67},{3,66},{4,69},{5,68},{6,71},{7,70},{8,73},{9,... | collective-permute-start | bytes 983048 | tf_op jit(solution)/shard_map/ppermute | solution.py:40
  49.2 12.6 %collective-permute-start.18 = (bf16[64,2560]{1,0:T(8,128)(2,1)S(1)}, bf16[64,2560]{1,0:T(8,128)(2,1)S(1)}, u32[]{:S(2)}, u32[]{:S(2)}) collective-permute-start(bf16[64,2560]{1,0:T(8,128)(2,1)S(1)} %collective-permute-done.8.refs_1_), channel_id=1, source_target_pairs={{0,2},{1,3},{2,4},{3,5},{4,6},{5,7},{6,0},{7,1},{8,10},{9,11},{10,... | collective-permute-start | bytes 983048 | tf_op jit(solution)/shard_map/ppermute | solution.py:40
  49.5 12.4 %collective-permute-start.19 = (bf16[64,2560]{1,0:T(8,128)(2,1)S(1)}, bf16[64,2560]{1,0:T(8,128)(2,1)S(1)}, u32[]{:S(2)}, u32[]{:S(2)}) collective-permute-start(bf16[64,2560]{1,0:T(8,128)(2,1)S(1)} %collective-permute-done.8.refs_1_), channel_id=1, source_target_pairs={{0,6},{1,7},{2,0},{3,1},{4,2},{5,3},{6,4},{7,5},{8,14},{9,15},{10,... | collective-permute-start | bytes 983048 | tf_op jit(solution)/shard_map/ppermute | solution.py:40
  55.8 8.5 %collective-permute-start.21 = (bf16[64,2560]{1,0:T(8,128)(2,1)S(1)}, bf16[64,2560]{1,0:T(8,128)(2,1)S(1)}, u32[]{:S(2)}, u32[]{:S(2)}) collective-permute-start(bf16[64,2560]{1,0:T(8,128)(2,1)S(1)} %collective-permute-done.20.refs_2_), channel_id=1, source_target_pairs={{0,65},{1,64},{2,67},{3,66},{4,69},{5,68},{6,71},{7,70},{8,73},{9,... | collective-permute-start | bytes 983048 | tf_op jit(solution)/shard_map/ppermute | solution.py:40
  66.2 5.3 %collective-permute-start.24 = (f32[8,512]{1,0:T(8,128)S(1)}, f32[8,512]{1,0:T(8,128)S(1)}, u32[]{:S(2)}, u32[]{:S(2)}) collective-permute-start(f32[8,512]{1,0:T(8,128)S(1)} %shard_map.72.refs_0_), channel_id=1, source_target_pairs={{0,4},{1,5},{2,6},{3,7},{4,0},{5,1},{6,2},{7,3},{8,12},{9,13},{10,... | collective-permute-start | bytes 49160 | tf_op jit(solution)/shard_map/ppermute | solution.py:40
  66.3 5.2 %collective-permute-start.23 = (f32[8,512]{1,0:T(8,128)S(1)}, f32[8,512]{1,0:T(8,128)S(1)}, u32[]{:S(2)}, u32[]{:S(2)}) collective-permute-start(f32[8,512]{1,0:T(8,128)S(1)} %shard_map.72.refs_0_), channel_id=1, source_target_pairs={{0,6},{1,7},{2,0},{3,1},{4,2},{5,3},{6,4},{7,5},{8,14},{9,15},{10,... | collective-permute-start | bytes 49160 | tf_op jit(solution)/shard_map/ppermute | solution.py:40
  68.0 4.9 %collective-permute-start.22 = (f32[8,512]{1,0:T(8,128)S(1)}, f32[8,512]{1,0:T(8,128)S(1)}, u32[]{:S(2)}, u32[]{:S(2)}) collective-permute-start(f32[8,512]{1,0:T(8,128)S(1)} %shard_map.72.refs_0_), channel_id=1, source_target_pairs={{0,2},{1,3},{2,4},{3,5},{4,6},{5,7},{6,0},{7,1},{8,10},{9,11},{10,... | collective-permute-start | bytes 49160 | tf_op jit(solution)/shard_map/ppermute | solution.py:40
  68.4 12.5 %collective-permute-start.27 = (bf16[512,2560]{1,0:T(8,128)(2,1)S(1)}, bf16[512,2560]{1,0:T(8,128)(2,1)S(1)}, u32[]{:S(2)}, u32[]{:S(2)}) collective-permute-start(bf16[512,2560]{1,0:T(8,128)(2,1)S(1)} %get-tuple-element.73.hidden), channel_id=1, source_target_pairs={{0,8},{1,9},{2,10},{3,11},{4,12},{5,13},{6,14},{7,15},{8,0},{9,1},... | collective-permute-start | bytes 7864328 | tf_op jit(solution)/shard_map/ppermute | solution.py:40
  73.1 5.0 %collective-permute-start.25 = (f32[8,512]{1,0:T(8,128)S(1)}, f32[8,512]{1,0:T(8,128)S(1)}, u32[]{:S(2)}, u32[]{:S(2)}) collective-permute-start(f32[8,512]{1,0:T(8,128)S(1)} %shard_map.73.refs_0_), channel_id=1, source_target_pairs={{0,65},{1,64},{2,67},{3,66},{4,69},{5,68},{6,71},{7,70},{8,73},{9,... | collective-permute-start | bytes 49160 | tf_op jit(solution)/shard_map/ppermute | solution.py:40
  78.8 2.1 %collective-permute-start.26 = (bf16[576,512]{1,0:T(8,128)(2,1)S(1)}, bf16[576,512]{1,0:T(8,128)(2,1)S(1)}, u32[]{:S(2)}, u32[]{:S(2)}) collective-permute-start(bf16[576,512]{1,0:T(8,128)(2,1)S(1)} %get-tuple-element.72), channel_id=1, source_target_pairs={{0,8},{1,9},{2,10},{3,11},{4,12},{5,13},{6,14},{7,15},{8,0},{9,1},... | collective-permute-start | bytes 1769480 | tf_op jit(solution)/shard_map/ppermute | solution.py:40
  83.0 10.7 %collective-permute-start.28 = (bf16[72,2560]{1,0:T(8,128)(2,1)S(1)}, bf16[72,2560]{1,0:T(8,128)(2,1)S(1)}, u32[]{:S(2)}, u32[]{:S(2)}) collective-permute-start(bf16[72,2560]{1,0:T(8,128)(2,1)S(1)} %get-tuple-element.74), channel_id=1, source_target_pairs={{0,64},{1,65},{2,66},{3,67},{4,68},{5,69},{6,70},{7,71},{8,72},{9,... | collective-permute-start | bytes 1105928 | tf_op jit(solution)/shard_map/ppermute | solution.py:40
  83.1 20.3 %collective-permute-start.29 = (bf16[144,2560]{1,0:T(8,128)(2,1)S(1)}, bf16[144,2560]{1,0:T(8,128)(2,1)S(1)}, u32[]{:S(2)}, u32[]{:S(2)}) collective-permute-start(bf16[144,2560]{1,0:T(8,128)(2,1)S(1)} %get-tuple-element.81), channel_id=1, source_target_pairs={{0,48},{1,49},{2,50},{3,51},{4,52},{5,53},{6,54},{7,55},{8,56},{9,... | collective-permute-start | bytes 2211848 | tf_op jit(solution)/shard_map/ppermute | solution.py:40
  87.3 19.5 %collective-permute-start.30 = (bf16[144,2560]{1,0:T(8,128)(2,1)S(1)}, bf16[144,2560]{1,0:T(8,128)(2,1)S(1)}, u32[]{:S(2)}, u32[]{:S(2)}) collective-permute-start(bf16[144,2560]{1,0:T(8,128)(2,1)S(1)} %get-tuple-element.82), channel_id=1, source_target_pairs={{0,16},{1,17},{2,18},{3,19},{4,20},{5,21},{6,22},{7,23},{8,24},{9,... | collective-permute-start | bytes 2211848 | tf_op jit(solution)/shard_map/ppermute | solution.py:40
  89.5 19.2 %collective-permute-start.33 = (bf16[128,2560]{1,0:T(8,128)(2,1)S(1)}, bf16[128,2560]{1,0:T(8,128)(2,1)S(1)}, u32[]{:S(2)}, u32[]{:S(2)}) collective-permute-start(bf16[128,2560]{1,0:T(8,128)(2,1)S(1)} %get-tuple-element.78), channel_id=1, source_target_pairs={{0,6},{1,7},{2,0},{3,1},{4,2},{5,3},{6,4},{7,5},{8,14},{9,15},{10,... | collective-permute-start | bytes 1966088 | tf_op jit(solution)/shard_map/ppermute | solution.py:40
  90.6 18.2 %collective-permute-start.34 = (bf16[128,2560]{1,0:T(8,128)(2,1)S(1)}, bf16[128,2560]{1,0:T(8,128)(2,1)S(1)}, u32[]{:S(2)}, u32[]{:S(2)}) collective-permute-start(bf16[128,2560]{1,0:T(8,128)(2,1)S(1)} %get-tuple-element.88), channel_id=1, source_target_pairs={{0,2},{1,3},{2,4},{3,5},{4,6},{5,7},{6,0},{7,1},{8,10},{9,11},{10,... | collective-permute-start | bytes 1966088 | tf_op jit(solution)/shard_map/ppermute | solution.py:40
  95.8 12.9 %collective-permute-start.35 = (bf16[64,2560]{1,0:T(8,128)(2,1)S(1)}, bf16[64,2560]{1,0:T(8,128)(2,1)S(1)}, u32[]{:S(2)}, u32[]{:S(2)}) collective-permute-start(bf16[64,2560]{1,0:T(8,128)(2,1)S(1)} %get-tuple-element.93), channel_id=1, source_target_pairs={{0,65},{1,64},{2,67},{3,66},{4,69},{5,68},{6,71},{7,70},{8,73},{9,... | collective-permute-start | bytes 983048 | tf_op jit(solution)/shard_map/ppermute | solution.py:40
  107.0 12.1 %collective-permute-start.32 = (bf16[72,2560]{1,0:T(8,128)(2,1)S(1)}, bf16[72,2560]{1,0:T(8,128)(2,1)S(1)}, u32[]{:S(2)}, u32[]{:S(2)}) collective-permute-start(bf16[72,2560]{1,0:T(8,128)(2,1)S(1)} %get-tuple-element.86), channel_id=1, source_target_pairs={{0,64},{1,65},{2,66},{3,67},{4,68},{5,69},{6,70},{7,71},{8,72},{9,... | collective-permute-start | bytes 1105928 | tf_op jit(solution)/shard_map/ppermute | solution.py:40
  108.7 10.4 %collective-permute-start.31 = (bf16[72,2560]{1,0:T(8,128)(2,1)S(1)}, bf16[72,2560]{1,0:T(8,128)(2,1)S(1)}, u32[]{:S(2)}, u32[]{:S(2)}) collective-permute-start(bf16[72,2560]{1,0:T(8,128)(2,1)S(1)} %get-tuple-element.85), channel_id=1, source_target_pairs={{0,32},{1,33},{2,34},{3,35},{4,36},{5,37},{6,38},{7,39},{8,40},{9,... | collective-permute-start | bytes 1105928 | tf_op jit(solution)/shard_map/ppermute | solution.py:40
  108.9 11.1 %collective-permute-start.36 = (bf16[64,2560]{1,0:T(8,128)(2,1)S(1)}, bf16[64,2560]{1,0:T(8,128)(2,1)S(1)}, u32[]{:S(2)}, u32[]{:S(2)}) collective-permute-start(bf16[64,2560]{1,0:T(8,128)(2,1)S(1)} %get-tuple-element.94), channel_id=1, source_target_pairs={{0,4},{1,5},{2,6},{3,7},{4,0},{5,1},{6,2},{7,3},{8,12},{9,13},{10,... | collective-permute-start | bytes 983048 | tf_op jit(solution)/shard_map/ppermute | solution.py:40
  109.4 10.6 %collective-permute-start.37 = (bf16[64,2560]{1,0:T(8,128)(2,1)S(1)}, bf16[64,2560]{1,0:T(8,128)(2,1)S(1)}, u32[]{:S(2)}, u32[]{:S(2)}) collective-permute-start(bf16[64,2560]{1,0:T(8,128)(2,1)S(1)} %get-tuple-element.95), channel_id=1, source_target_pairs={{0,65},{1,64},{2,67},{3,66},{4,69},{5,68},{6,71},{7,70},{8,73},{9,... | collective-permute-start | bytes 983048 | tf_op jit(solution)/shard_map/ppermute | solution.py:40

commit v6 on v5

--- a/solution.py
+++ b/solution.py
@@ -273,23 +273,32 @@
     return kernel_call(grad_kernel, (ids, total, logits), outs, [((half, 512), F32)] * 2, 5, LONG)
 
 
-def head_kernel(first, grad_mine, grad_from, hidden, hidden_from, *outs):
+def head_own_kernel(grad, hidden, out):
+    for j in range(0, hidden.shape[1], WIDE):
+        tile = slice(j, j + WIDE)
+        out[:, tile] = lax.dot_general(grad[...], hidden[:, tile], NN, preferred_element_type=F32)
+
+
+def head_own(grad, hidden):
+    outs = [((grad.shape[0], hidden.shape[1]), F32)]
+    return kernel_call(head_own_kernel, (grad, hidden), outs, [], 4)[0]
+
+
+def head_kernel(first, grad, hidden, own, *outs):
     n = sum(out.shape[0] for out in outs)
     rows = slice(first, first + n)
-    for j in range(hidden.shape[1] // WIDE):
-        tile = slice(j * WIDE, (j + 1) * WIDE)
-        product = lax.dot_general(grad_mine[rows, :], hidden[:, tile], NN, preferred_element_type=F32)
-        product += lax.dot_general(grad_from[rows, :], hidden_from[:, tile], NN, preferred_element_type=F32)
+    for j in range(0, hidden.shape[1], WIDE):
+        tile = slice(j, j + WIDE)
+        product = own[rows, tile] + lax.dot_general(grad[rows, :], hidden[:, tile], NN, preferred_element_type=F32)
         start = 0
         for out in outs:
             out[:, tile] = product[start:start + out.shape[0], :].astype(out.dtype)
             start += out.shape[0]
 
 
-def head_parts(first, outs, said, grad_mine, grad_from, hidden, hidden_from):
+def head_parts(first, outs, grad, hidden, own):
     outs = [((n, hidden.shape[1]), t) for n, t in outs]
-    arrays = (grad_mine, grad_from, hidden, hidden_from)
-    return kernel_call(functools.partial(head_kernel, first), arrays, outs, [], 4, said)
+    return kernel_call(functools.partial(head_kernel, first), (grad, hidden, own), outs, [], 4)
 
 
 def pass_on_kernel(near, far, lefts, rights, far_near, near_out, far_out):
@@ -335,20 +344,34 @@
     up, down, over = Link(X_UP), Link(X_DOWN), Link(Y_HI)
     half = teacher_hidden.shape[1] // 2
     t_a, t_b = teacher_hidden[:, :half], teacher_hidden[:, half:]
-    left, right, near = up(student_hidden), down(student_hidden), over(student_hidden)
+    t_b0 = t_b
+    left = up(student_hidden)
+    right = down(student_hidden)
+    near = over(student_hidden)
     ids_near = send(sampled_ids, Y_HI)
-    l_a, r_a, near_a = up(t_a), down(t_a), over(after(t_a, ids_near))
-    near_b = over(t_b)
     ids = kernel_call(ids_kernel, (sampled_ids, ids_near), [((1, 512), jnp.int32)], [], 1, LONG)[0]
-    t_b = after(t_b, ids)
-    far, right_near, left_near = up(left), down(near), over(left)
-    l_b, f_a, far_near = up(t_b), down(r_a), over(far)
-    ln_a, r_b, fn_a = up(near_a), down(t_b), over(f_a)
-    f_b, rn_a = up(l_b), down(near_a)
+    t_b0, t_b = t_b, after(t_b, ids)
+    l_b = up(t_b)
+    r_a = down(t_a)
+    near_a = over(after(t_a, ids_near))
+    far = up(left)
+    right_near = down(near)
+    near_b = over(t_b0)
+    l_a = up(t_a)
+    f_a = down(r_a)
+    left_near = over(left)
+    f_b = up(l_b)
+    r_b = down(t_b)
+    far_near = over(far)
+    ln_a = up(near_a)
+    rn_a = down(near_a)
+    fn_a = over(f_a)
+
     blocks = (student_hidden, near, left, right, left_near, right_near, far, far_near)
     logits, hidden, student_stats = student_logits(ids, blocks, student_head)
     fn_b = over(after(f_b, student_stats))
-    ln_b, rn_b = up(near_b), down(near_b)
+    ln_b = up(near_b)
+    rn_b = down(near_b)
 
     hidden_from = send(hidden, CORE)
     early = teacher_early((t_b, near_b, l_b, r_b), teacher_head)
@@ -357,13 +380,12 @@
     total = group_sum(teacher_second(ids, stats, (ln_b, rn_b, f_b, fn_b), teacher_head, teacher_logits))
 
     mine, other = logit_grads(ids, total, logits)
-    grads = (mine, send(other, CORE), hidden, hidden_from)
-    h_lefts, h_rights, h_fl = head_parts(0, ((144, BF16), (144, BF16), (72, BF16)), SHORT, *grads)
+    grad_from, sums = send(other, CORE), head_own(mine, hidden)
+    h_lefts, h_rights, h_fl = head_parts(0, ((144, BF16), (144, BF16), (72, BF16)), grad_from, hidden_from, sums)
     g_lefts, g_rights = hidden_outer(ids, after(total, h_fl), logits, student_head)
     from_fl = send(h_fl, Y_LO)
     g_own, g_near, g_far, g_far_near = hidden_inner(ids, after(total, from_fl), logits, student_head)
-    grads = (after(mine, g_lefts), *grads[1:])
-    h_f, h_y, h_own = head_parts(360, ((72, F32),) * 3, SHORT, *grads)
+    h_f, h_y, h_own = head_parts(360, ((72, F32),) * 3, after(grad_from, g_lefts), hidden_from, sums)
     from_lefts, from_rights = send(h_lefts, Z_DOWN), send(h_rights, Z_UP)
     h_y, h_f = pass_on((h_y, h_f, from_lefts, from_rights, from_fl))
     from_y, from_f = send(h_y, Y_LO), send(h_f, Z_FAR)

time: 121 us -> 120 us (level)
  waiting for transfers between devices: 48 us -> 43.8 us
  starting transfers between devices: 49.2 us -> 52.2 us
    ppermute x38, waiting for transfers between devices: 48 us -> 43.8 us  [send(): return lax.ppermute(a, AXES, to)]
    ppermute x38, starting transfers between devices: 49.2 us -> 52.2 us  [send(): return lax.ppermute(a, AXES, to)]
    pallas_call x16 -> x17, Pallas kernels: 21.1 us -> 21.3 us  [kernel_call(): pl.pallas_call(body, in_specs=[VMEM] * len(arrays), out_specs=[VMEM] * le...]
  transfers between devices with their start and end apart: 38 -> 38, of which waited for: 17 -> 20; matrix products, arithmetic and copies ran while one was open for 1% -> 1% of each run, Pallas kernels for 13% -> 14%
where the time goes in v6:
time: 120 us
  starting transfers between devices  52.2 us (44%)
  waiting for transfers between devices  43.8 us (36%)
  Pallas kernels  21.3 us (18%)
  local copies, waits for them, and re-layouts  1.82 us (2%)
    ppermute x38, starting transfers between devices, send(): return lax.ppermute(a, AXES, to)  52.2 us
    ppermute x38, waiting for transfers between devices, send(): return lax.ppermute(a, AXES, to)  43.8 us
    pallas_call x17, Pallas kernels, kernel_call(): pl.pallas_call(body, in_specs=[VMEM] * len(arrays), out_specs=[VMEM] * le...  21.3 us
  transfers between devices with their start and end apart: 38, of which 20 were waited for; matrix products, arithmetic and copies ran while one was open for 1% of the time, Pallas kernels for 14%

profile of v6, /device:TPU:0, one launch (start us, length us, event | category | flops | bytes accessed | tf_op | source)
XLA Modules:
  0.0 120.1 jit_solution(8412002096436169500)
XLA Ops:
  0.6 1.6 %collective-permute-start.2 = (bf16[64,2560]{1,0:T(8,128)(2,1)}, bf16[64,2560]{1,0:T(8,128)(2,1)S(1)}, u32[]{:S(2)}, u32[]{:S(2)}) collective-permute-start(bf16[64,2560]{1,0:T(8,128)(2,1)} %refs_0_.1), channel_id=1, source_target_pairs={{0,2},{1,3},{2,4},{3,5},{4,6},{5,7},{6,0},{7,1},{8,10},{9,11},{10,... | collective-permute-start | bytes 983048 | tf_op jit(solution)/shard_map/ppermute | solution.py:40
  2.3 3.0 %collective-permute-start.1 = (bf16[64,2560]{1,0:T(8,128)(2,1)}, bf16[64,2560]{1,0:T(8,128)(2,1)S(1)}, u32[]{:S(2)}, u32[]{:S(2)}) collective-permute-start(bf16[64,2560]{1,0:T(8,128)(2,1)} %refs_0_.1), channel_id=1, source_target_pairs={{0,65},{1,64},{2,67},{3,66},{4,69},{5,68},{6,71},{7,70},{8,73},{9,... | collective-permute-start | bytes 983048 | tf_op jit(solution)/shard_map/ppermute | solution.py:40
  5.3 1.7 %collective-permute-start.3 = (bf16[64,2560]{1,0:T(8,128)(2,1)}, bf16[64,2560]{1,0:T(8,128)(2,1)S(1)}, u32[]{:S(2)}, u32[]{:S(2)}) collective-permute-start(bf16[64,2560]{1,0:T(8,128)(2,1)} %refs_0_.1), channel_id=1, source_target_pairs={{0,6},{1,7},{2,0},{3,1},{4,2},{5,3},{6,4},{7,5},{8,14},{9,15},{10,... | collective-permute-start | bytes 983048 | tf_op jit(solution)/shard_map/ppermute | solution.py:40
  7.2 1.1 fusion
  8.3 1.7 %collective-permute-start.13 = (bf16[64,2560]{1,0:T(8,128)(2,1)S(1)}, bf16[64,2560]{1,0:T(8,128)(2,1)S(1)}, u32[]{:S(2)}, u32[]{:S(2)}) collective-permute-start(bf16[64,2560]{1,0:T(8,128)(2,1)S(1)} %get-tuple-element.58.refs_0_), channel_id=1, source_target_pairs={{0,6},{1,7},{2,0},{3,1},{4,2},{5,3},{6,4},{7,5},{8,14},{9,15},{10,... | collective-permute-start | bytes 983048 | tf_op jit(solution)/shard_map/ppermute | solution.py:40
  10.0 3.0 %collective-permute-done.near = s32[512]{0:T(512)S(1)} collective-permute-done((s32[512]{0:T(512)}, s32[512]{0:T(512)S(1)}, u32[]{:S(2)}, u32[]{:S(2)}) %collective-permute-start) | collective-permute-done | bytes 2080 | tf_op jit(solution)/shard_map/ppermute | solution.py:40
  13.0 0.7 copy-done.1
  13.9 1.6 %collective-permute-start.10 = (bf16[64,2560]{1,0:T(8,128)(2,1)S(1)}, bf16[64,2560]{1,0:T(8,128)(2,1)S(1)}, u32[]{:S(2)}, u32[]{:S(2)}) collective-permute-start(bf16[64,2560]{1,0:T(8,128)(2,1)S(1)} %get-tuple-element.57.refs_0_), channel_id=1, source_target_pairs={{0,2},{1,3},{2,4},{3,5},{4,6},{5,7},{6,0},{7,1},{8,10},{9,11},{10,... | collective-permute-start | bytes 983048 | tf_op jit(solution)/shard_map/ppermute | solution.py:40
  15.4 2.9 %collective-permute-start.4 = (bf16[64,2560]{1,0:T(8,128)(2,1)S(1)}, bf16[64,2560]{1,0:T(8,128)(2,1)S(1)}, u32[]{:S(2)}, u32[]{:S(2)}) collective-permute-start(bf16[64,2560]{1,0:T(8,128)(2,1)S(1)} %get-tuple-element.58.refs_0_), channel_id=1, source_target_pairs={{0,65},{1,64},{2,67},{3,66},{4,69},{5,68},{6,71},{7,70},{8,73},{9,... | collective-permute-start | bytes 983048 | tf_op jit(solution)/shard_map/ppermute | solution.py:40
  18.3 1.7 %collective-permute-start.6 = (bf16[64,2560]{1,0:T(8,128)(2,1)S(1)}, bf16[64,2560]{1,0:T(8,128)(2,1)S(1)}, u32[]{:S(2)}, u32[]{:S(2)}) collective-permute-start(bf16[64,2560]{1,0:T(8,128)(2,1)S(1)} %collective-permute-done.1.refs_1_), channel_id=1, source_target_pairs={{0,6},{1,7},{2,0},{3,1},{4,2},{5,3},{6,4},{7,5},{8,14},{9,15},{10,... | collective-permute-start | bytes 983048 | tf_op jit(solution)/shard_map/ppermute | solution.py:40
  20.1 0.3 collective-permute-start.7
  20.4 2.8 %collective-permute-done.13.refs_3_ = bf16[64,2560]{1,0:T(8,128)(2,1)S(1)} collective-permute-done((bf16[64,2560]{1,0:T(8,128)(2,1)S(1)}, bf16[64,2560]{1,0:T(8,128)(2,1)S(1)}, u32[]{:S(2)}, u32[]{:S(2)}) %collective-permute-start.13) | collective-permute-done | bytes 327712 | tf_op jit(solution)/shard_map/ppermute | solution.py:40
  23.2 0.2 collective-permute-start.8
  23.4 1.8 %collective-permute-done.10.refs_2_ = bf16[64,2560]{1,0:T(8,128)(2,1)S(1)} collective-permute-done((bf16[64,2560]{1,0:T(8,128)(2,1)S(1)}, bf16[64,2560]{1,0:T(8,128)(2,1)S(1)}, u32[]{:S(2)}, u32[]{:S(2)}) %collective-permute-start.10) | collective-permute-done | bytes 327712 | tf_op jit(solution)/shard_map/ppermute | solution.py:40
  25.2 1.1 collective-permute-start.15
  26.5 1.2 collective-permute-start.12
  27.7 2.5 %collective-permute-done.6.refs_5_ = bf16[64,2560]{1,0:T(8,128)(2,1)S(1)} collective-permute-done((bf16[64,2560]{1,0:T(8,128)(2,1)S(1)}, bf16[64,2560]{1,0:T(8,128)(2,1)S(1)}, u32[]{:S(2)}, u32[]{:S(2)}) %collective-permute-start.6) | collective-permute-done | bytes 327712 | tf_op jit(solution)/shard_map/ppermute | solution.py:40
  30.2 1.2 %collective-permute-start.5 = (bf16[64,2560]{1,0:T(8,128)(2,1)S(1)}, bf16[64,2560]{1,0:T(8,128)(2,1)S(1)}, u32[]{:S(2)}, u32[]{:S(2)}) collective-permute-start(bf16[64,2560]{1,0:T(8,128)(2,1)S(1)} %collective-permute-done.2.refs_2_), channel_id=1, source_target_pairs={{0,65},{1,64},{2,67},{3,66},{4,69},{5,68},{6,71},{7,70},{8,73},{9,... | collective-permute-start | bytes 983048 | tf_op jit(solution)/shard_map/ppermute | solution.py:40
  31.4 0.8 collective-permute-done.7.refs_6_
  32.3 1.2 collective-permute-start.11
  33.5 3.7 %collective-permute-start.9 = (bf16[64,2560]{1,0:T(8,128)(2,1)S(1)}, bf16[64,2560]{1,0:T(8,128)(2,1)S(1)}, u32[]{:S(2)}, u32[]{:S(2)}) collective-permute-start(bf16[64,2560]{1,0:T(8,128)(2,1)S(1)} %collective-permute-done.7.refs_6_), channel_id=1, source_target_pairs={{0,65},{1,64},{2,67},{3,66},{4,69},{5,68},{6,71},{7,70},{8,73},{9,... | collective-permute-start | bytes 983048 | tf_op jit(solution)/shard_map/ppermute | solution.py:40
  37.2 1.5 %collective-permute-start.18 = (bf16[64,2560]{1,0:T(8,128)(2,1)S(1)}, bf16[64,2560]{1,0:T(8,128)(2,1)S(1)}, u32[]{:S(2)}, u32[]{:S(2)}) collective-permute-start(bf16[64,2560]{1,0:T(8,128)(2,1)S(1)} %collective-permute-done.10.refs_2_), channel_id=1, source_target_pairs={{0,2},{1,3},{2,4},{3,5},{4,6},{5,7},{6,0},{7,1},{8,10},{9,11},{10,... | collective-permute-start | bytes 983048 | tf_op jit(solution)/shard_map/ppermute | solution.py:40
  38.7 1.8 %collective-permute-start.16 = (bf16[64,2560]{1,0:T(8,128)(2,1)S(1)}, bf16[64,2560]{1,0:T(8,128)(2,1)S(1)}, u32[]{:S(2)}, u32[]{:S(2)}) collective-permute-start(bf16[64,2560]{1,0:T(8,128)(2,1)S(1)} %collective-permute-done.4.refs_1_), channel_id=1, source_target_pairs={{0,6},{1,7},{2,0},{3,1},{4,2},{5,3},{6,4},{7,5},{8,14},{9,15},{10,... | collective-permute-start | bytes 983048 | tf_op jit(solution)/shard_map/ppermute | solution.py:40
  40.5 1.6 %collective-permute-done.5.refs_4_ = bf16[64,2560]{1,0:T(8,128)(2,1)S(1)} collective-permute-done((bf16[64,2560]{1,0:T(8,128)(2,1)S(1)}, bf16[64,2560]{1,0:T(8,128)(2,1)S(1)}, u32[]{:S(2)}, u32[]{:S(2)}) %collective-permute-start.5) | collective-permute-done | bytes 327712 | tf_op jit(solution)/shard_map/ppermute | solution.py:40
  42.1 1.4 %collective-permute-start.14 = (bf16[64,2560]{1,0:T(8,128)(2,1)S(1)}, bf16[64,2560]{1,0:T(8,128)(2,1)S(1)}, u32[]{:S(2)}, u32[]{:S(2)}) collective-permute-start(bf16[64,2560]{1,0:T(8,128)(2,1)S(1)} %collective-permute-done.4.refs_1_), channel_id=1, source_target_pairs={{0,2},{1,3},{2,4},{3,5},{4,6},{5,7},{6,0},{7,1},{8,10},{9,11},{10,... | collective-permute-start | bytes 983048 | tf_op jit(solution)/shard_map/ppermute | solution.py:40
  43.5 0.8 collective-permute-done.11.refs_3_
  44.2 1.2 %collective-permute-start.17 = (bf16[64,2560]{1,0:T(8,128)(2,1)S(1)}, bf16[64,2560]{1,0:T(8,128)(2,1)S(1)}, u32[]{:S(2)}, u32[]{:S(2)}) collective-permute-start(bf16[64,2560]{1,0:T(8,128)(2,1)S(1)} %collective-permute-done.15.refs_6_), channel_id=1, source_target_pairs={{0,65},{1,64},{2,67},{3,66},{4,69},{5,68},{6,71},{7,70},{8,73},{9,... | collective-permute-start | bytes 983048 | tf_op jit(solution)/shard_map/ppermute | solution.py:40
  45.5 1.7 %shard_map.70.early = f32[1152,256]{1,0:T(8,128)S(1)} custom-call(bf16[1152,5120]{1,0:T(8,128)(2,1)S(1)} %bitcast.3, bf16[64,2560]{1,0:T(8,128)(2,1)S(1)} %get-tuple-element.57.refs_0_, bf16[64,2560]{1,0:T(8,128)(2,1)S(1)} %collective-permute-done.8.refs_1_, bf16[64,2560]{1,0:T(8,128)(2,1)S(1)} %collective-permute-done.10.refs_2_, ...), custom_call_target="tpu_custom_call" | custom-call | flops 20000000000 | bytes 20000000 | tf_op jit(solution)/shard_map/pallas_call | solution.py:69
  47.2 1.0 collective-permute-done.18.refs_2_
  48.1 2.7 %collective-permute-start.20 = (bf16[64,2560]{1,0:T(8,128)(2,1)S(1)}, bf16[64,2560]{1,0:T(8,128)(2,1)S(1)}, u32[]{:S(2)}, u32[]{:S(2)}) collective-permute-start(bf16[64,2560]{1,0:T(8,128)(2,1)S(1)} %collective-permute-done.8.refs_1_), channel_id=1, source_target_pairs={{0,6},{1,7},{2,0},{3,1},{4,2},{5,3},{6,4},{7,5},{8,14},{9,15},{10,... | collective-permute-start | bytes 983048 | tf_op jit(solution)/shard_map/ppermute | solution.py:40
  50.9 3.4 %shard_map.69 = (f32[1152,512]{1,0:T(8,128)S(1)}, bf16[512,2560]{1,0:T(8,128)(2,1)S(1)}, f32[8,512]{1,0:T(8,128)S(1)}) custom-call(s32[1,512]{1,0:T(1,128)S(1)} %shard_map.68.ids, bf16[1152,2560]{1,0:T(8,128)(2,1)S(1)} %bitcast.1, bf16[64,2560]{1,0:T(8,128)(2,1)S(1)} %copy-done, bf16[64,2560]{1,0:T(8,128)(2,1)S(1)} %collective-permute-done.1.refs_1_, ...), custom_call_target="tpu_custom_call" | custom-call | flops 20000000000 | bytes 20000000 | tf_op jit(solution)/shard_map/pallas_call | solution.py:69
  54.2 1.9 %collective-permute-start.21 = (bf16[64,2560]{1,0:T(8,128)(2,1)S(1)}, bf16[64,2560]{1,0:T(8,128)(2,1)S(1)}, u32[]{:S(2)}, u32[]{:S(2)}) collective-permute-start(bf16[64,2560]{1,0:T(8,128)(2,1)S(1)} %collective-permute-done.18.refs_2_), channel_id=1, source_target_pairs={{0,65},{1,64},{2,67},{3,66},{4,69},{5,68},{6,71},{7,70},{8,73},{9,... | collective-permute-start | bytes 983048 | tf_op jit(solution)/shard_map/ppermute | solution.py:40
  56.1 3.3 %shard_map.71 = (f32[1152,256]{1,0:T(8,128)S(1)}, f32[8,512]{1,0:T(8,128)S(1)}) custom-call(s32[1,512]{1,0:T(1,128)S(1)} %shard_map.68.ids, f32[8,512]{1,0:T(8,128)S(1)} %get-tuple-element.55.student_stats, f32[1152,256]{1,0:T(8,128)S(1)} %shard_map.70.early, bf16[1152,5120]{1,0:T(8,128)(2,1)S(1)} %bitcast.3, ...), custom_call_target="tpu_custom_call" | custom-call | flops 20000000000 | bytes 20000000 | tf_op jit(solution)/shard_map/pallas_call | solution.py:69
  59.4 3.4 %collective-permute-done.21.refs_3_ = bf16[64,2560]{1,0:T(8,128)(2,1)S(1)} collective-permute-done((bf16[64,2560]{1,0:T(8,128)(2,1)S(1)}, bf16[64,2560]{1,0:T(8,128)(2,1)S(1)}, u32[]{:S(2)}, u32[]{:S(2)}) %collective-permute-start.21) | collective-permute-done | bytes 327712 | tf_op jit(solution)/shard_map/ppermute | solution.py:40
  62.8 1.9 %shard_map.72.refs_0_ = f32[8,512]{1,0:T(8,128)S(1)} custom-call(s32[1,512]{1,0:T(1,128)S(1)} %shard_map.68.ids, f32[8,512]{1,0:T(8,128)S(1)} %get-tuple-element.63.first_stats, bf16[1152,5120]{1,0:T(8,128)(2,1)S(1)} %bitcast.3, f32[1152,256]{1,0:T(8,128)S(1)} %get-tuple-element.64.logits, bf16[64,2560]{1,0:T(8,128)(2,1)S(1)} %collective-permute-done.19.refs_0_, ...), custom_call_target="tpu_custom_call" | custom-call | flops 20000000000 | bytes 20000000 | tf_op jit(solution)/shard_map/pallas_call | solution.py:69
  64.7 1.9 %collective-permute-start.24 = (f32[8,512]{1,0:T(8,128)S(1)}, f32[8,512]{1,0:T(8,128)S(1)}, u32[]{:S(2)}, u32[]{:S(2)}) collective-permute-start(f32[8,512]{1,0:T(8,128)S(1)} %shard_map.72.refs_0_), channel_id=1, source_target_pairs={{0,4},{1,5},{2,6},{3,7},{4,0},{5,1},{6,2},{7,3},{8,12},{9,13},{10,... | collective-permute-start | bytes 49160 | tf_op jit(solution)/shard_map/ppermute | solution.py:40
  66.5 1.5 %collective-permute-start.23 = (f32[8,512]{1,0:T(8,128)S(1)}, f32[8,512]{1,0:T(8,128)S(1)}, u32[]{:S(2)}, u32[]{:S(2)}) collective-permute-start(f32[8,512]{1,0:T(8,128)S(1)} %shard_map.72.refs_0_), channel_id=1, source_target_pairs={{0,6},{1,7},{2,0},{3,1},{4,2},{5,3},{6,4},{7,5},{8,14},{9,15},{10,... | collective-permute-start | bytes 49160 | tf_op jit(solution)/shard_map/ppermute | solution.py:40
  68.0 0.8 collective-permute-start.22
  68.8 1.2 collective-permute-done.24.refs_3_
  70.0 0.7 collective-permute-done.23.refs_2_
  70.7 2.3 %collective-permute-done.22.refs_1_ = f32[8,512]{1,0:T(8,128)S(1)} collective-permute-done((f32[8,512]{1,0:T(8,128)S(1)}, f32[8,512]{1,0:T(8,128)S(1)}, u32[]{:S(2)}, u32[]{:S(2)}) %collective-permute-start.22) | collective-permute-done | bytes 16416 | tf_op jit(solution)/shard_map/ppermute | solution.py:40
  73.1 1.5 %collective-permute-start.25 = (f32[8,512]{1,0:T(8,128)S(1)}, f32[8,512]{1,0:T(8,128)S(1)}, u32[]{:S(2)}, u32[]{:S(2)}) collective-permute-start(f32[8,512]{1,0:T(8,128)S(1)} %shard_map.73.refs_0_), channel_id=1, source_target_pairs={{0,65},{1,64},{2,67},{3,66},{4,69},{5,68},{6,71},{7,70},{8,73},{9,... | collective-permute-start | bytes 49160 | tf_op jit(solution)/shard_map/ppermute | solution.py:40
  74.6 3.5 %collective-permute-done.25.refs_1_ = f32[8,512]{1,0:T(8,128)S(1)} collective-permute-done((f32[8,512]{1,0:T(8,128)S(1)}, f32[8,512]{1,0:T(8,128)S(1)}, u32[]{:S(2)}, u32[]{:S(2)}) %collective-permute-start.25) | collective-permute-done | bytes 16416 | tf_op jit(solution)/shard_map/ppermute | solution.py:40
  78.2 0.6 shard_map.75
  78.9 1.7 %shard_map.76.own = f32[576,2560]{1,0:T(8,128)S(1)} custom-call(bf16[576,512]{1,0:T(8,128)(2,1)S(1)} %get-tuple-element.73.grad, bf16[512,2560]{1,0:T(8,128)(2,1)S(1)} %get-tuple-element.72.hidden), custom_call_target="tpu_custom_call" | custom-call | flops 1000000000 | bytes 1000000 | tf_op jit(solution)/shard_map/pallas_call | solution.py:69
  80.6 0.3 collective-permute-done.26.grad
  80.9 1.1 shard_map.77
  82.1 4.1 %collective-permute-start.29 = (bf16[144,2560]{1,0:T(8,128)(2,1)S(1)}, bf16[144,2560]{1,0:T(8,128)(2,1)S(1)}, u32[]{:S(2)}, u32[]{:S(2)}) collective-permute-start(bf16[144,2560]{1,0:T(8,128)(2,1)S(1)} %get-tuple-element.81), channel_id=1, source_target_pairs={{0,48},{1,49},{2,50},{3,51},{4,52},{5,53},{6,54},{7,55},{8,56},{9,... | collective-permute-start | bytes 2211848 | tf_op jit(solution)/shard_map/ppermute | solution.py:40
  86.2 2.2 %shard_map.79 = (bf16[128,2560]{1,0:T(8,128)(2,1)S(1)}, bf16[128,2560]{1,0:T(8,128)(2,1)S(1)}) custom-call(s32[1,512]{1,0:T(1,128)S(1)} %shard_map.68.ids, f32[8,512]{1,0:T(8,128)S(1)} %shard_map.74.total, f32[1152,512]{1,0:T(8,128)S(1)} %get-tuple-element.70.logits, bf16[1152,2560]{1,0:T(8,128)(2,1)S(1)} %bitcast.1), custom_call_target="tpu_custom_call" | custom-call | flops 20000000000 | bytes 20000000 | tf_op jit(solution)/shard_map/pallas_call | solution.py:69
  88.4 0.3 collective-permute-start.33
  88.7 1.8 %collective-permute-start.34 = (bf16[128,2560]{1,0:T(8,128)(2,1)S(1)}, bf16[128,2560]{1,0:T(8,128)(2,1)S(1)}, u32[]{:S(2)}, u32[]{:S(2)}) collective-permute-start(bf16[128,2560]{1,0:T(8,128)(2,1)S(1)} %get-tuple-element.88), channel_id=1, source_target_pairs={{0,2},{1,3},{2,4},{3,5},{4,6},{5,7},{6,0},{7,1},{8,10},{9,11},{10,... | collective-permute-start | bytes 1966088 | tf_op jit(solution)/shard_map/ppermute | solution.py:40
  90.5 0.8 shard_map.80
  91.2 1.6 %collective-permute-done.28.far_near = bf16[72,2560]{1,0:T(8,128)(2,1)S(1)} collective-permute-done((bf16[72,2560]{1,0:T(8,128)(2,1)S(1)}, bf16[72,2560]{1,0:T(8,128)(2,1)S(1)}, u32[]{:S(2)}, u32[]{:S(2)}) %collective-permute-start.28) | collective-permute-done | bytes 368672 | tf_op jit(solution)/shard_map/ppermute | solution.py:40
  92.8 2.1 %shard_map.78 = (f32[64,2560]{1,0:T(8,128)S(1)}, f32[64,2560]{1,0:T(8,128)S(1)}, f32[64,2560]{1,0:T(8,128)S(1)}, bf16[64,2560]{1,0:T(8,128)(2,1)S(1)}) custom-call(s32[1,512]{1,0:T(1,128)S(1)} %shard_map.68.ids, f32[8,512]{1,0:T(8,128)S(1)} %shard_map.74.total, f32[1152,512]{1,0:T(8,128)S(1)} %get-tuple-element.70.logits, bf16[1152,2560]{1,0:T(8,128)(2,1)S(1)} %bitcast.1), custom_call_target="tpu_custom_call" | custom-call | flops 1000000000 | bytes 1000000 | tf_op jit(solution)/shard_map/pallas_call | solution.py:69
  95.0 1.5 %collective-permute-start.35 = (bf16[64,2560]{1,0:T(8,128)(2,1)S(1)}, bf16[64,2560]{1,0:T(8,128)(2,1)S(1)}, u32[]{:S(2)}, u32[]{:S(2)}) collective-permute-start(bf16[64,2560]{1,0:T(8,128)(2,1)S(1)} %get-tuple-element.93), channel_id=1, source_target_pairs={{0,65},{1,64},{2,67},{3,66},{4,69},{5,68},{6,71},{7,70},{8,73},{9,... | collective-permute-start | bytes 983048 | tf_op jit(solution)/shard_map/ppermute | solution.py:40
  96.5 5.9 %collective-permute-done.29.lefts = bf16[144,2560]{1,0:T(8,128)(2,1)S(1)} collective-permute-done((bf16[144,2560]{1,0:T(8,128)(2,1)S(1)}, bf16[144,2560]{1,0:T(8,128)(2,1)S(1)}, u32[]{:S(2)}, u32[]{:S(2)}) %collective-permute-start.29) | collective-permute-done | bytes 737312 | tf_op jit(solution)/shard_map/ppermute | solution.py:40
  102.3 3.4 %collective-permute-done.30.rights = bf16[144,2560]{1,0:T(8,128)(2,1)S(1)} collective-permute-done((bf16[144,2560]{1,0:T(8,128)(2,1)S(1)}, bf16[144,2560]{1,0:T(8,128)(2,1)S(1)}, u32[]{:S(2)}, u32[]{:S(2)}) %collective-permute-start.30) | collective-permute-done | bytes 737312 | tf_op jit(solution)/shard_map/ppermute | solution.py:40
  105.8 0.2 shard_map.81
  106.0 1.7 %collective-permute-start.32 = (bf16[72,2560]{1,0:T(8,128)(2,1)S(1)}, bf16[72,2560]{1,0:T(8,128)(2,1)S(1)}, u32[]{:S(2)}, u32[]{:S(2)}) collective-permute-start(bf16[72,2560]{1,0:T(8,128)(2,1)S(1)} %get-tuple-element.86), channel_id=1, source_target_pairs={{0,64},{1,65},{2,66},{3,67},{4,68},{5,69},{6,70},{7,71},{8,72},{9,... | collective-permute-start | bytes 1105928 | tf_op jit(solution)/shard_map/ppermute | solution.py:40
  107.9 1.7 %collective-permute-start.36 = (bf16[64,2560]{1,0:T(8,128)(2,1)S(1)}, bf16[64,2560]{1,0:T(8,128)(2,1)S(1)}, u32[]{:S(2)}, u32[]{:S(2)}) collective-permute-start(bf16[64,2560]{1,0:T(8,128)(2,1)S(1)} %get-tuple-element.94), channel_id=1, source_target_pairs={{0,4},{1,5},{2,6},{3,7},{4,0},{5,1},{6,2},{7,3},{8,12},{9,13},{10,... | collective-permute-start | bytes 983048 | tf_op jit(solution)/shard_map/ppermute | solution.py:40
  109.6 1.4 %collective-permute-start.37 = (bf16[64,2560]{1,0:T(8,128)(2,1)S(1)}, bf16[64,2560]{1,0:T(8,128)(2,1)S(1)}, u32[]{:S(2)}, u32[]{:S(2)}) collective-permute-start(bf16[64,2560]{1,0:T(8,128)(2,1)S(1)} %get-tuple-element.95), channel_id=1, source_target_pairs={{0,65},{1,64},{2,67},{3,66},{4,69},{5,68},{6,71},{7,70},{8,73},{9,... | collective-permute-start | bytes 983048 | tf_op jit(solution)/shard_map/ppermute | solution.py:40
  111.1 7.1 %collective-permute-done.31.far = bf16[72,2560]{1,0:T(8,128)(2,1)S(1)} collective-permute-done((bf16[72,2560]{1,0:T(8,128)(2,1)S(1)}, bf16[72,2560]{1,0:T(8,128)(2,1)S(1)}, u32[]{:S(2)}, u32[]{:S(2)}) %collective-permute-start.31) | collective-permute-done | bytes 368672 | tf_op jit(solution)/shard_map/ppermute | solution.py:40
  118.2 1.0 shard_map.82
  119.2 0.9 shard_map.84
  (46 shorter events, 1.2 us)
Async XLA Ops:
  0.6 19.5 %collective-permute-start.2 = (bf16[64,2560]{1,0:T(8,128)(2,1)}, bf16[64,2560]{1,0:T(8,128)(2,1)S(1)}, u32[]{:S(2)}, u32[]{:S(2)}) collective-permute-start(bf16[64,2560]{1,0:T(8,128)(2,1)} %refs_0_.1), channel_id=1, source_target_pairs={{0,2},{1,3},{2,4},{3,5},{4,6},{5,7},{6,0},{7,1},{8,10},{9,11},{10,... | collective-permute-start | bytes 983048 | tf_op jit(solution)/shard_map/ppermute | solution.py:40
  2.3 13.1 %collective-permute-start.1 = (bf16[64,2560]{1,0:T(8,128)(2,1)}, bf16[64,2560]{1,0:T(8,128)(2,1)S(1)}, u32[]{:S(2)}, u32[]{:S(2)}) collective-permute-start(bf16[64,2560]{1,0:T(8,128)(2,1)} %refs_0_.1), channel_id=1, source_target_pairs={{0,65},{1,64},{2,67},{3,66},{4,69},{5,68},{6,71},{7,70},{8,73},{9,... | collective-permute-start | bytes 983048 | tf_op jit(solution)/shard_map/ppermute | solution.py:40
  5.3 13.1 %collective-permute-start.3 = (bf16[64,2560]{1,0:T(8,128)(2,1)}, bf16[64,2560]{1,0:T(8,128)(2,1)S(1)}, u32[]{:S(2)}, u32[]{:S(2)}) collective-permute-start(bf16[64,2560]{1,0:T(8,128)(2,1)} %refs_0_.1), channel_id=1, source_target_pairs={{0,6},{1,7},{2,0},{3,1},{4,2},{5,3},{6,4},{7,5},{8,14},{9,15},{10,... | collective-permute-start | bytes 983048 | tf_op jit(solution)/shard_map/ppermute | solution.py:40
  7.0 6.0 %collective-permute-start = (s32[512]{0:T(512)}, s32[512]{0:T(512)S(1)}, u32[]{:S(2)}, u32[]{:S(2)}) collective-permute-start(s32[512]{0:T(512)} %own.1), channel_id=1, source_target_pairs={{0,65},{1,64},{2,67},{3,66},{4,69},{5,68},{6,71},{7,70},{8,73},{9,... | collective-permute-start | bytes 6152 | tf_op jit(solution)/shard_map/ppermute | solution.py:40
  8.3 37.2 %slice-start.2 = ((s8[11796480]{0:T(1024)(128)(4,1)}), s8[4194304]{0:T(1024)(128)(4,1)S(1)}, s32[]{:S(2)}) async-start(s8[11796480]{0:T(1024)(128)(4,1)} %bitcast.2), calls=%async_computation.2 | async-start | bytes 8388608
  8.3 37.1 %slice-start.3 = ((s8[11796480]{0:T(1024)(128)(4,1)}), s8[4194304]{0:T(1024)(128)(4,1)S(1)}, s32[]{:S(2)}) async-start(s8[11796480]{0:T(1024)(128)(4,1)} %bitcast.2), calls=%async_computation.3 | async-start | bytes 8388608
  8.3 37.1 %slice-start.4 = ((s8[11796480]{0:T(1024)(128)(4,1)}), s8[3407872]{0:T(1024)(128)(4,1)S(1)}, s32[]{:S(2)}) async-start(s8[11796480]{0:T(1024)(128)(4,1)} %bitcast.2), calls=%async_computation.4 | async-start | bytes 6815744
  8.3 14.8 %collective-permute-start.13 = (bf16[64,2560]{1,0:T(8,128)(2,1)S(1)}, bf16[64,2560]{1,0:T(8,128)(2,1)S(1)}, u32[]{:S(2)}, u32[]{:S(2)}) collective-permute-start(bf16[64,2560]{1,0:T(8,128)(2,1)S(1)} %get-tuple-element.58.refs_0_), channel_id=1, source_target_pairs={{0,6},{1,7},{2,0},{3,1},{4,2},{5,3},{6,4},{7,5},{8,14},{9,15},{10,... | collective-permute-start | bytes 983048 | tf_op jit(solution)/shard_map/ppermute | solution.py:40
  13.0 0.7 copy-start.1
  13.9 37.0 %slice-start = ((s8[5898240]{0:T(1024)(128)(4,1)}), s8[4194304]{0:T(1024)(128)(4,1)S(1)}, s32[]{:S(2)}) async-start(s8[5898240]{0:T(1024)(128)(4,1)} %bitcast), calls=%async_computation | async-start | bytes 8388608
  13.9 37.0 %slice-start.1 = ((s8[5898240]{0:T(1024)(128)(4,1)}), s8[1703936]{0:T(1024)(128)(4,1)S(1)}, s32[]{:S(2)}) async-start(s8[5898240]{0:T(1024)(128)(4,1)} %bitcast), calls=%async_computation.1 | async-start | bytes 3407872
  13.9 37.0 %copy-start = (bf16[64,2560]{1,0:T(8,128)(2,1)S(1)}, bf16[64,2560]{1,0:T(8,128)(2,1)}, u32[]{:S(2)}) copy-start(bf16[64,2560]{1,0:T(8,128)(2,1)} %refs_0_.1) | copy-start | bytes 983044
  13.9 11.4 %collective-permute-start.10 = (bf16[64,2560]{1,0:T(8,128)(2,1)S(1)}, bf16[64,2560]{1,0:T(8,128)(2,1)S(1)}, u32[]{:S(2)}, u32[]{:S(2)}) collective-permute-start(bf16[64,2560]{1,0:T(8,128)(2,1)S(1)} %get-tuple-element.57.refs_0_), channel_id=1, source_target_pairs={{0,2},{1,3},{2,4},{3,5},{4,6},{5,7},{6,0},{7,1},{8,10},{9,11},{10,... | collective-permute-start | bytes 983048 | tf_op jit(solution)/shard_map/ppermute | solution.py:40
  15.4 11.1 %collective-permute-start.4 = (bf16[64,2560]{1,0:T(8,128)(2,1)S(1)}, bf16[64,2560]{1,0:T(8,128)(2,1)S(1)}, u32[]{:S(2)}, u32[]{:S(2)}) collective-permute-start(bf16[64,2560]{1,0:T(8,128)(2,1)S(1)} %get-tuple-element.58.refs_0_), channel_id=1, source_target_pairs={{0,65},{1,64},{2,67},{3,66},{4,69},{5,68},{6,71},{7,70},{8,73},{9,... | collective-permute-start | bytes 983048 | tf_op jit(solution)/shard_map/ppermute | solution.py:40
  18.3 11.8 %collective-permute-start.6 = (bf16[64,2560]{1,0:T(8,128)(2,1)S(1)}, bf16[64,2560]{1,0:T(8,128)(2,1)S(1)}, u32[]{:S(2)}, u32[]{:S(2)}) collective-permute-start(bf16[64,2560]{1,0:T(8,128)(2,1)S(1)} %collective-permute-done.1.refs_1_), channel_id=1, source_target_pairs={{0,6},{1,7},{2,0},{3,1},{4,2},{5,3},{6,4},{7,5},{8,14},{9,15},{10,... | collective-permute-start | bytes 983048 | tf_op jit(solution)/shard_map/ppermute | solution.py:40
  20.1 12.2 %collective-permute-start.7 = (bf16[64,2560]{1,0:T(8,128)(2,1)S(1)}, bf16[64,2560]{1,0:T(8,128)(2,1)S(1)}, u32[]{:S(2)}, u32[]{:S(2)}) collective-permute-start(bf16[64,2560]{1,0:T(8,128)(2,1)S(1)} %collective-permute-done.2.refs_2_), channel_id=1, source_target_pairs={{0,2},{1,3},{2,4},{3,5},{4,6},{5,7},{6,0},{7,1},{8,10},{9,11},{10,... | collective-permute-start | bytes 983048 | tf_op jit(solution)/shard_map/ppermute | solution.py:40
  23.2 10.4 %collective-permute-start.8 = (bf16[64,2560]{1,0:T(8,128)(2,1)S(1)}, bf16[64,2560]{1,0:T(8,128)(2,1)S(1)}, u32[]{:S(2)}, u32[]{:S(2)}) collective-permute-start(bf16[64,2560]{1,0:T(8,128)(2,1)S(1)} %get-tuple-element.57.refs_0_), channel_id=1, source_target_pairs={{0,65},{1,64},{2,67},{3,66},{4,69},{5,68},{6,71},{7,70},{8,73},{9,... | collective-permute-start | bytes 983048 | tf_op jit(solution)/shard_map/ppermute | solution.py:40
  25.2 12.0 %collective-permute-start.15 = (bf16[64,2560]{1,0:T(8,128)(2,1)S(1)}, bf16[64,2560]{1,0:T(8,128)(2,1)S(1)}, u32[]{:S(2)}, u32[]{:S(2)}) collective-permute-start(bf16[64,2560]{1,0:T(8,128)(2,1)S(1)} %collective-permute-done.13.refs_3_), channel_id=1, source_target_pairs={{0,6},{1,7},{2,0},{3,1},{4,2},{5,3},{6,4},{7,5},{8,14},{9,15},{10,... | collective-permute-start | bytes 983048 | tf_op jit(solution)/shard_map/ppermute | solution.py:40
  26.5 12.2 %collective-permute-start.12 = (bf16[64,2560]{1,0:T(8,128)(2,1)S(1)}, bf16[64,2560]{1,0:T(8,128)(2,1)S(1)}, u32[]{:S(2)}, u32[]{:S(2)}) collective-permute-start(bf16[64,2560]{1,0:T(8,128)(2,1)S(1)} %get-tuple-element.58.refs_0_), channel_id=1, source_target_pairs={{0,2},{1,3},{2,4},{3,5},{4,6},{5,7},{6,0},{7,1},{8,10},{9,11},{10,... | collective-permute-start | bytes 983048 | tf_op jit(solution)/shard_map/ppermute | solution.py:40
  30.2 11.9 %collective-permute-start.5 = (bf16[64,2560]{1,0:T(8,128)(2,1)S(1)}, bf16[64,2560]{1,0:T(8,128)(2,1)S(1)}, u32[]{:S(2)}, u32[]{:S(2)}) collective-permute-start(bf16[64,2560]{1,0:T(8,128)(2,1)S(1)} %collective-permute-done.2.refs_2_), channel_id=1, source_target_pairs={{0,65},{1,64},{2,67},{3,66},{4,69},{5,68},{6,71},{7,70},{8,73},{9,... | collective-permute-start | bytes 983048 | tf_op jit(solution)/shard_map/ppermute | solution.py:40
  32.3 12.0 %collective-permute-start.11 = (bf16[64,2560]{1,0:T(8,128)(2,1)S(1)}, bf16[64,2560]{1,0:T(8,128)(2,1)S(1)}, u32[]{:S(2)}, u32[]{:S(2)}) collective-permute-start(bf16[64,2560]{1,0:T(8,128)(2,1)S(1)} %get-tuple-element.57.refs_0_), channel_id=1, source_target_pairs={{0,6},{1,7},{2,0},{3,1},{4,2},{5,3},{6,4},{7,5},{8,14},{9,15},{10,... | collective-permute-start | bytes 983048 | tf_op jit(solution)/shard_map/ppermute | solution.py:40
  33.5 17.3 %collective-permute-start.9 = (bf16[64,2560]{1,0:T(8,128)(2,1)S(1)}, bf16[64,2560]{1,0:T(8,128)(2,1)S(1)}, u32[]{:S(2)}, u32[]{:S(2)}) collective-permute-start(bf16[64,2560]{1,0:T(8,128)(2,1)S(1)} %collective-permute-done.7.refs_6_), channel_id=1, source_target_pairs={{0,65},{1,64},{2,67},{3,66},{4,69},{5,68},{6,71},{7,70},{8,73},{9,... | collective-permute-start | bytes 983048 | tf_op jit(solution)/shard_map/ppermute | solution.py:40
  37.2 10.9 %collective-permute-start.18 = (bf16[64,2560]{1,0:T(8,128)(2,1)S(1)}, bf16[64,2560]{1,0:T(8,128)(2,1)S(1)}, u32[]{:S(2)}, u32[]{:S(2)}) collective-permute-start(bf16[64,2560]{1,0:T(8,128)(2,1)S(1)} %collective-permute-done.10.refs_2_), channel_id=1, source_target_pairs={{0,2},{1,3},{2,4},{3,5},{4,6},{5,7},{6,0},{7,1},{8,10},{9,11},{10,... | collective-permute-start | bytes 983048 | tf_op jit(solution)/shard_map/ppermute | solution.py:40
  38.7 15.5 %collective-permute-start.16 = (bf16[64,2560]{1,0:T(8,128)(2,1)S(1)}, bf16[64,2560]{1,0:T(8,128)(2,1)S(1)}, u32[]{:S(2)}, u32[]{:S(2)}) collective-permute-start(bf16[64,2560]{1,0:T(8,128)(2,1)S(1)} %collective-permute-done.4.refs_1_), channel_id=1, source_target_pairs={{0,6},{1,7},{2,0},{3,1},{4,2},{5,3},{6,4},{7,5},{8,14},{9,15},{10,... | collective-permute-start | bytes 983048 | tf_op jit(solution)/shard_map/ppermute | solution.py:40
  42.1 14.0 %collective-permute-start.14 = (bf16[64,2560]{1,0:T(8,128)(2,1)S(1)}, bf16[64,2560]{1,0:T(8,128)(2,1)S(1)}, u32[]{:S(2)}, u32[]{:S(2)}) collective-permute-start(bf16[64,2560]{1,0:T(8,128)(2,1)S(1)} %collective-permute-done.4.refs_1_), channel_id=1, source_target_pairs={{0,2},{1,3},{2,4},{3,5},{4,6},{5,7},{6,0},{7,1},{8,10},{9,11},{10,... | collective-permute-start | bytes 983048 | tf_op jit(solution)/shard_map/ppermute | solution.py:40
  44.2 11.9 %collective-permute-start.17 = (bf16[64,2560]{1,0:T(8,128)(2,1)S(1)}, bf16[64,2560]{1,0:T(8,128)(2,1)S(1)}, u32[]{:S(2)}, u32[]{:S(2)}) collective-permute-start(bf16[64,2560]{1,0:T(8,128)(2,1)S(1)} %collective-permute-done.15.refs_6_), channel_id=1, source_target_pairs={{0,65},{1,64},{2,67},{3,66},{4,69},{5,68},{6,71},{7,70},{8,73},{9,... | collective-permute-start | bytes 983048 | tf_op jit(solution)/shard_map/ppermute | solution.py:40
  48.1 11.3 %collective-permute-start.20 = (bf16[64,2560]{1,0:T(8,128)(2,1)S(1)}, bf16[64,2560]{1,0:T(8,128)(2,1)S(1)}, u32[]{:S(2)}, u32[]{:S(2)}) collective-permute-start(bf16[64,2560]{1,0:T(8,128)(2,1)S(1)} %collective-permute-done.8.refs_1_), channel_id=1, source_target_pairs={{0,6},{1,7},{2,0},{3,1},{4,2},{5,3},{6,4},{7,5},{8,14},{9,15},{10,... | collective-permute-start | bytes 983048 | tf_op jit(solution)/shard_map/ppermute | solution.py:40
  50.8 8.6 %collective-permute-start.19 = (bf16[64,2560]{1,0:T(8,128)(2,1)S(1)}, bf16[64,2560]{1,0:T(8,128)(2,1)S(1)}, u32[]{:S(2)}, u32[]{:S(2)}) collective-permute-start(bf16[64,2560]{1,0:T(8,128)(2,1)S(1)} %collective-permute-done.8.refs_1_), channel_id=1, source_target_pairs={{0,2},{1,3},{2,4},{3,5},{4,6},{5,7},{6,0},{7,1},{8,10},{9,11},{10,... | collective-permute-start | bytes 983048 | tf_op jit(solution)/shard_map/ppermute | solution.py:40
  54.2 8.5 %collective-permute-start.21 = (bf16[64,2560]{1,0:T(8,128)(2,1)S(1)}, bf16[64,2560]{1,0:T(8,128)(2,1)S(1)}, u32[]{:S(2)}, u32[]{:S(2)}) collective-permute-start(bf16[64,2560]{1,0:T(8,128)(2,1)S(1)} %collective-permute-done.18.refs_2_), channel_id=1, source_target_pairs={{0,65},{1,64},{2,67},{3,66},{4,69},{5,68},{6,71},{7,70},{8,73},{9,... | collective-permute-start | bytes 983048 | tf_op jit(solution)/shard_map/ppermute | solution.py:40
  64.7 5.3 %collective-permute-start.24 = (f32[8,512]{1,0:T(8,128)S(1)}, f32[8,512]{1,0:T(8,128)S(1)}, u32[]{:S(2)}, u32[]{:S(2)}) collective-permute-start(f32[8,512]{1,0:T(8,128)S(1)} %shard_map.72.refs_0_), channel_id=1, source_target_pairs={{0,4},{1,5},{2,6},{3,7},{4,0},{5,1},{6,2},{7,3},{8,12},{9,13},{10,... | collective-permute-start | bytes 49160 | tf_op jit(solution)/shard_map/ppermute | solution.py:40
  66.5 4.2 %collective-permute-start.23 = (f32[8,512]{1,0:T(8,128)S(1)}, f32[8,512]{1,0:T(8,128)S(1)}, u32[]{:S(2)}, u32[]{:S(2)}) collective-permute-start(f32[8,512]{1,0:T(8,128)S(1)} %shard_map.72.refs_0_), channel_id=1, source_target_pairs={{0,6},{1,7},{2,0},{3,1},{4,2},{5,3},{6,4},{7,5},{8,14},{9,15},{10,... | collective-permute-start | bytes 49160 | tf_op jit(solution)/shard_map/ppermute | solution.py:40
  68.0 4.9 %collective-permute-start.22 = (f32[8,512]{1,0:T(8,128)S(1)}, f32[8,512]{1,0:T(8,128)S(1)}, u32[]{:S(2)}, u32[]{:S(2)}) collective-permute-start(f32[8,512]{1,0:T(8,128)S(1)} %shard_map.72.refs_0_), channel_id=1, source_target_pairs={{0,2},{1,3},{2,4},{3,5},{4,6},{5,7},{6,0},{7,1},{8,10},{9,11},{10,... | collective-permute-start | bytes 49160 | tf_op jit(solution)/shard_map/ppermute | solution.py:40
  68.8 12.1 %collective-permute-start.27 = (bf16[512,2560]{1,0:T(8,128)(2,1)S(1)}, bf16[512,2560]{1,0:T(8,128)(2,1)S(1)}, u32[]{:S(2)}, u32[]{:S(2)}) collective-permute-start(bf16[512,2560]{1,0:T(8,128)(2,1)S(1)} %get-tuple-element.72.hidden), channel_id=1, source_target_pairs={{0,8},{1,9},{2,10},{3,11},{4,12},{5,13},{6,14},{7,15},{8,0},{9,1},... | collective-permute-start | bytes 7864328 | tf_op jit(solution)/shard_map/ppermute | solution.py:40
  73.1 5.0 %collective-permute-start.25 = (f32[8,512]{1,0:T(8,128)S(1)}, f32[8,512]{1,0:T(8,128)S(1)}, u32[]{:S(2)}, u32[]{:S(2)}) collective-permute-start(f32[8,512]{1,0:T(8,128)S(1)} %shard_map.73.refs_0_), channel_id=1, source_target_pairs={{0,65},{1,64},{2,67},{3,66},{4,69},{5,68},{6,71},{7,70},{8,73},{9,... | collective-permute-start | bytes 49160 | tf_op jit(solution)/shard_map/ppermute | solution.py:40
  78.8 2.1 %collective-permute-start.26 = (bf16[576,512]{1,0:T(8,128)(2,1)S(1)}, bf16[576,512]{1,0:T(8,128)(2,1)S(1)}, u32[]{:S(2)}, u32[]{:S(2)}) collective-permute-start(bf16[576,512]{1,0:T(8,128)(2,1)S(1)} %get-tuple-element.71), channel_id=1, source_target_pairs={{0,8},{1,9},{2,10},{3,11},{4,12},{5,13},{6,14},{7,15},{8,0},{9,1},... | collective-permute-start | bytes 1769480 | tf_op jit(solution)/shard_map/ppermute | solution.py:40
  82.0 10.8 %collective-permute-start.28 = (bf16[72,2560]{1,0:T(8,128)(2,1)S(1)}, bf16[72,2560]{1,0:T(8,128)(2,1)S(1)}, u32[]{:S(2)}, u32[]{:S(2)}) collective-permute-start(bf16[72,2560]{1,0:T(8,128)(2,1)S(1)} %get-tuple-element.74), channel_id=1, source_target_pairs={{0,64},{1,65},{2,66},{3,67},{4,68},{5,69},{6,70},{7,71},{8,72},{9,... | collective-permute-start | bytes 1105928 | tf_op jit(solution)/shard_map/ppermute | solution.py:40
  82.1 20.2 %collective-permute-start.29 = (bf16[144,2560]{1,0:T(8,128)(2,1)S(1)}, bf16[144,2560]{1,0:T(8,128)(2,1)S(1)}, u32[]{:S(2)}, u32[]{:S(2)}) collective-permute-start(bf16[144,2560]{1,0:T(8,128)(2,1)S(1)} %get-tuple-element.81), channel_id=1, source_target_pairs={{0,48},{1,49},{2,50},{3,51},{4,52},{5,53},{6,54},{7,55},{8,56},{9,... | collective-permute-start | bytes 2211848 | tf_op jit(solution)/shard_map/ppermute | solution.py:40
  86.2 19.5 %collective-permute-start.30 = (bf16[144,2560]{1,0:T(8,128)(2,1)S(1)}, bf16[144,2560]{1,0:T(8,128)(2,1)S(1)}, u32[]{:S(2)}, u32[]{:S(2)}) collective-permute-start(bf16[144,2560]{1,0:T(8,128)(2,1)S(1)} %get-tuple-element.82), channel_id=1, source_target_pairs={{0,16},{1,17},{2,18},{3,19},{4,20},{5,21},{6,22},{7,23},{8,24},{9,... | collective-permute-start | bytes 2211848 | tf_op jit(solution)/shard_map/ppermute | solution.py:40
  88.4 19.4 %collective-permute-start.33 = (bf16[128,2560]{1,0:T(8,128)(2,1)S(1)}, bf16[128,2560]{1,0:T(8,128)(2,1)S(1)}, u32[]{:S(2)}, u32[]{:S(2)}) collective-permute-start(bf16[128,2560]{1,0:T(8,128)(2,1)S(1)} %get-tuple-element.78), channel_id=1, source_target_pairs={{0,6},{1,7},{2,0},{3,1},{4,2},{5,3},{6,4},{7,5},{8,14},{9,15},{10,... | collective-permute-start | bytes 1966088 | tf_op jit(solution)/shard_map/ppermute | solution.py:40
  88.7 19.1 %collective-permute-start.34 = (bf16[128,2560]{1,0:T(8,128)(2,1)S(1)}, bf16[128,2560]{1,0:T(8,128)(2,1)S(1)}, u32[]{:S(2)}, u32[]{:S(2)}) collective-permute-start(bf16[128,2560]{1,0:T(8,128)(2,1)S(1)} %get-tuple-element.88), channel_id=1, source_target_pairs={{0,2},{1,3},{2,4},{3,5},{4,6},{5,7},{6,0},{7,1},{8,10},{9,11},{10,... | collective-permute-start | bytes 1966088 | tf_op jit(solution)/shard_map/ppermute | solution.py:40
  95.0 12.8 %collective-permute-start.35 = (bf16[64,2560]{1,0:T(8,128)(2,1)S(1)}, bf16[64,2560]{1,0:T(8,128)(2,1)S(1)}, u32[]{:S(2)}, u32[]{:S(2)}) collective-permute-start(bf16[64,2560]{1,0:T(8,128)(2,1)S(1)} %get-tuple-element.93), channel_id=1, source_target_pairs={{0,65},{1,64},{2,67},{3,66},{4,69},{5,68},{6,71},{7,70},{8,73},{9,... | collective-permute-start | bytes 983048 | tf_op jit(solution)/shard_map/ppermute | solution.py:40
  106.0 12.2 %collective-permute-start.32 = (bf16[72,2560]{1,0:T(8,128)(2,1)S(1)}, bf16[72,2560]{1,0:T(8,128)(2,1)S(1)}, u32[]{:S(2)}, u32[]{:S(2)}) collective-permute-start(bf16[72,2560]{1,0:T(8,128)(2,1)S(1)} %get-tuple-element.86), channel_id=1, source_target_pairs={{0,64},{1,65},{2,66},{3,67},{4,68},{5,69},{6,70},{7,71},{8,72},{9,... | collective-permute-start | bytes 1105928 | tf_op jit(solution)/shard_map/ppermute | solution.py:40
  107.7 10.5 %collective-permute-start.31 = (bf16[72,2560]{1,0:T(8,128)(2,1)S(1)}, bf16[72,2560]{1,0:T(8,128)(2,1)S(1)}, u32[]{:S(2)}, u32[]{:S(2)}) collective-permute-start(bf16[72,2560]{1,0:T(8,128)(2,1)S(1)} %get-tuple-element.85), channel_id=1, source_target_pairs={{0,32},{1,33},{2,34},{3,35},{4,36},{5,37},{6,38},{7,39},{8,40},{9,... | collective-permute-start | bytes 1105928 | tf_op jit(solution)/shard_map/ppermute | solution.py:40
  107.9 11.3 %collective-permute-start.36 = (bf16[64,2560]{1,0:T(8,128)(2,1)S(1)}, bf16[64,2560]{1,0:T(8,128)(2,1)S(1)}, u32[]{:S(2)}, u32[]{:S(2)}) collective-permute-start(bf16[64,2560]{1,0:T(8,128)(2,1)S(1)} %get-tuple-element.94), channel_id=1, source_target_pairs={{0,4},{1,5},{2,6},{3,7},{4,0},{5,1},{6,2},{7,3},{8,12},{9,13},{10,... | collective-permute-start | bytes 983048 | tf_op jit(solution)/shard_map/ppermute | solution.py:40
  109.6 9.5 %collective-permute-start.37 = (bf16[64,2560]{1,0:T(8,128)(2,1)S(1)}, bf16[64,2560]{1,0:T(8,128)(2,1)S(1)}, u32[]{:S(2)}, u32[]{:S(2)}) collective-permute-start(bf16[64,2560]{1,0:T(8,128)(2,1)S(1)} %get-tuple-element.95), channel_id=1, source_target_pairs={{0,65},{1,64},{2,67},{3,66},{4,69},{5,68},{6,71},{7,70},{8,73},{9,... | collective-permute-start | bytes 983048 | tf_op jit(solution)/shard_map/ppermute | solution.py:40

commit v7 on v6

--- a/solution.py
+++ b/solution.py
@@ -368,8 +368,8 @@
     fn_a = over(f_a)
 
     blocks = (student_hidden, near, left, right, left_near, right_near, far, far_near)
-    logits, hidden, student_stats = student_logits(ids, blocks, student_head)
-    fn_b = over(after(f_b, student_stats))
+    logits, hidden, student_stats = student_logits(after(ids, rn_a), blocks, student_head)
+    fn_b = over(f_b)
     ln_b = up(near_b)
     rn_b = down(near_b)
 

time: 120 us -> 120 us (level)
  starting transfers between devices: 52.2 us -> 50.5 us
  waiting for transfers between devices: 43.8 us -> 45.1 us
    ppermute x38, starting transfers between devices: 52.2 us -> 50.5 us  [send(): return lax.ppermute(a, AXES, to)]
    ppermute x38, waiting for transfers between devices: 43.8 us -> 45.1 us  [send(): return lax.ppermute(a, AXES, to)]
  transfers between devices with their start and end apart: 38 -> 38, of which waited for: 20 -> 20; matrix products, arithmetic and copies ran while one was open for 1% -> 1% of each run, Pallas kernels for 14% -> 15%
where the time goes in v7:
time: 120 us
  starting transfers between devices  50.5 us (42%)
  waiting for transfers between devices  45.1 us (38%)
  Pallas kernels  21.3 us (18%)
  local copies, waits for them, and re-layouts  1.82 us (2%)
    ppermute x38, starting transfers between devices, send(): return lax.ppermute(a, AXES, to)  50.5 us
    ppermute x38, waiting for transfers between devices, send(): return lax.ppermute(a, AXES, to)  45.1 us
    pallas_call x17, Pallas kernels, kernel_call(): pl.pallas_call(body, in_specs=[VMEM] * len(arrays), out_specs=[VMEM] * le...  21.3 us
  transfers between devices with their start and end apart: 38, of which 20 were waited for; matrix products, arithmetic and copies ran while one was open for 1% of the time, Pallas kernels for 15%

profile of v7, /device:TPU:0, one launch (start us, length us, event | category | flops | bytes accessed | tf_op | source)
XLA Modules:
  0.0 119.7 jit_solution(3485141588198015234)
XLA Ops:
  0.6 1.6 %collective-permute-start.6 = (bf16[64,2560]{1,0:T(8,128)(2,1)}, bf16[64,2560]{1,0:T(8,128)(2,1)S(1)}, u32[]{:S(2)}, u32[]{:S(2)}) collective-permute-start(bf16[64,2560]{1,0:T(8,128)(2,1)} %refs_0_.1), channel_id=1, source_target_pairs={{0,2},{1,3},{2,4},{3,5},{4,6},{5,7},{6,0},{7,1},{8,10},{9,11},{10,... | collective-permute-start | bytes 983048 | tf_op jit(solution)/shard_map/ppermute | solution.py:40
  2.3 3.0 %collective-permute-start.5 = (bf16[64,2560]{1,0:T(8,128)(2,1)}, bf16[64,2560]{1,0:T(8,128)(2,1)S(1)}, u32[]{:S(2)}, u32[]{:S(2)}) collective-permute-start(bf16[64,2560]{1,0:T(8,128)(2,1)} %refs_0_.1), channel_id=1, source_target_pairs={{0,65},{1,64},{2,67},{3,66},{4,69},{5,68},{6,71},{7,70},{8,73},{9,... | collective-permute-start | bytes 983048 | tf_op jit(solution)/shard_map/ppermute | solution.py:40
  5.3 1.7 %collective-permute-start.7 = (bf16[64,2560]{1,0:T(8,128)(2,1)}, bf16[64,2560]{1,0:T(8,128)(2,1)S(1)}, u32[]{:S(2)}, u32[]{:S(2)}) collective-permute-start(bf16[64,2560]{1,0:T(8,128)(2,1)} %refs_0_.1), channel_id=1, source_target_pairs={{0,6},{1,7},{2,0},{3,1},{4,2},{5,3},{6,4},{7,5},{8,14},{9,15},{10,... | collective-permute-start | bytes 983048 | tf_op jit(solution)/shard_map/ppermute | solution.py:40
  7.2 1.1 fusion
  8.3 1.7 %collective-permute-start.2 = (bf16[64,2560]{1,0:T(8,128)(2,1)S(1)}, bf16[64,2560]{1,0:T(8,128)(2,1)S(1)}, u32[]{:S(2)}, u32[]{:S(2)}) collective-permute-start(bf16[64,2560]{1,0:T(8,128)(2,1)S(1)} %get-tuple-element.61.refs_0_), channel_id=1, source_target_pairs={{0,6},{1,7},{2,0},{3,1},{4,2},{5,3},{6,4},{7,5},{8,14},{9,15},{10,... | collective-permute-start | bytes 983048 | tf_op jit(solution)/shard_map/ppermute | solution.py:40
  10.0 3.0 %collective-permute-done.near = s32[512]{0:T(512)S(1)} collective-permute-done((s32[512]{0:T(512)}, s32[512]{0:T(512)S(1)}, u32[]{:S(2)}, u32[]{:S(2)}) %collective-permute-start) | collective-permute-done | bytes 2080 | tf_op jit(solution)/shard_map/ppermute | solution.py:40
  13.0 0.7 copy-done.1
  13.9 1.6 %collective-permute-start.13 = (bf16[64,2560]{1,0:T(8,128)(2,1)S(1)}, bf16[64,2560]{1,0:T(8,128)(2,1)S(1)}, u32[]{:S(2)}, u32[]{:S(2)}) collective-permute-start(bf16[64,2560]{1,0:T(8,128)(2,1)S(1)} %get-tuple-element.60.refs_0_), channel_id=1, source_target_pairs={{0,2},{1,3},{2,4},{3,5},{4,6},{5,7},{6,0},{7,1},{8,10},{9,11},{10,... | collective-permute-start | bytes 983048 | tf_op jit(solution)/shard_map/ppermute | solution.py:40
  15.4 2.9 %collective-permute-start.1 = (bf16[64,2560]{1,0:T(8,128)(2,1)S(1)}, bf16[64,2560]{1,0:T(8,128)(2,1)S(1)}, u32[]{:S(2)}, u32[]{:S(2)}) collective-permute-start(bf16[64,2560]{1,0:T(8,128)(2,1)S(1)} %get-tuple-element.61.refs_0_), channel_id=1, source_target_pairs={{0,65},{1,64},{2,67},{3,66},{4,69},{5,68},{6,71},{7,70},{8,73},{9,... | collective-permute-start | bytes 983048 | tf_op jit(solution)/shard_map/ppermute | solution.py:40
  18.3 1.7 %collective-permute-start.9 = (bf16[64,2560]{1,0:T(8,128)(2,1)S(1)}, bf16[64,2560]{1,0:T(8,128)(2,1)S(1)}, u32[]{:S(2)}, u32[]{:S(2)}) collective-permute-start(bf16[64,2560]{1,0:T(8,128)(2,1)S(1)} %collective-permute-done.5.refs_1_), channel_id=1, source_target_pairs={{0,6},{1,7},{2,0},{3,1},{4,2},{5,3},{6,4},{7,5},{8,14},{9,15},{10,... | collective-permute-start | bytes 983048 | tf_op jit(solution)/shard_map/ppermute | solution.py:40
  20.1 0.3 collective-permute-start.10
  20.4 2.8 %collective-permute-done.2.refs_3_ = bf16[64,2560]{1,0:T(8,128)(2,1)S(1)} collective-permute-done((bf16[64,2560]{1,0:T(8,128)(2,1)S(1)}, bf16[64,2560]{1,0:T(8,128)(2,1)S(1)}, u32[]{:S(2)}, u32[]{:S(2)}) %collective-permute-start.2) | collective-permute-done | bytes 327712 | tf_op jit(solution)/shard_map/ppermute | solution.py:40
  23.2 0.2 collective-permute-start.11
  23.4 1.8 %collective-permute-done.13.refs_2_ = bf16[64,2560]{1,0:T(8,128)(2,1)S(1)} collective-permute-done((bf16[64,2560]{1,0:T(8,128)(2,1)S(1)}, bf16[64,2560]{1,0:T(8,128)(2,1)S(1)}, u32[]{:S(2)}, u32[]{:S(2)}) %collective-permute-start.13) | collective-permute-done | bytes 327712 | tf_op jit(solution)/shard_map/ppermute | solution.py:40
  25.2 1.1 collective-permute-start.3
  26.3 0.2 collective-permute-done.1.refs_1_
  26.5 1.2 %collective-permute-start.15 = (bf16[64,2560]{1,0:T(8,128)(2,1)S(1)}, bf16[64,2560]{1,0:T(8,128)(2,1)S(1)}, u32[]{:S(2)}, u32[]{:S(2)}) collective-permute-start(bf16[64,2560]{1,0:T(8,128)(2,1)S(1)} %get-tuple-element.61.refs_0_), channel_id=1, source_target_pairs={{0,2},{1,3},{2,4},{3,5},{4,6},{5,7},{6,0},{7,1},{8,10},{9,11},{10,... | collective-permute-start | bytes 983048 | tf_op jit(solution)/shard_map/ppermute | solution.py:40
  27.7 2.5 %collective-permute-done.9.refs_5_ = bf16[64,2560]{1,0:T(8,128)(2,1)S(1)} collective-permute-done((bf16[64,2560]{1,0:T(8,128)(2,1)S(1)}, bf16[64,2560]{1,0:T(8,128)(2,1)S(1)}, u32[]{:S(2)}, u32[]{:S(2)}) %collective-permute-start.9) | collective-permute-done | bytes 327712 | tf_op jit(solution)/shard_map/ppermute | solution.py:40
  30.2 1.2 %collective-permute-start.8 = (bf16[64,2560]{1,0:T(8,128)(2,1)S(1)}, bf16[64,2560]{1,0:T(8,128)(2,1)S(1)}, u32[]{:S(2)}, u32[]{:S(2)}) collective-permute-start(bf16[64,2560]{1,0:T(8,128)(2,1)S(1)} %collective-permute-done.6.refs_2_), channel_id=1, source_target_pairs={{0,65},{1,64},{2,67},{3,66},{4,69},{5,68},{6,71},{7,70},{8,73},{9,... | collective-permute-start | bytes 983048 | tf_op jit(solution)/shard_map/ppermute | solution.py:40
  31.4 0.8 collective-permute-done.10.refs_6_
  32.3 1.2 collective-permute-start.14
  33.5 3.7 %collective-permute-start.12 = (bf16[64,2560]{1,0:T(8,128)(2,1)S(1)}, bf16[64,2560]{1,0:T(8,128)(2,1)S(1)}, u32[]{:S(2)}, u32[]{:S(2)}) collective-permute-start(bf16[64,2560]{1,0:T(8,128)(2,1)S(1)} %collective-permute-done.10.refs_6_), channel_id=1, source_target_pairs={{0,65},{1,64},{2,67},{3,66},{4,69},{5,68},{6,71},{7,70},{8,73},{9,... | collective-permute-start | bytes 983048 | tf_op jit(solution)/shard_map/ppermute | solution.py:40
  37.2 1.5 %collective-permute-start.18 = (bf16[64,2560]{1,0:T(8,128)(2,1)S(1)}, bf16[64,2560]{1,0:T(8,128)(2,1)S(1)}, u32[]{:S(2)}, u32[]{:S(2)}) collective-permute-start(bf16[64,2560]{1,0:T(8,128)(2,1)S(1)} %collective-permute-done.13.refs_2_), channel_id=1, source_target_pairs={{0,2},{1,3},{2,4},{3,5},{4,6},{5,7},{6,0},{7,1},{8,10},{9,11},{10,... | collective-permute-start | bytes 983048 | tf_op jit(solution)/shard_map/ppermute | solution.py:40
  38.7 1.8 %collective-permute-start.4 = (bf16[64,2560]{1,0:T(8,128)(2,1)S(1)}, bf16[64,2560]{1,0:T(8,128)(2,1)S(1)}, u32[]{:S(2)}, u32[]{:S(2)}) collective-permute-start(bf16[64,2560]{1,0:T(8,128)(2,1)S(1)} %collective-permute-done.1.refs_1_), channel_id=1, source_target_pairs={{0,6},{1,7},{2,0},{3,1},{4,2},{5,3},{6,4},{7,5},{8,14},{9,15},{10,... | collective-permute-start | bytes 983048 | tf_op jit(solution)/shard_map/ppermute | solution.py:40
  40.5 1.6 %collective-permute-done.8.refs_4_ = bf16[64,2560]{1,0:T(8,128)(2,1)S(1)} collective-permute-done((bf16[64,2560]{1,0:T(8,128)(2,1)S(1)}, bf16[64,2560]{1,0:T(8,128)(2,1)S(1)}, u32[]{:S(2)}, u32[]{:S(2)}) %collective-permute-start.8) | collective-permute-done | bytes 327712 | tf_op jit(solution)/shard_map/ppermute | solution.py:40
  42.1 1.4 %collective-permute-start.16 = (bf16[64,2560]{1,0:T(8,128)(2,1)S(1)}, bf16[64,2560]{1,0:T(8,128)(2,1)S(1)}, u32[]{:S(2)}, u32[]{:S(2)}) collective-permute-start(bf16[64,2560]{1,0:T(8,128)(2,1)S(1)} %collective-permute-done.1.refs_1_), channel_id=1, source_target_pairs={{0,2},{1,3},{2,4},{3,5},{4,6},{5,7},{6,0},{7,1},{8,10},{9,11},{10,... | collective-permute-start | bytes 983048 | tf_op jit(solution)/shard_map/ppermute | solution.py:40
  43.5 0.8 collective-permute-done.14.refs_3_
  44.2 1.2 %collective-permute-start.17 = (bf16[64,2560]{1,0:T(8,128)(2,1)S(1)}, bf16[64,2560]{1,0:T(8,128)(2,1)S(1)}, u32[]{:S(2)}, u32[]{:S(2)}) collective-permute-start(bf16[64,2560]{1,0:T(8,128)(2,1)S(1)} %collective-permute-done.3.refs_6_), channel_id=1, source_target_pairs={{0,65},{1,64},{2,67},{3,66},{4,69},{5,68},{6,71},{7,70},{8,73},{9,... | collective-permute-start | bytes 983048 | tf_op jit(solution)/shard_map/ppermute | solution.py:40
  45.4 2.1 %collective-permute-done.12.refs_7_ = bf16[64,2560]{1,0:T(8,128)(2,1)S(1)} collective-permute-done((bf16[64,2560]{1,0:T(8,128)(2,1)S(1)}, bf16[64,2560]{1,0:T(8,128)(2,1)S(1)}, u32[]{:S(2)}, u32[]{:S(2)}) %collective-permute-start.12) | collective-permute-done | bytes 327712 | tf_op jit(solution)/shard_map/ppermute | solution.py:40
  47.6 1.7 %collective-permute-start.20 = (bf16[64,2560]{1,0:T(8,128)(2,1)S(1)}, bf16[64,2560]{1,0:T(8,128)(2,1)S(1)}, u32[]{:S(2)}, u32[]{:S(2)}) collective-permute-start(bf16[64,2560]{1,0:T(8,128)(2,1)S(1)} %collective-permute-done.11.refs_1_), channel_id=1, source_target_pairs={{0,6},{1,7},{2,0},{3,1},{4,2},{5,3},{6,4},{7,5},{8,14},{9,15},{10,... | collective-permute-start | bytes 983048 | tf_op jit(solution)/shard_map/ppermute | solution.py:40
  49.3 0.3 collective-permute-start.19
  49.6 1.7 %collective-permute-done.4.refs_5_ = bf16[64,2560]{1,0:T(8,128)(2,1)S(1)} collective-permute-done((bf16[64,2560]{1,0:T(8,128)(2,1)S(1)}, bf16[64,2560]{1,0:T(8,128)(2,1)S(1)}, u32[]{:S(2)}, u32[]{:S(2)}) %collective-permute-start.4) | collective-permute-done | bytes 327712 | tf_op jit(solution)/shard_map/ppermute | solution.py:40
  51.3 2.0 %collective-permute-start.21 = (bf16[64,2560]{1,0:T(8,128)(2,1)S(1)}, bf16[64,2560]{1,0:T(8,128)(2,1)S(1)}, u32[]{:S(2)}, u32[]{:S(2)}) collective-permute-start(bf16[64,2560]{1,0:T(8,128)(2,1)S(1)} %collective-permute-done.18.refs_2_), channel_id=1, source_target_pairs={{0,65},{1,64},{2,67},{3,66},{4,69},{5,68},{6,71},{7,70},{8,73},{9,... | collective-permute-start | bytes 983048 | tf_op jit(solution)/shard_map/ppermute | solution.py:40
  53.3 1.7 %shard_map.70.early = f32[1152,256]{1,0:T(8,128)S(1)} custom-call(bf16[1152,5120]{1,0:T(8,128)(2,1)S(1)} %bitcast.3, bf16[64,2560]{1,0:T(8,128)(2,1)S(1)} %get-tuple-element.60.refs_0_, bf16[64,2560]{1,0:T(8,128)(2,1)S(1)} %collective-permute-done.11.refs_1_, bf16[64,2560]{1,0:T(8,128)(2,1)S(1)} %collective-permute-done.13.refs_2_, ...), custom_call_target="tpu_custom_call" | custom-call | flops 20000000000 | bytes 20000000 | tf_op jit(solution)/shard_map/pallas_call | solution.py:69
  55.1 3.4 %shard_map.69 = (f32[1152,512]{1,0:T(8,128)S(1)}, bf16[512,2560]{1,0:T(8,128)(2,1)S(1)}, f32[8,512]{1,0:T(8,128)S(1)}) custom-call(s32[1,512]{1,0:T(1,128)S(1)} %shard_map.68.ids, bf16[1152,2560]{1,0:T(8,128)(2,1)S(1)} %bitcast.1, bf16[64,2560]{1,0:T(8,128)(2,1)S(1)} %copy-done, bf16[64,2560]{1,0:T(8,128)(2,1)S(1)} %collective-permute-done.5.refs_1_, ...), custom_call_target="tpu_custom_call" | custom-call | flops 20000000000 | bytes 20000000 | tf_op jit(solution)/shard_map/pallas_call | solution.py:69
  58.5 3.3 %shard_map.71 = (f32[1152,256]{1,0:T(8,128)S(1)}, f32[8,512]{1,0:T(8,128)S(1)}) custom-call(s32[1,512]{1,0:T(1,128)S(1)} %shard_map.68.ids, f32[8,512]{1,0:T(8,128)S(1)} %get-tuple-element.58.student_stats, f32[1152,256]{1,0:T(8,128)S(1)} %shard_map.70.early, bf16[1152,5120]{1,0:T(8,128)(2,1)S(1)} %bitcast.3, ...), custom_call_target="tpu_custom_call" | custom-call | flops 20000000000 | bytes 20000000 | tf_op jit(solution)/shard_map/pallas_call | solution.py:69
  61.8 1.9 %shard_map.72.refs_0_ = f32[8,512]{1,0:T(8,128)S(1)} custom-call(s32[1,512]{1,0:T(1,128)S(1)} %shard_map.68.ids, f32[8,512]{1,0:T(8,128)S(1)} %get-tuple-element.64.first_stats, bf16[1152,5120]{1,0:T(8,128)(2,1)S(1)} %bitcast.3, f32[1152,256]{1,0:T(8,128)S(1)} %get-tuple-element.65.logits, bf16[64,2560]{1,0:T(8,128)(2,1)S(1)} %collective-permute-done.19.refs_0_, ...), custom_call_target="tpu_custom_call" | custom-call | flops 20000000000 | bytes 20000000 | tf_op jit(solution)/shard_map/pallas_call | solution.py:69
  63.7 1.7 %collective-permute-start.24 = (f32[8,512]{1,0:T(8,128)S(1)}, f32[8,512]{1,0:T(8,128)S(1)}, u32[]{:S(2)}, u32[]{:S(2)}) collective-permute-start(f32[8,512]{1,0:T(8,128)S(1)} %shard_map.72.refs_0_), channel_id=1, source_target_pairs={{0,4},{1,5},{2,6},{3,7},{4,0},{5,1},{6,2},{7,3},{8,12},{9,13},{10,... | collective-permute-start | bytes 49160 | tf_op jit(solution)/shard_map/ppermute | solution.py:40
  65.4 2.3 %collective-permute-start.23 = (f32[8,512]{1,0:T(8,128)S(1)}, f32[8,512]{1,0:T(8,128)S(1)}, u32[]{:S(2)}, u32[]{:S(2)}) collective-permute-start(f32[8,512]{1,0:T(8,128)S(1)} %shard_map.72.refs_0_), channel_id=1, source_target_pairs={{0,6},{1,7},{2,0},{3,1},{4,2},{5,3},{6,4},{7,5},{8,14},{9,15},{10,... | collective-permute-start | bytes 49160 | tf_op jit(solution)/shard_map/ppermute | solution.py:40
  67.6 1.4 %collective-permute-done.24.refs_3_ = f32[8,512]{1,0:T(8,128)S(1)} collective-permute-done((f32[8,512]{1,0:T(8,128)S(1)}, f32[8,512]{1,0:T(8,128)S(1)}, u32[]{:S(2)}, u32[]{:S(2)}) %collective-permute-start.24) | collective-permute-done | bytes 16416 | tf_op jit(solution)/shard_map/ppermute | solution.py:40
  69.1 3.5 %collective-permute-done.22.refs_1_ = f32[8,512]{1,0:T(8,128)S(1)} collective-permute-done((f32[8,512]{1,0:T(8,128)S(1)}, f32[8,512]{1,0:T(8,128)S(1)}, u32[]{:S(2)}, u32[]{:S(2)}) %collective-permute-start.22) | collective-permute-done | bytes 16416 | tf_op jit(solution)/shard_map/ppermute | solution.py:40
  72.7 1.6 %collective-permute-start.25 = (f32[8,512]{1,0:T(8,128)S(1)}, f32[8,512]{1,0:T(8,128)S(1)}, u32[]{:S(2)}, u32[]{:S(2)}) collective-permute-start(f32[8,512]{1,0:T(8,128)S(1)} %shard_map.73.refs_0_), channel_id=1, source_target_pairs={{0,65},{1,64},{2,67},{3,66},{4,69},{5,68},{6,71},{7,70},{8,73},{9,... | collective-permute-start | bytes 49160 | tf_op jit(solution)/shard_map/ppermute | solution.py:40
  74.2 3.5 %collective-permute-done.25.refs_1_ = f32[8,512]{1,0:T(8,128)S(1)} collective-permute-done((f32[8,512]{1,0:T(8,128)S(1)}, f32[8,512]{1,0:T(8,128)S(1)}, u32[]{:S(2)}, u32[]{:S(2)}) %collective-permute-start.25) | collective-permute-done | bytes 16416 | tf_op jit(solution)/shard_map/ppermute | solution.py:40
  77.8 0.6 shard_map.75
  78.5 1.7 %shard_map.76.own = f32[576,2560]{1,0:T(8,128)S(1)} custom-call(bf16[576,512]{1,0:T(8,128)(2,1)S(1)} %get-tuple-element.73.grad, bf16[512,2560]{1,0:T(8,128)(2,1)S(1)} %get-tuple-element.72.hidden), custom_call_target="tpu_custom_call" | custom-call | flops 1000000000 | bytes 1000000 | tf_op jit(solution)/shard_map/pallas_call | solution.py:69
  80.2 0.3 collective-permute-done.26.grad
  80.5 1.1 shard_map.77
  81.7 4.1 %collective-permute-start.29 = (bf16[144,2560]{1,0:T(8,128)(2,1)S(1)}, bf16[144,2560]{1,0:T(8,128)(2,1)S(1)}, u32[]{:S(2)}, u32[]{:S(2)}) collective-permute-start(bf16[144,2560]{1,0:T(8,128)(2,1)S(1)} %get-tuple-element.81), channel_id=1, source_target_pairs={{0,48},{1,49},{2,50},{3,51},{4,52},{5,53},{6,54},{7,55},{8,56},{9,... | collective-permute-start | bytes 2211848 | tf_op jit(solution)/shard_map/ppermute | solution.py:40
  85.8 2.1 %shard_map.79 = (bf16[128,2560]{1,0:T(8,128)(2,1)S(1)}, bf16[128,2560]{1,0:T(8,128)(2,1)S(1)}) custom-call(s32[1,512]{1,0:T(1,128)S(1)} %shard_map.68.ids, f32[8,512]{1,0:T(8,128)S(1)} %shard_map.74.total, f32[1152,512]{1,0:T(8,128)S(1)} %get-tuple-element.70.logits, bf16[1152,2560]{1,0:T(8,128)(2,1)S(1)} %bitcast.1), custom_call_target="tpu_custom_call" | custom-call | flops 20000000000 | bytes 20000000 | tf_op jit(solution)/shard_map/pallas_call | solution.py:69
  88.0 2.0 %collective-permute-start.34 = (bf16[128,2560]{1,0:T(8,128)(2,1)S(1)}, bf16[128,2560]{1,0:T(8,128)(2,1)S(1)}, u32[]{:S(2)}, u32[]{:S(2)}) collective-permute-start(bf16[128,2560]{1,0:T(8,128)(2,1)S(1)} %get-tuple-element.88), channel_id=1, source_target_pairs={{0,2},{1,3},{2,4},{3,5},{4,6},{5,7},{6,0},{7,1},{8,10},{9,11},{10,... | collective-permute-start | bytes 1966088 | tf_op jit(solution)/shard_map/ppermute | solution.py:40
  90.1 0.8 shard_map.80
  90.8 1.6 %collective-permute-done.28.far_near = bf16[72,2560]{1,0:T(8,128)(2,1)S(1)} collective-permute-done((bf16[72,2560]{1,0:T(8,128)(2,1)S(1)}, bf16[72,2560]{1,0:T(8,128)(2,1)S(1)}, u32[]{:S(2)}, u32[]{:S(2)}) %collective-permute-start.28) | collective-permute-done | bytes 368672 | tf_op jit(solution)/shard_map/ppermute | solution.py:40
  92.4 2.1 %shard_map.78 = (f32[64,2560]{1,0:T(8,128)S(1)}, f32[64,2560]{1,0:T(8,128)S(1)}, f32[64,2560]{1,0:T(8,128)S(1)}, bf16[64,2560]{1,0:T(8,128)(2,1)S(1)}) custom-call(s32[1,512]{1,0:T(1,128)S(1)} %shard_map.68.ids, f32[8,512]{1,0:T(8,128)S(1)} %shard_map.74.total, f32[1152,512]{1,0:T(8,128)S(1)} %get-tuple-element.70.logits, bf16[1152,2560]{1,0:T(8,128)(2,1)S(1)} %bitcast.1), custom_call_target="tpu_custom_call" | custom-call | flops 1000000000 | bytes 1000000 | tf_op jit(solution)/shard_map/pallas_call | solution.py:69
  94.6 1.6 %collective-permute-start.35 = (bf16[64,2560]{1,0:T(8,128)(2,1)S(1)}, bf16[64,2560]{1,0:T(8,128)(2,1)S(1)}, u32[]{:S(2)}, u32[]{:S(2)}) collective-permute-start(bf16[64,2560]{1,0:T(8,128)(2,1)S(1)} %get-tuple-element.93), channel_id=1, source_target_pairs={{0,65},{1,64},{2,67},{3,66},{4,69},{5,68},{6,71},{7,70},{8,73},{9,... | collective-permute-start | bytes 983048 | tf_op jit(solution)/shard_map/ppermute | solution.py:40
  96.1 5.8 %collective-permute-done.29.lefts = bf16[144,2560]{1,0:T(8,128)(2,1)S(1)} collective-permute-done((bf16[144,2560]{1,0:T(8,128)(2,1)S(1)}, bf16[144,2560]{1,0:T(8,128)(2,1)S(1)}, u32[]{:S(2)}, u32[]{:S(2)}) %collective-permute-start.29) | collective-permute-done | bytes 737312 | tf_op jit(solution)/shard_map/ppermute | solution.py:40
  101.9 3.4 %collective-permute-done.30.rights = bf16[144,2560]{1,0:T(8,128)(2,1)S(1)} collective-permute-done((bf16[144,2560]{1,0:T(8,128)(2,1)S(1)}, bf16[144,2560]{1,0:T(8,128)(2,1)S(1)}, u32[]{:S(2)}, u32[]{:S(2)}) %collective-permute-start.30) | collective-permute-done | bytes 737312 | tf_op jit(solution)/shard_map/ppermute | solution.py:40
  105.3 0.2 shard_map.81
  105.6 1.7 %collective-permute-start.32 = (bf16[72,2560]{1,0:T(8,128)(2,1)S(1)}, bf16[72,2560]{1,0:T(8,128)(2,1)S(1)}, u32[]{:S(2)}, u32[]{:S(2)}) collective-permute-start(bf16[72,2560]{1,0:T(8,128)(2,1)S(1)} %get-tuple-element.86), channel_id=1, source_target_pairs={{0,64},{1,65},{2,66},{3,67},{4,68},{5,69},{6,70},{7,71},{8,72},{9,... | collective-permute-start | bytes 1105928 | tf_op jit(solution)/shard_map/ppermute | solution.py:40
  107.3 0.2 shard_map.83
  107.5 0.6 collective-permute-start.36
  108.1 1.5 %collective-permute-start.37 = (bf16[64,2560]{1,0:T(8,128)(2,1)S(1)}, bf16[64,2560]{1,0:T(8,128)(2,1)S(1)}, u32[]{:S(2)}, u32[]{:S(2)}) collective-permute-start(bf16[64,2560]{1,0:T(8,128)(2,1)S(1)} %get-tuple-element.95), channel_id=1, source_target_pairs={{0,65},{1,64},{2,67},{3,66},{4,69},{5,68},{6,71},{7,70},{8,73},{9,... | collective-permute-start | bytes 983048 | tf_op jit(solution)/shard_map/ppermute | solution.py:40
  109.6 8.2 %collective-permute-done.31.far = bf16[72,2560]{1,0:T(8,128)(2,1)S(1)} collective-permute-done((bf16[72,2560]{1,0:T(8,128)(2,1)S(1)}, bf16[72,2560]{1,0:T(8,128)(2,1)S(1)}, u32[]{:S(2)}, u32[]{:S(2)}) %collective-permute-start.31) | collective-permute-done | bytes 368672 | tf_op jit(solution)/shard_map/ppermute | solution.py:40
  117.8 1.0 shard_map.82
  118.8 0.9 shard_map.84
  (46 shorter events, 1.0 us)
Async XLA Ops:
  0.6 19.5 %collective-permute-start.6 = (bf16[64,2560]{1,0:T(8,128)(2,1)}, bf16[64,2560]{1,0:T(8,128)(2,1)S(1)}, u32[]{:S(2)}, u32[]{:S(2)}) collective-permute-start(bf16[64,2560]{1,0:T(8,128)(2,1)} %refs_0_.1), channel_id=1, source_target_pairs={{0,2},{1,3},{2,4},{3,5},{4,6},{5,7},{6,0},{7,1},{8,10},{9,11},{10,... | collective-permute-start | bytes 983048 | tf_op jit(solution)/shard_map/ppermute | solution.py:40
  2.3 13.1 %collective-permute-start.5 = (bf16[64,2560]{1,0:T(8,128)(2,1)}, bf16[64,2560]{1,0:T(8,128)(2,1)S(1)}, u32[]{:S(2)}, u32[]{:S(2)}) collective-permute-start(bf16[64,2560]{1,0:T(8,128)(2,1)} %refs_0_.1), channel_id=1, source_target_pairs={{0,65},{1,64},{2,67},{3,66},{4,69},{5,68},{6,71},{7,70},{8,73},{9,... | collective-permute-start | bytes 983048 | tf_op jit(solution)/shard_map/ppermute | solution.py:40
  5.3 13.1 %collective-permute-start.7 = (bf16[64,2560]{1,0:T(8,128)(2,1)}, bf16[64,2560]{1,0:T(8,128)(2,1)S(1)}, u32[]{:S(2)}, u32[]{:S(2)}) collective-permute-start(bf16[64,2560]{1,0:T(8,128)(2,1)} %refs_0_.1), channel_id=1, source_target_pairs={{0,6},{1,7},{2,0},{3,1},{4,2},{5,3},{6,4},{7,5},{8,14},{9,15},{10,... | collective-permute-start | bytes 983048 | tf_op jit(solution)/shard_map/ppermute | solution.py:40
  7.0 6.0 %collective-permute-start = (s32[512]{0:T(512)}, s32[512]{0:T(512)S(1)}, u32[]{:S(2)}, u32[]{:S(2)}) collective-permute-start(s32[512]{0:T(512)} %own.1), channel_id=1, source_target_pairs={{0,65},{1,64},{2,67},{3,66},{4,69},{5,68},{6,71},{7,70},{8,73},{9,... | collective-permute-start | bytes 6152 | tf_op jit(solution)/shard_map/ppermute | solution.py:40
  8.3 45.0 %slice-start.2 = ((s8[11796480]{0:T(1024)(128)(4,1)}), s8[4194304]{0:T(1024)(128)(4,1)S(1)}, s32[]{:S(2)}) async-start(s8[11796480]{0:T(1024)(128)(4,1)} %bitcast.2), calls=%async_computation.2 | async-start | bytes 8388608
  8.3 45.0 %slice-start.3 = ((s8[11796480]{0:T(1024)(128)(4,1)}), s8[4194304]{0:T(1024)(128)(4,1)S(1)}, s32[]{:S(2)}) async-start(s8[11796480]{0:T(1024)(128)(4,1)} %bitcast.2), calls=%async_computation.3 | async-start | bytes 8388608
  8.3 45.0 %slice-start.4 = ((s8[11796480]{0:T(1024)(128)(4,1)}), s8[3407872]{0:T(1024)(128)(4,1)S(1)}, s32[]{:S(2)}) async-start(s8[11796480]{0:T(1024)(128)(4,1)} %bitcast.2), calls=%async_computation.4 | async-start | bytes 6815744
  8.3 14.8 %collective-permute-start.2 = (bf16[64,2560]{1,0:T(8,128)(2,1)S(1)}, bf16[64,2560]{1,0:T(8,128)(2,1)S(1)}, u32[]{:S(2)}, u32[]{:S(2)}) collective-permute-start(bf16[64,2560]{1,0:T(8,128)(2,1)S(1)} %get-tuple-element.61.refs_0_), channel_id=1, source_target_pairs={{0,6},{1,7},{2,0},{3,1},{4,2},{5,3},{6,4},{7,5},{8,14},{9,15},{10,... | collective-permute-start | bytes 983048 | tf_op jit(solution)/shard_map/ppermute | solution.py:40
  13.0 0.7 copy-start.1
  13.9 41.2 %slice-start = ((s8[5898240]{0:T(1024)(128)(4,1)}), s8[4194304]{0:T(1024)(128)(4,1)S(1)}, s32[]{:S(2)}) async-start(s8[5898240]{0:T(1024)(128)(4,1)} %bitcast), calls=%async_computation | async-start | bytes 8388608
  13.9 41.2 %slice-start.1 = ((s8[5898240]{0:T(1024)(128)(4,1)}), s8[1703936]{0:T(1024)(128)(4,1)S(1)}, s32[]{:S(2)}) async-start(s8[5898240]{0:T(1024)(128)(4,1)} %bitcast), calls=%async_computation.1 | async-start | bytes 3407872
  13.9 41.2 %copy-start = (bf16[64,2560]{1,0:T(8,128)(2,1)S(1)}, bf16[64,2560]{1,0:T(8,128)(2,1)}, u32[]{:S(2)}) copy-start(bf16[64,2560]{1,0:T(8,128)(2,1)} %refs_0_.1) | copy-start | bytes 983044
  13.9 11.4 %collective-permute-start.13 = (bf16[64,2560]{1,0:T(8,128)(2,1)S(1)}, bf16[64,2560]{1,0:T(8,128)(2,1)S(1)}, u32[]{:S(2)}, u32[]{:S(2)}) collective-permute-start(bf16[64,2560]{1,0:T(8,128)(2,1)S(1)} %get-tuple-element.60.refs_0_), channel_id=1, source_target_pairs={{0,2},{1,3},{2,4},{3,5},{4,6},{5,7},{6,0},{7,1},{8,10},{9,11},{10,... | collective-permute-start | bytes 983048 | tf_op jit(solution)/shard_map/ppermute | solution.py:40
  15.4 11.1 %collective-permute-start.1 = (bf16[64,2560]{1,0:T(8,128)(2,1)S(1)}, bf16[64,2560]{1,0:T(8,128)(2,1)S(1)}, u32[]{:S(2)}, u32[]{:S(2)}) collective-permute-start(bf16[64,2560]{1,0:T(8,128)(2,1)S(1)} %get-tuple-element.61.refs_0_), channel_id=1, source_target_pairs={{0,65},{1,64},{2,67},{3,66},{4,69},{5,68},{6,71},{7,70},{8,73},{9,... | collective-permute-start | bytes 983048 | tf_op jit(solution)/shard_map/ppermute | solution.py:40
  18.3 11.8 %collective-permute-start.9 = (bf16[64,2560]{1,0:T(8,128)(2,1)S(1)}, bf16[64,2560]{1,0:T(8,128)(2,1)S(1)}, u32[]{:S(2)}, u32[]{:S(2)}) collective-permute-start(bf16[64,2560]{1,0:T(8,128)(2,1)S(1)} %collective-permute-done.5.refs_1_), channel_id=1, source_target_pairs={{0,6},{1,7},{2,0},{3,1},{4,2},{5,3},{6,4},{7,5},{8,14},{9,15},{10,... | collective-permute-start | bytes 983048 | tf_op jit(solution)/shard_map/ppermute | solution.py:40
  20.1 12.2 %collective-permute-start.10 = (bf16[64,2560]{1,0:T(8,128)(2,1)S(1)}, bf16[64,2560]{1,0:T(8,128)(2,1)S(1)}, u32[]{:S(2)}, u32[]{:S(2)}) collective-permute-start(bf16[64,2560]{1,0:T(8,128)(2,1)S(1)} %collective-permute-done.6.refs_2_), channel_id=1, source_target_pairs={{0,2},{1,3},{2,4},{3,5},{4,6},{5,7},{6,0},{7,1},{8,10},{9,11},{10,... | collective-permute-start | bytes 983048 | tf_op jit(solution)/shard_map/ppermute | solution.py:40
  23.2 10.4 %collective-permute-start.11 = (bf16[64,2560]{1,0:T(8,128)(2,1)S(1)}, bf16[64,2560]{1,0:T(8,128)(2,1)S(1)}, u32[]{:S(2)}, u32[]{:S(2)}) collective-permute-start(bf16[64,2560]{1,0:T(8,128)(2,1)S(1)} %get-tuple-element.60.refs_0_), channel_id=1, source_target_pairs={{0,65},{1,64},{2,67},{3,66},{4,69},{5,68},{6,71},{7,70},{8,73},{9,... | collective-permute-start | bytes 983048 | tf_op jit(solution)/shard_map/ppermute | solution.py:40
  25.2 12.0 %collective-permute-start.3 = (bf16[64,2560]{1,0:T(8,128)(2,1)S(1)}, bf16[64,2560]{1,0:T(8,128)(2,1)S(1)}, u32[]{:S(2)}, u32[]{:S(2)}) collective-permute-start(bf16[64,2560]{1,0:T(8,128)(2,1)S(1)} %collective-permute-done.2.refs_3_), channel_id=1, source_target_pairs={{0,6},{1,7},{2,0},{3,1},{4,2},{5,3},{6,4},{7,5},{8,14},{9,15},{10,... | collective-permute-start | bytes 983048 | tf_op jit(solution)/shard_map/ppermute | solution.py:40
  26.5 12.2 %collective-permute-start.15 = (bf16[64,2560]{1,0:T(8,128)(2,1)S(1)}, bf16[64,2560]{1,0:T(8,128)(2,1)S(1)}, u32[]{:S(2)}, u32[]{:S(2)}) collective-permute-start(bf16[64,2560]{1,0:T(8,128)(2,1)S(1)} %get-tuple-element.61.refs_0_), channel_id=1, source_target_pairs={{0,2},{1,3},{2,4},{3,5},{4,6},{5,7},{6,0},{7,1},{8,10},{9,11},{10,... | collective-permute-start | bytes 983048 | tf_op jit(solution)/shard_map/ppermute | solution.py:40
  30.2 11.9 %collective-permute-start.8 = (bf16[64,2560]{1,0:T(8,128)(2,1)S(1)}, bf16[64,2560]{1,0:T(8,128)(2,1)S(1)}, u32[]{:S(2)}, u32[]{:S(2)}) collective-permute-start(bf16[64,2560]{1,0:T(8,128)(2,1)S(1)} %collective-permute-done.6.refs_2_), channel_id=1, source_target_pairs={{0,65},{1,64},{2,67},{3,66},{4,69},{5,68},{6,71},{7,70},{8,73},{9,... | collective-permute-start | bytes 983048 | tf_op jit(solution)/shard_map/ppermute | solution.py:40
  32.3 12.0 %collective-permute-start.14 = (bf16[64,2560]{1,0:T(8,128)(2,1)S(1)}, bf16[64,2560]{1,0:T(8,128)(2,1)S(1)}, u32[]{:S(2)}, u32[]{:S(2)}) collective-permute-start(bf16[64,2560]{1,0:T(8,128)(2,1)S(1)} %get-tuple-element.60.refs_0_), channel_id=1, source_target_pairs={{0,6},{1,7},{2,0},{3,1},{4,2},{5,3},{6,4},{7,5},{8,14},{9,15},{10,... | collective-permute-start | bytes 983048 | tf_op jit(solution)/shard_map/ppermute | solution.py:40
  33.5 14.0 %collective-permute-start.12 = (bf16[64,2560]{1,0:T(8,128)(2,1)S(1)}, bf16[64,2560]{1,0:T(8,128)(2,1)S(1)}, u32[]{:S(2)}, u32[]{:S(2)}) collective-permute-start(bf16[64,2560]{1,0:T(8,128)(2,1)S(1)} %collective-permute-done.10.refs_6_), channel_id=1, source_target_pairs={{0,65},{1,64},{2,67},{3,66},{4,69},{5,68},{6,71},{7,70},{8,73},{9,... | collective-permute-start | bytes 983048 | tf_op jit(solution)/shard_map/ppermute | solution.py:40
  37.2 12.0 %collective-permute-start.18 = (bf16[64,2560]{1,0:T(8,128)(2,1)S(1)}, bf16[64,2560]{1,0:T(8,128)(2,1)S(1)}, u32[]{:S(2)}, u32[]{:S(2)}) collective-permute-start(bf16[64,2560]{1,0:T(8,128)(2,1)S(1)} %collective-permute-done.13.refs_2_), channel_id=1, source_target_pairs={{0,2},{1,3},{2,4},{3,5},{4,6},{5,7},{6,0},{7,1},{8,10},{9,11},{10,... | collective-permute-start | bytes 983048 | tf_op jit(solution)/shard_map/ppermute | solution.py:40
  38.7 12.5 %collective-permute-start.4 = (bf16[64,2560]{1,0:T(8,128)(2,1)S(1)}, bf16[64,2560]{1,0:T(8,128)(2,1)S(1)}, u32[]{:S(2)}, u32[]{:S(2)}) collective-permute-start(bf16[64,2560]{1,0:T(8,128)(2,1)S(1)} %collective-permute-done.1.refs_1_), channel_id=1, source_target_pairs={{0,6},{1,7},{2,0},{3,1},{4,2},{5,3},{6,4},{7,5},{8,14},{9,15},{10,... | collective-permute-start | bytes 983048 | tf_op jit(solution)/shard_map/ppermute | solution.py:40
  42.1 16.4 %collective-permute-start.16 = (bf16[64,2560]{1,0:T(8,128)(2,1)S(1)}, bf16[64,2560]{1,0:T(8,128)(2,1)S(1)}, u32[]{:S(2)}, u32[]{:S(2)}) collective-permute-start(bf16[64,2560]{1,0:T(8,128)(2,1)S(1)} %collective-permute-done.1.refs_1_), channel_id=1, source_target_pairs={{0,2},{1,3},{2,4},{3,5},{4,6},{5,7},{6,0},{7,1},{8,10},{9,11},{10,... | collective-permute-start | bytes 983048 | tf_op jit(solution)/shard_map/ppermute | solution.py:40
  44.2 14.2 %collective-permute-start.17 = (bf16[64,2560]{1,0:T(8,128)(2,1)S(1)}, bf16[64,2560]{1,0:T(8,128)(2,1)S(1)}, u32[]{:S(2)}, u32[]{:S(2)}) collective-permute-start(bf16[64,2560]{1,0:T(8,128)(2,1)S(1)} %collective-permute-done.3.refs_6_), channel_id=1, source_target_pairs={{0,65},{1,64},{2,67},{3,66},{4,69},{5,68},{6,71},{7,70},{8,73},{9,... | collective-permute-start | bytes 983048 | tf_op jit(solution)/shard_map/ppermute | solution.py:40
  47.6 14.2 %collective-permute-start.20 = (bf16[64,2560]{1,0:T(8,128)(2,1)S(1)}, bf16[64,2560]{1,0:T(8,128)(2,1)S(1)}, u32[]{:S(2)}, u32[]{:S(2)}) collective-permute-start(bf16[64,2560]{1,0:T(8,128)(2,1)S(1)} %collective-permute-done.11.refs_1_), channel_id=1, source_target_pairs={{0,6},{1,7},{2,0},{3,1},{4,2},{5,3},{6,4},{7,5},{8,14},{9,15},{10,... | collective-permute-start | bytes 983048 | tf_op jit(solution)/shard_map/ppermute | solution.py:40
  49.3 12.5 %collective-permute-start.19 = (bf16[64,2560]{1,0:T(8,128)(2,1)S(1)}, bf16[64,2560]{1,0:T(8,128)(2,1)S(1)}, u32[]{:S(2)}, u32[]{:S(2)}) collective-permute-start(bf16[64,2560]{1,0:T(8,128)(2,1)S(1)} %collective-permute-done.11.refs_1_), channel_id=1, source_target_pairs={{0,2},{1,3},{2,4},{3,5},{4,6},{5,7},{6,0},{7,1},{8,10},{9,11},{10,... | collective-permute-start | bytes 983048 | tf_op jit(solution)/shard_map/ppermute | solution.py:40
  51.3 10.5 %collective-permute-start.21 = (bf16[64,2560]{1,0:T(8,128)(2,1)S(1)}, bf16[64,2560]{1,0:T(8,128)(2,1)S(1)}, u32[]{:S(2)}, u32[]{:S(2)}) collective-permute-start(bf16[64,2560]{1,0:T(8,128)(2,1)S(1)} %collective-permute-done.18.refs_2_), channel_id=1, source_target_pairs={{0,65},{1,64},{2,67},{3,66},{4,69},{5,68},{6,71},{7,70},{8,73},{9,... | collective-permute-start | bytes 983048 | tf_op jit(solution)/shard_map/ppermute | solution.py:40
  63.7 5.3 %collective-permute-start.24 = (f32[8,512]{1,0:T(8,128)S(1)}, f32[8,512]{1,0:T(8,128)S(1)}, u32[]{:S(2)}, u32[]{:S(2)}) collective-permute-start(f32[8,512]{1,0:T(8,128)S(1)} %shard_map.72.refs_0_), channel_id=1, source_target_pairs={{0,4},{1,5},{2,6},{3,7},{4,0},{5,1},{6,2},{7,3},{8,12},{9,13},{10,... | collective-permute-start | bytes 49160 | tf_op jit(solution)/shard_map/ppermute | solution.py:40
  65.4 3.7 %collective-permute-start.23 = (f32[8,512]{1,0:T(8,128)S(1)}, f32[8,512]{1,0:T(8,128)S(1)}, u32[]{:S(2)}, u32[]{:S(2)}) collective-permute-start(f32[8,512]{1,0:T(8,128)S(1)} %shard_map.72.refs_0_), channel_id=1, source_target_pairs={{0,6},{1,7},{2,0},{3,1},{4,2},{5,3},{6,4},{7,5},{8,14},{9,15},{10,... | collective-permute-start | bytes 49160 | tf_op jit(solution)/shard_map/ppermute | solution.py:40
  67.6 4.9 %collective-permute-start.22 = (f32[8,512]{1,0:T(8,128)S(1)}, f32[8,512]{1,0:T(8,128)S(1)}, u32[]{:S(2)}, u32[]{:S(2)}) collective-permute-start(f32[8,512]{1,0:T(8,128)S(1)} %shard_map.72.refs_0_), channel_id=1, source_target_pairs={{0,2},{1,3},{2,4},{3,5},{4,6},{5,7},{6,0},{7,1},{8,10},{9,11},{10,... | collective-permute-start | bytes 49160 | tf_op jit(solution)/shard_map/ppermute | solution.py:40
  67.6 12.8 %collective-permute-start.27 = (bf16[512,2560]{1,0:T(8,128)(2,1)S(1)}, bf16[512,2560]{1,0:T(8,128)(2,1)S(1)}, u32[]{:S(2)}, u32[]{:S(2)}) collective-permute-start(bf16[512,2560]{1,0:T(8,128)(2,1)S(1)} %get-tuple-element.72.hidden), channel_id=1, source_target_pairs={{0,8},{1,9},{2,10},{3,11},{4,12},{5,13},{6,14},{7,15},{8,0},{9,1},... | collective-permute-start | bytes 7864328 | tf_op jit(solution)/shard_map/ppermute | solution.py:40
  72.7 5.0 %collective-permute-start.25 = (f32[8,512]{1,0:T(8,128)S(1)}, f32[8,512]{1,0:T(8,128)S(1)}, u32[]{:S(2)}, u32[]{:S(2)}) collective-permute-start(f32[8,512]{1,0:T(8,128)S(1)} %shard_map.73.refs_0_), channel_id=1, source_target_pairs={{0,65},{1,64},{2,67},{3,66},{4,69},{5,68},{6,71},{7,70},{8,73},{9,... | collective-permute-start | bytes 49160 | tf_op jit(solution)/shard_map/ppermute | solution.py:40
  78.4 2.1 %collective-permute-start.26 = (bf16[576,512]{1,0:T(8,128)(2,1)S(1)}, bf16[576,512]{1,0:T(8,128)(2,1)S(1)}, u32[]{:S(2)}, u32[]{:S(2)}) collective-permute-start(bf16[576,512]{1,0:T(8,128)(2,1)S(1)} %get-tuple-element.71), channel_id=1, source_target_pairs={{0,8},{1,9},{2,10},{3,11},{4,12},{5,13},{6,14},{7,15},{8,0},{9,1},... | collective-permute-start | bytes 1769480 | tf_op jit(solution)/shard_map/ppermute | solution.py:40
  81.6 10.8 %collective-permute-start.28 = (bf16[72,2560]{1,0:T(8,128)(2,1)S(1)}, bf16[72,2560]{1,0:T(8,128)(2,1)S(1)}, u32[]{:S(2)}, u32[]{:S(2)}) collective-permute-start(bf16[72,2560]{1,0:T(8,128)(2,1)S(1)} %get-tuple-element.74), channel_id=1, source_target_pairs={{0,64},{1,65},{2,66},{3,67},{4,68},{5,69},{6,70},{7,71},{8,72},{9,... | collective-permute-start | bytes 1105928 | tf_op jit(solution)/shard_map/ppermute | solution.py:40
  81.7 20.2 %collective-permute-start.29 = (bf16[144,2560]{1,0:T(8,128)(2,1)S(1)}, bf16[144,2560]{1,0:T(8,128)(2,1)S(1)}, u32[]{:S(2)}, u32[]{:S(2)}) collective-permute-start(bf16[144,2560]{1,0:T(8,128)(2,1)S(1)} %get-tuple-element.81), channel_id=1, source_target_pairs={{0,48},{1,49},{2,50},{3,51},{4,52},{5,53},{6,54},{7,55},{8,56},{9,... | collective-permute-start | bytes 2211848 | tf_op jit(solution)/shard_map/ppermute | solution.py:40
  85.8 19.5 %collective-permute-start.30 = (bf16[144,2560]{1,0:T(8,128)(2,1)S(1)}, bf16[144,2560]{1,0:T(8,128)(2,1)S(1)}, u32[]{:S(2)}, u32[]{:S(2)}) collective-permute-start(bf16[144,2560]{1,0:T(8,128)(2,1)S(1)} %get-tuple-element.82), channel_id=1, source_target_pairs={{0,16},{1,17},{2,18},{3,19},{4,20},{5,21},{6,22},{7,23},{8,24},{9,... | collective-permute-start | bytes 2211848 | tf_op jit(solution)/shard_map/ppermute | solution.py:40
  88.0 19.4 %collective-permute-start.33 = (bf16[128,2560]{1,0:T(8,128)(2,1)S(1)}, bf16[128,2560]{1,0:T(8,128)(2,1)S(1)}, u32[]{:S(2)}, u32[]{:S(2)}) collective-permute-start(bf16[128,2560]{1,0:T(8,128)(2,1)S(1)} %get-tuple-element.78), channel_id=1, source_target_pairs={{0,6},{1,7},{2,0},{3,1},{4,2},{5,3},{6,4},{7,5},{8,14},{9,15},{10,... | collective-permute-start | bytes 1966088 | tf_op jit(solution)/shard_map/ppermute | solution.py:40
  88.0 19.3 %collective-permute-start.34 = (bf16[128,2560]{1,0:T(8,128)(2,1)S(1)}, bf16[128,2560]{1,0:T(8,128)(2,1)S(1)}, u32[]{:S(2)}, u32[]{:S(2)}) collective-permute-start(bf16[128,2560]{1,0:T(8,128)(2,1)S(1)} %get-tuple-element.88), channel_id=1, source_target_pairs={{0,2},{1,3},{2,4},{3,5},{4,6},{5,7},{6,0},{7,1},{8,10},{9,11},{10,... | collective-permute-start | bytes 1966088 | tf_op jit(solution)/shard_map/ppermute | solution.py:40
  94.6 12.8 %collective-permute-start.35 = (bf16[64,2560]{1,0:T(8,128)(2,1)S(1)}, bf16[64,2560]{1,0:T(8,128)(2,1)S(1)}, u32[]{:S(2)}, u32[]{:S(2)}) collective-permute-start(bf16[64,2560]{1,0:T(8,128)(2,1)S(1)} %get-tuple-element.93), channel_id=1, source_target_pairs={{0,65},{1,64},{2,67},{3,66},{4,69},{5,68},{6,71},{7,70},{8,73},{9,... | collective-permute-start | bytes 983048 | tf_op jit(solution)/shard_map/ppermute | solution.py:40
  105.6 12.2 %collective-permute-start.32 = (bf16[72,2560]{1,0:T(8,128)(2,1)S(1)}, bf16[72,2560]{1,0:T(8,128)(2,1)S(1)}, u32[]{:S(2)}, u32[]{:S(2)}) collective-permute-start(bf16[72,2560]{1,0:T(8,128)(2,1)S(1)} %get-tuple-element.86), channel_id=1, source_target_pairs={{0,64},{1,65},{2,66},{3,67},{4,68},{5,69},{6,70},{7,71},{8,72},{9,... | collective-permute-start | bytes 1105928 | tf_op jit(solution)/shard_map/ppermute | solution.py:40
  107.3 10.5 %collective-permute-start.31 = (bf16[72,2560]{1,0:T(8,128)(2,1)S(1)}, bf16[72,2560]{1,0:T(8,128)(2,1)S(1)}, u32[]{:S(2)}, u32[]{:S(2)}) collective-permute-start(bf16[72,2560]{1,0:T(8,128)(2,1)S(1)} %get-tuple-element.85), channel_id=1, source_target_pairs={{0,32},{1,33},{2,34},{3,35},{4,36},{5,37},{6,38},{7,39},{8,40},{9,... | collective-permute-start | bytes 1105928 | tf_op jit(solution)/shard_map/ppermute | solution.py:40
  107.5 11.3 %collective-permute-start.36 = (bf16[64,2560]{1,0:T(8,128)(2,1)S(1)}, bf16[64,2560]{1,0:T(8,128)(2,1)S(1)}, u32[]{:S(2)}, u32[]{:S(2)}) collective-permute-start(bf16[64,2560]{1,0:T(8,128)(2,1)S(1)} %get-tuple-element.94), channel_id=1, source_target_pairs={{0,4},{1,5},{2,6},{3,7},{4,0},{5,1},{6,2},{7,3},{8,12},{9,13},{10,... | collective-permute-start | bytes 983048 | tf_op jit(solution)/shard_map/ppermute | solution.py:40
  108.1 10.7 %collective-permute-start.37 = (bf16[64,2560]{1,0:T(8,128)(2,1)S(1)}, bf16[64,2560]{1,0:T(8,128)(2,1)S(1)}, u32[]{:S(2)}, u32[]{:S(2)}) collective-permute-start(bf16[64,2560]{1,0:T(8,128)(2,1)S(1)} %get-tuple-element.95), channel_id=1, source_target_pairs={{0,65},{1,64},{2,67},{3,66},{4,69},{5,68},{6,71},{7,70},{8,73},{9,... | collective-permute-start | bytes 983048 | tf_op jit(solution)/shard_map/ppermute | solution.py:40

commit v8 on v7

--- a/solution.py
+++ b/solution.py
@@ -109,7 +109,7 @@
 
 NT = (((1,), (1,)), ((), ()))
 NN = (((1,), (0,)), ((), ()))
-TILE = 384
+TILE = 576
 WIDE = 512
 STATS = (8, 512)
 

time: 120 us -> 120 us (level)
  no operation moved by 1% of the time
where the time goes in v8:
time: 120 us
  starting transfers between devices  50.6 us (42%)
  waiting for transfers between devices  45 us (38%)
  Pallas kernels  21.4 us (18%)
  local copies, waits for them, and re-layouts  1.82 us (2%)
    ppermute x38, starting transfers between devices, send(): return lax.ppermute(a, AXES, to)  50.6 us
    ppermute x38, waiting for transfers between devices, send(): return lax.ppermute(a, AXES, to)  45 us
    pallas_call x17, Pallas kernels, kernel_call(): pl.pallas_call(body, in_specs=[VMEM] * len(arrays), out_specs=[VMEM] * le...  21.4 us
  transfers between devices with their start and end apart: 38, of which 20 were waited for; matrix products, arithmetic and copies ran while one was open for 1% of the time, Pallas kernels for 15%

profile of v8, /device:TPU:0, one launch (start us, length us, event | category | flops | bytes accessed | tf_op | source)
XLA Modules:
  0.0 119.7 jit_solution(12185620814940187040)
XLA Ops:
  0.6 1.6 %collective-permute-start.6 = (bf16[64,2560]{1,0:T(8,128)(2,1)}, bf16[64,2560]{1,0:T(8,128)(2,1)S(1)}, u32[]{:S(2)}, u32[]{:S(2)}) collective-permute-start(bf16[64,2560]{1,0:T(8,128)(2,1)} %refs_0_.1), channel_id=1, source_target_pairs={{0,2},{1,3},{2,4},{3,5},{4,6},{5,7},{6,0},{7,1},{8,10},{9,11},{10,... | collective-permute-start | bytes 983048 | tf_op jit(solution)/shard_map/ppermute | solution.py:40
  2.3 3.0 %collective-permute-start.5 = (bf16[64,2560]{1,0:T(8,128)(2,1)}, bf16[64,2560]{1,0:T(8,128)(2,1)S(1)}, u32[]{:S(2)}, u32[]{:S(2)}) collective-permute-start(bf16[64,2560]{1,0:T(8,128)(2,1)} %refs_0_.1), channel_id=1, source_target_pairs={{0,65},{1,64},{2,67},{3,66},{4,69},{5,68},{6,71},{7,70},{8,73},{9,... | collective-permute-start | bytes 983048 | tf_op jit(solution)/shard_map/ppermute | solution.py:40
  5.3 1.7 %collective-permute-start.7 = (bf16[64,2560]{1,0:T(8,128)(2,1)}, bf16[64,2560]{1,0:T(8,128)(2,1)S(1)}, u32[]{:S(2)}, u32[]{:S(2)}) collective-permute-start(bf16[64,2560]{1,0:T(8,128)(2,1)} %refs_0_.1), channel_id=1, source_target_pairs={{0,6},{1,7},{2,0},{3,1},{4,2},{5,3},{6,4},{7,5},{8,14},{9,15},{10,... | collective-permute-start | bytes 983048 | tf_op jit(solution)/shard_map/ppermute | solution.py:40
  7.2 1.1 fusion
  8.3 1.7 %collective-permute-start.2 = (bf16[64,2560]{1,0:T(8,128)(2,1)S(1)}, bf16[64,2560]{1,0:T(8,128)(2,1)S(1)}, u32[]{:S(2)}, u32[]{:S(2)}) collective-permute-start(bf16[64,2560]{1,0:T(8,128)(2,1)S(1)} %get-tuple-element.61.refs_0_), channel_id=1, source_target_pairs={{0,6},{1,7},{2,0},{3,1},{4,2},{5,3},{6,4},{7,5},{8,14},{9,15},{10,... | collective-permute-start | bytes 983048 | tf_op jit(solution)/shard_map/ppermute | solution.py:40
  10.0 3.0 %collective-permute-done.near = s32[512]{0:T(512)S(1)} collective-permute-done((s32[512]{0:T(512)}, s32[512]{0:T(512)S(1)}, u32[]{:S(2)}, u32[]{:S(2)}) %collective-permute-start) | collective-permute-done | bytes 2080 | tf_op jit(solution)/shard_map/ppermute | solution.py:40
  13.0 0.7 copy-done.1
  13.9 1.6 %collective-permute-start.13 = (bf16[64,2560]{1,0:T(8,128)(2,1)S(1)}, bf16[64,2560]{1,0:T(8,128)(2,1)S(1)}, u32[]{:S(2)}, u32[]{:S(2)}) collective-permute-start(bf16[64,2560]{1,0:T(8,128)(2,1)S(1)} %get-tuple-element.60.refs_0_), channel_id=1, source_target_pairs={{0,2},{1,3},{2,4},{3,5},{4,6},{5,7},{6,0},{7,1},{8,10},{9,11},{10,... | collective-permute-start | bytes 983048 | tf_op jit(solution)/shard_map/ppermute | solution.py:40
  15.4 2.9 %collective-permute-start.1 = (bf16[64,2560]{1,0:T(8,128)(2,1)S(1)}, bf16[64,2560]{1,0:T(8,128)(2,1)S(1)}, u32[]{:S(2)}, u32[]{:S(2)}) collective-permute-start(bf16[64,2560]{1,0:T(8,128)(2,1)S(1)} %get-tuple-element.61.refs_0_), channel_id=1, source_target_pairs={{0,65},{1,64},{2,67},{3,66},{4,69},{5,68},{6,71},{7,70},{8,73},{9,... | collective-permute-start | bytes 983048 | tf_op jit(solution)/shard_map/ppermute | solution.py:40
  18.3 1.7 %collective-permute-start.9 = (bf16[64,2560]{1,0:T(8,128)(2,1)S(1)}, bf16[64,2560]{1,0:T(8,128)(2,1)S(1)}, u32[]{:S(2)}, u32[]{:S(2)}) collective-permute-start(bf16[64,2560]{1,0:T(8,128)(2,1)S(1)} %collective-permute-done.5.refs_1_), channel_id=1, source_target_pairs={{0,6},{1,7},{2,0},{3,1},{4,2},{5,3},{6,4},{7,5},{8,14},{9,15},{10,... | collective-permute-start | bytes 983048 | tf_op jit(solution)/shard_map/ppermute | solution.py:40
  20.1 0.3 collective-permute-start.10
  20.4 2.8 %collective-permute-done.2.refs_3_ = bf16[64,2560]{1,0:T(8,128)(2,1)S(1)} collective-permute-done((bf16[64,2560]{1,0:T(8,128)(2,1)S(1)}, bf16[64,2560]{1,0:T(8,128)(2,1)S(1)}, u32[]{:S(2)}, u32[]{:S(2)}) %collective-permute-start.2) | collective-permute-done | bytes 327712 | tf_op jit(solution)/shard_map/ppermute | solution.py:40
  23.2 0.2 collective-permute-start.11
  23.4 1.8 %collective-permute-done.13.refs_2_ = bf16[64,2560]{1,0:T(8,128)(2,1)S(1)} collective-permute-done((bf16[64,2560]{1,0:T(8,128)(2,1)S(1)}, bf16[64,2560]{1,0:T(8,128)(2,1)S(1)}, u32[]{:S(2)}, u32[]{:S(2)}) %collective-permute-start.13) | collective-permute-done | bytes 327712 | tf_op jit(solution)/shard_map/ppermute | solution.py:40
  25.2 1.1 collective-permute-start.3
  26.3 0.2 collective-permute-done.1.refs_1_
  26.5 1.2 %collective-permute-start.15 = (bf16[64,2560]{1,0:T(8,128)(2,1)S(1)}, bf16[64,2560]{1,0:T(8,128)(2,1)S(1)}, u32[]{:S(2)}, u32[]{:S(2)}) collective-permute-start(bf16[64,2560]{1,0:T(8,128)(2,1)S(1)} %get-tuple-element.61.refs_0_), channel_id=1, source_target_pairs={{0,2},{1,3},{2,4},{3,5},{4,6},{5,7},{6,0},{7,1},{8,10},{9,11},{10,... | collective-permute-start | bytes 983048 | tf_op jit(solution)/shard_map/ppermute | solution.py:40
  27.7 2.5 %collective-permute-done.9.refs_5_ = bf16[64,2560]{1,0:T(8,128)(2,1)S(1)} collective-permute-done((bf16[64,2560]{1,0:T(8,128)(2,1)S(1)}, bf16[64,2560]{1,0:T(8,128)(2,1)S(1)}, u32[]{:S(2)}, u32[]{:S(2)}) %collective-permute-start.9) | collective-permute-done | bytes 327712 | tf_op jit(solution)/shard_map/ppermute | solution.py:40
  30.2 1.2 %collective-permute-start.8 = (bf16[64,2560]{1,0:T(8,128)(2,1)S(1)}, bf16[64,2560]{1,0:T(8,128)(2,1)S(1)}, u32[]{:S(2)}, u32[]{:S(2)}) collective-permute-start(bf16[64,2560]{1,0:T(8,128)(2,1)S(1)} %collective-permute-done.6.refs_2_), channel_id=1, source_target_pairs={{0,65},{1,64},{2,67},{3,66},{4,69},{5,68},{6,71},{7,70},{8,73},{9,... | collective-permute-start | bytes 983048 | tf_op jit(solution)/shard_map/ppermute | solution.py:40
  31.4 0.8 collective-permute-done.10.refs_6_
  32.3 1.2 collective-permute-start.14
  33.5 3.7 %collective-permute-start.12 = (bf16[64,2560]{1,0:T(8,128)(2,1)S(1)}, bf16[64,2560]{1,0:T(8,128)(2,1)S(1)}, u32[]{:S(2)}, u32[]{:S(2)}) collective-permute-start(bf16[64,2560]{1,0:T(8,128)(2,1)S(1)} %collective-permute-done.10.refs_6_), channel_id=1, source_target_pairs={{0,65},{1,64},{2,67},{3,66},{4,69},{5,68},{6,71},{7,70},{8,73},{9,... | collective-permute-start | bytes 983048 | tf_op jit(solution)/shard_map/ppermute | solution.py:40
  37.2 1.5 %collective-permute-start.18 = (bf16[64,2560]{1,0:T(8,128)(2,1)S(1)}, bf16[64,2560]{1,0:T(8,128)(2,1)S(1)}, u32[]{:S(2)}, u32[]{:S(2)}) collective-permute-start(bf16[64,2560]{1,0:T(8,128)(2,1)S(1)} %collective-permute-done.13.refs_2_), channel_id=1, source_target_pairs={{0,2},{1,3},{2,4},{3,5},{4,6},{5,7},{6,0},{7,1},{8,10},{9,11},{10,... | collective-permute-start | bytes 983048 | tf_op jit(solution)/shard_map/ppermute | solution.py:40
  38.7 1.8 %collective-permute-start.4 = (bf16[64,2560]{1,0:T(8,128)(2,1)S(1)}, bf16[64,2560]{1,0:T(8,128)(2,1)S(1)}, u32[]{:S(2)}, u32[]{:S(2)}) collective-permute-start(bf16[64,2560]{1,0:T(8,128)(2,1)S(1)} %collective-permute-done.1.refs_1_), channel_id=1, source_target_pairs={{0,6},{1,7},{2,0},{3,1},{4,2},{5,3},{6,4},{7,5},{8,14},{9,15},{10,... | collective-permute-start | bytes 983048 | tf_op jit(solution)/shard_map/ppermute | solution.py:40
  40.5 1.6 %collective-permute-done.8.refs_4_ = bf16[64,2560]{1,0:T(8,128)(2,1)S(1)} collective-permute-done((bf16[64,2560]{1,0:T(8,128)(2,1)S(1)}, bf16[64,2560]{1,0:T(8,128)(2,1)S(1)}, u32[]{:S(2)}, u32[]{:S(2)}) %collective-permute-start.8) | collective-permute-done | bytes 327712 | tf_op jit(solution)/shard_map/ppermute | solution.py:40
  42.1 1.4 %collective-permute-start.16 = (bf16[64,2560]{1,0:T(8,128)(2,1)S(1)}, bf16[64,2560]{1,0:T(8,128)(2,1)S(1)}, u32[]{:S(2)}, u32[]{:S(2)}) collective-permute-start(bf16[64,2560]{1,0:T(8,128)(2,1)S(1)} %collective-permute-done.1.refs_1_), channel_id=1, source_target_pairs={{0,2},{1,3},{2,4},{3,5},{4,6},{5,7},{6,0},{7,1},{8,10},{9,11},{10,... | collective-permute-start | bytes 983048 | tf_op jit(solution)/shard_map/ppermute | solution.py:40
  43.5 0.8 collective-permute-done.14.refs_3_
  44.2 1.2 %collective-permute-start.17 = (bf16[64,2560]{1,0:T(8,128)(2,1)S(1)}, bf16[64,2560]{1,0:T(8,128)(2,1)S(1)}, u32[]{:S(2)}, u32[]{:S(2)}) collective-permute-start(bf16[64,2560]{1,0:T(8,128)(2,1)S(1)} %collective-permute-done.3.refs_6_), channel_id=1, source_target_pairs={{0,65},{1,64},{2,67},{3,66},{4,69},{5,68},{6,71},{7,70},{8,73},{9,... | collective-permute-start | bytes 983048 | tf_op jit(solution)/shard_map/ppermute | solution.py:40
  45.4 2.1 %collective-permute-done.12.refs_7_ = bf16[64,2560]{1,0:T(8,128)(2,1)S(1)} collective-permute-done((bf16[64,2560]{1,0:T(8,128)(2,1)S(1)}, bf16[64,2560]{1,0:T(8,128)(2,1)S(1)}, u32[]{:S(2)}, u32[]{:S(2)}) %collective-permute-start.12) | collective-permute-done | bytes 327712 | tf_op jit(solution)/shard_map/ppermute | solution.py:40
  47.6 1.7 %collective-permute-start.20 = (bf16[64,2560]{1,0:T(8,128)(2,1)S(1)}, bf16[64,2560]{1,0:T(8,128)(2,1)S(1)}, u32[]{:S(2)}, u32[]{:S(2)}) collective-permute-start(bf16[64,2560]{1,0:T(8,128)(2,1)S(1)} %collective-permute-done.11.refs_1_), channel_id=1, source_target_pairs={{0,6},{1,7},{2,0},{3,1},{4,2},{5,3},{6,4},{7,5},{8,14},{9,15},{10,... | collective-permute-start | bytes 983048 | tf_op jit(solution)/shard_map/ppermute | solution.py:40
  49.3 0.3 collective-permute-start.19
  49.6 1.7 %collective-permute-done.4.refs_5_ = bf16[64,2560]{1,0:T(8,128)(2,1)S(1)} collective-permute-done((bf16[64,2560]{1,0:T(8,128)(2,1)S(1)}, bf16[64,2560]{1,0:T(8,128)(2,1)S(1)}, u32[]{:S(2)}, u32[]{:S(2)}) %collective-permute-start.4) | collective-permute-done | bytes 327712 | tf_op jit(solution)/shard_map/ppermute | solution.py:40
  51.3 2.0 %collective-permute-start.21 = (bf16[64,2560]{1,0:T(8,128)(2,1)S(1)}, bf16[64,2560]{1,0:T(8,128)(2,1)S(1)}, u32[]{:S(2)}, u32[]{:S(2)}) collective-permute-start(bf16[64,2560]{1,0:T(8,128)(2,1)S(1)} %collective-permute-done.18.refs_2_), channel_id=1, source_target_pairs={{0,65},{1,64},{2,67},{3,66},{4,69},{5,68},{6,71},{7,70},{8,73},{9,... | collective-permute-start | bytes 983048 | tf_op jit(solution)/shard_map/ppermute | solution.py:40
  53.3 1.7 %shard_map.70.early = f32[1152,256]{1,0:T(8,128)S(1)} custom-call(bf16[1152,5120]{1,0:T(8,128)(2,1)S(1)} %bitcast.3, bf16[64,2560]{1,0:T(8,128)(2,1)S(1)} %get-tuple-element.60.refs_0_, bf16[64,2560]{1,0:T(8,128)(2,1)S(1)} %collective-permute-done.11.refs_1_, bf16[64,2560]{1,0:T(8,128)(2,1)S(1)} %collective-permute-done.13.refs_2_, ...), custom_call_target="tpu_custom_call" | custom-call | flops 20000000000 | bytes 20000000 | tf_op jit(solution)/shard_map/pallas_call | solution.py:69
  55.1 3.4 %shard_map.69 = (f32[1152,512]{1,0:T(8,128)S(1)}, bf16[512,2560]{1,0:T(8,128)(2,1)S(1)}, f32[8,512]{1,0:T(8,128)S(1)}) custom-call(s32[1,512]{1,0:T(1,128)S(1)} %shard_map.68.ids, bf16[1152,2560]{1,0:T(8,128)(2,1)S(1)} %bitcast.1, bf16[64,2560]{1,0:T(8,128)(2,1)S(1)} %copy-done, bf16[64,2560]{1,0:T(8,128)(2,1)S(1)} %collective-permute-done.5.refs_1_, ...), custom_call_target="tpu_custom_call" | custom-call | flops 20000000000 | bytes 20000000 | tf_op jit(solution)/shard_map/pallas_call | solution.py:69
  58.5 3.3 %shard_map.71 = (f32[1152,256]{1,0:T(8,128)S(1)}, f32[8,512]{1,0:T(8,128)S(1)}) custom-call(s32[1,512]{1,0:T(1,128)S(1)} %shard_map.68.ids, f32[8,512]{1,0:T(8,128)S(1)} %get-tuple-element.58.student_stats, f32[1152,256]{1,0:T(8,128)S(1)} %shard_map.70.early, bf16[1152,5120]{1,0:T(8,128)(2,1)S(1)} %bitcast.3, ...), custom_call_target="tpu_custom_call" | custom-call | flops 20000000000 | bytes 20000000 | tf_op jit(solution)/shard_map/pallas_call | solution.py:69
  61.8 1.9 %shard_map.72.refs_0_ = f32[8,512]{1,0:T(8,128)S(1)} custom-call(s32[1,512]{1,0:T(1,128)S(1)} %shard_map.68.ids, f32[8,512]{1,0:T(8,128)S(1)} %get-tuple-element.64.first_stats, bf16[1152,5120]{1,0:T(8,128)(2,1)S(1)} %bitcast.3, f32[1152,256]{1,0:T(8,128)S(1)} %get-tuple-element.65.logits, bf16[64,2560]{1,0:T(8,128)(2,1)S(1)} %collective-permute-done.19.refs_0_, ...), custom_call_target="tpu_custom_call" | custom-call | flops 20000000000 | bytes 20000000 | tf_op jit(solution)/shard_map/pallas_call | solution.py:69
  63.7 1.7 %collective-permute-start.24 = (f32[8,512]{1,0:T(8,128)S(1)}, f32[8,512]{1,0:T(8,128)S(1)}, u32[]{:S(2)}, u32[]{:S(2)}) collective-permute-start(f32[8,512]{1,0:T(8,128)S(1)} %shard_map.72.refs_0_), channel_id=1, source_target_pairs={{0,4},{1,5},{2,6},{3,7},{4,0},{5,1},{6,2},{7,3},{8,12},{9,13},{10,... | collective-permute-start | bytes 49160 | tf_op jit(solution)/shard_map/ppermute | solution.py:40
  65.3 2.3 %collective-permute-start.23 = (f32[8,512]{1,0:T(8,128)S(1)}, f32[8,512]{1,0:T(8,128)S(1)}, u32[]{:S(2)}, u32[]{:S(2)}) collective-permute-start(f32[8,512]{1,0:T(8,128)S(1)} %shard_map.72.refs_0_), channel_id=1, source_target_pairs={{0,6},{1,7},{2,0},{3,1},{4,2},{5,3},{6,4},{7,5},{8,14},{9,15},{10,... | collective-permute-start | bytes 49160 | tf_op jit(solution)/shard_map/ppermute | solution.py:40
  67.6 1.4 %collective-permute-done.24.refs_3_ = f32[8,512]{1,0:T(8,128)S(1)} collective-permute-done((f32[8,512]{1,0:T(8,128)S(1)}, f32[8,512]{1,0:T(8,128)S(1)}, u32[]{:S(2)}, u32[]{:S(2)}) %collective-permute-start.24) | collective-permute-done | bytes 16416 | tf_op jit(solution)/shard_map/ppermute | solution.py:40
  69.1 3.5 %collective-permute-done.22.refs_1_ = f32[8,512]{1,0:T(8,128)S(1)} collective-permute-done((f32[8,512]{1,0:T(8,128)S(1)}, f32[8,512]{1,0:T(8,128)S(1)}, u32[]{:S(2)}, u32[]{:S(2)}) %collective-permute-start.22) | collective-permute-done | bytes 16416 | tf_op jit(solution)/shard_map/ppermute | solution.py:40
  72.7 1.6 %collective-permute-start.25 = (f32[8,512]{1,0:T(8,128)S(1)}, f32[8,512]{1,0:T(8,128)S(1)}, u32[]{:S(2)}, u32[]{:S(2)}) collective-permute-start(f32[8,512]{1,0:T(8,128)S(1)} %shard_map.73.refs_0_), channel_id=1, source_target_pairs={{0,65},{1,64},{2,67},{3,66},{4,69},{5,68},{6,71},{7,70},{8,73},{9,... | collective-permute-start | bytes 49160 | tf_op jit(solution)/shard_map/ppermute | solution.py:40
  74.3 3.4 %collective-permute-done.25.refs_1_ = f32[8,512]{1,0:T(8,128)S(1)} collective-permute-done((f32[8,512]{1,0:T(8,128)S(1)}, f32[8,512]{1,0:T(8,128)S(1)}, u32[]{:S(2)}, u32[]{:S(2)}) %collective-permute-start.25) | collective-permute-done | bytes 16416 | tf_op jit(solution)/shard_map/ppermute | solution.py:40
  77.8 0.6 shard_map.75
  78.5 1.7 %shard_map.76.own = f32[576,2560]{1,0:T(8,128)S(1)} custom-call(bf16[576,512]{1,0:T(8,128)(2,1)S(1)} %get-tuple-element.73.grad, bf16[512,2560]{1,0:T(8,128)(2,1)S(1)} %get-tuple-element.72.hidden), custom_call_target="tpu_custom_call" | custom-call | flops 1000000000 | bytes 1000000 | tf_op jit(solution)/shard_map/pallas_call | solution.py:69
  80.2 0.3 collective-permute-done.26.grad
  80.5 1.1 shard_map.77
  81.7 4.1 %collective-permute-start.29 = (bf16[144,2560]{1,0:T(8,128)(2,1)S(1)}, bf16[144,2560]{1,0:T(8,128)(2,1)S(1)}, u32[]{:S(2)}, u32[]{:S(2)}) collective-permute-start(bf16[144,2560]{1,0:T(8,128)(2,1)S(1)} %get-tuple-element.81), channel_id=1, source_target_pairs={{0,48},{1,49},{2,50},{3,51},{4,52},{5,53},{6,54},{7,55},{8,56},{9,... | collective-permute-start | bytes 2211848 | tf_op jit(solution)/shard_map/ppermute | solution.py:40
  85.8 2.1 %shard_map.79 = (bf16[128,2560]{1,0:T(8,128)(2,1)S(1)}, bf16[128,2560]{1,0:T(8,128)(2,1)S(1)}) custom-call(s32[1,512]{1,0:T(1,128)S(1)} %shard_map.68.ids, f32[8,512]{1,0:T(8,128)S(1)} %shard_map.74.total, f32[1152,512]{1,0:T(8,128)S(1)} %get-tuple-element.70.logits, bf16[1152,2560]{1,0:T(8,128)(2,1)S(1)} %bitcast.1), custom_call_target="tpu_custom_call" | custom-call | flops 20000000000 | bytes 20000000 | tf_op jit(solution)/shard_map/pallas_call | solution.py:69
  88.1 2.0 %collective-permute-start.34 = (bf16[128,2560]{1,0:T(8,128)(2,1)S(1)}, bf16[128,2560]{1,0:T(8,128)(2,1)S(1)}, u32[]{:S(2)}, u32[]{:S(2)}) collective-permute-start(bf16[128,2560]{1,0:T(8,128)(2,1)S(1)} %get-tuple-element.88), channel_id=1, source_target_pairs={{0,2},{1,3},{2,4},{3,5},{4,6},{5,7},{6,0},{7,1},{8,10},{9,11},{10,... | collective-permute-start | bytes 1966088 | tf_op jit(solution)/shard_map/ppermute | solution.py:40
  90.1 0.8 shard_map.80
  90.8 1.6 %collective-permute-done.28.far_near = bf16[72,2560]{1,0:T(8,128)(2,1)S(1)} collective-permute-done((bf16[72,2560]{1,0:T(8,128)(2,1)S(1)}, bf16[72,2560]{1,0:T(8,128)(2,1)S(1)}, u32[]{:S(2)}, u32[]{:S(2)}) %collective-permute-start.28) | collective-permute-done | bytes 368672 | tf_op jit(solution)/shard_map/ppermute | solution.py:40
  92.4 2.1 %shard_map.78 = (f32[64,2560]{1,0:T(8,128)S(1)}, f32[64,2560]{1,0:T(8,128)S(1)}, f32[64,2560]{1,0:T(8,128)S(1)}, bf16[64,2560]{1,0:T(8,128)(2,1)S(1)}) custom-call(s32[1,512]{1,0:T(1,128)S(1)} %shard_map.68.ids, f32[8,512]{1,0:T(8,128)S(1)} %shard_map.74.total, f32[1152,512]{1,0:T(8,128)S(1)} %get-tuple-element.70.logits, bf16[1152,2560]{1,0:T(8,128)(2,1)S(1)} %bitcast.1), custom_call_target="tpu_custom_call" | custom-call | flops 1000000000 | bytes 1000000 | tf_op jit(solution)/shard_map/pallas_call | solution.py:69
  94.6 1.6 %collective-permute-start.35 = (bf16[64,2560]{1,0:T(8,128)(2,1)S(1)}, bf16[64,2560]{1,0:T(8,128)(2,1)S(1)}, u32[]{:S(2)}, u32[]{:S(2)}) collective-permute-start(bf16[64,2560]{1,0:T(8,128)(2,1)S(1)} %get-tuple-element.93), channel_id=1, source_target_pairs={{0,65},{1,64},{2,67},{3,66},{4,69},{5,68},{6,71},{7,70},{8,73},{9,... | collective-permute-start | bytes 983048 | tf_op jit(solution)/shard_map/ppermute | solution.py:40
  96.2 5.8 %collective-permute-done.29.lefts = bf16[144,2560]{1,0:T(8,128)(2,1)S(1)} collective-permute-done((bf16[144,2560]{1,0:T(8,128)(2,1)S(1)}, bf16[144,2560]{1,0:T(8,128)(2,1)S(1)}, u32[]{:S(2)}, u32[]{:S(2)}) %collective-permute-start.29) | collective-permute-done | bytes 737312 | tf_op jit(solution)/shard_map/ppermute | solution.py:40
  102.0 3.4 %collective-permute-done.30.rights = bf16[144,2560]{1,0:T(8,128)(2,1)S(1)} collective-permute-done((bf16[144,2560]{1,0:T(8,128)(2,1)S(1)}, bf16[144,2560]{1,0:T(8,128)(2,1)S(1)}, u32[]{:S(2)}, u32[]{:S(2)}) %collective-permute-start.30) | collective-permute-done | bytes 737312 | tf_op jit(solution)/shard_map/ppermute | solution.py:40
  105.4 0.2 shard_map.81
  105.6 1.7 %collective-permute-start.32 = (bf16[72,2560]{1,0:T(8,128)(2,1)S(1)}, bf16[72,2560]{1,0:T(8,128)(2,1)S(1)}, u32[]{:S(2)}, u32[]{:S(2)}) collective-permute-start(bf16[72,2560]{1,0:T(8,128)(2,1)S(1)} %get-tuple-element.86), channel_id=1, source_target_pairs={{0,64},{1,65},{2,66},{3,67},{4,68},{5,69},{6,70},{7,71},{8,72},{9,... | collective-permute-start | bytes 1105928 | tf_op jit(solution)/shard_map/ppermute | solution.py:40
  107.3 0.2 shard_map.83
  107.5 0.6 collective-permute-start.36
  108.1 1.5 %collective-permute-start.37 = (bf16[64,2560]{1,0:T(8,128)(2,1)S(1)}, bf16[64,2560]{1,0:T(8,128)(2,1)S(1)}, u32[]{:S(2)}, u32[]{:S(2)}) collective-permute-start(bf16[64,2560]{1,0:T(8,128)(2,1)S(1)} %get-tuple-element.95), channel_id=1, source_target_pairs={{0,65},{1,64},{2,67},{3,66},{4,69},{5,68},{6,71},{7,70},{8,73},{9,... | collective-permute-start | bytes 983048 | tf_op jit(solution)/shard_map/ppermute | solution.py:40
  109.6 8.2 %collective-permute-done.31.far = bf16[72,2560]{1,0:T(8,128)(2,1)S(1)} collective-permute-done((bf16[72,2560]{1,0:T(8,128)(2,1)S(1)}, bf16[72,2560]{1,0:T(8,128)(2,1)S(1)}, u32[]{:S(2)}, u32[]{:S(2)}) %collective-permute-start.31) | collective-permute-done | bytes 368672 | tf_op jit(solution)/shard_map/ppermute | solution.py:40
  117.8 1.0 shard_map.82
  118.8 0.9 shard_map.84
  (46 shorter events, 0.9 us)
Async XLA Ops:
  0.6 19.5 %collective-permute-start.6 = (bf16[64,2560]{1,0:T(8,128)(2,1)}, bf16[64,2560]{1,0:T(8,128)(2,1)S(1)}, u32[]{:S(2)}, u32[]{:S(2)}) collective-permute-start(bf16[64,2560]{1,0:T(8,128)(2,1)} %refs_0_.1), channel_id=1, source_target_pairs={{0,2},{1,3},{2,4},{3,5},{4,6},{5,7},{6,0},{7,1},{8,10},{9,11},{10,... | collective-permute-start | bytes 983048 | tf_op jit(solution)/shard_map/ppermute | solution.py:40
  2.3 13.1 %collective-permute-start.5 = (bf16[64,2560]{1,0:T(8,128)(2,1)}, bf16[64,2560]{1,0:T(8,128)(2,1)S(1)}, u32[]{:S(2)}, u32[]{:S(2)}) collective-permute-start(bf16[64,2560]{1,0:T(8,128)(2,1)} %refs_0_.1), channel_id=1, source_target_pairs={{0,65},{1,64},{2,67},{3,66},{4,69},{5,68},{6,71},{7,70},{8,73},{9,... | collective-permute-start | bytes 983048 | tf_op jit(solution)/shard_map/ppermute | solution.py:40
  5.3 13.1 %collective-permute-start.7 = (bf16[64,2560]{1,0:T(8,128)(2,1)}, bf16[64,2560]{1,0:T(8,128)(2,1)S(1)}, u32[]{:S(2)}, u32[]{:S(2)}) collective-permute-start(bf16[64,2560]{1,0:T(8,128)(2,1)} %refs_0_.1), channel_id=1, source_target_pairs={{0,6},{1,7},{2,0},{3,1},{4,2},{5,3},{6,4},{7,5},{8,14},{9,15},{10,... | collective-permute-start | bytes 983048 | tf_op jit(solution)/shard_map/ppermute | solution.py:40
  7.0 6.0 %collective-permute-start = (s32[512]{0:T(512)}, s32[512]{0:T(512)S(1)}, u32[]{:S(2)}, u32[]{:S(2)}) collective-permute-start(s32[512]{0:T(512)} %own.1), channel_id=1, source_target_pairs={{0,65},{1,64},{2,67},{3,66},{4,69},{5,68},{6,71},{7,70},{8,73},{9,... | collective-permute-start | bytes 6152 | tf_op jit(solution)/shard_map/ppermute | solution.py:40
  8.3 45.0 %slice-start.2 = ((s8[11796480]{0:T(1024)(128)(4,1)}), s8[4194304]{0:T(1024)(128)(4,1)S(1)}, s32[]{:S(2)}) async-start(s8[11796480]{0:T(1024)(128)(4,1)} %bitcast.2), calls=%async_computation.2 | async-start | bytes 8388608
  8.3 45.0 %slice-start.3 = ((s8[11796480]{0:T(1024)(128)(4,1)}), s8[4194304]{0:T(1024)(128)(4,1)S(1)}, s32[]{:S(2)}) async-start(s8[11796480]{0:T(1024)(128)(4,1)} %bitcast.2), calls=%async_computation.3 | async-start | bytes 8388608
  8.3 45.0 %slice-start.4 = ((s8[11796480]{0:T(1024)(128)(4,1)}), s8[3407872]{0:T(1024)(128)(4,1)S(1)}, s32[]{:S(2)}) async-start(s8[11796480]{0:T(1024)(128)(4,1)} %bitcast.2), calls=%async_computation.4 | async-start | bytes 6815744
  8.3 14.8 %collective-permute-start.2 = (bf16[64,2560]{1,0:T(8,128)(2,1)S(1)}, bf16[64,2560]{1,0:T(8,128)(2,1)S(1)}, u32[]{:S(2)}, u32[]{:S(2)}) collective-permute-start(bf16[64,2560]{1,0:T(8,128)(2,1)S(1)} %get-tuple-element.61.refs_0_), channel_id=1, source_target_pairs={{0,6},{1,7},{2,0},{3,1},{4,2},{5,3},{6,4},{7,5},{8,14},{9,15},{10,... | collective-permute-start | bytes 983048 | tf_op jit(solution)/shard_map/ppermute | solution.py:40
  13.0 0.7 copy-start.1
  13.9 41.2 %slice-start = ((s8[5898240]{0:T(1024)(128)(4,1)}), s8[4194304]{0:T(1024)(128)(4,1)S(1)}, s32[]{:S(2)}) async-start(s8[5898240]{0:T(1024)(128)(4,1)} %bitcast), calls=%async_computation | async-start | bytes 8388608
  13.9 41.2 %slice-start.1 = ((s8[5898240]{0:T(1024)(128)(4,1)}), s8[1703936]{0:T(1024)(128)(4,1)S(1)}, s32[]{:S(2)}) async-start(s8[5898240]{0:T(1024)(128)(4,1)} %bitcast), calls=%async_computation.1 | async-start | bytes 3407872
  13.9 41.2 %copy-start = (bf16[64,2560]{1,0:T(8,128)(2,1)S(1)}, bf16[64,2560]{1,0:T(8,128)(2,1)}, u32[]{:S(2)}) copy-start(bf16[64,2560]{1,0:T(8,128)(2,1)} %refs_0_.1) | copy-start | bytes 983044
  13.9 11.4 %collective-permute-start.13 = (bf16[64,2560]{1,0:T(8,128)(2,1)S(1)}, bf16[64,2560]{1,0:T(8,128)(2,1)S(1)}, u32[]{:S(2)}, u32[]{:S(2)}) collective-permute-start(bf16[64,2560]{1,0:T(8,128)(2,1)S(1)} %get-tuple-element.60.refs_0_), channel_id=1, source_target_pairs={{0,2},{1,3},{2,4},{3,5},{4,6},{5,7},{6,0},{7,1},{8,10},{9,11},{10,... | collective-permute-start | bytes 983048 | tf_op jit(solution)/shard_map/ppermute | solution.py:40
  15.4 11.1 %collective-permute-start.1 = (bf16[64,2560]{1,0:T(8,128)(2,1)S(1)}, bf16[64,2560]{1,0:T(8,128)(2,1)S(1)}, u32[]{:S(2)}, u32[]{:S(2)}) collective-permute-start(bf16[64,2560]{1,0:T(8,128)(2,1)S(1)} %get-tuple-element.61.refs_0_), channel_id=1, source_target_pairs={{0,65},{1,64},{2,67},{3,66},{4,69},{5,68},{6,71},{7,70},{8,73},{9,... | collective-permute-start | bytes 983048 | tf_op jit(solution)/shard_map/ppermute | solution.py:40
  18.3 11.8 %collective-permute-start.9 = (bf16[64,2560]{1,0:T(8,128)(2,1)S(1)}, bf16[64,2560]{1,0:T(8,128)(2,1)S(1)}, u32[]{:S(2)}, u32[]{:S(2)}) collective-permute-start(bf16[64,2560]{1,0:T(8,128)(2,1)S(1)} %collective-permute-done.5.refs_1_), channel_id=1, source_target_pairs={{0,6},{1,7},{2,0},{3,1},{4,2},{5,3},{6,4},{7,5},{8,14},{9,15},{10,... | collective-permute-start | bytes 983048 | tf_op jit(solution)/shard_map/ppermute | solution.py:40
  20.1 12.2 %collective-permute-start.10 = (bf16[64,2560]{1,0:T(8,128)(2,1)S(1)}, bf16[64,2560]{1,0:T(8,128)(2,1)S(1)}, u32[]{:S(2)}, u32[]{:S(2)}) collective-permute-start(bf16[64,2560]{1,0:T(8,128)(2,1)S(1)} %collective-permute-done.6.refs_2_), channel_id=1, source_target_pairs={{0,2},{1,3},{2,4},{3,5},{4,6},{5,7},{6,0},{7,1},{8,10},{9,11},{10,... | collective-permute-start | bytes 983048 | tf_op jit(solution)/shard_map/ppermute | solution.py:40
  23.2 10.4 %collective-permute-start.11 = (bf16[64,2560]{1,0:T(8,128)(2,1)S(1)}, bf16[64,2560]{1,0:T(8,128)(2,1)S(1)}, u32[]{:S(2)}, u32[]{:S(2)}) collective-permute-start(bf16[64,2560]{1,0:T(8,128)(2,1)S(1)} %get-tuple-element.60.refs_0_), channel_id=1, source_target_pairs={{0,65},{1,64},{2,67},{3,66},{4,69},{5,68},{6,71},{7,70},{8,73},{9,... | collective-permute-start | bytes 983048 | tf_op jit(solution)/shard_map/ppermute | solution.py:40
  25.2 12.0 %collective-permute-start.3 = (bf16[64,2560]{1,0:T(8,128)(2,1)S(1)}, bf16[64,2560]{1,0:T(8,128)(2,1)S(1)}, u32[]{:S(2)}, u32[]{:S(2)}) collective-permute-start(bf16[64,2560]{1,0:T(8,128)(2,1)S(1)} %collective-permute-done.2.refs_3_), channel_id=1, source_target_pairs={{0,6},{1,7},{2,0},{3,1},{4,2},{5,3},{6,4},{7,5},{8,14},{9,15},{10,... | collective-permute-start | bytes 983048 | tf_op jit(solution)/shard_map/ppermute | solution.py:40
  26.5 12.2 %collective-permute-start.15 = (bf16[64,2560]{1,0:T(8,128)(2,1)S(1)}, bf16[64,2560]{1,0:T(8,128)(2,1)S(1)}, u32[]{:S(2)}, u32[]{:S(2)}) collective-permute-start(bf16[64,2560]{1,0:T(8,128)(2,1)S(1)} %get-tuple-element.61.refs_0_), channel_id=1, source_target_pairs={{0,2},{1,3},{2,4},{3,5},{4,6},{5,7},{6,0},{7,1},{8,10},{9,11},{10,... | collective-permute-start | bytes 983048 | tf_op jit(solution)/shard_map/ppermute | solution.py:40
  30.2 11.9 %collective-permute-start.8 = (bf16[64,2560]{1,0:T(8,128)(2,1)S(1)}, bf16[64,2560]{1,0:T(8,128)(2,1)S(1)}, u32[]{:S(2)}, u32[]{:S(2)}) collective-permute-start(bf16[64,2560]{1,0:T(8,128)(2,1)S(1)} %collective-permute-done.6.refs_2_), channel_id=1, source_target_pairs={{0,65},{1,64},{2,67},{3,66},{4,69},{5,68},{6,71},{7,70},{8,73},{9,... | collective-permute-start | bytes 983048 | tf_op jit(solution)/shard_map/ppermute | solution.py:40
  32.3 12.0 %collective-permute-start.14 = (bf16[64,2560]{1,0:T(8,128)(2,1)S(1)}, bf16[64,2560]{1,0:T(8,128)(2,1)S(1)}, u32[]{:S(2)}, u32[]{:S(2)}) collective-permute-start(bf16[64,2560]{1,0:T(8,128)(2,1)S(1)} %get-tuple-element.60.refs_0_), channel_id=1, source_target_pairs={{0,6},{1,7},{2,0},{3,1},{4,2},{5,3},{6,4},{7,5},{8,14},{9,15},{10,... | collective-permute-start | bytes 983048 | tf_op jit(solution)/shard_map/ppermute | solution.py:40
  33.5 14.0 %collective-permute-start.12 = (bf16[64,2560]{1,0:T(8,128)(2,1)S(1)}, bf16[64,2560]{1,0:T(8,128)(2,1)S(1)}, u32[]{:S(2)}, u32[]{:S(2)}) collective-permute-start(bf16[64,2560]{1,0:T(8,128)(2,1)S(1)} %collective-permute-done.10.refs_6_), channel_id=1, source_target_pairs={{0,65},{1,64},{2,67},{3,66},{4,69},{5,68},{6,71},{7,70},{8,73},{9,... | collective-permute-start | bytes 983048 | tf_op jit(solution)/shard_map/ppermute | solution.py:40
  37.2 12.0 %collective-permute-start.18 = (bf16[64,2560]{1,0:T(8,128)(2,1)S(1)}, bf16[64,2560]{1,0:T(8,128)(2,1)S(1)}, u32[]{:S(2)}, u32[]{:S(2)}) collective-permute-start(bf16[64,2560]{1,0:T(8,128)(2,1)S(1)} %collective-permute-done.13.refs_2_), channel_id=1, source_target_pairs={{0,2},{1,3},{2,4},{3,5},{4,6},{5,7},{6,0},{7,1},{8,10},{9,11},{10,... | collective-permute-start | bytes 983048 | tf_op jit(solution)/shard_map/ppermute | solution.py:40
  38.7 12.5 %collective-permute-start.4 = (bf16[64,2560]{1,0:T(8,128)(2,1)S(1)}, bf16[64,2560]{1,0:T(8,128)(2,1)S(1)}, u32[]{:S(2)}, u32[]{:S(2)}) collective-permute-start(bf16[64,2560]{1,0:T(8,128)(2,1)S(1)} %collective-permute-done.1.refs_1_), channel_id=1, source_target_pairs={{0,6},{1,7},{2,0},{3,1},{4,2},{5,3},{6,4},{7,5},{8,14},{9,15},{10,... | collective-permute-start | bytes 983048 | tf_op jit(solution)/shard_map/ppermute | solution.py:40
  42.1 16.4 %collective-permute-start.16 = (bf16[64,2560]{1,0:T(8,128)(2,1)S(1)}, bf16[64,2560]{1,0:T(8,128)(2,1)S(1)}, u32[]{:S(2)}, u32[]{:S(2)}) collective-permute-start(bf16[64,2560]{1,0:T(8,128)(2,1)S(1)} %collective-permute-done.1.refs_1_), channel_id=1, source_target_pairs={{0,2},{1,3},{2,4},{3,5},{4,6},{5,7},{6,0},{7,1},{8,10},{9,11},{10,... | collective-permute-start | bytes 983048 | tf_op jit(solution)/shard_map/ppermute | solution.py:40
  44.2 14.2 %collective-permute-start.17 = (bf16[64,2560]{1,0:T(8,128)(2,1)S(1)}, bf16[64,2560]{1,0:T(8,128)(2,1)S(1)}, u32[]{:S(2)}, u32[]{:S(2)}) collective-permute-start(bf16[64,2560]{1,0:T(8,128)(2,1)S(1)} %collective-permute-done.3.refs_6_), channel_id=1, source_target_pairs={{0,65},{1,64},{2,67},{3,66},{4,69},{5,68},{6,71},{7,70},{8,73},{9,... | collective-permute-start | bytes 983048 | tf_op jit(solution)/shard_map/ppermute | solution.py:40
  47.6 14.2 %collective-permute-start.20 = (bf16[64,2560]{1,0:T(8,128)(2,1)S(1)}, bf16[64,2560]{1,0:T(8,128)(2,1)S(1)}, u32[]{:S(2)}, u32[]{:S(2)}) collective-permute-start(bf16[64,2560]{1,0:T(8,128)(2,1)S(1)} %collective-permute-done.11.refs_1_), channel_id=1, source_target_pairs={{0,6},{1,7},{2,0},{3,1},{4,2},{5,3},{6,4},{7,5},{8,14},{9,15},{10,... | collective-permute-start | bytes 983048 | tf_op jit(solution)/shard_map/ppermute | solution.py:40
  49.3 12.5 %collective-permute-start.19 = (bf16[64,2560]{1,0:T(8,128)(2,1)S(1)}, bf16[64,2560]{1,0:T(8,128)(2,1)S(1)}, u32[]{:S(2)}, u32[]{:S(2)}) collective-permute-start(bf16[64,2560]{1,0:T(8,128)(2,1)S(1)} %collective-permute-done.11.refs_1_), channel_id=1, source_target_pairs={{0,2},{1,3},{2,4},{3,5},{4,6},{5,7},{6,0},{7,1},{8,10},{9,11},{10,... | collective-permute-start | bytes 983048 | tf_op jit(solution)/shard_map/ppermute | solution.py:40
  51.3 10.5 %collective-permute-start.21 = (bf16[64,2560]{1,0:T(8,128)(2,1)S(1)}, bf16[64,2560]{1,0:T(8,128)(2,1)S(1)}, u32[]{:S(2)}, u32[]{:S(2)}) collective-permute-start(bf16[64,2560]{1,0:T(8,128)(2,1)S(1)} %collective-permute-done.18.refs_2_), channel_id=1, source_target_pairs={{0,65},{1,64},{2,67},{3,66},{4,69},{5,68},{6,71},{7,70},{8,73},{9,... | collective-permute-start | bytes 983048 | tf_op jit(solution)/shard_map/ppermute | solution.py:40
  63.7 5.3 %collective-permute-start.24 = (f32[8,512]{1,0:T(8,128)S(1)}, f32[8,512]{1,0:T(8,128)S(1)}, u32[]{:S(2)}, u32[]{:S(2)}) collective-permute-start(f32[8,512]{1,0:T(8,128)S(1)} %shard_map.72.refs_0_), channel_id=1, source_target_pairs={{0,4},{1,5},{2,6},{3,7},{4,0},{5,1},{6,2},{7,3},{8,12},{9,13},{10,... | collective-permute-start | bytes 49160 | tf_op jit(solution)/shard_map/ppermute | solution.py:40
  65.3 3.7 %collective-permute-start.23 = (f32[8,512]{1,0:T(8,128)S(1)}, f32[8,512]{1,0:T(8,128)S(1)}, u32[]{:S(2)}, u32[]{:S(2)}) collective-permute-start(f32[8,512]{1,0:T(8,128)S(1)} %shard_map.72.refs_0_), channel_id=1, source_target_pairs={{0,6},{1,7},{2,0},{3,1},{4,2},{5,3},{6,4},{7,5},{8,14},{9,15},{10,... | collective-permute-start | bytes 49160 | tf_op jit(solution)/shard_map/ppermute | solution.py:40
  67.6 4.9 %collective-permute-start.22 = (f32[8,512]{1,0:T(8,128)S(1)}, f32[8,512]{1,0:T(8,128)S(1)}, u32[]{:S(2)}, u32[]{:S(2)}) collective-permute-start(f32[8,512]{1,0:T(8,128)S(1)} %shard_map.72.refs_0_), channel_id=1, source_target_pairs={{0,2},{1,3},{2,4},{3,5},{4,6},{5,7},{6,0},{7,1},{8,10},{9,11},{10,... | collective-permute-start | bytes 49160 | tf_op jit(solution)/shard_map/ppermute | solution.py:40
  67.6 12.8 %collective-permute-start.27 = (bf16[512,2560]{1,0:T(8,128)(2,1)S(1)}, bf16[512,2560]{1,0:T(8,128)(2,1)S(1)}, u32[]{:S(2)}, u32[]{:S(2)}) collective-permute-start(bf16[512,2560]{1,0:T(8,128)(2,1)S(1)} %get-tuple-element.72.hidden), channel_id=1, source_target_pairs={{0,8},{1,9},{2,10},{3,11},{4,12},{5,13},{6,14},{7,15},{8,0},{9,1},... | collective-permute-start | bytes 7864328 | tf_op jit(solution)/shard_map/ppermute | solution.py:40
  72.7 5.0 %collective-permute-start.25 = (f32[8,512]{1,0:T(8,128)S(1)}, f32[8,512]{1,0:T(8,128)S(1)}, u32[]{:S(2)}, u32[]{:S(2)}) collective-permute-start(f32[8,512]{1,0:T(8,128)S(1)} %shard_map.73.refs_0_), channel_id=1, source_target_pairs={{0,65},{1,64},{2,67},{3,66},{4,69},{5,68},{6,71},{7,70},{8,73},{9,... | collective-permute-start | bytes 49160 | tf_op jit(solution)/shard_map/ppermute | solution.py:40
  78.4 2.1 %collective-permute-start.26 = (bf16[576,512]{1,0:T(8,128)(2,1)S(1)}, bf16[576,512]{1,0:T(8,128)(2,1)S(1)}, u32[]{:S(2)}, u32[]{:S(2)}) collective-permute-start(bf16[576,512]{1,0:T(8,128)(2,1)S(1)} %get-tuple-element.71), channel_id=1, source_target_pairs={{0,8},{1,9},{2,10},{3,11},{4,12},{5,13},{6,14},{7,15},{8,0},{9,1},... | collective-permute-start | bytes 1769480 | tf_op jit(solution)/shard_map/ppermute | solution.py:40
  81.6 10.8 %collective-permute-start.28 = (bf16[72,2560]{1,0:T(8,128)(2,1)S(1)}, bf16[72,2560]{1,0:T(8,128)(2,1)S(1)}, u32[]{:S(2)}, u32[]{:S(2)}) collective-permute-start(bf16[72,2560]{1,0:T(8,128)(2,1)S(1)} %get-tuple-element.74), channel_id=1, source_target_pairs={{0,64},{1,65},{2,66},{3,67},{4,68},{5,69},{6,70},{7,71},{8,72},{9,... | collective-permute-start | bytes 1105928 | tf_op jit(solution)/shard_map/ppermute | solution.py:40
  81.7 20.2 %collective-permute-start.29 = (bf16[144,2560]{1,0:T(8,128)(2,1)S(1)}, bf16[144,2560]{1,0:T(8,128)(2,1)S(1)}, u32[]{:S(2)}, u32[]{:S(2)}) collective-permute-start(bf16[144,2560]{1,0:T(8,128)(2,1)S(1)} %get-tuple-element.81), channel_id=1, source_target_pairs={{0,48},{1,49},{2,50},{3,51},{4,52},{5,53},{6,54},{7,55},{8,56},{9,... | collective-permute-start | bytes 2211848 | tf_op jit(solution)/shard_map/ppermute | solution.py:40
  85.8 19.5 %collective-permute-start.30 = (bf16[144,2560]{1,0:T(8,128)(2,1)S(1)}, bf16[144,2560]{1,0:T(8,128)(2,1)S(1)}, u32[]{:S(2)}, u32[]{:S(2)}) collective-permute-start(bf16[144,2560]{1,0:T(8,128)(2,1)S(1)} %get-tuple-element.82), channel_id=1, source_target_pairs={{0,16},{1,17},{2,18},{3,19},{4,20},{5,21},{6,22},{7,23},{8,24},{9,... | collective-permute-start | bytes 2211848 | tf_op jit(solution)/shard_map/ppermute | solution.py:40
  88.0 19.4 %collective-permute-start.33 = (bf16[128,2560]{1,0:T(8,128)(2,1)S(1)}, bf16[128,2560]{1,0:T(8,128)(2,1)S(1)}, u32[]{:S(2)}, u32[]{:S(2)}) collective-permute-start(bf16[128,2560]{1,0:T(8,128)(2,1)S(1)} %get-tuple-element.78), channel_id=1, source_target_pairs={{0,6},{1,7},{2,0},{3,1},{4,2},{5,3},{6,4},{7,5},{8,14},{9,15},{10,... | collective-permute-start | bytes 1966088 | tf_op jit(solution)/shard_map/ppermute | solution.py:40
  88.1 19.3 %collective-permute-start.34 = (bf16[128,2560]{1,0:T(8,128)(2,1)S(1)}, bf16[128,2560]{1,0:T(8,128)(2,1)S(1)}, u32[]{:S(2)}, u32[]{:S(2)}) collective-permute-start(bf16[128,2560]{1,0:T(8,128)(2,1)S(1)} %get-tuple-element.88), channel_id=1, source_target_pairs={{0,2},{1,3},{2,4},{3,5},{4,6},{5,7},{6,0},{7,1},{8,10},{9,11},{10,... | collective-permute-start | bytes 1966088 | tf_op jit(solution)/shard_map/ppermute | solution.py:40
  94.6 12.8 %collective-permute-start.35 = (bf16[64,2560]{1,0:T(8,128)(2,1)S(1)}, bf16[64,2560]{1,0:T(8,128)(2,1)S(1)}, u32[]{:S(2)}, u32[]{:S(2)}) collective-permute-start(bf16[64,2560]{1,0:T(8,128)(2,1)S(1)} %get-tuple-element.93), channel_id=1, source_target_pairs={{0,65},{1,64},{2,67},{3,66},{4,69},{5,68},{6,71},{7,70},{8,73},{9,... | collective-permute-start | bytes 983048 | tf_op jit(solution)/shard_map/ppermute | solution.py:40
  105.6 12.2 %collective-permute-start.32 = (bf16[72,2560]{1,0:T(8,128)(2,1)S(1)}, bf16[72,2560]{1,0:T(8,128)(2,1)S(1)}, u32[]{:S(2)}, u32[]{:S(2)}) collective-permute-start(bf16[72,2560]{1,0:T(8,128)(2,1)S(1)} %get-tuple-element.86), channel_id=1, source_target_pairs={{0,64},{1,65},{2,66},{3,67},{4,68},{5,69},{6,70},{7,71},{8,72},{9,... | collective-permute-start | bytes 1105928 | tf_op jit(solution)/shard_map/ppermute | solution.py:40
  107.3 10.5 %collective-permute-start.31 = (bf16[72,2560]{1,0:T(8,128)(2,1)S(1)}, bf16[72,2560]{1,0:T(8,128)(2,1)S(1)}, u32[]{:S(2)}, u32[]{:S(2)}) collective-permute-start(bf16[72,2560]{1,0:T(8,128)(2,1)S(1)} %get-tuple-element.85), channel_id=1, source_target_pairs={{0,32},{1,33},{2,34},{3,35},{4,36},{5,37},{6,38},{7,39},{8,40},{9,... | collective-permute-start | bytes 1105928 | tf_op jit(solution)/shard_map/ppermute | solution.py:40
  107.5 11.3 %collective-permute-start.36 = (bf16[64,2560]{1,0:T(8,128)(2,1)S(1)}, bf16[64,2560]{1,0:T(8,128)(2,1)S(1)}, u32[]{:S(2)}, u32[]{:S(2)}) collective-permute-start(bf16[64,2560]{1,0:T(8,128)(2,1)S(1)} %get-tuple-element.94), channel_id=1, source_target_pairs={{0,4},{1,5},{2,6},{3,7},{4,0},{5,1},{6,2},{7,3},{8,12},{9,13},{10,... | collective-permute-start | bytes 983048 | tf_op jit(solution)/shard_map/ppermute | solution.py:40
  108.1 10.7 %collective-permute-start.37 = (bf16[64,2560]{1,0:T(8,128)(2,1)S(1)}, bf16[64,2560]{1,0:T(8,128)(2,1)S(1)}, u32[]{:S(2)}, u32[]{:S(2)}) collective-permute-start(bf16[64,2560]{1,0:T(8,128)(2,1)S(1)} %get-tuple-element.95), channel_id=1, source_target_pairs={{0,65},{1,64},{2,67},{3,66},{4,69},{5,68},{6,71},{7,70},{8,73},{9,... | collective-permute-start | bytes 983048 | tf_op jit(solution)/shard_map/ppermute | solution.py:40
